TPU v7x, 256 devices: a whole 4x4x8 slice. The times are simulated.
256 devices in a mesh: box: 64 (over x, z, core), cone: 4 (over y).
Axes of the slice: x: 4, y: 4, z: 8, core: 2. Of those that a mesh axis runs over, the one named last changes fastest.
Arguments:
- mom_current: bfloat16 [16384, 512], P('box'), may hold values from -6 to 6
- mom_radiate: bfloat16 [8, 512, 512], P('cone'), may hold values from -0.25 to 0.25
- po_receive: bfloat16 [8, 512, 512], P('cone'), may hold values from -0.09375 to 0.09375
- po_radiate: bfloat16 [8, 512, 512], P('cone'), may hold values from -0.25 to 0.25
- mom_receive: bfloat16 [8, 512, 512], P('cone'), may hold values from -0.03125 to 0.03125
- dirs: float32 [8, 3, 256], P('cone'), may hold values from -4 to 4
- mom_center: float32 [3, 16384], replicated, may hold values from 0 to 4
- po_center: float32 [3, 32768], replicated, may hold values from 0 to 4
- po_src: int32 [8, 32768], P(None, 'box'), may hold values from 0 to 16383, as said below
- po_weight: float32 [8, 32768], P(None, 'box'), may hold values from 0.2 to 2
- mom_src: int32 [8, 16384], P(None, 'box'), may hold values from 0 to 32767, as said below
- mom_weight: float32 [8, 16384], P(None, 'box'), may hold values from 0.2 to 2
- lit: int32 [8, 32768], P('cone', 'box'), may hold values 0 or 1
Outputs:
- mom_field: float32 [16384, 512], P('box', 'cone')
- po_current: bfloat16 [32768, 512], P('box', 'cone')
Inputs may be any that keep to these rules, and one draw needn't show every extreme that they name: |po_src[l, q] - q * 256 // 512| <= 256 for every entry. |mom_src[l, m] - m * 2| <= 512 for every entry.
All inputs are finite; a program needn't handle non-finite values. No bound on the sum of `lit` on one device may be relied on, other than what follows from the above.
Results may differ from a plain program's by a relative error of at most 0.0085.
Values may be sent and summed in bfloat16 or wider, within the bound.
No kernel may reach another device: no remote copies, remote signals or barrier semaphores. Data moves between devices by JAX's collectives and lax.ppermute only.
A program may use at most 64 MiB of HBM per device.

v0:
```python
import jax
import jax.numpy as jnp
from jax import lax
from jax.sharding import PartitionSpec as P


def padded_2(shard, sides, width):
    for axis, dim in sides:
        size, length = (lax.axis_size(axis), shard.shape[dim])
        up = [(i, (i + 1) % size) for i in range(size - 1)]
        down = [(j, i) for i, j in up]
        last = lax.slice_in_dim(shard, length - width, length, axis=dim)
        leading = lax.slice_in_dim(shard, 0, width, axis=dim)
        before = lax.ppermute(last, axis, up)
        after = lax.ppermute(leading, axis, down)
        shard = jnp.concatenate([before, shard, after], axis=dim)
    return shard


def phases(dirs, centers):
    return (
        centers[0][:, None, None] * dirs[None, :, 0, :]
        + centers[1][:, None, None] * dirs[None, :, 1, :]
        + centers[2][:, None, None] * dirs[None, :, 2, :]
    )


def rotate(waves, theta, orient):
    samples = theta.shape[-1]
    real_part = waves[..., :samples]
    imag_part = waves[..., samples:]
    cosine = jnp.cos(theta)
    sine = orient * jnp.sin(theta)
    return jnp.concatenate(
        [real_part * cosine - imag_part * sine, real_part * sine + imag_part * cosine], axis=-1
    )


def collect(padded, sources, weights, offset):
    rows_all, cone_count, width = padded.shape
    flat = padded.reshape(rows_all, cone_count * width)
    total = jnp.zeros((sources.shape[1], cone_count * width), jnp.float32)
    for slot in range(sources.shape[0]):
        picked = jnp.take(flat, sources[slot] - offset, axis=0).astype(jnp.float32)
        total = total + weights[slot][:, None] * picked
    return total.reshape(sources.shape[1], cone_count, width)


def shards(
    mom_current,
    mom_radiate,
    po_receive,
    po_radiate,
    mom_receive,
    dirs,
    mom_center,
    po_center,
    po_src,
    po_weight,
    mom_src,
    mom_weight,
    lit,
):
    box_index = lax.axis_index("box")
    mom_rows = mom_current.shape[0]
    po_rows = lit.shape[1]
    mom_theta = phases(
        dirs, lax.dynamic_slice_in_dim(mom_center, box_index * mom_rows, mom_rows, 1)
    )
    po_theta = phases(dirs, lax.dynamic_slice_in_dim(po_center, box_index * po_rows, po_rows, 1))
    radiated = jnp.einsum(
        "rn,cnk->rck", mom_current, mom_radiate, preferred_element_type=jnp.float32
    )
    mom_waves = rotate(radiated, mom_theta, -1.0).astype(jnp.bfloat16)
    mom_padded = padded_2(mom_waves, (("box", 0),), mom_rows)
    gathered = collect(mom_padded, po_src, po_weight, (box_index - 1) * mom_rows)
    lit_rows = jnp.transpose(lit).astype(jnp.float32)
    po_lit = (rotate(gathered, po_theta, 1.0) * lit_rows[:, :, None]).astype(jnp.bfloat16)
    partial_value = jnp.einsum(
        "rck,ckn->rn", po_lit, po_receive, preferred_element_type=jnp.float32
    )
    po_whole = lax.psum(partial_value, "cone").astype(jnp.bfloat16)
    share = po_whole.shape[1] // lax.axis_size("cone")
    po_share = lax.dynamic_slice_in_dim(po_whole, lax.axis_index("cone") * share, share, 1)
    radiated = jnp.einsum("rn,cnk->rck", po_whole, po_radiate, preferred_element_type=jnp.float32)
    po_waves = rotate(radiated, po_theta, -1.0).astype(jnp.bfloat16)
    po_padded = padded_2(po_waves, (("box", 0),), po_rows)
    returned = collect(po_padded, mom_src, mom_weight, (box_index - 1) * po_rows)
    mom_incident = rotate(returned, mom_theta, 1.0).astype(jnp.bfloat16)
    mom_partial = jnp.einsum(
        "rck,ckn->rn", mom_incident, mom_receive, preferred_element_type=jnp.float32
    )
    mom_field = lax.psum_scatter(mom_partial, "cone", scatter_dimension=1, tiled=True)
    return (mom_field, po_share)


def solution(mesh):
    in_specs = (
        P("box", None),
        P("cone", None, None),
        P("cone", None, None),
        P("cone", None, None),
        P("cone", None, None),
        P("cone", None, None),
        P(),
        P(),
        P(None, "box"),
        P(None, "box"),
        P(None, "box"),
        P(None, "box"),
        P("cone", "box"),
    )
    out_specs = (P("box", "cone"), P("box", "cone"))
    return jax.shard_map(shards, mesh=mesh, in_specs=in_specs, out_specs=out_specs, check_vma=False)
```

profile of v0, /device:TPU:6, one launch (start us, length us, event | category | flops | bytes accessed | tf_op | source)
XLA Modules:
  0.0 209.9 jit_solution(1306298672080685042)
XLA Ops:
  7.2 0.8 slice_bitcast_fusion.2
  8.0 1.8 fusion.14
  9.8 0.9 constant_dynamic-slice_fusion
  10.7 2.5 %subtract_convert_fusion.2 = (bf16[256,2,256]{2,0,1:T(8,128)(2,1)S(1)}, bf16[256,2,256]{2,0,1:T(8,128)(2,1)S(1)}) fusion(f32[256,2,512]{2,0,1:T(8,128)S(1)} %fusion.14, f32[2,256]{1,0:T(2,128)S(1)} %get-tuple-element.53, f32[256]{0:T(256)S(1)} %bitcast.110, f32[2,256]{1,0:T(2,128)S(1)} %get-tuple-element.54, f32[256]{0:T(256)S(1)} %bitcast.108, ...), kind=kLoop, calls=%fused_computation.43 | loop fusion | flops 1835008 | bytes 1582080 | tf_op jit(solution)/shard_map/convert.4
  13.3 1.9 collective-permute-start
  15.2 7.5 %collective-permute-start.1 = (bf16[256,2,512]{2,0,1:T(8,128)(2,1)S(1)}, bf16[256,2,512]{2,0,1:T(8,128)(2,1)}, u32[]{:S(2)}, u32[]{:S(2)}) collective-permute-start(bf16[256,2,512]{2,0,1:T(8,128)(2,1)S(1)} %pad_maximum_fusion.3), channel_id=1, source_target_pairs={{4,0},{8,4},{12,8},{16,12},{20,16},{24,20},{28,24},{32,28},{36,32}... | collective-permute-start | bytes 1572872 | tf_op jit(solution)/shard_map/ppermute | solution.py:15
  23.1 0.9 constant_dynamic-slice_fusion.2
  24.1 3.5 %collective-permute-done = bf16[256,2,512]{2,0,1:T(8,128)(2,1)S(1)} collective-permute-done((bf16[256,2,512]{2,0,1:T(8,128)(2,1)S(1)}, bf16[256,2,512]{2,0,1:T(8,128)(2,1)S(1)}, u32[]{:S(2)}, u32[]{:S(2)}) %collective-permute-start) | collective-permute-done | bytes 524320 | tf_op jit(solution)/shard_map/ppermute | solution.py:14
  27.6 0.8 copy-done.2
  28.4 1.0 collective-permute-done.1
  29.3 1.3 pad_maximum_fusion.1
  30.6 1.6 copy.26
  32.3 1.7 copy.27
  34.0 2.8 %gather_fusion = bf16[512,1024]{1,0:T(8,128)(2,1)} fusion(bf16[768,1024]{1,0:T(8,128)(2,1)S(1)} %copy.27, s32[1024]{0:T(1024)S(1)} %pad_clamp_fusion.15), kind=kCustom, calls=%fused_computation.clone | custom fusion | bytes 2099200 | tf_op jit(solution)/shard_map/jit(_take)/gather | solution.py:44
  36.8 2.8 %gather_fusion.1 = bf16[512,1024]{1,0:T(8,128)(2,1)} fusion(bf16[768,1024]{1,0:T(8,128)(2,1)S(1)} %copy.27, s32[1024]{0:T(1024)S(1)} %pad_clamp_fusion.14), kind=kCustom, calls=%fused_computation.2.clone | custom fusion | bytes 2099200 | tf_op jit(solution)/shard_map/jit(_take)/gather | solution.py:44
  39.6 2.8 %gather_fusion.2 = bf16[512,1024]{1,0:T(8,128)(2,1)} fusion(bf16[768,1024]{1,0:T(8,128)(2,1)S(1)} %copy.27, s32[1024]{0:T(1024)S(1)} %pad_clamp_fusion.13), kind=kCustom, calls=%fused_computation.3.clone | custom fusion | bytes 2099200 | tf_op jit(solution)/shard_map/jit(_take)/gather | solution.py:44
  42.4 2.8 %gather_fusion.3 = bf16[512,1024]{1,0:T(8,128)(2,1)} fusion(bf16[768,1024]{1,0:T(8,128)(2,1)S(1)} %copy.27, s32[1024]{0:T(1024)S(1)} %pad_clamp_fusion.12), kind=kCustom, calls=%fused_computation.4.clone | custom fusion | bytes 2099200 | tf_op jit(solution)/shard_map/jit(_take)/gather | solution.py:44
  45.1 2.8 %gather_fusion.4 = bf16[512,1024]{1,0:T(8,128)(2,1)} fusion(bf16[768,1024]{1,0:T(8,128)(2,1)S(1)} %copy.27, s32[1024]{0:T(1024)S(1)} %pad_clamp_fusion.11), kind=kCustom, calls=%fused_computation.5.clone | custom fusion | bytes 2099200 | tf_op jit(solution)/shard_map/jit(_take)/gather | solution.py:44
  47.9 2.8 %gather_fusion.5 = bf16[512,1024]{1,0:T(8,128)(2,1)} fusion(bf16[768,1024]{1,0:T(8,128)(2,1)S(1)} %copy.27, s32[1024]{0:T(1024)S(1)} %pad_clamp_fusion.10), kind=kCustom, calls=%fused_computation.6.clone | custom fusion | bytes 2099200 | tf_op jit(solution)/shard_map/jit(_take)/gather | solution.py:44
  50.7 2.8 %gather_fusion.6 = bf16[512,1024]{1,0:T(8,128)(2,1)} fusion(bf16[768,1024]{1,0:T(8,128)(2,1)S(1)} %copy.27, s32[1024]{0:T(1024)S(1)} %pad_clamp_fusion.9), kind=kCustom, calls=%fused_computation.7.clone | custom fusion | bytes 2099200 | tf_op jit(solution)/shard_map/jit(_take)/gather | solution.py:44
  53.4 2.8 %gather_fusion.7 = bf16[512,1024]{1,0:T(8,128)(2,1)} fusion(bf16[768,1024]{1,0:T(8,128)(2,1)S(1)} %copy.27, s32[1024]{0:T(1024)S(1)} %pad_clamp_fusion.8), kind=kCustom, calls=%fused_computation.8.clone | custom fusion | bytes 2099200 | tf_op jit(solution)/shard_map/jit(_take)/gather | solution.py:44
  56.2 5.2 %multiply_add_fusion = f32[512,1024]{1,0:T(8,128)S(1)} fusion(bf16[512,1024]{1,0:T(8,128)(2,1)} %gather_fusion.7, bf16[512,1024]{1,0:T(8,128)(2,1)} %gather_fusion.6, bf16[512,1024]{1,0:T(8,128)(2,1)} %gather_fusion.5, bf16[512,1024]{1,0:T(8,128)(2,1)} %gather_fusion.4, bf16[512,1024]{1,0:T(8,128)(2,1)} %gather_fusion.3, bf16[512,1024]{1,0:T(8,128)(2,1)} %gather_fusion.2, ...), kind=kLoop, calls=%fused_computation.19 | loop fusion | flops 16252928 | bytes 10506240 | tf_op jit(solution)/shard_map/add | solution.py:45
  61.4 1.8 copy.35
  63.3 7.1 %multiply_subtract_fusion = (f32[512,2,256]{0,2,1:T(8,128)S(1)}, f32[512,2,256]{0,2,1:T(8,128)S(1)}) fusion(f32[512,2,512]{0,2,1:T(8,128)} %bitcast.65, f32[2,256]{1,0:T(2,128)S(1)} %get-tuple-element.53, f32[512]{0:T(512)S(1)} %bitcast.72, f32[2,256]{1,0:T(2,128)S(1)} %get-tuple-element.54, f32[512]{0:T(512)S(1)} %bitcast.70, ...), kind=kLoop, calls=%fused_computation.29 | loop fusion | flops 2883584 | bytes 4206592 | tf_op jit(solution)/shard_map/sub | solution.py:35
  70.4 0.7 convolution_bitcast_fusion
  71.2 33.9 %all-reduce.1 = bf16[512,512]{1,0:T(8,128)(2,1)S(1)} all-reduce(f32[512,512]{1,0:T(8,128)S(1)} %convolution_bitcast_fusion), channel_id=1, replica_groups=mesh['box'=64,'cone'=4] {'cone'}, use_global_device_ids=true, to_apply=%region_0.0 | all-reduce | flops 262144 | bytes 1572864 | tf_op jit(solution)/shard_map/psum | solution.py:82
  105.1 0.8 fusion.9
  105.9 4.6 %subtract_convert_fusion = (bf16[512,2,256]{0,2,1:T(8,128)(2,1)S(1)}, bf16[512,2,256]{0,2,1:T(8,128)(2,1)S(1)}) fusion(f32[512,2,512]{0,2,1:T(8,128)S(1)} %fusion.9, f32[2,256]{1,0:T(2,128)S(1)} %get-tuple-element.53, f32[512]{0:T(512)S(1)} %bitcast.73, f32[2,256]{1,0:T(2,128)S(1)} %get-tuple-element.54, f32[512]{0:T(512)S(1)} %bitcast.71, ...), kind=kLoop, calls=%fused_computation.26 | loop fusion | flops 3670016 | bytes 3158016 | tf_op jit(solution)/shard_map/convert.2
  110.5 1.9 collective-permute-start.2
  112.5 5.8 %collective-permute-start.3 = (bf16[512,2,512]{0,2,1:T(8,128)(2,1)S(1)}, bf16[512,2,512]{0,2,1:T(8,128)(2,1)S(1)}, u32[]{:S(2)}, u32[]{:S(2)}) collective-permute-start(bf16[512,2,512]{0,2,1:T(8,128)(2,1)S(1)} %pad_maximum_fusion.2), channel_id=1, source_target_pairs={{4,0},{8,4},{12,8},{16,12},{20,16},{24,20},{28,24},{32,28},{36,32}... | collective-permute-start | bytes 3145736 | tf_op jit(solution)/shard_map/ppermute | solution.py:15
  118.3 10.4 %collective-permute-done.2 = bf16[512,2,512]{0,2,1:T(8,128)(2,1)S(1)} collective-permute-done((bf16[512,2,512]{0,2,1:T(8,128)(2,1)S(1)}, bf16[512,2,512]{0,2,1:T(8,128)(2,1)S(1)}, u32[]{:S(2)}, u32[]{:S(2)}) %collective-permute-start.2) | collective-permute-done | bytes 1048608 | tf_op jit(solution)/shard_map/ppermute | solution.py:14
  128.8 1.8 collective-permute-done.3
  130.5 1.8 pad_maximum_fusion
  132.3 4.7 %copy.38 = bf16[1536,1024]{1,0:T(8,128)(2,1)} copy(bf16[1536,1024]{0,1:T(8,128)(2,1)} %bitcast.64) | data formatting | bytes 6291456 | tf_op jit(solution)/shard_map/reshape | solution.py:41
  137.0 3.8 %gather_fusion.8 = bf16[256,1024]{1,0:T(8,128)(2,1)S(1)} fusion(bf16[1536,1024]{1,0:T(8,128)(2,1)} %copy.38, s32[1024]{0:T(1024)S(1)} %pad_clamp_fusion.7), kind=kCustom, calls=%fused_computation.1.clone | custom fusion | bytes 1049600 | tf_op jit(solution)/shard_map/jit(_take)/gather | solution.py:44
  140.8 3.9 %gather_fusion.9 = bf16[256,1024]{1,0:T(8,128)(2,1)S(1)} fusion(bf16[1536,1024]{1,0:T(8,128)(2,1)} %copy.38, s32[1024]{0:T(1024)S(1)} %pad_clamp_fusion.6), kind=kCustom, calls=%fused_computation.9.clone | custom fusion | bytes 1049600 | tf_op jit(solution)/shard_map/jit(_take)/gather | solution.py:44
  144.7 4.7 %gather_fusion.10 = bf16[256,1024]{1,0:T(8,128)(2,1)} fusion(bf16[1536,1024]{1,0:T(8,128)(2,1)} %copy.38, s32[1024]{0:T(1024)S(1)} %pad_clamp_fusion.5), kind=kCustom, calls=%fused_computation.10.clone | custom fusion | bytes 1049600 | tf_op jit(solution)/shard_map/jit(_take)/gather | solution.py:44
  149.3 4.6 %gather_fusion.11 = bf16[256,1024]{1,0:T(8,128)(2,1)} fusion(bf16[1536,1024]{1,0:T(8,128)(2,1)} %copy.38, s32[1024]{0:T(1024)S(1)} %pad_clamp_fusion.4), kind=kCustom, calls=%fused_computation.11.clone | custom fusion | bytes 1049600 | tf_op jit(solution)/shard_map/jit(_take)/gather | solution.py:44
  154.0 4.7 %gather_fusion.12 = bf16[256,1024]{1,0:T(8,128)(2,1)} fusion(bf16[1536,1024]{1,0:T(8,128)(2,1)} %copy.38, s32[1024]{0:T(1024)S(1)} %pad_clamp_fusion.3), kind=kCustom, calls=%fused_computation.12.clone | custom fusion | bytes 1049600 | tf_op jit(solution)/shard_map/jit(_take)/gather | solution.py:44
  158.7 4.7 %gather_fusion.13 = bf16[256,1024]{1,0:T(8,128)(2,1)} fusion(bf16[1536,1024]{1,0:T(8,128)(2,1)} %copy.38, s32[1024]{0:T(1024)S(1)} %pad_clamp_fusion.2), kind=kCustom, calls=%fused_computation.13.clone | custom fusion | bytes 1049600 | tf_op jit(solution)/shard_map/jit(_take)/gather | solution.py:44
  163.3 4.6 %gather_fusion.14 = bf16[256,1024]{1,0:T(8,128)(2,1)} fusion(bf16[1536,1024]{1,0:T(8,128)(2,1)} %copy.38, s32[1024]{0:T(1024)S(1)} %pad_clamp_fusion.1), kind=kCustom, calls=%fused_computation.14.clone | custom fusion | bytes 1049600 | tf_op jit(solution)/shard_map/jit(_take)/gather | solution.py:44
  168.0 4.6 %gather_fusion.15 = bf16[256,1024]{1,0:T(8,128)(2,1)} fusion(bf16[1536,1024]{1,0:T(8,128)(2,1)} %copy.38, s32[1024]{0:T(1024)S(1)} %pad_clamp_fusion), kind=kCustom, calls=%fused_computation.15.clone | custom fusion | bytes 1049600 | tf_op jit(solution)/shard_map/jit(_take)/gather | solution.py:44
  172.6 2.7 %multiply_add_fusion.1 = f32[256,1024]{1,0:T(8,128)S(1)} fusion(bf16[256,1024]{1,0:T(8,128)(2,1)} %gather_fusion.15, bf16[256,1024]{1,0:T(8,128)(2,1)} %gather_fusion.14, bf16[256,1024]{1,0:T(8,128)(2,1)} %gather_fusion.13, bf16[256,1024]{1,0:T(8,128)(2,1)} %gather_fusion.12, bf16[256,1024]{1,0:T(8,128)(2,1)} %gather_fusion.11, ...), kind=kLoop, calls=%fused_computation.24 | loop fusion | flops 8126464 | bytes 5253120 | tf_op jit(solution)/shard_map/add | solution.py:45
  175.4 0.3 copy.46
  176.2 2.5 %subtract_convert_fusion.1 = (bf16[256,2,256]{2,0,1:T(8,128)(2,1)S(1)}, bf16[256,2,256]{2,0,1:T(8,128)(2,1)S(1)}) fusion(f32[256,2,256]{2,0,1:T(8,128)S(1)} %copy.52, f32[256,2,256]{2,0,1:T(8,128)S(1)} %copy.51, f32[2,256]{1,0:T(2,128)S(1)} %get-tuple-element.53, f32[256]{0:T(256)S(1)} %bitcast.111, f32[2,256]{1,0:T(2,128)S(1)} %get-tuple-element.54, ...), kind=kLoop, calls=%fused_computation.41 | loop fusion | flops 1703936 | bytes 1582080 | tf_op jit(solution)/shard_map/convert
  178.7 2.5 %convolution_bitcast_fusion.1 = f32[256,512]{1,0:T(8,128)} fusion(bf16[2,512,512]{2,1,0:T(8,128)(2,1)} %param.21, bf16[256,2,256]{2,0,1:T(8,128)(2,1)S(1)} %get-tuple-element.9, bf16[256,2,256]{2,0,1:T(8,128)(2,1)S(1)} %get-tuple-element.8), kind=kOutput, calls=%fused_computation.22 | convolution fusion | flops 269484032 | bytes 2097152 | tf_op jit(solution)/shard_map/rck,ckn->rn/dot_general | solution.py:90
  181.2 1.6 constant_dynamic-slice_fusion.1
  182.8 20.3 %reduce-scatter.2.cloned.1.call-done = f32[256,128]{1,0:T(8,128)} async-done(((f32[256,512]{1,0:T(8,128)}), f32[256,128]{1,0:T(8,128)}) %reduce-scatter.2.cloned.1.call-update) | async-done | bytes 131088 | tf_op jit(solution)/shard_map/reduce_scatter | solution.py:93
  (65 shorter events, 1.0 us)
Async XLA Ops:
  7.2 97.9 %copy-start = (bf16[2,512,512]{2,1,0:T(8,128)(2,1)S(1)}, bf16[2,512,512]{2,1,0:T(8,128)(2,1)}, u32[]{:S(2)}) copy-start(bf16[2,512,512]{2,1,0:T(8,128)(2,1)} %param.20) | copy-start | bytes 3145732
  7.2 195.9 %reduce-scatter.2.cloned.1.call-start = ((), (), s32[]{:S(2)}) async-start(), calls=%async_computation.1 | async-start | bytes 655360 | tf_op jit(solution)/shard_map/reduce_scatter | solution.py:93
  8.0 14.6 %copy-start.3 = (s32[8,512]{1,0:T(8,128)S(1)}, s32[8,512]{1,0:T(8,128)}, u32[]{:S(2)}) copy-start(s32[8,512]{1,0:T(8,128)} %param.25) | copy-start | bytes 49156
  8.0 14.8 %copy-start.5 = (s32[8,256]{1,0:T(8,128)S(1)}, s32[8,256]{1,0:T(8,128)}, u32[]{:S(2)}) copy-start(s32[8,256]{1,0:T(8,128)} %param.27) | copy-start | bytes 24580
  8.0 16.0 %copy-start.7 = (s32[2,512]{1,0:T(2,128)S(1)}, s32[2,512]{1,0:T(2,128)}, u32[]{:S(2)}) copy-start(s32[2,512]{1,0:T(2,128)} %param.29) | copy-start | bytes 12292
  8.0 16.0 %copy-start.4 = (f32[8,512]{1,0:T(8,128)S(1)}, f32[8,512]{1,0:T(8,128)}, u32[]{:S(2)}) copy-start(f32[8,512]{1,0:T(8,128)} %param.26) | copy-start | bytes 49156
  13.3 14.3 %collective-permute-start = (bf16[256,2,512]{2,0,1:T(8,128)(2,1)S(1)}, bf16[256,2,512]{2,0,1:T(8,128)(2,1)S(1)}, u32[]{:S(2)}, u32[]{:S(2)}) collective-permute-start(bf16[256,2,512]{2,0,1:T(8,128)(2,1)S(1)} %pad_maximum_fusion.3), channel_id=1, source_target_pairs={{0,4},{4,8},{8,12},{12,16},{16,20},{20,24},{24,28},{28,32},{32,36}... | collective-permute-start | bytes 1572872 | tf_op jit(solution)/shard_map/ppermute | solution.py:14
  15.2 14.2 %collective-permute-start.1 = (bf16[256,2,512]{2,0,1:T(8,128)(2,1)S(1)}, bf16[256,2,512]{2,0,1:T(8,128)(2,1)}, u32[]{:S(2)}, u32[]{:S(2)}) collective-permute-start(bf16[256,2,512]{2,0,1:T(8,128)(2,1)S(1)} %pad_maximum_fusion.3), channel_id=1, source_target_pairs={{4,0},{8,4},{12,8},{16,12},{20,16},{24,20},{28,24},{32,28},{36,32}... | collective-permute-start | bytes 1572872 | tf_op jit(solution)/shard_map/ppermute | solution.py:15
  27.6 0.8 copy-start.2
  63.3 7.1 %copy-start.8 = (bf16[2,512,512]{2,1,0:T(8,128)(2,1)S(1)}, bf16[2,512,512]{2,1,0:T(8,128)(2,1)}, u32[]{:S(2)}) copy-start(bf16[2,512,512]{2,1,0:T(8,128)(2,1)} %param.19) | copy-start | bytes 3145732
  105.1 5.4 %copy-start.1 = (bf16[512,512]{1,0:T(8,128)(2,1)}, bf16[512,512]{1,0:T(8,128)(2,1)S(1)}, u32[]{:S(2)}) copy-start(bf16[512,512]{1,0:T(8,128)(2,1)S(1)} %all-reduce.1) | copy-start | bytes 1572868
  105.9 12.4 %copy-start.6 = (f32[8,256]{1,0:T(8,128)S(1)}, f32[8,256]{1,0:T(8,128)}, u32[]{:S(2)}) copy-start(f32[8,256]{1,0:T(8,128)} %param.28) | copy-start | bytes 24580
  110.5 18.2 %collective-permute-start.2 = (bf16[512,2,512]{0,2,1:T(8,128)(2,1)S(1)}, bf16[512,2,512]{0,2,1:T(8,128)(2,1)S(1)}, u32[]{:S(2)}, u32[]{:S(2)}) collective-permute-start(bf16[512,2,512]{0,2,1:T(8,128)(2,1)S(1)} %pad_maximum_fusion.2), channel_id=1, source_target_pairs={{0,4},{4,8},{8,12},{12,16},{16,20},{20,24},{24,28},{28,32},{32,36}... | collective-permute-start | bytes 3145736 | tf_op jit(solution)/shard_map/ppermute | solution.py:14
  112.5 18.1 %collective-permute-start.3 = (bf16[512,2,512]{0,2,1:T(8,128)(2,1)S(1)}, bf16[512,2,512]{0,2,1:T(8,128)(2,1)S(1)}, u32[]{:S(2)}, u32[]{:S(2)}) collective-permute-start(bf16[512,2,512]{0,2,1:T(8,128)(2,1)S(1)} %pad_maximum_fusion.2), channel_id=1, source_target_pairs={{4,0},{8,4},{12,8},{16,12},{20,16},{24,20},{28,24},{32,28},{36,32}... | collective-permute-start | bytes 3145736 | tf_op jit(solution)/shard_map/ppermute | solution.py:15
Sparse Core Ops, SparseCore 0:
  181.3 21.7 reduce-scatter.1
where the time goes:
time: 211 us; the launch traced here: 210 us
  local copies, waits for them, and re-layouts  73.5 us (35%)
  waiting for transfers between devices  37 us (18%)
  blocking collectives  33.9 us (16%)
  other arithmetic  28.1 us (13%)
  starting transfers between devices  17.1 us (8%)
  between operations  14.7 us (7%)
  matrix products  5.74 us (3%)
    gather x16, local copies, waits for them, and re-layouts, collect(): picked = jnp.take(flat, sources[slot] - offset, axis=0).astype(jnp.float32)  57.9 us
    psum x1, blocking collectives, shards(): po_whole = lax.psum(partial_value, 'cone').astype(jnp.bfloat16)  33.9 us
    reduce_scatter x1, waiting for transfers between devices, shards(): lax.psum_scatter(mom_partial, 'cone', scatter_dimension=1, tiled=True)  20.3 us
    ppermute x2, waiting for transfers between devices, padded_2(): before = lax.ppermute(last, axis, up)  13.9 us
    ppermute x2, starting transfers between devices, padded_2(): after = lax.ppermute(leading, axis, down)  13.2 us
    another operation x3, other arithmetic  9.56 us
    add x2, other arithmetic, collect(): total = total + weights[slot][:, None] * picked  7.95 us
    sub x1, other arithmetic, rotate(): real_part * cosine - imag_part * sine  7.12 us
  transfers between devices with their start and end apart: 5, of which 5 were waited for; matrix products, arithmetic and copies ran while one was open for 1% of the time, Pallas kernels for 0%

commit v1 on v0

v1 whole, which is shorter than its diff:
```python
import math

import jax
import jax.numpy as jnp
from jax import lax
from jax.experimental import pallas as pl
from jax.experimental.pallas import tpu as pltpu
from jax.sharding import PartitionSpec as P

BF = jnp.bfloat16
F32 = jnp.float32
MIB = 1 << 20
TILE = 128

SIN = (6.283184911827348, -41.34158830218017, 81.59991361943669, -76.61414030096898, 41.34136538554672, -12.468818618465846)
COS = (0.9999991998413442, -19.738978175861465, 64.92858783993753, -85.27084362694508, 58.786940763161404, -21.065429407715534)
MAGIC = 12582912.0


def horner(coeffs, u):
    total = coeffs[-1] * u + coeffs[-2]
    for value in coeffs[-3::-1]:
        total = total * u + value
    return total


def turn(turns):
    f = turns - ((turns + MAGIC) - MAGIC)
    u = f * f
    return horner(COS, u), f * horner(SIN, u)


def mm(a, b):
    return jnp.dot(a, b, preferred_element_type=F32)


def hot(src_col, w_col, width):
    lanes = lax.broadcasted_iota(jnp.int32, (src_col.shape[0], width), 1)
    total = jnp.zeros((src_col.shape[0], width), F32)
    for slot in range(src_col.shape[1]):
        total = total + jnp.where(lanes == src_col[:, slot : slot + 1], w_col[:, slot : slot + 1], 0.0)
    return total.astype(BF)


def trig(center, dirs_ref, cos_ref, sin_ref):
    rows = center.shape[1]
    cones = dirs_ref.shape[0]
    columns = jnp.concatenate([center, jnp.zeros((5, rows), F32)], axis=0).T
    step = 64
    for c in range(cones):
        waves = dirs_ref[c] * (0.5 / math.pi)
        for r in range(0, rows, step):
            part = columns[r : r + step]
            turns = part[:, 0:1] * waves[0:1] + part[:, 1:2] * waves[1:2] + part[:, 2:3] * waves[2:3]
            cosine, sine = turn(turns)
            cos_ref[c, r : r + step] = cosine
            sin_ref[c, r : r + step] = sine


def rotated(value, cosine, sine, orient):
    k = cosine.shape[-1]
    re, im = value[:, :k], value[:, k:]
    if orient < 0:
        return re * cosine + im * sine, im * cosine - re * sine
    return re * cosine - im * sine, re * sine + im * cosine


def prepare(
    current_ref, radiate_ref, dirs_ref, mom_center_ref, po_center_ref, src_ref, weight_ref, mom_src_ref, mom_weight_ref,
    mom_cos, mom_sin, po_cos, po_sin, pick_ref, wave_ref, list_ref,
    mom_c, po_c, sems,
):
    box = lax.axis_index("box")
    boxes = lax.axis_size("box")
    m = current_ref.shape[0]
    q = src_ref.shape[1]
    copies = []
    for i, other in enumerate((jnp.maximum(box - 1, 0), box, jnp.minimum(box + 1, boxes - 1))):
        at = pl.multiple_of(other * m, 128)
        copies.append(pltpu.make_async_copy(mom_center_ref.at[:, pl.ds(at, m)], mom_c.at[:, pl.ds(i * m, m)], sems.at[i]))
    at = pl.multiple_of(box * q, 128)
    copies.append(pltpu.make_async_copy(po_center_ref.at[:, pl.ds(at, q)], po_c, sems.at[3]))
    for copy in copies:
        copy.start()
    list_ref[0:8] = mom_src_ref[...].astype(F32)
    list_ref[8:16] = mom_weight_ref[...]
    first = (box - 1) * m
    src_col = (src_ref[...] - first).T
    w_col = weight_ref[...].T
    step = 32
    for r in range(0, q, step):
        pick_ref[r : r + step] = hot(src_col[r : r + step], w_col[r : r + step], 3 * m)
    for copy in copies:
        copy.wait()
    trig(mom_c[...], dirs_ref, mom_cos, mom_sin)
    k2 = radiate_ref.shape[2]
    k = k2 // 2
    for c in range(radiate_ref.shape[0]):
        for r in range(0, m, TILE):
            value = mm(current_ref[r : r + TILE], radiate_ref[c])
            re, im = rotated(value, mom_cos[c, m + r : m + r + TILE], mom_sin[c, m + r : m + r + TILE], -1)
            wave_ref[r : r + TILE, c * k2 : c * k2 + k] = re.astype(BF)
            wave_ref[r : r + TILE, c * k2 + k : (c + 1) * k2] = im.astype(BF)
    trig(po_c[...], dirs_ref, po_cos, po_sin)


def incident(
    before_ref, after_ref, wave_ref, pick_ref, radiate_ref, receive_ref, mom_cos, mom_sin, po_cos, po_sin, lit_ref,
    own_ref, s1_ref, s2_ref, s3_ref,
    table, chunks,
):
    cone = lax.axis_index("cone")
    count = chunks.shape[0]
    m = before_ref.shape[0]
    q = pick_ref.shape[0]
    cones, _, k2 = radiate_ref.shape
    k = k2 // 2
    share = chunks.shape[2]
    table[m : 2 * m] = wave_ref[...]
    for c in range(cones):
        for src, base in ((before_ref, 0), (after_ref, 2 * m)):
            for r in range(0, m, TILE):
                value = mm(src[r : r + TILE], radiate_ref[c])
                at = slice(base + r, base + r + TILE)
                re, im = rotated(value, mom_cos[c, at], mom_sin[c, at], -1)
                table[at, c * k2 : c * k2 + k] = re.astype(BF)
                table[at, c * k2 + k : (c + 1) * k2] = im.astype(BF)
    lit_col = jnp.concatenate([lit_ref[...].astype(F32), jnp.zeros((8 - cones, q), F32)], axis=0).T
    for r in range(0, q, TILE):
        at = slice(r, r + TILE)
        total = None
        for c in range(cones):
            value = mm(pick_ref[at], table[:, c * k2 : (c + 1) * k2])
            mask = lit_col[at, c : c + 1]
            re, im = rotated(value, po_cos[c, at] * mask, po_sin[c, at] * mask, 1)
            part = mm(re.astype(BF), receive_ref[c, :k]) + mm(im.astype(BF), receive_ref[c, k:])
            total = part if total is None else total + part
        for j in range(count):
            slot = lax.rem(j - cone + count, count)
            chunks[slot, at] = total[:, j * share : (j + 1) * share]
    own_ref[...] = chunks[0]
    s1_ref[...] = chunks[1].astype(BF)
    s2_ref[...] = chunks[2].astype(BF)
    s3_ref[...] = chunks[3].astype(BF)


def lists(before_ref, own_ref, after_ref, pick_ref):
    box = lax.axis_index("box")
    m = own_ref.shape[1]
    q = pick_ref.shape[1]
    first = (box * q).astype(F32)
    for i, ref in enumerate((before_ref, own_ref, after_ref)):
        src_col = (ref[0:8] - first).astype(jnp.int32).T
        w_col = ref[8:16].T
        step = 32
        for r in range(0, m, step):
            pick_ref[i * m + r : i * m + r + step] = hot(src_col[r : r + step], w_col[r : r + step], q)


def tested(rows, base, pick_ref, waves, receive_ref, mom_cos, mom_sin, put):
    cones, k2, _ = receive_ref.shape
    k = k2 // 2
    for r in range(0, rows, TILE):
        at = slice(base + r, base + r + TILE)
        total = None
        for c in range(cones):
            value = mm(pick_ref[at], waves[:, c * k2 : (c + 1) * k2])
            re, im = rotated(value, mom_cos[c, at], mom_sin[c, at], 1)
            part = mm(re.astype(BF), receive_ref[c, :k]) + mm(im.astype(BF), receive_ref[c, k:])
            total = part if total is None else total + part
        put(r, total)


def scattered(
    p0_ref, p1_ref, p2_ref, p3_ref, radiate_ref, receive_ref, pick_ref, po_cos, po_sin, mom_cos, mom_sin,
    waves_ref, down_ref, up_ref,
    whole,
):
    cone = lax.axis_index("cone")
    q, share = p0_ref.shape
    m = pick_ref.shape[0] // 3
    cones, _, k2 = radiate_ref.shape
    k = k2 // 2
    count = whole.shape[1] // share
    for s, ref in enumerate((p0_ref, p1_ref, p2_ref, p3_ref)):
        owner = lax.rem(cone - s + count, count)
        whole[:, pl.ds(pl.multiple_of(owner * share, share), share)] = ref[...]
    for c in range(cones):
        for r in range(0, q, TILE):
            at = slice(r, r + TILE)
            value = mm(whole[at], radiate_ref[c])
            re, im = rotated(value, po_cos[c, at], po_sin[c, at], -1)
            waves_ref[at, c * k2 : c * k2 + k] = re.astype(BF)
            waves_ref[at, c * k2 + k : (c + 1) * k2] = im.astype(BF)

    for base, out in ((0, down_ref), (2 * m, up_ref)):

        def put(r, total, out=out):
            for j in range(count):
                slot = lax.rem(j - cone + count, count)
                out[slot, r : r + TILE] = total[:, j * share : (j + 1) * share].astype(BF)

        tested(m, base, pick_ref, waves_ref, receive_ref, mom_cos, mom_sin, put)


def returned(waves_ref, receive_ref, pick_ref, mom_cos, mom_sin, own_ref):
    cone = lax.axis_index("cone")
    count, m, share = own_ref.shape

    def put(r, total):
        for j in range(count):
            slot = lax.rem(j - cone + count, count)
            own_ref[slot, r : r + TILE] = total[:, j * share : (j + 1) * share]

    tested(m, m, pick_ref, waves_ref, receive_ref, mom_cos, mom_sin, put)


def call(body, outs, ins, scratch=(), spaces=None, flops=0, vmem=24):
    specs = [pl.BlockSpec(memory_space=pltpu.VMEM if spaces is None else spaces[i]) for i in range(len(ins))]
    return pl.pallas_call(
        body,
        out_shape=outs,
        in_specs=specs,
        out_specs=jax.tree.map(lambda _: pl.BlockSpec(memory_space=pltpu.VMEM), outs),
        scratch_shapes=list(scratch),
        compiler_params=pltpu.CompilerParams(vmem_limit_bytes=vmem * MIB),
        cost_estimate=pl.CostEstimate(flops=flops, bytes_accessed=4 * MIB, transcendentals=0),
        name=body.__name__,
    )(*ins)


def turned(value, shift):
    count = lax.axis_size("cone")
    return lax.ppermute(value, "cone", [(i, (i + shift) % count) for i in range(count)])


def upward(value):
    return lax.ppermute(value, "box", [(i, i + 1) for i in range(lax.axis_size("box") - 1)])


def downward(value):
    return lax.ppermute(value, "box", [(i + 1, i) for i in range(lax.axis_size("box") - 1)])


def shards(
    mom_current, mom_radiate, po_receive, po_radiate, mom_receive, dirs, mom_center, po_center, po_src, po_weight, mom_src,
    mom_weight, lit,
):
    shape = jax.ShapeDtypeStruct
    m, n = mom_current.shape
    cones, q = lit.shape
    k2 = mom_radiate.shape[2]
    k = k2 // 2
    count = lax.axis_size("cone")
    share = n // count
    width = cones * k2

    before = upward(mom_current)
    after = downward(mom_current)
    any_, vmem = pl.ANY, pltpu.VMEM
    mom_cos, mom_sin, po_cos, po_sin, pick, wave, entries = call(
        prepare,
        (
            shape((cones, 3 * m, k), F32), shape((cones, 3 * m, k), F32), shape((cones, q, k), F32), shape((cones, q, k), F32),
            shape((q, 3 * m), BF), shape((m, width), BF), shape((16, m), F32),
        ),
        (mom_current, mom_radiate, dirs, mom_center, po_center, po_src, po_weight, mom_src, mom_weight),
        (pltpu.VMEM((3, 3 * m), F32), pltpu.VMEM((3, q), F32), pltpu.SemaphoreType.DMA((4,))),
        (vmem, vmem, vmem, any_, any_, vmem, vmem, vmem, vmem),
        flops=4_000_000_000,
    )
    own, s1, s2, s3 = call(
        incident,
        (shape((q, share), F32),) + (shape((q, share), BF),) * 3,
        (before, after, wave, pick, mom_radiate, po_receive, mom_cos, mom_sin, po_cos, po_sin, lit),
        (pltpu.VMEM((3 * m, width), BF), pltpu.VMEM((count, q, share), F32)),
        flops=2_000_000_000,
    )
    s2 = turned(s2, 2)
    s1 = turned(s1, 1)
    s3 = turned(s3, 3)
    before_list = upward(entries)
    after_list = downward(entries)
    back = call(lists, shape((3 * m, q), BF), (before_list, entries, after_list), flops=1_000_000_000)
    po_share = (own + s1.astype(F32) + s2.astype(F32) + s3.astype(F32)).astype(BF)
    p2 = turned(po_share, 2)
    p1 = turned(po_share, 1)
    p3 = turned(po_share, 3)
    waves, down, up = call(
        scattered,
        (shape((q, width), BF), shape((count, m, share), BF), shape((count, m, share), BF)),
        (po_share, p1, p2, p3, po_radiate, mom_receive, back, po_cos, po_sin, mom_cos, mom_sin),
        (pltpu.VMEM((q, n), BF),),
        flops=2_000_000_000,
    )
    from_before = upward(up)
    from_after = downward(down)
    field = call(returned, shape((count, m, share), F32), (waves, mom_receive, back, mom_cos, mom_sin), flops=1_000_000_000)
    field = field + from_before.astype(F32) + from_after.astype(F32)
    f2 = turned(field[2].astype(BF), 2)
    f1 = turned(field[1].astype(BF), 1)
    f3 = turned(field[3].astype(BF), 3)
    mom_field = field[0] + f1.astype(F32) + f2.astype(F32) + f3.astype(F32)
    return mom_field, po_share


def solution(mesh):
    in_specs = (
        P("box", None),
        P("cone", None, None),
        P("cone", None, None),
        P("cone", None, None),
        P("cone", None, None),
        P("cone", None, None),
        P(),
        P(),
        P(None, "box"),
        P(None, "box"),
        P(None, "box"),
        P(None, "box"),
        P("cone", "box"),
    )
    out_specs = (P("box", "cone"), P("box", "cone"))
    return jax.shard_map(shards, mesh=mesh, in_specs=in_specs, out_specs=out_specs, check_vma=False)
```

time: 211 us -> 79.5 us (0.38)
  local copies, waits for them, and re-layouts: 73.5 us -> 7.72 us
  blocking collectives: 33.9 us -> 0 us
  other arithmetic: 28.1 us -> 0.85 us
  waiting for transfers between devices: 37 us -> 16.7 us
  starting transfers between devices: 17.1 us -> 37 us
  Pallas kernels: 0 us -> 15.6 us
  between operations: 14.7 us -> 0.84 us
  matrix products: 5.74 us -> 0 us
    gather x16 -> x0, local copies, waits for them, and re-layouts: 57.9 us -> none  [collect(): picked = jnp.take(flat, sources[slot] - offset, axis=0).astype(jnp.float32)]
    psum x1 -> x0, blocking collectives: 33.9 us -> none  [shards(): po_whole = lax.psum(partial_value, 'cone').astype(jnp.bfloat16)]
    reduce_scatter x1 -> x0, waiting for transfers between devices: 20.3 us -> none  [shards(): lax.psum_scatter(mom_partial, 'cone', scatter_dimension=1, tiled=True)]
    ppermute x4 -> x15, starting transfers between devices: 17.1 us -> 37 us  [the longest x9 15.5 us: turned(): lax.ppermute(value, 'cone', [(i, (i + shift) % count) for i in range(coun...]
    pallas_call x0 -> x5, Pallas kernels: none -> 15.6 us  [call(): pl.pallas_call(body, out_shape=outs, in_specs=specs, out_specs=jax.tree.m...]
    another operation x3 -> x1, other arithmetic: 9.56 us -> 0.09 us
    add x2 -> x1, other arithmetic: 7.95 us -> 0.69 us  [shards(): mom_field = field[0] + f1.astype(F32) + f2.astype(F32) + f3.astype(F32)]
    sub x3 -> x0, other arithmetic: 7.15 us -> none  [the longest x1 7.12 us: rotate(): real_part * cosine - imag_part * sine]
  transfers between devices with their start and end apart: 5 -> 15, of which waited for: 5 -> 9; matrix products, arithmetic and copies ran while one was open for 1% -> 1% of each run, Pallas kernels for 0% -> 12%
where the time goes in v1:
time: 79.5 us; the launch traced here: 78.8 us
  starting transfers between devices  37 us (47%)
  waiting for transfers between devices  16.7 us (21%)
  Pallas kernels  15.6 us (20%)
  local copies, waits for them, and re-layouts  7.72 us (10%)
  other arithmetic  0.85 us (1%)
  between operations  0.84 us (1%)
    pallas_call x5, Pallas kernels, call(): pl.pallas_call(body, out_shape=outs, in_specs=specs, out_specs=jax.tree.m...  15.6 us
    ppermute x9, starting transfers between devices, turned(): lax.ppermute(value, 'cone', [(i, (i + shift) % count) for i in range(coun...  15.5 us
    ppermute x3, starting transfers between devices, downward(): lax.ppermute(value, 'box', [(i + 1, i) for i in range(lax.axis_size('box'...  15.3 us
    ppermute x9, waiting for transfers between devices, turned(): lax.ppermute(value, 'cone', [(i, (i + shift) % count) for i in range(coun...  9.33 us
    unnamed x27, local copies, waits for them, and re-layouts  7.71 us
    ppermute x3, starting transfers between devices, upward(): lax.ppermute(value, 'box', [(i, i + 1) for i in range(lax.axis_size('box'...  6.25 us
    ppermute x3, waiting for transfers between devices, upward(): lax.ppermute(value, 'box', [(i, i + 1) for i in range(lax.axis_size('box'...  5.65 us
    ppermute x3, waiting for transfers between devices, downward(): lax.ppermute(value, 'box', [(i + 1, i) for i in range(lax.axis_size('box'...  1.76 us
  transfers between devices with their start and end apart: 15, of which 9 were waited for; matrix products, arithmetic and copies ran while one was open for 1% of the time, Pallas kernels for 12%

profile of v1, /device:TPU:6, one launch (start us, length us, event | category | flops | bytes accessed | tf_op | source)
XLA Modules:
  0.0 78.8 jit_solution(13043772983177738786)
XLA Ops:
  0.6 1.9 %collective-permute-start = (bf16[256,512]{1,0:T(8,128)(2,1)}, bf16[256,512]{1,0:T(8,128)(2,1)S(1)}, u32[]{:S(2)}, u32[]{:S(2)}) collective-permute-start(bf16[256,512]{1,0:T(8,128)(2,1)} %current_ref.1), channel_id=1, source_target_pairs={{0,4},{4,8},{8,12},{12,16},{16,20},{20,24},{24,28},{28,32},{32,36}... | collective-permute-start | bytes 786440 | tf_op jit(solution)/shard_map/ppermute | solution.py:238
  2.6 7.5 %collective-permute-start.1 = (bf16[256,512]{1,0:T(8,128)(2,1)}, bf16[256,512]{1,0:T(8,128)(2,1)S(1)}, u32[]{:S(2)}, u32[]{:S(2)}) collective-permute-start(bf16[256,512]{1,0:T(8,128)(2,1)} %current_ref.1), channel_id=1, source_target_pairs={{4,0},{8,4},{12,8},{16,12},{20,16},{24,20},{28,24},{32,28},{36,32}... | collective-permute-start | bytes 786440 | tf_op jit(solution)/shard_map/ppermute | solution.py:242
  10.0 0.7 copy.15.dirs_ref
  10.7 1.2 %copy-done.2 = bf16[2,512,512]{2,1,0:T(8,128)(2,1)S(1)} copy-done((bf16[2,512,512]{2,1,0:T(8,128)(2,1)S(1)}, bf16[2,512,512]{2,1,0:T(8,128)(2,1)}, u32[]{:S(2)}) %copy-start.2) | copy-done | bytes 1048600
  12.0 1.0 %copy-done.6 = f32[3,32768]{1,0:T(4,128)S(1)} copy-done((f32[3,32768]{1,0:T(4,128)S(1)}, f32[3,32768]{1,0:T(4,128)}, u32[]{:S(2)}) %copy-start.6) | copy-done | bytes 393240
  13.0 0.9 %copy-done.7 = f32[3,16384]{1,0:T(4,128)S(1)} copy-done((f32[3,16384]{1,0:T(4,128)S(1)}, f32[3,16384]{1,0:T(4,128)}, u32[]{:S(2)}) %copy-start.7) | copy-done | bytes 196632
  14.0 0.9 %copy-done.8 = bf16[256,512]{1,0:T(8,128)(2,1)S(1)} copy-done((bf16[256,512]{1,0:T(8,128)(2,1)S(1)}, bf16[256,512]{1,0:T(8,128)(2,1)}, u32[]{:S(2)}) %copy-start.8) | copy-done | bytes 262168
  14.9 0.7 copy-done.9
  15.6 0.7 copy-done.10
  16.3 0.7 copy-done.11
  17.0 0.7 copy-done.12
  17.7 5.5 %prepare.1 = (f32[2,768,256]{2,1,0:T(8,128)S(1)}, f32[2,768,256]{2,1,0:T(8,128)S(1)}, f32[2,512,256]{2,1,0:T(8,128)S(1)}, f32[2,512,256]{2,1,0:T(8,128)S(1)}, bf...) custom-call(bf16[256,512]{1,0:T(8,128)(2,1)S(1)} %copy-done.8, ...), custom_call_target="tpu_custom_call" | custom-call | flops 4000000000 | bytes 4194304 | tf_op jit(solution)/shard_map/prepare/pallas_call | solution.py:220
  23.3 0.0 collective-permute-done.before_ref
  23.3 0.0 collective-permute-done.1.after_ref
  23.3 3.3 %incident.1 = (f32[512,128]{1,0:T(8,128)S(1)}, bf16[512,128]{1,0:T(8,128)(2,1)S(1)}, bf16[512,128]{1,0:T(8,128)(2,1)S(1)}, bf16[512,128]{1,0:T(8,128)(2,1)S(1)}) custom-call(bf16[256,512]{1,0:T(8,128)(2,1)S(1)} %collective-permute-done.before_ref, bf16[256,512]{1,0:T(8,128)(2,1)S(1)} %collective-permute-done.1.after_ref, ...), custom_call_target="tpu_custom_call" | custom-call | flops 2000000000 | bytes 4194304 | tf_op jit(solution)/shard_map/incident/pallas_call | solution.py:220
  26.6 1.6 %collective-permute-start.2 = (bf16[512,128]{1,0:T(8,128)(2,1)S(1)}, bf16[512,128]{1,0:T(8,128)(2,1)S(1)}, u32[]{:S(2)}, u32[]{:S(2)}) collective-permute-start(bf16[512,128]{1,0:T(8,128)(2,1)S(1)} %get-tuple-element.23), channel_id=1, source_target_pairs={{0,1},{1,2},{2,3},{3,0},{4,5},{5,6},{6,7},{7,4},{8,9},{9,10},{10,1... | collective-permute-start | bytes 393224 | tf_op jit(solution)/shard_map/ppermute | solution.py:234
  28.2 2.9 %collective-permute-start.3 = (bf16[512,128]{1,0:T(8,128)(2,1)S(1)}, bf16[512,128]{1,0:T(8,128)(2,1)S(1)}, u32[]{:S(2)}, u32[]{:S(2)}) collective-permute-start(bf16[512,128]{1,0:T(8,128)(2,1)S(1)} %get-tuple-element.24), channel_id=1, source_target_pairs={{0,2},{1,3},{2,0},{3,1},{4,6},{5,7},{6,4},{7,5},{8,10},{9,11},{10,... | collective-permute-start | bytes 393224 | tf_op jit(solution)/shard_map/ppermute | solution.py:234
  31.1 1.3 %collective-permute-start.4 = (bf16[512,128]{1,0:T(8,128)(2,1)S(1)}, bf16[512,128]{1,0:T(8,128)(2,1)S(1)}, u32[]{:S(2)}, u32[]{:S(2)}) collective-permute-start(bf16[512,128]{1,0:T(8,128)(2,1)S(1)} %get-tuple-element.25), channel_id=1, source_target_pairs={{0,3},{1,0},{2,1},{3,2},{4,7},{5,4},{6,5},{7,6},{8,11},{9,8},{10,9... | collective-permute-start | bytes 393224 | tf_op jit(solution)/shard_map/ppermute | solution.py:234
  32.5 0.4 collective-permute-done.2
  32.8 2.6 %collective-permute-done.3 = bf16[512,128]{1,0:T(8,128)(2,1)S(1)} collective-permute-done((bf16[512,128]{1,0:T(8,128)(2,1)S(1)}, bf16[512,128]{1,0:T(8,128)(2,1)S(1)}, u32[]{:S(2)}, u32[]{:S(2)}) %collective-permute-start.3) | collective-permute-done | bytes 131104 | tf_op jit(solution)/shard_map/ppermute | solution.py:234
  35.5 2.0 %collective-permute-done.4 = bf16[512,128]{1,0:T(8,128)(2,1)S(1)} collective-permute-done((bf16[512,128]{1,0:T(8,128)(2,1)S(1)}, bf16[512,128]{1,0:T(8,128)(2,1)S(1)}, u32[]{:S(2)}, u32[]{:S(2)}) %collective-permute-start.4) | collective-permute-done | bytes 131104 | tf_op jit(solution)/shard_map/ppermute | solution.py:234
  37.5 0.1 add_convert_fusion.p0_ref
  37.6 0.0 copy-start.4
  37.6 3.9 %collective-permute-start.7 = (bf16[512,128]{1,0:T(8,128)(2,1)S(1)}, bf16[512,128]{1,0:T(8,128)(2,1)S(1)}, u32[]{:S(2)}, u32[]{:S(2)}) collective-permute-start(bf16[512,128]{1,0:T(8,128)(2,1)S(1)} %add_convert_fusion.p0_ref), channel_id=1, source_target_pairs={{0,3},{1,0},{2,1},{3,2},{4,7},{5,4},{6,5},{7,6},{8,11},{9,8},{10,9... | collective-permute-start | bytes 393224 | tf_op jit(solution)/shard_map/ppermute | solution.py:234
  41.5 0.0 collective-permute-start.6
  41.5 1.0 %collective-permute-start.5 = (bf16[512,128]{1,0:T(8,128)(2,1)S(1)}, bf16[512,128]{1,0:T(8,128)(2,1)S(1)}, u32[]{:S(2)}, u32[]{:S(2)}) collective-permute-start(bf16[512,128]{1,0:T(8,128)(2,1)S(1)} %add_convert_fusion.p0_ref), channel_id=1, source_target_pairs={{0,1},{1,2},{2,3},{3,0},{4,5},{5,6},{6,7},{7,4},{8,9},{9,10},{10,1... | collective-permute-start | bytes 393224 | tf_op jit(solution)/shard_map/ppermute | solution.py:234
  42.5 2.0 %collective-permute-start.9 = (f32[16,256]{1,0:T(8,128)S(1)}, f32[16,256]{1,0:T(8,128)S(1)}, u32[]{:S(2)}, u32[]{:S(2)}) collective-permute-start(f32[16,256]{1,0:T(8,128)S(1)} %get-tuple-element.26.own_ref), channel_id=1, source_target_pairs={{4,0},{8,4},{12,8},{16,12},{20,16},{24,20},{28,24},{32,28},{36,32}... | collective-permute-start | bytes 49160 | tf_op jit(solution)/shard_map/ppermute | solution.py:242
  44.5 2.4 %collective-permute-start.8 = (f32[16,256]{1,0:T(8,128)S(1)}, f32[16,256]{1,0:T(8,128)S(1)}, u32[]{:S(2)}, u32[]{:S(2)}) collective-permute-start(f32[16,256]{1,0:T(8,128)S(1)} %get-tuple-element.26.own_ref), channel_id=1, source_target_pairs={{0,4},{4,8},{8,12},{12,16},{16,20},{20,24},{24,28},{28,32},{32,36}... | collective-permute-start | bytes 49160 | tf_op jit(solution)/shard_map/ppermute | solution.py:238
  46.9 0.0 collective-permute-done.9.after_ref
  46.9 4.7 %collective-permute-done.8.before_ref = f32[16,256]{1,0:T(8,128)S(1)} collective-permute-done((f32[16,256]{1,0:T(8,128)S(1)}, f32[16,256]{1,0:T(8,128)S(1)}, u32[]{:S(2)}, u32[]{:S(2)}) %collective-permute-start.8) | collective-permute-done | bytes 16416 | tf_op jit(solution)/shard_map/ppermute | solution.py:238
  51.7 2.8 %lists.1.pick_ref = bf16[768,512]{1,0:T(8,128)(2,1)S(1)} custom-call(f32[16,256]{1,0:T(8,128)S(1)} %collective-permute-done.8.before_ref, f32[16,256]{1,0:T(8,128)S(1)} %get-tuple-element.26.own_ref, f32[16,256]{1,0:T(8,128)S(1)} %collective-permute-done.9.after_ref), custom_call_target="tpu_custom_call" | custom-call | flops 1000000000 | bytes 4194304 | tf_op jit(solution)/shard_map/lists/pallas_call | solution.py:220
  54.4 0.0 collective-permute-done.7.p3_ref
  54.4 0.0 collective-permute-done.6.p2_ref
  54.5 0.0 collective-permute-done.5.p1_ref
  54.5 2.9 %scattered.1 = (bf16[512,1024]{1,0:T(8,128)(2,1)S(1)}, bf16[4,256,128]{2,1,0:T(8,128)(2,1)S(1)}, bf16[4,256,128]{2,1,0:T(8,128)(2,1)S(1)}) custom-call(bf16[512,128]{1,0:T(8,128)(2,1)S(1)} %add_convert_fusion.p0_ref, bf16[512,128]{1,0:T(8,128)(2,1)S(1)} %collective-permute-done.5.p1_ref, bf16[512,128]{1,0:T(8,128)(2,1)S(1)} %collective-permute-done.6.p2_ref, ...), custom_call_target="tpu_custom_call" | custom-call | flops 2000000000 | bytes 4194304 | tf_op jit(solution)/shard_map/scattered/pallas_call | solution.py:220
  57.4 1.9 %collective-permute-start.10 = (bf16[4,256,128]{2,1,0:T(8,128)(2,1)S(1)}, bf16[4,256,128]{2,1,0:T(8,128)(2,1)S(1)}, u32[]{:S(2)}, u32[]{:S(2)}) collective-permute-start(bf16[4,256,128]{2,1,0:T(8,128)(2,1)S(1)} %get-tuple-element.28), channel_id=1, source_target_pairs={{0,4},{4,8},{8,12},{12,16},{16,20},{20,24},{24,28},{28,32},{32,36}... | collective-permute-start | bytes 786440 | tf_op jit(solution)/shard_map/ppermute | solution.py:238
  59.3 5.8 %collective-permute-start.11 = (bf16[4,256,128]{2,1,0:T(8,128)(2,1)S(1)}, bf16[4,256,128]{2,1,0:T(8,128)(2,1)S(1)}, u32[]{:S(2)}, u32[]{:S(2)}) collective-permute-start(bf16[4,256,128]{2,1,0:T(8,128)(2,1)S(1)} %get-tuple-element.29), channel_id=1, source_target_pairs={{4,0},{8,4},{12,8},{16,12},{20,16},{24,20},{28,24},{32,28},{36,32}... | collective-permute-start | bytes 786440 | tf_op jit(solution)/shard_map/ppermute | solution.py:242
  65.1 1.2 %returned.1 = f32[4,256,128]{2,1,0:T(8,128)S(1)} custom-call(bf16[512,1024]{1,0:T(8,128)(2,1)S(1)} %get-tuple-element.27.waves_ref, bf16[2,512,512]{2,1,0:T(8,128)(2,1)S(1)} %copy-done, bf16[768,512]{1,0:T(8,128)(2,1)S(1)} %lists.1.pick_ref, f32[2,768,256]{2,1,0:T(8,128)S(1)} %get-tuple-element.18.mom_cos, f32[2,768,256]{2,1,0:T(8,128)S(1)} %get-tuple-element.19.mom_sin), custom_call_target="tpu_custom_call" | custom-call | flops 1000000000 | bytes 4194304 | tf_op jit(solution)/shard_map/returned/pallas_call | solution.py:220
  66.3 0.9 %collective-permute-done.10 = bf16[4,256,128]{2,1,0:T(8,128)(2,1)S(1)} collective-permute-done((bf16[4,256,128]{2,1,0:T(8,128)(2,1)S(1)}, bf16[4,256,128]{2,1,0:T(8,128)(2,1)S(1)}, u32[]{:S(2)}, u32[]{:S(2)}) %collective-permute-start.10) | collective-permute-done | bytes 262176 | tf_op jit(solution)/shard_map/ppermute | solution.py:238
  67.2 1.8 %collective-permute-done.11 = bf16[4,256,128]{2,1,0:T(8,128)(2,1)S(1)} collective-permute-done((bf16[4,256,128]{2,1,0:T(8,128)(2,1)S(1)}, bf16[4,256,128]{2,1,0:T(8,128)(2,1)S(1)}, u32[]{:S(2)}, u32[]{:S(2)}) %collective-permute-start.11) | collective-permute-done | bytes 262176 | tf_op jit(solution)/shard_map/ppermute | solution.py:242
  68.9 0.1 fusion.3
  69.0 2.6 %collective-permute-start.12 = (bf16[256,128]{1,0:T(8,128)(2,1)S(1)}, bf16[256,128]{1,0:T(8,128)(2,1)S(1)}, u32[]{:S(2)}, u32[]{:S(2)}) collective-permute-start(bf16[256,128]{1,0:T(8,128)(2,1)S(1)} %get-tuple-element.32), channel_id=1, source_target_pairs={{0,1},{1,2},{2,3},{3,0},{4,5},{5,6},{6,7},{7,4},{8,9},{9,10},{10,1... | collective-permute-start | bytes 196616 | tf_op jit(solution)/shard_map/ppermute | solution.py:234
  71.7 0.7 collective-permute-start.14
  72.4 1.5 %collective-permute-start.13 = (bf16[256,128]{1,0:T(8,128)(2,1)S(1)}, bf16[256,128]{1,0:T(8,128)(2,1)S(1)}, u32[]{:S(2)}, u32[]{:S(2)}) collective-permute-start(bf16[256,128]{1,0:T(8,128)(2,1)S(1)} %get-tuple-element.34), channel_id=1, source_target_pairs={{0,2},{1,3},{2,0},{3,1},{4,6},{5,7},{6,4},{7,5},{8,10},{9,11},{10,... | collective-permute-start | bytes 196616 | tf_op jit(solution)/shard_map/ppermute | solution.py:234
  73.8 0.8 collective-permute-done.12
  74.6 1.3 %collective-permute-done.14 = bf16[256,128]{1,0:T(8,128)(2,1)S(1)} collective-permute-done((bf16[256,128]{1,0:T(8,128)(2,1)S(1)}, bf16[256,128]{1,0:T(8,128)(2,1)S(1)}, u32[]{:S(2)}, u32[]{:S(2)}) %collective-permute-start.14) | collective-permute-done | bytes 65568 | tf_op jit(solution)/shard_map/ppermute | solution.py:234
  75.9 2.2 %collective-permute-done.13 = bf16[256,128]{1,0:T(8,128)(2,1)S(1)} collective-permute-done((bf16[256,128]{1,0:T(8,128)(2,1)S(1)}, bf16[256,128]{1,0:T(8,128)(2,1)S(1)}, u32[]{:S(2)}, u32[]{:S(2)}) %collective-permute-start.13) | collective-permute-done | bytes 65568 | tf_op jit(solution)/shard_map/ppermute | solution.py:234
  78.1 0.7 fusion.2
  (18 shorter events, 0.0 us)
Async XLA Ops:
  0.6 22.6 %collective-permute-start = (bf16[256,512]{1,0:T(8,128)(2,1)}, bf16[256,512]{1,0:T(8,128)(2,1)S(1)}, u32[]{:S(2)}, u32[]{:S(2)}) collective-permute-start(bf16[256,512]{1,0:T(8,128)(2,1)} %current_ref.1), channel_id=1, source_target_pairs={{0,4},{4,8},{8,12},{12,16},{16,20},{20,24},{24,28},{28,32},{32,36}... | collective-permute-start | bytes 786440 | tf_op jit(solution)/shard_map/ppermute | solution.py:238
  2.6 20.7 %collective-permute-start.1 = (bf16[256,512]{1,0:T(8,128)(2,1)}, bf16[256,512]{1,0:T(8,128)(2,1)S(1)}, u32[]{:S(2)}, u32[]{:S(2)}) collective-permute-start(bf16[256,512]{1,0:T(8,128)(2,1)} %current_ref.1), channel_id=1, source_target_pairs={{4,0},{8,4},{12,8},{16,12},{20,16},{24,20},{28,24},{32,28},{36,32}... | collective-permute-start | bytes 786440 | tf_op jit(solution)/shard_map/ppermute | solution.py:242
  10.7 1.2 %copy-start.2 = (bf16[2,512,512]{2,1,0:T(8,128)(2,1)S(1)}, bf16[2,512,512]{2,1,0:T(8,128)(2,1)}, u32[]{:S(2)}) copy-start(bf16[2,512,512]{2,1,0:T(8,128)(2,1)} %radiate_ref.4) | copy-start | bytes 3145732
  12.0 1.0 %copy-start.6 = (f32[3,32768]{1,0:T(4,128)S(1)}, f32[3,32768]{1,0:T(4,128)}, u32[]{:S(2)}) copy-start(f32[3,32768]{1,0:T(4,128)} %po_center_ref.1) | copy-start | bytes 1179652
  13.0 0.9 %copy-start.7 = (f32[3,16384]{1,0:T(4,128)S(1)}, f32[3,16384]{1,0:T(4,128)}, u32[]{:S(2)}) copy-start(f32[3,16384]{1,0:T(4,128)} %mom_center_ref.1) | copy-start | bytes 589828
  14.0 0.9 %copy-start.8 = (bf16[256,512]{1,0:T(8,128)(2,1)S(1)}, bf16[256,512]{1,0:T(8,128)(2,1)}, u32[]{:S(2)}) copy-start(bf16[256,512]{1,0:T(8,128)(2,1)} %current_ref.1) | copy-start | bytes 786436
  14.9 0.7 copy-start.9
  15.6 0.7 copy-start.10
  16.3 0.7 copy-start.11
  17.0 0.7 copy-start.12
  17.7 5.6 %copy-start.3 = (bf16[2,512,512]{2,1,0:T(8,128)(2,1)S(1)}, bf16[2,512,512]{2,1,0:T(8,128)(2,1)}, u32[]{:S(2)}) copy-start(bf16[2,512,512]{2,1,0:T(8,128)(2,1)} %receive_ref.3) | copy-start | bytes 3145732
  17.7 5.6 %copy-start.5 = (s32[2,512]{1,0:T(2,128)S(1)}, s32[2,512]{1,0:T(2,128)}, u32[]{:S(2)}) copy-start(s32[2,512]{1,0:T(2,128)} %lit_ref.1) | copy-start | bytes 12292
  26.6 6.3 %collective-permute-start.2 = (bf16[512,128]{1,0:T(8,128)(2,1)S(1)}, bf16[512,128]{1,0:T(8,128)(2,1)S(1)}, u32[]{:S(2)}, u32[]{:S(2)}) collective-permute-start(bf16[512,128]{1,0:T(8,128)(2,1)S(1)} %get-tuple-element.23), channel_id=1, source_target_pairs={{0,1},{1,2},{2,3},{3,0},{4,5},{5,6},{6,7},{7,4},{8,9},{9,10},{10,1... | collective-permute-start | bytes 393224 | tf_op jit(solution)/shard_map/ppermute | solution.py:234
  28.2 7.2 %collective-permute-start.3 = (bf16[512,128]{1,0:T(8,128)(2,1)S(1)}, bf16[512,128]{1,0:T(8,128)(2,1)S(1)}, u32[]{:S(2)}, u32[]{:S(2)}) collective-permute-start(bf16[512,128]{1,0:T(8,128)(2,1)S(1)} %get-tuple-element.24), channel_id=1, source_target_pairs={{0,2},{1,3},{2,0},{3,1},{4,6},{5,7},{6,4},{7,5},{8,10},{9,11},{10,... | collective-permute-start | bytes 393224 | tf_op jit(solution)/shard_map/ppermute | solution.py:234
  31.1 6.4 %collective-permute-start.4 = (bf16[512,128]{1,0:T(8,128)(2,1)S(1)}, bf16[512,128]{1,0:T(8,128)(2,1)S(1)}, u32[]{:S(2)}, u32[]{:S(2)}) collective-permute-start(bf16[512,128]{1,0:T(8,128)(2,1)S(1)} %get-tuple-element.25), channel_id=1, source_target_pairs={{0,3},{1,0},{2,1},{3,2},{4,7},{5,4},{6,5},{7,6},{8,11},{9,8},{10,9... | collective-permute-start | bytes 393224 | tf_op jit(solution)/shard_map/ppermute | solution.py:234
  37.6 16.9 %copy-start.4 = (bf16[512,128]{1,0:T(8,128)(2,1)}, bf16[512,128]{1,0:T(8,128)(2,1)S(1)}, u32[]{:S(2)}) copy-start(bf16[512,128]{1,0:T(8,128)(2,1)S(1)} %add_convert_fusion.p0_ref) | copy-start | bytes 393220
  37.6 16.9 %collective-permute-start.7 = (bf16[512,128]{1,0:T(8,128)(2,1)S(1)}, bf16[512,128]{1,0:T(8,128)(2,1)S(1)}, u32[]{:S(2)}, u32[]{:S(2)}) collective-permute-start(bf16[512,128]{1,0:T(8,128)(2,1)S(1)} %add_convert_fusion.p0_ref), channel_id=1, source_target_pairs={{0,3},{1,0},{2,1},{3,2},{4,7},{5,4},{6,5},{7,6},{8,11},{9,8},{10,9... | collective-permute-start | bytes 393224 | tf_op jit(solution)/shard_map/ppermute | solution.py:234
  41.5 13.0 %collective-permute-start.6 = (bf16[512,128]{1,0:T(8,128)(2,1)S(1)}, bf16[512,128]{1,0:T(8,128)(2,1)S(1)}, u32[]{:S(2)}, u32[]{:S(2)}) collective-permute-start(bf16[512,128]{1,0:T(8,128)(2,1)S(1)} %add_convert_fusion.p0_ref), channel_id=1, source_target_pairs={{0,2},{1,3},{2,0},{3,1},{4,6},{5,7},{6,4},{7,5},{8,10},{9,11},{10,... | collective-permute-start | bytes 393224 | tf_op jit(solution)/shard_map/ppermute | solution.py:234
  41.5 13.0 %collective-permute-start.5 = (bf16[512,128]{1,0:T(8,128)(2,1)S(1)}, bf16[512,128]{1,0:T(8,128)(2,1)S(1)}, u32[]{:S(2)}, u32[]{:S(2)}) collective-permute-start(bf16[512,128]{1,0:T(8,128)(2,1)S(1)} %add_convert_fusion.p0_ref), channel_id=1, source_target_pairs={{0,1},{1,2},{2,3},{3,0},{4,5},{5,6},{6,7},{7,4},{8,9},{9,10},{10,1... | collective-permute-start | bytes 393224 | tf_op jit(solution)/shard_map/ppermute | solution.py:234
  42.4 12.0 %copy-start = (bf16[2,512,512]{2,1,0:T(8,128)(2,1)S(1)}, bf16[2,512,512]{2,1,0:T(8,128)(2,1)}, u32[]{:S(2)}) copy-start(bf16[2,512,512]{2,1,0:T(8,128)(2,1)} %receive_ref.5) | copy-start | bytes 3145732
  42.4 12.0 %copy-start.1 = (bf16[2,512,512]{2,1,0:T(8,128)(2,1)S(1)}, bf16[2,512,512]{2,1,0:T(8,128)(2,1)}, u32[]{:S(2)}) copy-start(bf16[2,512,512]{2,1,0:T(8,128)(2,1)} %radiate_ref.5) | copy-start | bytes 3145732
  42.5 4.5 %collective-permute-start.9 = (f32[16,256]{1,0:T(8,128)S(1)}, f32[16,256]{1,0:T(8,128)S(1)}, u32[]{:S(2)}, u32[]{:S(2)}) collective-permute-start(f32[16,256]{1,0:T(8,128)S(1)} %get-tuple-element.26.own_ref), channel_id=1, source_target_pairs={{4,0},{8,4},{12,8},{16,12},{20,16},{24,20},{28,24},{32,28},{36,32}... | collective-permute-start | bytes 49160 | tf_op jit(solution)/shard_map/ppermute | solution.py:242
  44.5 7.2 %collective-permute-start.8 = (f32[16,256]{1,0:T(8,128)S(1)}, f32[16,256]{1,0:T(8,128)S(1)}, u32[]{:S(2)}, u32[]{:S(2)}) collective-permute-start(f32[16,256]{1,0:T(8,128)S(1)} %get-tuple-element.26.own_ref), channel_id=1, source_target_pairs={{0,4},{4,8},{8,12},{12,16},{16,20},{20,24},{24,28},{28,32},{32,36}... | collective-permute-start | bytes 49160 | tf_op jit(solution)/shard_map/ppermute | solution.py:238
  57.4 9.8 %collective-permute-start.10 = (bf16[4,256,128]{2,1,0:T(8,128)(2,1)S(1)}, bf16[4,256,128]{2,1,0:T(8,128)(2,1)S(1)}, u32[]{:S(2)}, u32[]{:S(2)}) collective-permute-start(bf16[4,256,128]{2,1,0:T(8,128)(2,1)S(1)} %get-tuple-element.28), channel_id=1, source_target_pairs={{0,4},{4,8},{8,12},{12,16},{16,20},{20,24},{24,28},{28,32},{32,36}... | collective-permute-start | bytes 786440 | tf_op jit(solution)/shard_map/ppermute | solution.py:238
  59.3 9.6 %collective-permute-start.11 = (bf16[4,256,128]{2,1,0:T(8,128)(2,1)S(1)}, bf16[4,256,128]{2,1,0:T(8,128)(2,1)S(1)}, u32[]{:S(2)}, u32[]{:S(2)}) collective-permute-start(bf16[4,256,128]{2,1,0:T(8,128)(2,1)S(1)} %get-tuple-element.29), channel_id=1, source_target_pairs={{4,0},{8,4},{12,8},{16,12},{20,16},{24,20},{28,24},{32,28},{36,32}... | collective-permute-start | bytes 786440 | tf_op jit(solution)/shard_map/ppermute | solution.py:242
  69.0 5.6 %collective-permute-start.12 = (bf16[256,128]{1,0:T(8,128)(2,1)S(1)}, bf16[256,128]{1,0:T(8,128)(2,1)S(1)}, u32[]{:S(2)}, u32[]{:S(2)}) collective-permute-start(bf16[256,128]{1,0:T(8,128)(2,1)S(1)} %get-tuple-element.32), channel_id=1, source_target_pairs={{0,1},{1,2},{2,3},{3,0},{4,5},{5,6},{6,7},{7,4},{8,9},{9,10},{10,1... | collective-permute-start | bytes 196616 | tf_op jit(solution)/shard_map/ppermute | solution.py:234
  71.7 4.3 %collective-permute-start.14 = (bf16[256,128]{1,0:T(8,128)(2,1)S(1)}, bf16[256,128]{1,0:T(8,128)(2,1)S(1)}, u32[]{:S(2)}, u32[]{:S(2)}) collective-permute-start(bf16[256,128]{1,0:T(8,128)(2,1)S(1)} %get-tuple-element.33), channel_id=1, source_target_pairs={{0,3},{1,0},{2,1},{3,2},{4,7},{5,4},{6,5},{7,6},{8,11},{9,8},{10,9... | collective-permute-start | bytes 196616 | tf_op jit(solution)/shard_map/ppermute | solution.py:234
  72.4 5.8 %collective-permute-start.13 = (bf16[256,128]{1,0:T(8,128)(2,1)S(1)}, bf16[256,128]{1,0:T(8,128)(2,1)S(1)}, u32[]{:S(2)}, u32[]{:S(2)}) collective-permute-start(bf16[256,128]{1,0:T(8,128)(2,1)S(1)} %get-tuple-element.34), channel_id=1, source_target_pairs={{0,2},{1,3},{2,0},{3,1},{4,6},{5,7},{6,4},{7,5},{8,10},{9,11},{10,... | collective-permute-start | bytes 196616 | tf_op jit(solution)/shard_map/ppermute | solution.py:234

commit v2 on v1

v2 whole, which is shorter than its diff:
```python
import math

import jax
import jax.numpy as jnp
from jax import lax
from jax.experimental import pallas as pl
from jax.experimental.pallas import tpu as pltpu
from jax.sharding import PartitionSpec as P

BF = jnp.bfloat16
F32 = jnp.float32
MIB = 1 << 20
TILE = 128

SIN = (6.283184911827348, -41.34158830218017, 81.59991361943669, -76.61414030096898, 41.34136538554672, -12.468818618465846)
COS = (0.9999991998413442, -19.738978175861465, 64.92858783993753, -85.27084362694508, 58.786940763161404, -21.065429407715534)
MAGIC = 12582912.0


def horner(coeffs, u):
    total = coeffs[-1] * u + coeffs[-2]
    for value in coeffs[-3::-1]:
        total = total * u + value
    return total


def turn(turns):
    f = turns - ((turns + MAGIC) - MAGIC)
    u = f * f
    return horner(COS, u), f * horner(SIN, u)


def mm(a, b):
    return jnp.dot(a, b, preferred_element_type=F32)


def hot(src_col, w_col, first, width):
    lanes = lax.broadcasted_iota(jnp.int32, (src_col.shape[0], width), 1) + first
    total = jnp.zeros((src_col.shape[0], width), F32)
    for slot in range(src_col.shape[1]):
        total = total + jnp.where(lanes == src_col[:, slot : slot + 1], w_col[:, slot : slot + 1], 0.0)
    return total.astype(BF)


def fill(pick_ref, at, low, high, src_col, w_col):
    whole = pick_ref.shape[1]
    low = max(low // 128 * 128, 0)
    high = min(-(-high // 128) * 128, whole)
    pick_ref[at, low:high] = hot(src_col, w_col, low, high - low)
    for a, b in ((0, low), (high, whole)):
        if a < b:
            pick_ref[at, a:b] = jnp.zeros((at.stop - at.start, b - a), BF)


def trig(center, dirs_ref, cos_ref, sin_ref):
    rows = center.shape[1]
    columns = jnp.concatenate([center, jnp.zeros((5, rows), F32)], axis=0).T
    step = 64
    for c in range(dirs_ref.shape[1]):
        waves = [dirs_ref[i, c : c + 1] * (0.5 / math.pi) for i in range(3)]
        for r in range(0, rows, step):
            part = columns[r : r + step]
            turns = part[:, 0:1] * waves[0] + part[:, 1:2] * waves[1] + part[:, 2:3] * waves[2]
            cosine, sine = turn(turns)
            cos_ref[c, r : r + step] = cosine
            sin_ref[c, r : r + step] = sine


def rotated(value, cosine, sine, orient):
    k = cosine.shape[-1]
    re, im = value[:, :k], value[:, k:]
    if orient < 0:
        return re * cosine + im * sine, im * cosine - re * sine
    return re * cosine - im * sine, re * sine + im * cosine


def radiated(rows_ref, at, radiate_ref, cos_ref, sin_ref, out_ref, base, cs_base):
    cones, _, k2 = radiate_ref.shape
    k = k2 // 2
    here = slice(base + at.start, base + at.stop)
    there = slice(cs_base + at.start, cs_base + at.stop)
    for c in range(cones):
        re, im = rotated(mm(rows_ref[at], radiate_ref[c]), cos_ref[c, there], sin_ref[c, there], -1)
        out_ref[here, c * k2 : c * k2 + k] = re.astype(BF)
        out_ref[here, c * k2 + k : (c + 1) * k2] = im.astype(BF)


def tiles(rows):
    return [slice(r, r + TILE) for r in range(0, rows, TILE)]


def prepare(
    current_hbm, radiate_hbm, dirs_hbm, mom_center_hbm, po_center_hbm, src_hbm, weight_hbm, mom_src_hbm, mom_weight_hbm,
    mom_cos, mom_sin, po_cos, po_sin, pick_ref, wave_ref, list_ref,
    current_ref, radiate_ref, dirs_ref, src_ref, weight_ref, mom_src_ref, mom_weight_ref, mom_c, po_c, sems,
):
    box = lax.axis_index("box")
    boxes = lax.axis_size("box")
    m = current_ref.shape[0]
    q = src_ref.shape[1]
    pairs = [(src_hbm, src_ref), (weight_hbm, weight_ref), (dirs_hbm, dirs_ref)]
    for i, other in enumerate((jnp.maximum(box - 1, 0), box, jnp.minimum(box + 1, boxes - 1))):
        at = pl.multiple_of(other * m, 128)
        pairs.append((mom_center_hbm.at[:, pl.ds(at, m)], mom_c.at[:, pl.ds(i * m, m)]))
    at = pl.multiple_of(box * q, 128)
    pairs.append((po_center_hbm.at[:, pl.ds(at, q)], po_c))
    pairs += [(current_hbm, current_ref), (radiate_hbm, radiate_ref), (mom_src_hbm, mom_src_ref), (mom_weight_hbm, mom_weight_ref)]
    copies = [pltpu.make_async_copy(here, there, sems.at[i]) for i, (here, there) in enumerate(pairs)]
    for copy in copies:
        copy.start()
    for copy in copies[:2]:
        copy.wait()
    src_col = (src_ref[...] - (box - 1) * m).T
    w_col = weight_ref[...].T
    step = 32
    for r in range(0, q, step):
        at = slice(r, r + step)
        fill(pick_ref, at, r * m // q, (r + step - 1) * m // q + 2 * m + 1, src_col[at], w_col[at])
    for copy in copies[2:]:
        copy.wait()
    list_ref[0:8] = mom_src_ref[...].astype(F32)
    list_ref[8:16] = mom_weight_ref[...]
    trig(mom_c[...], dirs_ref, mom_cos, mom_sin)
    for at in tiles(m):
        radiated(current_ref, at, radiate_ref, mom_cos, mom_sin, wave_ref, 0, m)
    trig(po_c[...], dirs_ref, po_cos, po_sin)


def incident(
    before_ref, after_ref, wave_ref, pick_ref, radiate_ref, receive_ref, mom_cos, mom_sin, po_cos, po_sin, lit_ref,
    far_ref, po_lit_ref,
    table,
):
    cone = lax.axis_index("cone")
    count = lax.axis_size("cone")
    m = before_ref.shape[0]
    q, share = far_ref.shape
    cones, _, k2 = radiate_ref.shape
    k = k2 // 2
    table[m : 2 * m] = wave_ref[...]
    for at in tiles(m):
        radiated(before_ref, at, radiate_ref, mom_cos, mom_sin, table, 0, 0)
        radiated(after_ref, at, radiate_ref, mom_cos, mom_sin, table, 2 * m, 2 * m)
    lit_col = jnp.concatenate([lit_ref[...].astype(F32), jnp.zeros((8 - cones, q), F32)], axis=0).T
    columns = pl.ds(pl.multiple_of(lax.rem(cone + 2, count) * share, share), share)
    for at in tiles(q):
        total = None
        for c in range(cones):
            value = mm(pick_ref[at], table[:, c * k2 : (c + 1) * k2])
            mask = lit_col[at, c : c + 1]
            re, im = rotated(value, po_cos[c, at] * mask, po_sin[c, at] * mask, 1)
            re, im = re.astype(BF), im.astype(BF)
            po_lit_ref[at, c * k2 : c * k2 + k] = re
            po_lit_ref[at, c * k2 + k : (c + 1) * k2] = im
            part = mm(re, receive_ref[c, :k, columns]) + mm(im, receive_ref[c, k:, columns])
            total = part if total is None else total + part
        far_ref[at] = total.astype(BF)


def received(po_lit_ref, receive_ref, own_ref, s1_ref, s3_ref, chunks):
    cones, k2, n = receive_ref.shape
    for at in tiles(po_lit_ref.shape[0]):
        total = None
        for c in range(cones):
            part = mm(po_lit_ref[at, c * k2 : (c + 1) * k2], receive_ref[c])
            total = part if total is None else total + part
        put_chunks(chunks, at, total)
    own_ref[...] = chunks[0]
    s1_ref[...] = chunks[1].astype(BF)
    s3_ref[...] = chunks[3].astype(BF)


def lists(before_ref, own_ref, after_ref, pick_ref):
    box = lax.axis_index("box")
    m = own_ref.shape[1]
    q = pick_ref.shape[1]
    ratio = q // m
    first = (box * q).astype(F32)
    for i, ref in enumerate((before_ref, own_ref, after_ref)):
        src_col = (ref[0:8] - first).astype(jnp.int32).T
        w_col = ref[8:16].T
        step = 32
        for r in range(0, m, step):
            middle = (i - 1) * q + r * ratio
            at = slice(i * m + r, i * m + r + step)
            fill(pick_ref, at, middle - q, middle + (step - 1) * ratio + q + 1, src_col[r : r + step], w_col[r : r + step])


def put_chunks(out, at, total):
    cone = lax.axis_index("cone")
    count, _, share = out.shape
    for j in range(count):
        slot = lax.rem(j - cone + count, count)
        out[slot, at] = total[:, j * share : (j + 1) * share].astype(out.dtype)


def scattered(
    p0_ref, p1_ref, p2_ref, p3_ref, radiate_ref, receive_ref, pick_ref, po_cos, po_sin, mom_cos, mom_sin,
    waves_ref, out_ref,
    whole,
):
    cone = lax.axis_index("cone")
    q, share = p0_ref.shape
    count = whole.shape[1] // share
    for s, ref in enumerate((p0_ref, p1_ref, p2_ref, p3_ref)):
        owner = lax.rem(cone - s + count, count)
        whole[:, pl.ds(pl.multiple_of(owner * share, share), share)] = ref[...]
    for at in tiles(q):
        radiated(whole, at, radiate_ref, po_cos, po_sin, waves_ref, 0, 0)
    tested(0, waves_ref, receive_ref, pick_ref, mom_cos, mom_sin, out_ref)


def tested(part, waves_ref, receive_ref, pick_ref, mom_cos, mom_sin, out_ref):
    cones, k2, _ = receive_ref.shape
    k = k2 // 2
    rows = out_ref.shape[1]
    q = waves_ref.shape[0]
    ratio = q // rows
    for at in tiles(rows):
        here = slice(part * rows + at.start, part * rows + at.stop)
        low = max((part - 1) * q + at.start * ratio - q, 0) // 256 * 256
        high = min(-(-((part - 1) * q + (at.stop - 1) * ratio + q + 1) // 256) * 256, q)
        total = None
        for c in range(cones):
            value = mm(pick_ref[here, low:high], waves_ref[low:high, c * k2 : (c + 1) * k2])
            re, im = rotated(value, mom_cos[c, here], mom_sin[c, here], 1)
            piece = mm(re.astype(BF), receive_ref[c, :k]) + mm(im.astype(BF), receive_ref[c, k:])
            total = piece if total is None else total + piece
        put_chunks(out_ref, at, total)


def tested_after(*refs):
    tested(2, *refs)


def tested_own(*refs):
    tested(1, *refs)


def call(body, outs, ins, scratch=(), space=pltpu.VMEM, flops=0, vmem=24):
    return pl.pallas_call(
        body,
        out_shape=outs,
        in_specs=[pl.BlockSpec(memory_space=space) for _ in ins],
        out_specs=jax.tree.map(lambda _: pl.BlockSpec(memory_space=pltpu.VMEM), outs),
        scratch_shapes=list(scratch),
        compiler_params=pltpu.CompilerParams(vmem_limit_bytes=vmem * MIB),
        cost_estimate=pl.CostEstimate(flops=flops, bytes_accessed=4 * MIB, transcendentals=0),
        name=body.__name__,
    )(*ins)


def turned(value, shift):
    count = lax.axis_size("cone")
    return lax.ppermute(value, "cone", [(i, (i + shift) % count) for i in range(count)])


def upward(value):
    return lax.ppermute(value, "box", [(i, i + 1) for i in range(lax.axis_size("box") - 1)])


def downward(value):
    return lax.ppermute(value, "box", [(i + 1, i) for i in range(lax.axis_size("box") - 1)])


def shards(
    mom_current, mom_radiate, po_receive, po_radiate, mom_receive, dirs, mom_center, po_center, po_src, po_weight, mom_src,
    mom_weight, lit,
):
    shape = jax.ShapeDtypeStruct
    m, n = mom_current.shape
    cones, q = lit.shape
    k2 = mom_radiate.shape[2]
    k = k2 // 2
    count = lax.axis_size("cone")
    share = n // count
    width = cones * k2

    before = upward(mom_current)
    after = downward(mom_current)
    waves3 = jnp.transpose(dirs, (1, 0, 2))
    staged = (mom_current, mom_radiate, waves3, po_src, po_weight, mom_src, mom_weight)
    mom_cos, mom_sin, po_cos, po_sin, pick, wave, entries = call(
        prepare,
        (
            shape((cones, 3 * m, k), F32), shape((cones, 3 * m, k), F32), shape((cones, q, k), F32), shape((cones, q, k), F32),
            shape((q, 3 * m), BF), shape((m, width), BF), shape((16, m), F32),
        ),
        (mom_current, mom_radiate, waves3, mom_center, po_center, po_src, po_weight, mom_src, mom_weight),
        tuple(pltpu.VMEM(value.shape, value.dtype) for value in staged)
        + (pltpu.VMEM((3, 3 * m), F32), pltpu.VMEM((3, q), F32), pltpu.SemaphoreType.DMA((11,))),
        pltpu.HBM,
        flops=4_000_000_000,
    )
    s2, po_lit = call(
        incident,
        (shape((q, share), BF), shape((q, width), BF)),
        (before, after, wave, pick, mom_radiate, po_receive, mom_cos, mom_sin, po_cos, po_sin, lit),
        (pltpu.VMEM((3 * m, width), BF),),
        flops=2_000_000_000,
    )
    s2 = turned(s2, 2)
    own, s1, s3 = call(
        received,
        (shape((q, share), F32), shape((q, share), BF), shape((q, share), BF)),
        (po_lit, po_receive),
        (pltpu.VMEM((count, q, share), F32),),
        flops=1_000_000_000,
    )
    s1 = turned(s1, 1)
    s3 = turned(s3, 3)
    own, entries = lax.optimization_barrier((own, entries))
    before_list = upward(entries)
    after_list = downward(entries)
    back = call(lists, shape((3 * m, q), BF), (before_list, entries, after_list), flops=1_000_000_000)
    po_share = (own + s1.astype(F32) + s2.astype(F32) + s3.astype(F32)).astype(BF)
    p2 = turned(po_share, 2)
    p1 = turned(po_share, 1)
    p3 = turned(po_share, 3)
    waves, down = call(
        scattered,
        (shape((q, width), BF), shape((count, m, share), BF)),
        (po_share, p1, p2, p3, po_radiate, mom_receive, back, po_cos, po_sin, mom_cos, mom_sin),
        (pltpu.VMEM((q, n), BF),),
        flops=2_000_000_000,
    )
    rest = (mom_receive, back, mom_cos, mom_sin)
    from_after = downward(down)
    up = call(tested_after, shape((count, m, share), BF), (waves,) + rest, flops=1_000_000_000)
    from_before = upward(up)
    up, own_waves = lax.optimization_barrier((up, waves))
    field = call(tested_own, shape((count, m, share), F32), (own_waves,) + rest, flops=1_000_000_000)
    field = field + from_before.astype(F32) + from_after.astype(F32)
    f2 = turned(field[2].astype(BF), 2)
    f1 = turned(field[1].astype(BF), 1)
    f3 = turned(field[3].astype(BF), 3)
    mom_field = field[0] + f1.astype(F32) + f2.astype(F32) + f3.astype(F32)
    return mom_field, po_share


def solution(mesh):
    in_specs = (
        P("box", None),
        P("cone", None, None),
        P("cone", None, None),
        P("cone", None, None),
        P("cone", None, None),
        P("cone", None, None),
        P(),
        P(),
        P(None, "box"),
        P(None, "box"),
        P(None, "box"),
        P(None, "box"),
        P("cone", "box"),
    )
    out_specs = (P("box", "cone"), P("box", "cone"))
    return jax.shard_map(shards, mesh=mesh, in_specs=in_specs, out_specs=out_specs, check_vma=False)
```

time: 79.5 us -> 78 us (0.981)
  starting transfers between devices: 37 us -> 35.8 us
    ppermute x9, starting transfers between devices: 15.5 us -> 14.4 us  [turned(): lax.ppermute(value, 'cone', [(i, (i + shift) % count) for i in range(coun...]
    pallas_call x5 -> x7, Pallas kernels: 15.6 us -> 16 us  [call(): pl.pallas_call(body, out_shape=outs, in_specs=[pl.BlockSpec(memory_space=...]
    unnamed x27 -> x28, local copies, waits for them, and re-layouts: 7.71 us -> 7.7 us
  transfers between devices with their start and end apart: 15 -> 15, of which waited for: 9 -> 9; matrix products, arithmetic and copies ran while one was open for 1% -> 0% of each run, Pallas kernels for 12% -> 12%
where the time goes in v2:
time: 78 us; the launch traced here: 77.4 us
  starting transfers between devices  35.8 us (46%)
  waiting for transfers between devices  16.2 us (21%)
  Pallas kernels  16 us (21%)
  local copies, waits for them, and re-layouts  7.72 us (10%)
  between operations  0.88 us (1%)
  other arithmetic  0.85 us (1%)
    pallas_call x7, Pallas kernels, call(): pl.pallas_call(body, out_shape=outs, in_specs=[pl.BlockSpec(memory_space=...  16 us
    ppermute x3, starting transfers between devices, downward(): lax.ppermute(value, 'box', [(i + 1, i) for i in range(lax.axis_size('box'...  15.1 us
    ppermute x9, starting transfers between devices, turned(): lax.ppermute(value, 'cone', [(i, (i + shift) % count) for i in range(coun...  14.4 us
    ppermute x9, waiting for transfers between devices, turned(): lax.ppermute(value, 'cone', [(i, (i + shift) % count) for i in range(coun...  8.84 us
    unnamed x28, local copies, waits for them, and re-layouts  7.7 us
    ppermute x3, starting transfers between devices, upward(): lax.ppermute(value, 'box', [(i, i + 1) for i in range(lax.axis_size('box'...  6.25 us
    ppermute x3, waiting for transfers between devices, upward(): lax.ppermute(value, 'box', [(i, i + 1) for i in range(lax.axis_size('box'...  5.62 us
    ppermute x3, waiting for transfers between devices, downward(): lax.ppermute(value, 'box', [(i + 1, i) for i in range(lax.axis_size('box'...  1.76 us
  transfers between devices with their start and end apart: 15, of which 9 were waited for; matrix products, arithmetic and copies ran while one was open for 0% of the time, Pallas kernels for 12%

profile of v2, /device:TPU:6, one launch (start us, length us, event | category | flops | bytes accessed | tf_op | source)
XLA Modules:
  0.0 77.4 jit_solution(7261731623082954608)
XLA Ops:
  0.6 1.9 %collective-permute-start = (bf16[256,512]{1,0:T(8,128)(2,1)}, bf16[256,512]{1,0:T(8,128)(2,1)S(1)}, u32[]{:S(2)}, u32[]{:S(2)}) collective-permute-start(bf16[256,512]{1,0:T(8,128)(2,1)} %current_hbm.1), channel_id=1, source_target_pairs={{0,4},{4,8},{8,12},{12,16},{16,20},{20,24},{24,28},{28,32},{32,36}... | collective-permute-start | bytes 786440 | tf_op jit(solution)/shard_map/ppermute | solution.py:259
  2.6 7.5 %collective-permute-start.1 = (bf16[256,512]{1,0:T(8,128)(2,1)}, bf16[256,512]{1,0:T(8,128)(2,1)S(1)}, u32[]{:S(2)}, u32[]{:S(2)}) collective-permute-start(bf16[256,512]{1,0:T(8,128)(2,1)} %current_hbm.1), channel_id=1, source_target_pairs={{4,0},{8,4},{12,8},{16,12},{20,16},{24,20},{28,24},{32,28},{36,32}... | collective-permute-start | bytes 786440 | tf_op jit(solution)/shard_map/ppermute | solution.py:263
  10.0 1.2 %copy-done.2 = bf16[2,512,512]{2,1,0:T(8,128)(2,1)S(1)} copy-done((bf16[2,512,512]{2,1,0:T(8,128)(2,1)S(1)}, bf16[2,512,512]{2,1,0:T(8,128)(2,1)}, u32[]{:S(2)}) %copy-start.2) | copy-done | bytes 1048600
  11.3 1.0 %copy-done.6 = f32[3,32768]{1,0:T(4,128)S(1)} copy-done((f32[3,32768]{1,0:T(4,128)S(1)}, f32[3,32768]{1,0:T(4,128)}, u32[]{:S(2)}) %copy-start.6) | copy-done | bytes 393240
  12.3 0.9 %copy-done.7 = f32[3,16384]{1,0:T(4,128)S(1)} copy-done((f32[3,16384]{1,0:T(4,128)S(1)}, f32[3,16384]{1,0:T(4,128)}, u32[]{:S(2)}) %copy-start.7) | copy-done | bytes 196632
  13.3 0.9 %copy-done.8 = bf16[256,512]{1,0:T(8,128)(2,1)S(1)} copy-done((bf16[256,512]{1,0:T(8,128)(2,1)S(1)}, bf16[256,512]{1,0:T(8,128)(2,1)}, u32[]{:S(2)}) %copy-start.8) | copy-done | bytes 262168
  14.2 0.7 copy-done.9
  14.9 0.7 copy-done.10
  15.6 0.7 copy-done.11
  16.3 0.7 copy-done.12
  17.0 0.7 copy-done.13
  17.7 5.3 %prepare.1 = (f32[2,768,256]{2,1,0:T(8,128)S(1)}, f32[2,768,256]{2,1,0:T(8,128)S(1)}, f32[2,512,256]{2,1,0:T(8,128)S(1)}, f32[2,512,256]{2,1,0:T(8,128)S(1)}, bf...) custom-call(bf16[256,512]{1,0:T(8,128)(2,1)S(1)} %copy-done.8, ...), custom_call_target="tpu_custom_call" | custom-call | flops 4000000000 | bytes 4194304 | tf_op jit(solution)/shard_map/prepare/pallas_call | solution.py:241
  23.1 3.0 %incident.1 = (bf16[512,128]{1,0:T(8,128)(2,1)S(1)}, bf16[512,1024]{1,0:T(8,128)(2,1)S(1)}) custom-call(bf16[256,512]{1,0:T(8,128)(2,1)S(1)} %collective-permute-done.before_ref, bf16[256,512]{1,0:T(8,128)(2,1)S(1)} %collective-permute-done.1.after_ref, bf16[256,1024]{1,0:T(8,128)(2,1)S(1)} %get-tuple-element.19.wave_ref, ...), custom_call_target="tpu_custom_call" | custom-call | flops 2000000000 | bytes 4194304 | tf_op jit(solution)/shard_map/incident/pallas_call | solution.py:241
  26.1 0.9 %received.1 = (f32[512,128]{1,0:T(8,128)S(1)}, bf16[512,128]{1,0:T(8,128)(2,1)S(1)}, bf16[512,128]{1,0:T(8,128)(2,1)S(1)}) custom-call(bf16[512,1024]{1,0:T(8,128)(2,1)S(1)} %get-tuple-element.25.po_lit_ref, bf16[2,512,512]{2,1,0:T(8,128)(2,1)S(1)} %copy-done.3), custom_call_target="tpu_custom_call" | custom-call | flops 1000000000 | bytes 4194304 | tf_op jit(solution)/shard_map/received/pallas_call | solution.py:241
  27.0 1.7 %collective-permute-start.2 = (bf16[512,128]{1,0:T(8,128)(2,1)S(1)}, bf16[512,128]{1,0:T(8,128)(2,1)S(1)}, u32[]{:S(2)}, u32[]{:S(2)}) collective-permute-start(bf16[512,128]{1,0:T(8,128)(2,1)S(1)} %get-tuple-element.29), channel_id=1, source_target_pairs={{0,1},{1,2},{2,3},{3,0},{4,5},{5,6},{6,7},{7,4},{8,9},{9,10},{10,1... | collective-permute-start | bytes 393224 | tf_op jit(solution)/shard_map/ppermute | solution.py:255
  28.6 1.7 %collective-permute-start.4 = (bf16[512,128]{1,0:T(8,128)(2,1)S(1)}, bf16[512,128]{1,0:T(8,128)(2,1)S(1)}, u32[]{:S(2)}, u32[]{:S(2)}) collective-permute-start(bf16[512,128]{1,0:T(8,128)(2,1)S(1)} %get-tuple-element.31), channel_id=1, source_target_pairs={{0,3},{1,0},{2,1},{3,2},{4,7},{5,4},{6,5},{7,6},{8,11},{9,8},{10,9... | collective-permute-start | bytes 393224 | tf_op jit(solution)/shard_map/ppermute | solution.py:255
  30.3 2.0 %collective-permute-start.3 = (bf16[512,128]{1,0:T(8,128)(2,1)S(1)}, bf16[512,128]{1,0:T(8,128)(2,1)S(1)}, u32[]{:S(2)}, u32[]{:S(2)}) collective-permute-start(bf16[512,128]{1,0:T(8,128)(2,1)S(1)} %get-tuple-element.30), channel_id=1, source_target_pairs={{0,2},{1,3},{2,0},{3,1},{4,6},{5,7},{6,4},{7,5},{8,10},{9,11},{10,... | collective-permute-start | bytes 393224 | tf_op jit(solution)/shard_map/ppermute | solution.py:255
  32.3 1.0 %collective-permute-done.2 = bf16[512,128]{1,0:T(8,128)(2,1)S(1)} collective-permute-done((bf16[512,128]{1,0:T(8,128)(2,1)S(1)}, bf16[512,128]{1,0:T(8,128)(2,1)S(1)}, u32[]{:S(2)}, u32[]{:S(2)}) %collective-permute-start.2) | collective-permute-done | bytes 131104 | tf_op jit(solution)/shard_map/ppermute | solution.py:255
  33.2 0.4 collective-permute-done.4
  33.6 3.2 %collective-permute-done.3 = bf16[512,128]{1,0:T(8,128)(2,1)S(1)} collective-permute-done((bf16[512,128]{1,0:T(8,128)(2,1)S(1)}, bf16[512,128]{1,0:T(8,128)(2,1)S(1)}, u32[]{:S(2)}, u32[]{:S(2)}) %collective-permute-start.3) | collective-permute-done | bytes 131104 | tf_op jit(solution)/shard_map/ppermute | solution.py:255
  36.8 0.1 add_convert_fusion.p0_ref
  36.8 0.0 copy-start.4
  36.8 0.0 copy-start
  36.9 0.0 copy-start.1
  36.9 3.4 %collective-permute-start.7 = (bf16[512,128]{1,0:T(8,128)(2,1)S(1)}, bf16[512,128]{1,0:T(8,128)(2,1)S(1)}, u32[]{:S(2)}, u32[]{:S(2)}) collective-permute-start(bf16[512,128]{1,0:T(8,128)(2,1)S(1)} %add_convert_fusion.p0_ref), channel_id=1, source_target_pairs={{0,3},{1,0},{2,1},{3,2},{4,7},{5,4},{6,5},{7,6},{8,11},{9,8},{10,9... | collective-permute-start | bytes 393224 | tf_op jit(solution)/shard_map/ppermute | solution.py:255
  40.3 0.9 %collective-permute-start.6 = (bf16[512,128]{1,0:T(8,128)(2,1)S(1)}, bf16[512,128]{1,0:T(8,128)(2,1)S(1)}, u32[]{:S(2)}, u32[]{:S(2)}) collective-permute-start(bf16[512,128]{1,0:T(8,128)(2,1)S(1)} %add_convert_fusion.p0_ref), channel_id=1, source_target_pairs={{0,2},{1,3},{2,0},{3,1},{4,6},{5,7},{6,4},{7,5},{8,10},{9,11},{10,... | collective-permute-start | bytes 393224 | tf_op jit(solution)/shard_map/ppermute | solution.py:255
  41.2 0.1 collective-permute-start.5
  41.2 1.9 %collective-permute-start.9 = (f32[16,256]{1,0:T(8,128)S(1)}, f32[16,256]{1,0:T(8,128)S(1)}, u32[]{:S(2)}, u32[]{:S(2)}) collective-permute-start(f32[16,256]{1,0:T(8,128)S(1)} %get-tuple-element.32.own_ref), channel_id=1, source_target_pairs={{4,0},{8,4},{12,8},{16,12},{20,16},{24,20},{28,24},{32,28},{36,32}... | collective-permute-start | bytes 49160 | tf_op jit(solution)/shard_map/ppermute | solution.py:263
  43.1 2.4 %collective-permute-start.8 = (f32[16,256]{1,0:T(8,128)S(1)}, f32[16,256]{1,0:T(8,128)S(1)}, u32[]{:S(2)}, u32[]{:S(2)}) collective-permute-start(f32[16,256]{1,0:T(8,128)S(1)} %get-tuple-element.32.own_ref), channel_id=1, source_target_pairs={{0,4},{4,8},{8,12},{12,16},{16,20},{20,24},{24,28},{28,32},{32,36}... | collective-permute-start | bytes 49160 | tf_op jit(solution)/shard_map/ppermute | solution.py:259
  45.6 4.7 %collective-permute-done.8.before_ref = f32[16,256]{1,0:T(8,128)S(1)} collective-permute-done((f32[16,256]{1,0:T(8,128)S(1)}, f32[16,256]{1,0:T(8,128)S(1)}, u32[]{:S(2)}, u32[]{:S(2)}) %collective-permute-start.8) | collective-permute-done | bytes 16416 | tf_op jit(solution)/shard_map/ppermute | solution.py:259
  50.3 2.6 %lists.1.pick_ref.refs_2_ = bf16[768,512]{1,0:T(8,128)(2,1)S(1)} custom-call(f32[16,256]{1,0:T(8,128)S(1)} %collective-permute-done.8.before_ref, f32[16,256]{1,0:T(8,128)S(1)} %get-tuple-element.32.own_ref, f32[16,256]{1,0:T(8,128)S(1)} %collective-permute-done.9.after_ref), custom_call_target="tpu_custom_call" | custom-call | flops 1000000000 | bytes 4194304 | tf_op jit(solution)/shard_map/lists/pallas_call | solution.py:241
  52.9 0.0 collective-permute-done.6.p2_ref
  52.9 0.0 collective-permute-done.5.p1_ref
  52.9 1.8 %scattered.1 = (bf16[512,1024]{1,0:T(8,128)(2,1)S(1)}, bf16[4,256,128]{2,1,0:T(8,128)(2,1)S(1)}) custom-call(bf16[512,128]{1,0:T(8,128)(2,1)S(1)} %add_convert_fusion.p0_ref, bf16[512,128]{1,0:T(8,128)(2,1)S(1)} %collective-permute-done.5.p1_ref, bf16[512,128]{1,0:T(8,128)(2,1)S(1)} %collective-permute-done.6.p2_ref, ...), custom_call_target="tpu_custom_call" | custom-call | flops 2000000000 | bytes 4194304 | tf_op jit(solution)/shard_map/scattered/pallas_call | solution.py:241
  54.8 1.2 %tested_after.1 = bf16[4,256,128]{2,1,0:T(8,128)(2,1)S(1)} custom-call(bf16[512,1024]{1,0:T(8,128)(2,1)S(1)} %get-tuple-element.34.refs_0_, bf16[2,512,512]{2,1,0:T(8,128)(2,1)S(1)} %copy-done, bf16[768,512]{1,0:T(8,128)(2,1)S(1)} %lists.1.pick_ref.refs_2_, f32[2,768,256]{2,1,0:T(8,128)S(1)} %get-tuple-element.21.mom_cos.refs_3_, ...), custom_call_target="tpu_custom_call" | custom-call | flops 1000000000 | bytes 4194304 | tf_op jit(solution)/shard_map/tested_after/pallas_call | solution.py:241
  55.9 1.9 %collective-permute-start.10 = (bf16[4,256,128]{2,1,0:T(8,128)(2,1)S(1)}, bf16[4,256,128]{2,1,0:T(8,128)(2,1)S(1)}, u32[]{:S(2)}, u32[]{:S(2)}) collective-permute-start(bf16[4,256,128]{2,1,0:T(8,128)(2,1)S(1)} %tested_after.1), channel_id=1, source_target_pairs={{0,4},{4,8},{8,12},{12,16},{16,20},{20,24},{24,28},{28,32},{32,36}... | collective-permute-start | bytes 786440 | tf_op jit(solution)/shard_map/ppermute | solution.py:259
  57.9 5.8 %collective-permute-start.11 = (bf16[4,256,128]{2,1,0:T(8,128)(2,1)S(1)}, bf16[4,256,128]{2,1,0:T(8,128)(2,1)S(1)}, u32[]{:S(2)}, u32[]{:S(2)}) collective-permute-start(bf16[4,256,128]{2,1,0:T(8,128)(2,1)S(1)} %get-tuple-element.35), channel_id=1, source_target_pairs={{4,0},{8,4},{12,8},{16,12},{20,16},{24,20},{28,24},{32,28},{36,32}... | collective-permute-start | bytes 786440 | tf_op jit(solution)/shard_map/ppermute | solution.py:263
  63.6 1.2 %tested_own.1 = f32[4,256,128]{2,1,0:T(8,128)S(1)} custom-call(bf16[512,1024]{1,0:T(8,128)(2,1)S(1)} %get-tuple-element.34.refs_0_, bf16[2,512,512]{2,1,0:T(8,128)(2,1)S(1)} %copy-done, bf16[768,512]{1,0:T(8,128)(2,1)S(1)} %lists.1.pick_ref.refs_2_, f32[2,768,256]{2,1,0:T(8,128)S(1)} %get-tuple-element.21.mom_cos.refs_3_, ...), custom_call_target="tpu_custom_call" | custom-call | flops 1000000000 | bytes 4194304 | tf_op jit(solution)/shard_map/tested_own/pallas_call | solution.py:241
  64.9 0.9 %collective-permute-done.10 = bf16[4,256,128]{2,1,0:T(8,128)(2,1)S(1)} collective-permute-done((bf16[4,256,128]{2,1,0:T(8,128)(2,1)S(1)}, bf16[4,256,128]{2,1,0:T(8,128)(2,1)S(1)}, u32[]{:S(2)}, u32[]{:S(2)}) %collective-permute-start.10) | collective-permute-done | bytes 262176 | tf_op jit(solution)/shard_map/ppermute | solution.py:259
  65.7 1.8 %collective-permute-done.11 = bf16[4,256,128]{2,1,0:T(8,128)(2,1)S(1)} collective-permute-done((bf16[4,256,128]{2,1,0:T(8,128)(2,1)S(1)}, bf16[4,256,128]{2,1,0:T(8,128)(2,1)S(1)}, u32[]{:S(2)}, u32[]{:S(2)}) %collective-permute-start.11) | collective-permute-done | bytes 262176 | tf_op jit(solution)/shard_map/ppermute | solution.py:263
  67.5 0.1 fusion.3
  67.6 2.6 %collective-permute-start.12 = (bf16[256,128]{1,0:T(8,128)(2,1)S(1)}, bf16[256,128]{1,0:T(8,128)(2,1)S(1)}, u32[]{:S(2)}, u32[]{:S(2)}) collective-permute-start(bf16[256,128]{1,0:T(8,128)(2,1)S(1)} %get-tuple-element.38), channel_id=1, source_target_pairs={{0,1},{1,2},{2,3},{3,0},{4,5},{5,6},{6,7},{7,4},{8,9},{9,10},{10,1... | collective-permute-start | bytes 196616 | tf_op jit(solution)/shard_map/ppermute | solution.py:255
  70.2 0.7 collective-permute-start.14
  70.9 1.4 %collective-permute-start.13 = (bf16[256,128]{1,0:T(8,128)(2,1)S(1)}, bf16[256,128]{1,0:T(8,128)(2,1)S(1)}, u32[]{:S(2)}, u32[]{:S(2)}) collective-permute-start(bf16[256,128]{1,0:T(8,128)(2,1)S(1)} %get-tuple-element.40), channel_id=1, source_target_pairs={{0,2},{1,3},{2,0},{3,1},{4,6},{5,7},{6,4},{7,5},{8,10},{9,11},{10,... | collective-permute-start | bytes 196616 | tf_op jit(solution)/shard_map/ppermute | solution.py:255
  72.4 0.8 %collective-permute-done.12 = bf16[256,128]{1,0:T(8,128)(2,1)S(1)} collective-permute-done((bf16[256,128]{1,0:T(8,128)(2,1)S(1)}, bf16[256,128]{1,0:T(8,128)(2,1)S(1)}, u32[]{:S(2)}, u32[]{:S(2)}) %collective-permute-start.12) | collective-permute-done | bytes 65568 | tf_op jit(solution)/shard_map/ppermute | solution.py:255
  73.2 1.3 %collective-permute-done.14 = bf16[256,128]{1,0:T(8,128)(2,1)S(1)} collective-permute-done((bf16[256,128]{1,0:T(8,128)(2,1)S(1)}, bf16[256,128]{1,0:T(8,128)(2,1)S(1)}, u32[]{:S(2)}, u32[]{:S(2)}) %collective-permute-start.14) | collective-permute-done | bytes 65568 | tf_op jit(solution)/shard_map/ppermute | solution.py:255
  74.5 2.2 %collective-permute-done.13 = bf16[256,128]{1,0:T(8,128)(2,1)S(1)} collective-permute-done((bf16[256,128]{1,0:T(8,128)(2,1)S(1)}, bf16[256,128]{1,0:T(8,128)(2,1)S(1)}, u32[]{:S(2)}, u32[]{:S(2)}) %collective-permute-start.13) | collective-permute-done | bytes 65568 | tf_op jit(solution)/shard_map/ppermute | solution.py:255
  76.7 0.7 fusion.2
  (21 shorter events, 0.1 us)
Async XLA Ops:
  0.6 22.4 %collective-permute-start = (bf16[256,512]{1,0:T(8,128)(2,1)}, bf16[256,512]{1,0:T(8,128)(2,1)S(1)}, u32[]{:S(2)}, u32[]{:S(2)}) collective-permute-start(bf16[256,512]{1,0:T(8,128)(2,1)} %current_hbm.1), channel_id=1, source_target_pairs={{0,4},{4,8},{8,12},{12,16},{16,20},{20,24},{24,28},{28,32},{32,36}... | collective-permute-start | bytes 786440 | tf_op jit(solution)/shard_map/ppermute | solution.py:259
  2.6 20.5 %collective-permute-start.1 = (bf16[256,512]{1,0:T(8,128)(2,1)}, bf16[256,512]{1,0:T(8,128)(2,1)S(1)}, u32[]{:S(2)}, u32[]{:S(2)}) collective-permute-start(bf16[256,512]{1,0:T(8,128)(2,1)} %current_hbm.1), channel_id=1, source_target_pairs={{4,0},{8,4},{12,8},{16,12},{20,16},{24,20},{28,24},{32,28},{36,32}... | collective-permute-start | bytes 786440 | tf_op jit(solution)/shard_map/ppermute | solution.py:263
  10.0 1.2 %copy-start.2 = (bf16[2,512,512]{2,1,0:T(8,128)(2,1)S(1)}, bf16[2,512,512]{2,1,0:T(8,128)(2,1)}, u32[]{:S(2)}) copy-start(bf16[2,512,512]{2,1,0:T(8,128)(2,1)} %radiate_ref.2) | copy-start | bytes 3145732
  11.3 1.0 %copy-start.6 = (f32[3,32768]{1,0:T(4,128)S(1)}, f32[3,32768]{1,0:T(4,128)}, u32[]{:S(2)}) copy-start(f32[3,32768]{1,0:T(4,128)} %po_center_hbm.1) | copy-start | bytes 1179652
  12.3 0.9 %copy-start.7 = (f32[3,16384]{1,0:T(4,128)S(1)}, f32[3,16384]{1,0:T(4,128)}, u32[]{:S(2)}) copy-start(f32[3,16384]{1,0:T(4,128)} %mom_center_hbm.1) | copy-start | bytes 589828
  13.3 0.9 %copy-start.8 = (bf16[256,512]{1,0:T(8,128)(2,1)S(1)}, bf16[256,512]{1,0:T(8,128)(2,1)}, u32[]{:S(2)}) copy-start(bf16[256,512]{1,0:T(8,128)(2,1)} %current_hbm.1) | copy-start | bytes 786436
  14.2 0.7 copy-start.9
  14.9 0.7 copy-start.10
  15.6 0.7 copy-start.11
  16.3 0.7 copy-start.12
  17.0 0.7 copy-start.13
  17.7 5.4 %copy-start.3 = (bf16[2,512,512]{2,1,0:T(8,128)(2,1)S(1)}, bf16[2,512,512]{2,1,0:T(8,128)(2,1)}, u32[]{:S(2)}) copy-start(bf16[2,512,512]{2,1,0:T(8,128)(2,1)} %receive_ref.4) | copy-start | bytes 3145732
  17.7 5.4 %copy-start.5 = (s32[2,512]{1,0:T(2,128)S(1)}, s32[2,512]{1,0:T(2,128)}, u32[]{:S(2)}) copy-start(s32[2,512]{1,0:T(2,128)} %lit_ref.1) | copy-start | bytes 12292
  27.0 6.3 %collective-permute-start.2 = (bf16[512,128]{1,0:T(8,128)(2,1)S(1)}, bf16[512,128]{1,0:T(8,128)(2,1)S(1)}, u32[]{:S(2)}, u32[]{:S(2)}) collective-permute-start(bf16[512,128]{1,0:T(8,128)(2,1)S(1)} %get-tuple-element.29), channel_id=1, source_target_pairs={{0,1},{1,2},{2,3},{3,0},{4,5},{5,6},{6,7},{7,4},{8,9},{9,10},{10,1... | collective-permute-start | bytes 393224 | tf_op jit(solution)/shard_map/ppermute | solution.py:255
  28.6 5.0 %collective-permute-start.4 = (bf16[512,128]{1,0:T(8,128)(2,1)S(1)}, bf16[512,128]{1,0:T(8,128)(2,1)S(1)}, u32[]{:S(2)}, u32[]{:S(2)}) collective-permute-start(bf16[512,128]{1,0:T(8,128)(2,1)S(1)} %get-tuple-element.31), channel_id=1, source_target_pairs={{0,3},{1,0},{2,1},{3,2},{4,7},{5,4},{6,5},{7,6},{8,11},{9,8},{10,9... | collective-permute-start | bytes 393224 | tf_op jit(solution)/shard_map/ppermute | solution.py:255
  30.3 6.5 %collective-permute-start.3 = (bf16[512,128]{1,0:T(8,128)(2,1)S(1)}, bf16[512,128]{1,0:T(8,128)(2,1)S(1)}, u32[]{:S(2)}, u32[]{:S(2)}) collective-permute-start(bf16[512,128]{1,0:T(8,128)(2,1)S(1)} %get-tuple-element.30), channel_id=1, source_target_pairs={{0,2},{1,3},{2,0},{3,1},{4,6},{5,7},{6,4},{7,5},{8,10},{9,11},{10,... | collective-permute-start | bytes 393224 | tf_op jit(solution)/shard_map/ppermute | solution.py:255
  36.8 16.1 %copy-start.4 = (bf16[512,128]{1,0:T(8,128)(2,1)}, bf16[512,128]{1,0:T(8,128)(2,1)S(1)}, u32[]{:S(2)}) copy-start(bf16[512,128]{1,0:T(8,128)(2,1)S(1)} %add_convert_fusion.p0_ref) | copy-start | bytes 393220
  36.8 16.1 %copy-start = (bf16[2,512,512]{2,1,0:T(8,128)(2,1)S(1)}, bf16[2,512,512]{2,1,0:T(8,128)(2,1)}, u32[]{:S(2)}) copy-start(bf16[2,512,512]{2,1,0:T(8,128)(2,1)} %refs_1_.3) | copy-start | bytes 3145732
  36.9 16.1 %copy-start.1 = (bf16[2,512,512]{2,1,0:T(8,128)(2,1)S(1)}, bf16[2,512,512]{2,1,0:T(8,128)(2,1)}, u32[]{:S(2)}) copy-start(bf16[2,512,512]{2,1,0:T(8,128)(2,1)} %radiate_ref.3) | copy-start | bytes 3145732
  36.9 16.0 %collective-permute-start.7 = (bf16[512,128]{1,0:T(8,128)(2,1)S(1)}, bf16[512,128]{1,0:T(8,128)(2,1)S(1)}, u32[]{:S(2)}, u32[]{:S(2)}) collective-permute-start(bf16[512,128]{1,0:T(8,128)(2,1)S(1)} %add_convert_fusion.p0_ref), channel_id=1, source_target_pairs={{0,3},{1,0},{2,1},{3,2},{4,7},{5,4},{6,5},{7,6},{8,11},{9,8},{10,9... | collective-permute-start | bytes 393224 | tf_op jit(solution)/shard_map/ppermute | solution.py:255
  40.3 12.6 %collective-permute-start.6 = (bf16[512,128]{1,0:T(8,128)(2,1)S(1)}, bf16[512,128]{1,0:T(8,128)(2,1)S(1)}, u32[]{:S(2)}, u32[]{:S(2)}) collective-permute-start(bf16[512,128]{1,0:T(8,128)(2,1)S(1)} %add_convert_fusion.p0_ref), channel_id=1, source_target_pairs={{0,2},{1,3},{2,0},{3,1},{4,6},{5,7},{6,4},{7,5},{8,10},{9,11},{10,... | collective-permute-start | bytes 393224 | tf_op jit(solution)/shard_map/ppermute | solution.py:255
  41.2 11.8 %collective-permute-start.5 = (bf16[512,128]{1,0:T(8,128)(2,1)S(1)}, bf16[512,128]{1,0:T(8,128)(2,1)S(1)}, u32[]{:S(2)}, u32[]{:S(2)}) collective-permute-start(bf16[512,128]{1,0:T(8,128)(2,1)S(1)} %add_convert_fusion.p0_ref), channel_id=1, source_target_pairs={{0,1},{1,2},{2,3},{3,0},{4,5},{5,6},{6,7},{7,4},{8,9},{9,10},{10,1... | collective-permute-start | bytes 393224 | tf_op jit(solution)/shard_map/ppermute | solution.py:255
  41.2 4.3 %collective-permute-start.9 = (f32[16,256]{1,0:T(8,128)S(1)}, f32[16,256]{1,0:T(8,128)S(1)}, u32[]{:S(2)}, u32[]{:S(2)}) collective-permute-start(f32[16,256]{1,0:T(8,128)S(1)} %get-tuple-element.32.own_ref), channel_id=1, source_target_pairs={{4,0},{8,4},{12,8},{16,12},{20,16},{24,20},{28,24},{32,28},{36,32}... | collective-permute-start | bytes 49160 | tf_op jit(solution)/shard_map/ppermute | solution.py:263
  43.1 7.2 %collective-permute-start.8 = (f32[16,256]{1,0:T(8,128)S(1)}, f32[16,256]{1,0:T(8,128)S(1)}, u32[]{:S(2)}, u32[]{:S(2)}) collective-permute-start(f32[16,256]{1,0:T(8,128)S(1)} %get-tuple-element.32.own_ref), channel_id=1, source_target_pairs={{0,4},{4,8},{8,12},{12,16},{16,20},{20,24},{24,28},{28,32},{32,36}... | collective-permute-start | bytes 49160 | tf_op jit(solution)/shard_map/ppermute | solution.py:259
  55.9 9.8 %collective-permute-start.10 = (bf16[4,256,128]{2,1,0:T(8,128)(2,1)S(1)}, bf16[4,256,128]{2,1,0:T(8,128)(2,1)S(1)}, u32[]{:S(2)}, u32[]{:S(2)}) collective-permute-start(bf16[4,256,128]{2,1,0:T(8,128)(2,1)S(1)} %tested_after.1), channel_id=1, source_target_pairs={{0,4},{4,8},{8,12},{12,16},{16,20},{20,24},{24,28},{28,32},{32,36}... | collective-permute-start | bytes 786440 | tf_op jit(solution)/shard_map/ppermute | solution.py:259
  57.9 9.6 %collective-permute-start.11 = (bf16[4,256,128]{2,1,0:T(8,128)(2,1)S(1)}, bf16[4,256,128]{2,1,0:T(8,128)(2,1)S(1)}, u32[]{:S(2)}, u32[]{:S(2)}) collective-permute-start(bf16[4,256,128]{2,1,0:T(8,128)(2,1)S(1)} %get-tuple-element.35), channel_id=1, source_target_pairs={{4,0},{8,4},{12,8},{16,12},{20,16},{24,20},{28,24},{32,28},{36,32}... | collective-permute-start | bytes 786440 | tf_op jit(solution)/shard_map/ppermute | solution.py:263
  67.6 5.6 %collective-permute-start.12 = (bf16[256,128]{1,0:T(8,128)(2,1)S(1)}, bf16[256,128]{1,0:T(8,128)(2,1)S(1)}, u32[]{:S(2)}, u32[]{:S(2)}) collective-permute-start(bf16[256,128]{1,0:T(8,128)(2,1)S(1)} %get-tuple-element.38), channel_id=1, source_target_pairs={{0,1},{1,2},{2,3},{3,0},{4,5},{5,6},{6,7},{7,4},{8,9},{9,10},{10,1... | collective-permute-start | bytes 196616 | tf_op jit(solution)/shard_map/ppermute | solution.py:255
  70.2 4.3 %collective-permute-start.14 = (bf16[256,128]{1,0:T(8,128)(2,1)S(1)}, bf16[256,128]{1,0:T(8,128)(2,1)S(1)}, u32[]{:S(2)}, u32[]{:S(2)}) collective-permute-start(bf16[256,128]{1,0:T(8,128)(2,1)S(1)} %get-tuple-element.39), channel_id=1, source_target_pairs={{0,3},{1,0},{2,1},{3,2},{4,7},{5,4},{6,5},{7,6},{8,11},{9,8},{10,9... | collective-permute-start | bytes 196616 | tf_op jit(solution)/shard_map/ppermute | solution.py:255
  70.9 5.8 %collective-permute-start.13 = (bf16[256,128]{1,0:T(8,128)(2,1)S(1)}, bf16[256,128]{1,0:T(8,128)(2,1)S(1)}, u32[]{:S(2)}, u32[]{:S(2)}) collective-permute-start(bf16[256,128]{1,0:T(8,128)(2,1)S(1)} %get-tuple-element.40), channel_id=1, source_target_pairs={{0,2},{1,3},{2,0},{3,1},{4,6},{5,7},{6,4},{7,5},{8,10},{9,11},{10,... | collective-permute-start | bytes 196616 | tf_op jit(solution)/shard_map/ppermute | solution.py:255

commit v3 on v2

--- a/solution.py
+++ b/solution.py
@@ -238,6 +238,8 @@
 
 
 def call(body, outs, ins, scratch=(), space=pltpu.VMEM, flops=0, vmem=24):
+    if space is pltpu.HBM:
+        ins = [pltpu.with_memory_space_constraint(value, space) for value in ins]
     return pl.pallas_call(
         body,
         out_shape=outs,

time: 78 us -> 70.9 us (0.909)
  local copies, waits for them, and re-layouts: 7.72 us -> 0.05 us
    unnamed x28 -> x12, local copies, waits for them, and re-layouts: 7.7 us -> 0.03 us
  transfers between devices with their start and end apart: 15 -> 15, of which waited for: 9 -> 9; matrix products, arithmetic and copies ran while one was open for 0% -> 0% of each run, Pallas kernels for 12% -> 14%
where the time goes in v3:
time: 70.9 us; the launch traced here: 70.7 us
  starting transfers between devices  36.1 us (51%)
  Pallas kernels  16.7 us (24%)
  waiting for transfers between devices  16.1 us (23%)
  between operations  0.9 us (1%)
  other arithmetic  0.85 us (1%)
    pallas_call x7, Pallas kernels, call(): pl.pallas_call(body, out_shape=outs, in_specs=[pl.BlockSpec(memory_space=...  16.7 us
    ppermute x3, starting transfers between devices, downward(): lax.ppermute(value, 'box', [(i + 1, i) for i in range(lax.axis_size('box'...  15.4 us
    ppermute x9, starting transfers between devices, turned(): lax.ppermute(value, 'cone', [(i, (i + shift) % count) for i in range(coun...  14.8 us
    ppermute x9, waiting for transfers between devices, turned(): lax.ppermute(value, 'cone', [(i, (i + shift) % count) for i in range(coun...  8.48 us
    ppermute x3, starting transfers between devices, upward(): lax.ppermute(value, 'box', [(i, i + 1) for i in range(lax.axis_size('box'...  6 us
    ppermute x3, waiting for transfers between devices, upward(): lax.ppermute(value, 'box', [(i, i + 1) for i in range(lax.axis_size('box'...  5.87 us
    ppermute x3, waiting for transfers between devices, downward(): lax.ppermute(value, 'box', [(i + 1, i) for i in range(lax.axis_size('box'...  1.76 us
  transfers between devices with their start and end apart: 15, of which 9 were waited for; matrix products, arithmetic and copies ran while one was open for 0% of the time, Pallas kernels for 14%

profile of v3, /device:TPU:6, one launch (start us, length us, event | category | flops | bytes accessed | tf_op | source)
XLA Modules:
  0.0 70.7 jit_solution(5033511672656029862)
XLA Ops:
  0.6 1.9 %collective-permute-start = (bf16[256,512]{1,0:T(8,128)(2,1)}, bf16[256,512]{1,0:T(8,128)(2,1)S(1)}, u32[]{:S(2)}, u32[]{:S(2)}) collective-permute-start(bf16[256,512]{1,0:T(8,128)(2,1)} %current_hbm.1), channel_id=1, source_target_pairs={{0,4},{4,8},{8,12},{12,16},{16,20},{20,24},{24,28},{28,32},{32,36}... | collective-permute-start | bytes 786440 | tf_op jit(solution)/shard_map/ppermute | solution.py:261
  2.6 7.5 %collective-permute-start.1 = (bf16[256,512]{1,0:T(8,128)(2,1)}, bf16[256,512]{1,0:T(8,128)(2,1)S(1)}, u32[]{:S(2)}, u32[]{:S(2)}) collective-permute-start(bf16[256,512]{1,0:T(8,128)(2,1)} %current_hbm.1), channel_id=1, source_target_pairs={{4,0},{8,4},{12,8},{16,12},{20,16},{24,20},{28,24},{32,28},{36,32}... | collective-permute-start | bytes 786440 | tf_op jit(solution)/shard_map/ppermute | solution.py:265
  10.0 0.0 copy-start.2
  10.0 0.0 copy-start.3
  10.1 6.0 %prepare.1 = (f32[2,768,256]{2,1,0:T(8,128)S(1)}, f32[2,768,256]{2,1,0:T(8,128)S(1)}, f32[2,512,256]{2,1,0:T(8,128)S(1)}, f32[2,512,256]{2,1,0:T(8,128)S(1)}, bf...) custom-call(bf16[256,512]{1,0:T(8,128)(2,1)} %current_hbm.1, ...), custom_call_target="tpu_custom_call" | custom-call | flops 4000000000 | bytes 4194304 | tf_op jit(solution)/shard_map/prepare/pallas_call | solution.py:243
  16.1 0.0 collective-permute-done.before_ref
  16.1 0.0 collective-permute-done.1.after_ref
  16.2 3.0 %incident.1 = (bf16[512,128]{1,0:T(8,128)(2,1)S(1)}, bf16[512,1024]{1,0:T(8,128)(2,1)S(1)}) custom-call(bf16[256,512]{1,0:T(8,128)(2,1)S(1)} %collective-permute-done.before_ref, bf16[256,512]{1,0:T(8,128)(2,1)S(1)} %collective-permute-done.1.after_ref, bf16[256,1024]{1,0:T(8,128)(2,1)S(1)} %get-tuple-element.19.wave_ref, ...), custom_call_target="tpu_custom_call" | custom-call | flops 2000000000 | bytes 4194304 | tf_op jit(solution)/shard_map/incident/pallas_call | solution.py:243
  19.1 0.9 %received.1 = (f32[512,128]{1,0:T(8,128)S(1)}, bf16[512,128]{1,0:T(8,128)(2,1)S(1)}, bf16[512,128]{1,0:T(8,128)(2,1)S(1)}) custom-call(bf16[512,1024]{1,0:T(8,128)(2,1)S(1)} %get-tuple-element.25.po_lit_ref, bf16[2,512,512]{2,1,0:T(8,128)(2,1)S(1)} %copy-done.3), custom_call_target="tpu_custom_call" | custom-call | flops 1000000000 | bytes 4194304 | tf_op jit(solution)/shard_map/received/pallas_call | solution.py:243
  20.0 1.7 %collective-permute-start.2 = (bf16[512,128]{1,0:T(8,128)(2,1)S(1)}, bf16[512,128]{1,0:T(8,128)(2,1)S(1)}, u32[]{:S(2)}, u32[]{:S(2)}) collective-permute-start(bf16[512,128]{1,0:T(8,128)(2,1)S(1)} %get-tuple-element.29), channel_id=1, source_target_pairs={{0,1},{1,2},{2,3},{3,0},{4,5},{5,6},{6,7},{7,4},{8,9},{9,10},{10,1... | collective-permute-start | bytes 393224 | tf_op jit(solution)/shard_map/ppermute | solution.py:257
  21.7 1.6 %collective-permute-start.4 = (bf16[512,128]{1,0:T(8,128)(2,1)S(1)}, bf16[512,128]{1,0:T(8,128)(2,1)S(1)}, u32[]{:S(2)}, u32[]{:S(2)}) collective-permute-start(bf16[512,128]{1,0:T(8,128)(2,1)S(1)} %get-tuple-element.31), channel_id=1, source_target_pairs={{0,3},{1,0},{2,1},{3,2},{4,7},{5,4},{6,5},{7,6},{8,11},{9,8},{10,9... | collective-permute-start | bytes 393224 | tf_op jit(solution)/shard_map/ppermute | solution.py:257
  23.3 2.0 %collective-permute-start.3 = (bf16[512,128]{1,0:T(8,128)(2,1)S(1)}, bf16[512,128]{1,0:T(8,128)(2,1)S(1)}, u32[]{:S(2)}, u32[]{:S(2)}) collective-permute-start(bf16[512,128]{1,0:T(8,128)(2,1)S(1)} %get-tuple-element.30), channel_id=1, source_target_pairs={{0,2},{1,3},{2,0},{3,1},{4,6},{5,7},{6,4},{7,5},{8,10},{9,11},{10,... | collective-permute-start | bytes 393224 | tf_op jit(solution)/shard_map/ppermute | solution.py:257
  25.3 1.0 %collective-permute-done.2 = bf16[512,128]{1,0:T(8,128)(2,1)S(1)} collective-permute-done((bf16[512,128]{1,0:T(8,128)(2,1)S(1)}, bf16[512,128]{1,0:T(8,128)(2,1)S(1)}, u32[]{:S(2)}, u32[]{:S(2)}) %collective-permute-start.2) | collective-permute-done | bytes 131104 | tf_op jit(solution)/shard_map/ppermute | solution.py:257
  26.3 0.3 collective-permute-done.4
  26.6 3.1 %collective-permute-done.3 = bf16[512,128]{1,0:T(8,128)(2,1)S(1)} collective-permute-done((bf16[512,128]{1,0:T(8,128)(2,1)S(1)}, bf16[512,128]{1,0:T(8,128)(2,1)S(1)}, u32[]{:S(2)}, u32[]{:S(2)}) %collective-permute-start.3) | collective-permute-done | bytes 131104 | tf_op jit(solution)/shard_map/ppermute | solution.py:257
  29.8 0.1 add_convert_fusion.p0_ref
  29.9 0.0 copy-start.4
  29.9 0.0 copy-start
  29.9 0.0 copy-start.1
  29.9 3.4 %collective-permute-start.7 = (bf16[512,128]{1,0:T(8,128)(2,1)S(1)}, bf16[512,128]{1,0:T(8,128)(2,1)S(1)}, u32[]{:S(2)}, u32[]{:S(2)}) collective-permute-start(bf16[512,128]{1,0:T(8,128)(2,1)S(1)} %add_convert_fusion.p0_ref), channel_id=1, source_target_pairs={{0,3},{1,0},{2,1},{3,2},{4,7},{5,4},{6,5},{7,6},{8,11},{9,8},{10,9... | collective-permute-start | bytes 393224 | tf_op jit(solution)/shard_map/ppermute | solution.py:257
  33.3 0.9 %collective-permute-start.6 = (bf16[512,128]{1,0:T(8,128)(2,1)S(1)}, bf16[512,128]{1,0:T(8,128)(2,1)S(1)}, u32[]{:S(2)}, u32[]{:S(2)}) collective-permute-start(bf16[512,128]{1,0:T(8,128)(2,1)S(1)} %add_convert_fusion.p0_ref), channel_id=1, source_target_pairs={{0,2},{1,3},{2,0},{3,1},{4,6},{5,7},{6,4},{7,5},{8,10},{9,11},{10,... | collective-permute-start | bytes 393224 | tf_op jit(solution)/shard_map/ppermute | solution.py:257
  34.2 0.1 collective-permute-start.5
  34.3 2.2 %collective-permute-start.9 = (f32[16,256]{1,0:T(8,128)S(1)}, f32[16,256]{1,0:T(8,128)S(1)}, u32[]{:S(2)}, u32[]{:S(2)}) collective-permute-start(f32[16,256]{1,0:T(8,128)S(1)} %get-tuple-element.32.own_ref), channel_id=1, source_target_pairs={{4,0},{8,4},{12,8},{16,12},{20,16},{24,20},{28,24},{32,28},{36,32}... | collective-permute-start | bytes 49160 | tf_op jit(solution)/shard_map/ppermute | solution.py:265
  36.4 2.2 %collective-permute-start.8 = (f32[16,256]{1,0:T(8,128)S(1)}, f32[16,256]{1,0:T(8,128)S(1)}, u32[]{:S(2)}, u32[]{:S(2)}) collective-permute-start(f32[16,256]{1,0:T(8,128)S(1)} %get-tuple-element.32.own_ref), channel_id=1, source_target_pairs={{0,4},{4,8},{8,12},{12,16},{16,20},{20,24},{24,28},{28,32},{32,36}... | collective-permute-start | bytes 49160 | tf_op jit(solution)/shard_map/ppermute | solution.py:261
  38.6 0.0 collective-permute-done.9.after_ref
  38.6 5.0 %collective-permute-done.8.before_ref = f32[16,256]{1,0:T(8,128)S(1)} collective-permute-done((f32[16,256]{1,0:T(8,128)S(1)}, f32[16,256]{1,0:T(8,128)S(1)}, u32[]{:S(2)}, u32[]{:S(2)}) %collective-permute-start.8) | collective-permute-done | bytes 16416 | tf_op jit(solution)/shard_map/ppermute | solution.py:261
  43.6 2.6 %lists.1.pick_ref.refs_2_ = bf16[768,512]{1,0:T(8,128)(2,1)S(1)} custom-call(f32[16,256]{1,0:T(8,128)S(1)} %collective-permute-done.8.before_ref, f32[16,256]{1,0:T(8,128)S(1)} %get-tuple-element.32.own_ref, f32[16,256]{1,0:T(8,128)S(1)} %collective-permute-done.9.after_ref), custom_call_target="tpu_custom_call" | custom-call | flops 1000000000 | bytes 4194304 | tf_op jit(solution)/shard_map/lists/pallas_call | solution.py:243
  46.2 0.0 collective-permute-done.7.p3_ref
  46.2 0.0 collective-permute-done.6.p2_ref
  46.2 0.0 collective-permute-done.5.p1_ref
  46.2 0.0 copy-done.4
  46.2 0.0 copy-done
  46.2 0.0 copy-done.1
  46.3 1.8 %scattered.1 = (bf16[512,1024]{1,0:T(8,128)(2,1)S(1)}, bf16[4,256,128]{2,1,0:T(8,128)(2,1)S(1)}) custom-call(bf16[512,128]{1,0:T(8,128)(2,1)S(1)} %add_convert_fusion.p0_ref, bf16[512,128]{1,0:T(8,128)(2,1)S(1)} %collective-permute-done.5.p1_ref, bf16[512,128]{1,0:T(8,128)(2,1)S(1)} %collective-permute-done.6.p2_ref, ...), custom_call_target="tpu_custom_call" | custom-call | flops 2000000000 | bytes 4194304 | tf_op jit(solution)/shard_map/scattered/pallas_call | solution.py:243
  48.1 1.2 %tested_after.1 = bf16[4,256,128]{2,1,0:T(8,128)(2,1)S(1)} custom-call(bf16[512,1024]{1,0:T(8,128)(2,1)S(1)} %get-tuple-element.34.refs_0_, bf16[2,512,512]{2,1,0:T(8,128)(2,1)S(1)} %copy-done, bf16[768,512]{1,0:T(8,128)(2,1)S(1)} %lists.1.pick_ref.refs_2_, f32[2,768,256]{2,1,0:T(8,128)S(1)} %get-tuple-element.21.mom_cos.refs_3_, ...), custom_call_target="tpu_custom_call" | custom-call | flops 1000000000 | bytes 4194304 | tf_op jit(solution)/shard_map/tested_after/pallas_call | solution.py:243
  49.3 1.9 %collective-permute-start.10 = (bf16[4,256,128]{2,1,0:T(8,128)(2,1)S(1)}, bf16[4,256,128]{2,1,0:T(8,128)(2,1)S(1)}, u32[]{:S(2)}, u32[]{:S(2)}) collective-permute-start(bf16[4,256,128]{2,1,0:T(8,128)(2,1)S(1)} %tested_after.1), channel_id=1, source_target_pairs={{0,4},{4,8},{8,12},{12,16},{16,20},{20,24},{24,28},{28,32},{32,36}... | collective-permute-start | bytes 786440 | tf_op jit(solution)/shard_map/ppermute | solution.py:261
  51.2 5.8 %collective-permute-start.11 = (bf16[4,256,128]{2,1,0:T(8,128)(2,1)S(1)}, bf16[4,256,128]{2,1,0:T(8,128)(2,1)S(1)}, u32[]{:S(2)}, u32[]{:S(2)}) collective-permute-start(bf16[4,256,128]{2,1,0:T(8,128)(2,1)S(1)} %get-tuple-element.35), channel_id=1, source_target_pairs={{4,0},{8,4},{12,8},{16,12},{20,16},{24,20},{28,24},{32,28},{36,32}... | collective-permute-start | bytes 786440 | tf_op jit(solution)/shard_map/ppermute | solution.py:265
  56.9 1.2 %tested_own.1 = f32[4,256,128]{2,1,0:T(8,128)S(1)} custom-call(bf16[512,1024]{1,0:T(8,128)(2,1)S(1)} %get-tuple-element.34.refs_0_, bf16[2,512,512]{2,1,0:T(8,128)(2,1)S(1)} %copy-done, bf16[768,512]{1,0:T(8,128)(2,1)S(1)} %lists.1.pick_ref.refs_2_, f32[2,768,256]{2,1,0:T(8,128)S(1)} %get-tuple-element.21.mom_cos.refs_3_, ...), custom_call_target="tpu_custom_call" | custom-call | flops 1000000000 | bytes 4194304 | tf_op jit(solution)/shard_map/tested_own/pallas_call | solution.py:243
  58.2 0.9 %collective-permute-done.10 = bf16[4,256,128]{2,1,0:T(8,128)(2,1)S(1)} collective-permute-done((bf16[4,256,128]{2,1,0:T(8,128)(2,1)S(1)}, bf16[4,256,128]{2,1,0:T(8,128)(2,1)S(1)}, u32[]{:S(2)}, u32[]{:S(2)}) %collective-permute-start.10) | collective-permute-done | bytes 262176 | tf_op jit(solution)/shard_map/ppermute | solution.py:261
  59.1 1.8 %collective-permute-done.11 = bf16[4,256,128]{2,1,0:T(8,128)(2,1)S(1)} collective-permute-done((bf16[4,256,128]{2,1,0:T(8,128)(2,1)S(1)}, bf16[4,256,128]{2,1,0:T(8,128)(2,1)S(1)}, u32[]{:S(2)}, u32[]{:S(2)}) %collective-permute-start.11) | collective-permute-done | bytes 262176 | tf_op jit(solution)/shard_map/ppermute | solution.py:265
  60.8 0.1 fusion.3
  60.9 2.4 %collective-permute-start.12 = (bf16[256,128]{1,0:T(8,128)(2,1)S(1)}, bf16[256,128]{1,0:T(8,128)(2,1)S(1)}, u32[]{:S(2)}, u32[]{:S(2)}) collective-permute-start(bf16[256,128]{1,0:T(8,128)(2,1)S(1)} %get-tuple-element.38), channel_id=1, source_target_pairs={{0,1},{1,2},{2,3},{3,0},{4,5},{5,6},{6,7},{7,4},{8,9},{9,10},{10,1... | collective-permute-start | bytes 196616 | tf_op jit(solution)/shard_map/ppermute | solution.py:257
  63.3 1.0 %collective-permute-start.14 = (bf16[256,128]{1,0:T(8,128)(2,1)S(1)}, bf16[256,128]{1,0:T(8,128)(2,1)S(1)}, u32[]{:S(2)}, u32[]{:S(2)}) collective-permute-start(bf16[256,128]{1,0:T(8,128)(2,1)S(1)} %get-tuple-element.39), channel_id=1, source_target_pairs={{0,3},{1,0},{2,1},{3,2},{4,7},{5,4},{6,5},{7,6},{8,11},{9,8},{10,9... | collective-permute-start | bytes 196616 | tf_op jit(solution)/shard_map/ppermute | solution.py:257
  64.2 1.8 %collective-permute-start.13 = (bf16[256,128]{1,0:T(8,128)(2,1)S(1)}, bf16[256,128]{1,0:T(8,128)(2,1)S(1)}, u32[]{:S(2)}, u32[]{:S(2)}) collective-permute-start(bf16[256,128]{1,0:T(8,128)(2,1)S(1)} %get-tuple-element.40), channel_id=1, source_target_pairs={{0,2},{1,3},{2,0},{3,1},{4,6},{5,7},{6,4},{7,5},{8,10},{9,11},{10,... | collective-permute-start | bytes 196616 | tf_op jit(solution)/shard_map/ppermute | solution.py:257
  66.0 0.5 collective-permute-done.12
  66.5 1.1 %collective-permute-done.14 = bf16[256,128]{1,0:T(8,128)(2,1)S(1)} collective-permute-done((bf16[256,128]{1,0:T(8,128)(2,1)S(1)}, bf16[256,128]{1,0:T(8,128)(2,1)S(1)}, u32[]{:S(2)}, u32[]{:S(2)}) %collective-permute-start.14) | collective-permute-done | bytes 65568 | tf_op jit(solution)/shard_map/ppermute | solution.py:257
  67.6 2.5 %collective-permute-done.13 = bf16[256,128]{1,0:T(8,128)(2,1)S(1)} collective-permute-done((bf16[256,128]{1,0:T(8,128)(2,1)S(1)}, bf16[256,128]{1,0:T(8,128)(2,1)S(1)}, u32[]{:S(2)}, u32[]{:S(2)}) %collective-permute-start.13) | collective-permute-done | bytes 65568 | tf_op jit(solution)/shard_map/ppermute | solution.py:257
  70.0 0.7 fusion.2
  (5 shorter events, 0.0 us)
Async XLA Ops:
  0.6 15.5 %collective-permute-start = (bf16[256,512]{1,0:T(8,128)(2,1)}, bf16[256,512]{1,0:T(8,128)(2,1)S(1)}, u32[]{:S(2)}, u32[]{:S(2)}) collective-permute-start(bf16[256,512]{1,0:T(8,128)(2,1)} %current_hbm.1), channel_id=1, source_target_pairs={{0,4},{4,8},{8,12},{12,16},{16,20},{20,24},{24,28},{28,32},{32,36}... | collective-permute-start | bytes 786440 | tf_op jit(solution)/shard_map/ppermute | solution.py:261
  2.6 13.6 %collective-permute-start.1 = (bf16[256,512]{1,0:T(8,128)(2,1)}, bf16[256,512]{1,0:T(8,128)(2,1)S(1)}, u32[]{:S(2)}, u32[]{:S(2)}) collective-permute-start(bf16[256,512]{1,0:T(8,128)(2,1)} %current_hbm.1), channel_id=1, source_target_pairs={{4,0},{8,4},{12,8},{16,12},{20,16},{24,20},{28,24},{32,28},{36,32}... | collective-permute-start | bytes 786440 | tf_op jit(solution)/shard_map/ppermute | solution.py:265
  10.0 6.1 %copy-start.2 = (bf16[2,512,512]{2,1,0:T(8,128)(2,1)S(1)}, bf16[2,512,512]{2,1,0:T(8,128)(2,1)}, u32[]{:S(2)}) copy-start(bf16[2,512,512]{2,1,0:T(8,128)(2,1)} %radiate_ref.2) | copy-start | bytes 3145732
  10.0 6.1 %copy-start.3 = (bf16[2,512,512]{2,1,0:T(8,128)(2,1)S(1)}, bf16[2,512,512]{2,1,0:T(8,128)(2,1)}, u32[]{:S(2)}) copy-start(bf16[2,512,512]{2,1,0:T(8,128)(2,1)} %receive_ref.4) | copy-start | bytes 3145732
  10.1 6.1 %copy-start.5 = (s32[2,512]{1,0:T(2,128)S(1)}, s32[2,512]{1,0:T(2,128)}, u32[]{:S(2)}) copy-start(s32[2,512]{1,0:T(2,128)} %lit_ref.1) | copy-start | bytes 12292
  20.0 6.3 %collective-permute-start.2 = (bf16[512,128]{1,0:T(8,128)(2,1)S(1)}, bf16[512,128]{1,0:T(8,128)(2,1)S(1)}, u32[]{:S(2)}, u32[]{:S(2)}) collective-permute-start(bf16[512,128]{1,0:T(8,128)(2,1)S(1)} %get-tuple-element.29), channel_id=1, source_target_pairs={{0,1},{1,2},{2,3},{3,0},{4,5},{5,6},{6,7},{7,4},{8,9},{9,10},{10,1... | collective-permute-start | bytes 393224 | tf_op jit(solution)/shard_map/ppermute | solution.py:257
  21.7 5.0 %collective-permute-start.4 = (bf16[512,128]{1,0:T(8,128)(2,1)S(1)}, bf16[512,128]{1,0:T(8,128)(2,1)S(1)}, u32[]{:S(2)}, u32[]{:S(2)}) collective-permute-start(bf16[512,128]{1,0:T(8,128)(2,1)S(1)} %get-tuple-element.31), channel_id=1, source_target_pairs={{0,3},{1,0},{2,1},{3,2},{4,7},{5,4},{6,5},{7,6},{8,11},{9,8},{10,9... | collective-permute-start | bytes 393224 | tf_op jit(solution)/shard_map/ppermute | solution.py:257
  23.3 6.5 %collective-permute-start.3 = (bf16[512,128]{1,0:T(8,128)(2,1)S(1)}, bf16[512,128]{1,0:T(8,128)(2,1)S(1)}, u32[]{:S(2)}, u32[]{:S(2)}) collective-permute-start(bf16[512,128]{1,0:T(8,128)(2,1)S(1)} %get-tuple-element.30), channel_id=1, source_target_pairs={{0,2},{1,3},{2,0},{3,1},{4,6},{5,7},{6,4},{7,5},{8,10},{9,11},{10,... | collective-permute-start | bytes 393224 | tf_op jit(solution)/shard_map/ppermute | solution.py:257
  29.9 16.3 %copy-start.4 = (bf16[512,128]{1,0:T(8,128)(2,1)}, bf16[512,128]{1,0:T(8,128)(2,1)S(1)}, u32[]{:S(2)}) copy-start(bf16[512,128]{1,0:T(8,128)(2,1)S(1)} %add_convert_fusion.p0_ref) | copy-start | bytes 393220
  29.9 16.3 %copy-start = (bf16[2,512,512]{2,1,0:T(8,128)(2,1)S(1)}, bf16[2,512,512]{2,1,0:T(8,128)(2,1)}, u32[]{:S(2)}) copy-start(bf16[2,512,512]{2,1,0:T(8,128)(2,1)} %refs_1_.3) | copy-start | bytes 3145732
  29.9 16.3 %copy-start.1 = (bf16[2,512,512]{2,1,0:T(8,128)(2,1)S(1)}, bf16[2,512,512]{2,1,0:T(8,128)(2,1)}, u32[]{:S(2)}) copy-start(bf16[2,512,512]{2,1,0:T(8,128)(2,1)} %radiate_ref.3) | copy-start | bytes 3145732
  29.9 16.3 %collective-permute-start.7 = (bf16[512,128]{1,0:T(8,128)(2,1)S(1)}, bf16[512,128]{1,0:T(8,128)(2,1)S(1)}, u32[]{:S(2)}, u32[]{:S(2)}) collective-permute-start(bf16[512,128]{1,0:T(8,128)(2,1)S(1)} %add_convert_fusion.p0_ref), channel_id=1, source_target_pairs={{0,3},{1,0},{2,1},{3,2},{4,7},{5,4},{6,5},{7,6},{8,11},{9,8},{10,9... | collective-permute-start | bytes 393224 | tf_op jit(solution)/shard_map/ppermute | solution.py:257
  33.3 12.9 %collective-permute-start.6 = (bf16[512,128]{1,0:T(8,128)(2,1)S(1)}, bf16[512,128]{1,0:T(8,128)(2,1)S(1)}, u32[]{:S(2)}, u32[]{:S(2)}) collective-permute-start(bf16[512,128]{1,0:T(8,128)(2,1)S(1)} %add_convert_fusion.p0_ref), channel_id=1, source_target_pairs={{0,2},{1,3},{2,0},{3,1},{4,6},{5,7},{6,4},{7,5},{8,10},{9,11},{10,... | collective-permute-start | bytes 393224 | tf_op jit(solution)/shard_map/ppermute | solution.py:257
  34.2 12.0 %collective-permute-start.5 = (bf16[512,128]{1,0:T(8,128)(2,1)S(1)}, bf16[512,128]{1,0:T(8,128)(2,1)S(1)}, u32[]{:S(2)}, u32[]{:S(2)}) collective-permute-start(bf16[512,128]{1,0:T(8,128)(2,1)S(1)} %add_convert_fusion.p0_ref), channel_id=1, source_target_pairs={{0,1},{1,2},{2,3},{3,0},{4,5},{5,6},{6,7},{7,4},{8,9},{9,10},{10,1... | collective-permute-start | bytes 393224 | tf_op jit(solution)/shard_map/ppermute | solution.py:257
  34.3 4.3 %collective-permute-start.9 = (f32[16,256]{1,0:T(8,128)S(1)}, f32[16,256]{1,0:T(8,128)S(1)}, u32[]{:S(2)}, u32[]{:S(2)}) collective-permute-start(f32[16,256]{1,0:T(8,128)S(1)} %get-tuple-element.32.own_ref), channel_id=1, source_target_pairs={{4,0},{8,4},{12,8},{16,12},{20,16},{24,20},{28,24},{32,28},{36,32}... | collective-permute-start | bytes 49160 | tf_op jit(solution)/shard_map/ppermute | solution.py:265
  36.4 7.2 %collective-permute-start.8 = (f32[16,256]{1,0:T(8,128)S(1)}, f32[16,256]{1,0:T(8,128)S(1)}, u32[]{:S(2)}, u32[]{:S(2)}) collective-permute-start(f32[16,256]{1,0:T(8,128)S(1)} %get-tuple-element.32.own_ref), channel_id=1, source_target_pairs={{0,4},{4,8},{8,12},{12,16},{16,20},{20,24},{24,28},{28,32},{32,36}... | collective-permute-start | bytes 49160 | tf_op jit(solution)/shard_map/ppermute | solution.py:261
  49.3 9.8 %collective-permute-start.10 = (bf16[4,256,128]{2,1,0:T(8,128)(2,1)S(1)}, bf16[4,256,128]{2,1,0:T(8,128)(2,1)S(1)}, u32[]{:S(2)}, u32[]{:S(2)}) collective-permute-start(bf16[4,256,128]{2,1,0:T(8,128)(2,1)S(1)} %tested_after.1), channel_id=1, source_target_pairs={{0,4},{4,8},{8,12},{12,16},{16,20},{20,24},{24,28},{28,32},{32,36}... | collective-permute-start | bytes 786440 | tf_op jit(solution)/shard_map/ppermute | solution.py:261
  51.2 9.6 %collective-permute-start.11 = (bf16[4,256,128]{2,1,0:T(8,128)(2,1)S(1)}, bf16[4,256,128]{2,1,0:T(8,128)(2,1)S(1)}, u32[]{:S(2)}, u32[]{:S(2)}) collective-permute-start(bf16[4,256,128]{2,1,0:T(8,128)(2,1)S(1)} %get-tuple-element.35), channel_id=1, source_target_pairs={{4,0},{8,4},{12,8},{16,12},{20,16},{24,20},{28,24},{32,28},{36,32}... | collective-permute-start | bytes 786440 | tf_op jit(solution)/shard_map/ppermute | solution.py:265
  60.9 5.6 %collective-permute-start.12 = (bf16[256,128]{1,0:T(8,128)(2,1)S(1)}, bf16[256,128]{1,0:T(8,128)(2,1)S(1)}, u32[]{:S(2)}, u32[]{:S(2)}) collective-permute-start(bf16[256,128]{1,0:T(8,128)(2,1)S(1)} %get-tuple-element.38), channel_id=1, source_target_pairs={{0,1},{1,2},{2,3},{3,0},{4,5},{5,6},{6,7},{7,4},{8,9},{9,10},{10,1... | collective-permute-start | bytes 196616 | tf_op jit(solution)/shard_map/ppermute | solution.py:257
  63.3 4.3 %collective-permute-start.14 = (bf16[256,128]{1,0:T(8,128)(2,1)S(1)}, bf16[256,128]{1,0:T(8,128)(2,1)S(1)}, u32[]{:S(2)}, u32[]{:S(2)}) collective-permute-start(bf16[256,128]{1,0:T(8,128)(2,1)S(1)} %get-tuple-element.39), channel_id=1, source_target_pairs={{0,3},{1,0},{2,1},{3,2},{4,7},{5,4},{6,5},{7,6},{8,11},{9,8},{10,9... | collective-permute-start | bytes 196616 | tf_op jit(solution)/shard_map/ppermute | solution.py:257
  64.2 5.8 %collective-permute-start.13 = (bf16[256,128]{1,0:T(8,128)(2,1)S(1)}, bf16[256,128]{1,0:T(8,128)(2,1)S(1)}, u32[]{:S(2)}, u32[]{:S(2)}) collective-permute-start(bf16[256,128]{1,0:T(8,128)(2,1)S(1)} %get-tuple-element.40), channel_id=1, source_target_pairs={{0,2},{1,3},{2,0},{3,1},{4,6},{5,7},{6,4},{7,5},{8,10},{9,11},{10,... | collective-permute-start | bytes 196616 | tf_op jit(solution)/shard_map/ppermute | solution.py:257

commit v4 on v3

--- a/solution.py
+++ b/solution.py
@@ -74,11 +74,17 @@
     return re * cosine - im * sine, re * sine + im * cosine
 
 
+def rows_at(base, at):
+    if isinstance(base, int):
+        return slice(base + at.start, base + at.stop)
+    return pl.ds(pl.multiple_of(base + at.start, TILE), at.stop - at.start)
+
+
 def radiated(rows_ref, at, radiate_ref, cos_ref, sin_ref, out_ref, base, cs_base):
     cones, _, k2 = radiate_ref.shape
     k = k2 // 2
-    here = slice(base + at.start, base + at.stop)
-    there = slice(cs_base + at.start, cs_base + at.stop)
+    here = rows_at(base, at)
+    there = rows_at(cs_base, at)
     for c in range(cones):
         re, im = rotated(mm(rows_ref[at], radiate_ref[c]), cos_ref[c, there], sin_ref[c, there], -1)
         out_ref[here, c * k2 : c * k2 + k] = re.astype(BF)
@@ -127,22 +133,23 @@
 
 
 def incident(
-    before_ref, after_ref, wave_ref, pick_ref, radiate_ref, receive_ref, mom_cos, mom_sin, po_cos, po_sin, lit_ref,
-    far_ref, po_lit_ref,
+    odd_ref, even_ref, wave_ref, pick_ref, radiate_ref, receive_ref, mom_cos, mom_sin, po_cos, po_sin, lit_ref,
+    first_ref, po_lit_ref,
     table,
 ):
     cone = lax.axis_index("cone")
     count = lax.axis_size("cone")
-    m = before_ref.shape[0]
-    q, share = far_ref.shape
+    box = lax.axis_index("box")
+    m = even_ref.shape[0]
+    q, share = first_ref.shape
     cones, _, k2 = radiate_ref.shape
     k = k2 // 2
     table[m : 2 * m] = wave_ref[...]
     for at in tiles(m):
-        radiated(before_ref, at, radiate_ref, mom_cos, mom_sin, table, 0, 0)
-        radiated(after_ref, at, radiate_ref, mom_cos, mom_sin, table, 2 * m, 2 * m)
+        for rows_ref, after in ((even_ref, 1 - lax.rem(box, 2)), (odd_ref, lax.rem(box, 2))):
+            radiated(rows_ref, at, radiate_ref, mom_cos, mom_sin, table, after * 2 * m, after * 2 * m)
     lit_col = jnp.concatenate([lit_ref[...].astype(F32), jnp.zeros((8 - cones, q), F32)], axis=0).T
-    columns = pl.ds(pl.multiple_of(lax.rem(cone + 2, count) * share, share), share)
+    columns = pl.ds(pl.multiple_of(lax.rem(cone + 1, count) * share, share), share)
     for at in tiles(q):
         total = None
         for c in range(cones):
@@ -154,10 +161,10 @@
             po_lit_ref[at, c * k2 + k : (c + 1) * k2] = im
             part = mm(re, receive_ref[c, :k, columns]) + mm(im, receive_ref[c, k:, columns])
             total = part if total is None else total + part
-        far_ref[at] = total.astype(BF)
-
-
-def received(po_lit_ref, receive_ref, own_ref, s1_ref, s3_ref, chunks):
+        first_ref[at] = total.astype(BF)
+
+
+def received(po_lit_ref, receive_ref, own_ref, s2_ref, s3_ref, chunks):
     cones, k2, n = receive_ref.shape
     for at in tiles(po_lit_ref.shape[0]):
         total = None
@@ -166,19 +173,22 @@
             total = part if total is None else total + part
         put_chunks(chunks, at, total)
     own_ref[...] = chunks[0]
-    s1_ref[...] = chunks[1].astype(BF)
+    s2_ref[...] = chunks[2].astype(BF)
     s3_ref[...] = chunks[3].astype(BF)
 
 
-def lists(before_ref, own_ref, after_ref, pick_ref):
+def lists(even_ref, own_ref, odd_ref, pick_ref):
     box = lax.axis_index("box")
+    even = lax.rem(box, 2) == 0
+    e, o = even_ref[...], odd_ref[...]
+    entries = (jnp.where(even, o, e), own_ref[...], jnp.where(even, e, o))
     m = own_ref.shape[1]
     q = pick_ref.shape[1]
     ratio = q // m
     first = (box * q).astype(F32)
-    for i, ref in enumerate((before_ref, own_ref, after_ref)):
-        src_col = (ref[0:8] - first).astype(jnp.int32).T
-        w_col = ref[8:16].T
+    for i, value in enumerate(entries):
+        src_col = (value[0:8] - first).astype(jnp.int32).T
+        w_col = value[8:16].T
         step = 32
         for r in range(0, m, step):
             middle = (i - 1) * q + r * ratio
@@ -195,7 +205,7 @@
 
 
 def scattered(
-    p0_ref, p1_ref, p2_ref, p3_ref, radiate_ref, receive_ref, pick_ref, po_cos, po_sin, mom_cos, mom_sin,
+    p0_ref, p2_ref, p3_ref, p1_ref, radiate_ref, receive_ref, pick_ref, po_cos, po_sin, mom_cos, mom_sin,
     waves_ref, out_ref,
     whole,
 ):
@@ -207,37 +217,40 @@
         whole[:, pl.ds(pl.multiple_of(owner * share, share), share)] = ref[...]
     for at in tiles(q):
         radiated(whole, at, radiate_ref, po_cos, po_sin, waves_ref, 0, 0)
-    tested(0, waves_ref, receive_ref, pick_ref, mom_cos, mom_sin, out_ref)
+    after = lax.rem(lax.axis_index("box"), 2)
+    tested(2 * after, waves_ref, receive_ref, pick_ref, mom_cos, mom_sin, out_ref)
 
 
 def tested(part, waves_ref, receive_ref, pick_ref, mom_cos, mom_sin, out_ref):
     cones, k2, _ = receive_ref.shape
     k = k2 // 2
     rows = out_ref.shape[1]
-    q = waves_ref.shape[0]
-    ratio = q // rows
     for at in tiles(rows):
-        here = slice(part * rows + at.start, part * rows + at.stop)
-        low = max((part - 1) * q + at.start * ratio - q, 0) // 256 * 256
-        high = min(-(-((part - 1) * q + (at.stop - 1) * ratio + q + 1) // 256) * 256, q)
+        here = rows_at(part * rows, at)
         total = None
         for c in range(cones):
-            value = mm(pick_ref[here, low:high], waves_ref[low:high, c * k2 : (c + 1) * k2])
+            value = mm(pick_ref[here], waves_ref[:, c * k2 : (c + 1) * k2])
             re, im = rotated(value, mom_cos[c, here], mom_sin[c, here], 1)
             piece = mm(re.astype(BF), receive_ref[c, :k]) + mm(im.astype(BF), receive_ref[c, k:])
             total = piece if total is None else total + piece
         put_chunks(out_ref, at, total)
 
 
-def tested_after(*refs):
-    tested(2, *refs)
+def tested_even(*refs):
+    tested(2 - 2 * lax.rem(lax.axis_index("box"), 2), *refs)
 
 
 def tested_own(*refs):
     tested(1, *refs)
 
 
-def call(body, outs, ins, scratch=(), space=pltpu.VMEM, flops=0, vmem=24):
+def merged(even_ref, odd_ref, own_ref, *outs):
+    for slot, out in enumerate(outs):
+        total = own_ref[slot] + odd_ref[slot].astype(F32) + even_ref[slot].astype(F32)
+        out[...] = total.astype(out.dtype)
+
+
+def call(body, outs, ins, scratch=(), space=pltpu.VMEM, vmem=24):
     if space is pltpu.HBM:
         ins = [pltpu.with_memory_space_constraint(value, space) for value in ins]
     return pl.pallas_call(
@@ -247,7 +260,7 @@
         out_specs=jax.tree.map(lambda _: pl.BlockSpec(memory_space=pltpu.VMEM), outs),
         scratch_shapes=list(scratch),
         compiler_params=pltpu.CompilerParams(vmem_limit_bytes=vmem * MIB),
-        cost_estimate=pl.CostEstimate(flops=flops, bytes_accessed=4 * MIB, transcendentals=0),
+        cost_estimate=pl.CostEstimate(flops=1, bytes_accessed=1, transcendentals=0),
         name=body.__name__,
     )(*ins)
 
@@ -257,12 +270,12 @@
     return lax.ppermute(value, "cone", [(i, (i + shift) % count) for i in range(count)])
 
 
-def upward(value):
-    return lax.ppermute(value, "box", [(i, i + 1) for i in range(lax.axis_size("box") - 1)])
-
-
-def downward(value):
-    return lax.ppermute(value, "box", [(i + 1, i) for i in range(lax.axis_size("box") - 1)])
+def swapped_even(value):
+    return lax.ppermute(value, "box", [(i, i ^ 1) for i in range(lax.axis_size("box"))])
+
+
+def swapped_odd(value):
+    return lax.ppermute(value, "box", [(i, ((i + 1) ^ 1) - 1) for i in range(1, lax.axis_size("box") - 1)])
 
 
 def shards(
@@ -278,8 +291,8 @@
     share = n // count
     width = cones * k2
 
-    before = upward(mom_current)
-    after = downward(mom_current)
+    odd = swapped_odd(mom_current)
+    even = swapped_even(mom_current)
     waves3 = jnp.transpose(dirs, (1, 0, 2))
     staged = (mom_current, mom_radiate, waves3, po_src, po_weight, mom_src, mom_weight)
     mom_cos, mom_sin, po_cos, po_sin, pick, wave, entries = call(
@@ -292,51 +305,52 @@
         tuple(pltpu.VMEM(value.shape, value.dtype) for value in staged)
         + (pltpu.VMEM((3, 3 * m), F32), pltpu.VMEM((3, q), F32), pltpu.SemaphoreType.DMA((11,))),
         pltpu.HBM,
-        flops=4_000_000_000,
-    )
-    s2, po_lit = call(
+    )
+    s1, po_lit = call(
         incident,
         (shape((q, share), BF), shape((q, width), BF)),
-        (before, after, wave, pick, mom_radiate, po_receive, mom_cos, mom_sin, po_cos, po_sin, lit),
+        (odd, even, wave, pick, mom_radiate, po_receive, mom_cos, mom_sin, po_cos, po_sin, lit),
         (pltpu.VMEM((3 * m, width), BF),),
-        flops=2_000_000_000,
-    )
-    s2 = turned(s2, 2)
-    own, s1, s3 = call(
+    )
+    s1 = turned(s1, 1)
+    own, s2, s3 = call(
         received,
         (shape((q, share), F32), shape((q, share), BF), shape((q, share), BF)),
         (po_lit, po_receive),
         (pltpu.VMEM((count, q, share), F32),),
-        flops=1_000_000_000,
-    )
-    s1 = turned(s1, 1)
+    )
+    s2 = turned(s2, 2)
     s3 = turned(s3, 3)
     own, entries = lax.optimization_barrier((own, entries))
-    before_list = upward(entries)
-    after_list = downward(entries)
-    back = call(lists, shape((3 * m, q), BF), (before_list, entries, after_list), flops=1_000_000_000)
+    odd_list = swapped_odd(entries)
+    even_list = swapped_even(entries)
+    s1, even_list, odd_list = lax.optimization_barrier((s1, even_list, odd_list))
+    back = call(lists, shape((3 * m, q), BF), (even_list, entries, odd_list))
     po_share = (own + s1.astype(F32) + s2.astype(F32) + s3.astype(F32)).astype(BF)
     p2 = turned(po_share, 2)
     p1 = turned(po_share, 1)
     p3 = turned(po_share, 3)
-    waves, down = call(
+    waves, for_odd = call(
         scattered,
         (shape((q, width), BF), shape((count, m, share), BF)),
-        (po_share, p1, p2, p3, po_radiate, mom_receive, back, po_cos, po_sin, mom_cos, mom_sin),
+        (po_share, p2, p3, p1, po_radiate, mom_receive, back, po_cos, po_sin, mom_cos, mom_sin),
         (pltpu.VMEM((q, n), BF),),
-        flops=2_000_000_000,
     )
     rest = (mom_receive, back, mom_cos, mom_sin)
-    from_after = downward(down)
-    up = call(tested_after, shape((count, m, share), BF), (waves,) + rest, flops=1_000_000_000)
-    from_before = upward(up)
-    up, own_waves = lax.optimization_barrier((up, waves))
-    field = call(tested_own, shape((count, m, share), F32), (own_waves,) + rest, flops=1_000_000_000)
-    field = field + from_before.astype(F32) + from_after.astype(F32)
-    f2 = turned(field[2].astype(BF), 2)
-    f1 = turned(field[1].astype(BF), 1)
-    f3 = turned(field[3].astype(BF), 3)
-    mom_field = field[0] + f1.astype(F32) + f2.astype(F32) + f3.astype(F32)
+    from_odd = swapped_odd(for_odd)
+    for_even = call(tested_even, shape((count, m, share), BF), (waves,) + rest)
+    from_even = swapped_even(for_even)
+    for_even, own_waves = lax.optimization_barrier((for_even, waves))
+    field = call(tested_own, shape((count, m, share), F32), (own_waves,) + rest)
+    f0, f1, f2, f3 = call(
+        merged,
+        (shape((m, share), F32),) + (shape((m, share), BF),) * 3,
+        (from_even, from_odd, field),
+    )
+    f2 = turned(f2, 2)
+    f1 = turned(f1, 1)
+    f3 = turned(f3, 3)
+    mom_field = f0 + f1.astype(F32) + f2.astype(F32) + f3.astype(F32)
     return mom_field, po_share
 
 

time: 70.9 us -> 62.6 us (0.88)
  starting transfers between devices: 36.1 us -> 26.9 us
  waiting for transfers between devices: 16.1 us -> 17 us
    ppermute x6, starting transfers between devices: 21.4 us -> 14.1 us  [the longest x3 13.9 us: swapped_odd(): lax.ppermute(value, 'box', [(i, (i + 1 ^ 1) - 1) for i in range(1, lax.ax...]
    ppermute x9, starting transfers between devices: 14.8 us -> 12.8 us  [turned(): lax.ppermute(value, 'cone', [(i, (i + shift) % count) for i in range(coun...]
    ppermute x6, waiting for transfers between devices: 7.63 us -> 9.34 us  [the longest x3 9.33 us: swapped_odd(): lax.ppermute(value, 'box', [(i, (i + 1 ^ 1) - 1) for i in range(1, lax.ax...]
    ppermute x9, waiting for transfers between devices: 8.48 us -> 7.69 us  [turned(): lax.ppermute(value, 'cone', [(i, (i + shift) % count) for i in range(coun...]
    pallas_call x7 -> x8, Pallas kernels: 16.7 us -> 16.8 us  [call(): pl.pallas_call(body, out_shape=outs, in_specs=[pl.BlockSpec(memory_space=...]
  transfers between devices with their start and end apart: 15 -> 15, of which waited for: 9 -> 6; matrix products, arithmetic and copies ran while one was open for 0% -> 0% of each run, Pallas kernels for 14% -> 17%
where the time goes in v4:
time: 62.6 us; the launch traced here: 62.4 us
  starting transfers between devices  26.9 us (43%)
  waiting for transfers between devices  17 us (27%)
  Pallas kernels  16.8 us (27%)
  between operations  0.86 us (1%)
  other arithmetic  0.75 us (1%)
    pallas_call x8, Pallas kernels, call(): pl.pallas_call(body, out_shape=outs, in_specs=[pl.BlockSpec(memory_space=...  16.8 us
    ppermute x3, starting transfers between devices, swapped_odd(): lax.ppermute(value, 'box', [(i, (i + 1 ^ 1) - 1) for i in range(1, lax.ax...  13.9 us
    ppermute x9, starting transfers between devices, turned(): lax.ppermute(value, 'cone', [(i, (i + shift) % count) for i in range(coun...  12.8 us
    ppermute x3, waiting for transfers between devices, swapped_odd(): lax.ppermute(value, 'box', [(i, (i + 1 ^ 1) - 1) for i in range(1, lax.ax...  9.33 us
    ppermute x9, waiting for transfers between devices, turned(): lax.ppermute(value, 'cone', [(i, (i + shift) % count) for i in range(coun...  7.69 us
  transfers between devices with their start and end apart: 15, of which 6 were waited for; matrix products, arithmetic and copies ran while one was open for 0% of the time, Pallas kernels for 17%

profile of v4, /device:TPU:6, one launch (start us, length us, event | category | flops | bytes accessed | tf_op | source)
XLA Modules:
  0.0 62.4 jit_solution(5183358112848679380)
XLA Ops:
  0.6 0.0 copy-start.1
  0.6 0.0 copy-start.2
  0.7 0.0 copy-start.5
  0.7 7.6 %collective-permute-start = (bf16[256,512]{1,0:T(8,128)(2,1)}, bf16[256,512]{1,0:T(8,128)(2,1)S(1)}, u32[]{:S(2)}, u32[]{:S(2)}) collective-permute-start(bf16[256,512]{1,0:T(8,128)(2,1)} %current_hbm.1), channel_id=1, source_target_pairs={{4,8},{8,4},{12,16},{16,12},{20,24},{24,20},{28,32},{32,28},{36,40... | collective-permute-start | bytes 786440 | tf_op jit(solution)/shard_map/ppermute | solution.py:278
  8.3 0.1 collective-permute-start.1
  8.4 5.9 %prepare.1 = (f32[2,768,256]{2,1,0:T(8,128)S(1)}, f32[2,768,256]{2,1,0:T(8,128)S(1)}, f32[2,512,256]{2,1,0:T(8,128)S(1)}, f32[2,512,256]{2,1,0:T(8,128)S(1)}, bf...) custom-call(bf16[256,512]{1,0:T(8,128)(2,1)} %current_hbm.1, ...), custom_call_target="tpu_custom_call" | custom-call | flops 1 | bytes 1 | tf_op jit(solution)/shard_map/prepare/pallas_call | solution.py:256
  14.3 0.0 collective-permute-done.odd_ref
  14.3 0.0 collective-permute-done.1.even_ref
  14.3 0.0 copy-done.1
  14.3 0.0 copy-done.2
  14.3 0.0 copy-done.5
  14.3 3.0 %incident.1 = (bf16[512,128]{1,0:T(8,128)(2,1)S(1)}, bf16[512,1024]{1,0:T(8,128)(2,1)S(1)}) custom-call(bf16[256,512]{1,0:T(8,128)(2,1)S(1)} %collective-permute-done.odd_ref, bf16[256,512]{1,0:T(8,128)(2,1)S(1)} %collective-permute-done.1.even_ref, bf16[256,1024]{1,0:T(8,128)(2,1)S(1)} %get-tuple-element.26.wave_ref, ...), custom_call_target="tpu_custom_call" | custom-call | flops 1 | bytes 1 | tf_op jit(solution)/shard_map/incident/pallas_call | solution.py:256
  17.4 1.6 %collective-permute-start.2 = (bf16[512,128]{1,0:T(8,128)(2,1)S(1)}, bf16[512,128]{1,0:T(8,128)(2,1)S(1)}, u32[]{:S(2)}, u32[]{:S(2)}) collective-permute-start(bf16[512,128]{1,0:T(8,128)(2,1)S(1)} %get-tuple-element.36), channel_id=1, source_target_pairs={{0,1},{1,2},{2,3},{3,0},{4,5},{5,6},{6,7},{7,4},{8,9},{9,10},{10,1... | collective-permute-start | bytes 393224 | tf_op jit(solution)/shard_map/ppermute | solution.py:270
  19.0 0.9 %received.1 = (f32[512,128]{1,0:T(8,128)S(1)}, bf16[512,128]{1,0:T(8,128)(2,1)S(1)}, bf16[512,128]{1,0:T(8,128)(2,1)S(1)}) custom-call(bf16[512,1024]{1,0:T(8,128)(2,1)S(1)} %get-tuple-element.32.po_lit_ref, bf16[2,512,512]{2,1,0:T(8,128)(2,1)S(1)} %copy-done.2), custom_call_target="tpu_custom_call" | custom-call | flops 1 | bytes 1 | tf_op jit(solution)/shard_map/received/pallas_call | solution.py:256
  19.9 3.0 %collective-permute-start.5 = (bf16[512,128]{1,0:T(8,128)(2,1)S(1)}, bf16[512,128]{1,0:T(8,128)(2,1)S(1)}, u32[]{:S(2)}, u32[]{:S(2)}) collective-permute-start(bf16[512,128]{1,0:T(8,128)(2,1)S(1)} %get-tuple-element.39), channel_id=1, source_target_pairs={{0,2},{1,3},{2,0},{3,1},{4,6},{5,7},{6,4},{7,5},{8,10},{9,11},{10,... | collective-permute-start | bytes 393224 | tf_op jit(solution)/shard_map/ppermute | solution.py:270
  22.9 1.3 %collective-permute-start.6 = (bf16[512,128]{1,0:T(8,128)(2,1)S(1)}, bf16[512,128]{1,0:T(8,128)(2,1)S(1)}, u32[]{:S(2)}, u32[]{:S(2)}) collective-permute-start(bf16[512,128]{1,0:T(8,128)(2,1)S(1)} %get-tuple-element.40), channel_id=1, source_target_pairs={{0,3},{1,0},{2,1},{3,2},{4,7},{5,4},{6,5},{7,6},{8,11},{9,8},{10,9... | collective-permute-start | bytes 393224 | tf_op jit(solution)/shard_map/ppermute | solution.py:270
  24.2 3.1 %collective-permute-start.4 = (f32[16,256]{1,0:T(8,128)S(1)}, f32[16,256]{1,0:T(8,128)S(1)}, u32[]{:S(2)}, u32[]{:S(2)}) collective-permute-start(f32[16,256]{1,0:T(8,128)S(1)} %get-tuple-element.37.own_ref), channel_id=1, source_target_pairs={{4,8},{8,4},{12,16},{16,12},{20,24},{24,20},{28,32},{32,28},{36,40... | collective-permute-start | bytes 49160 | tf_op jit(solution)/shard_map/ppermute | solution.py:278
  27.3 0.1 collective-permute-start.3
  27.4 3.9 %collective-permute-done.4.odd_ref = f32[16,256]{1,0:T(8,128)S(1)} collective-permute-done((f32[16,256]{1,0:T(8,128)S(1)}, f32[16,256]{1,0:T(8,128)S(1)}, u32[]{:S(2)}, u32[]{:S(2)}) %collective-permute-start.4) | collective-permute-done | bytes 16416 | tf_op jit(solution)/shard_map/ppermute | solution.py:278
  31.4 0.0 collective-permute-done.3.even_ref
  31.4 0.0 collective-permute-done.2
  31.4 0.0 collective-permute-done.5
  31.4 0.0 collective-permute-done.6
  31.4 0.1 add_convert_fusion.p0_ref
  31.5 0.0 copy-start.4
  31.5 0.9 %collective-permute-start.9 = (bf16[512,128]{1,0:T(8,128)(2,1)S(1)}, bf16[512,128]{1,0:T(8,128)(2,1)S(1)}, u32[]{:S(2)}, u32[]{:S(2)}) collective-permute-start(bf16[512,128]{1,0:T(8,128)(2,1)S(1)} %add_convert_fusion.p0_ref), channel_id=1, source_target_pairs={{0,1},{1,2},{2,3},{3,0},{4,5},{5,6},{6,7},{7,4},{8,9},{9,10},{10,1... | collective-permute-start | bytes 393224 | tf_op jit(solution)/shard_map/ppermute | solution.py:270
  32.4 2.6 %collective-permute-start.8 = (bf16[512,128]{1,0:T(8,128)(2,1)S(1)}, bf16[512,128]{1,0:T(8,128)(2,1)S(1)}, u32[]{:S(2)}, u32[]{:S(2)}) collective-permute-start(bf16[512,128]{1,0:T(8,128)(2,1)S(1)} %add_convert_fusion.p0_ref), channel_id=1, source_target_pairs={{0,3},{1,0},{2,1},{3,2},{4,7},{5,4},{6,5},{7,6},{8,11},{9,8},{10,9... | collective-permute-start | bytes 393224 | tf_op jit(solution)/shard_map/ppermute | solution.py:270
  35.0 0.0 collective-permute-start.7
  35.0 2.6 %lists.1.pick_ref.refs_2_ = bf16[768,512]{1,0:T(8,128)(2,1)S(1)} custom-call(f32[16,256]{1,0:T(8,128)S(1)} %collective-permute-done.3.even_ref, f32[16,256]{1,0:T(8,128)S(1)} %get-tuple-element.37.own_ref, f32[16,256]{1,0:T(8,128)S(1)} %collective-permute-done.4.odd_ref), custom_call_target="tpu_custom_call" | custom-call | flops 1 | bytes 1 | tf_op jit(solution)/shard_map/lists/pallas_call | solution.py:256
  37.6 1.6 %collective-permute-done.9.p1_ref = bf16[512,128]{1,0:T(8,128)(2,1)S(1)} collective-permute-done((bf16[512,128]{1,0:T(8,128)(2,1)S(1)}, bf16[512,128]{1,0:T(8,128)(2,1)S(1)}, u32[]{:S(2)}, u32[]{:S(2)}) %collective-permute-start.9) | collective-permute-done | bytes 131104 | tf_op jit(solution)/shard_map/ppermute | solution.py:270
  39.2 0.0 collective-permute-done.8.p3_ref
  39.2 2.3 %collective-permute-done.7.p2_ref = bf16[512,128]{1,0:T(8,128)(2,1)S(1)} collective-permute-done((bf16[512,128]{1,0:T(8,128)(2,1)S(1)}, bf16[512,128]{1,0:T(8,128)(2,1)S(1)}, u32[]{:S(2)}, u32[]{:S(2)}) %collective-permute-start.7) | collective-permute-done | bytes 131104 | tf_op jit(solution)/shard_map/ppermute | solution.py:270
  41.4 0.0 copy-done
  41.4 1.9 %scattered.1 = (bf16[512,1024]{1,0:T(8,128)(2,1)S(1)}, bf16[4,256,128]{2,1,0:T(8,128)(2,1)S(1)}) custom-call(bf16[512,128]{1,0:T(8,128)(2,1)S(1)} %add_convert_fusion.p0_ref, bf16[512,128]{1,0:T(8,128)(2,1)S(1)} %collective-permute-done.7.p2_ref, bf16[512,128]{1,0:T(8,128)(2,1)S(1)} %collective-permute-done.8.p3_ref, ...), custom_call_target="tpu_custom_call" | custom-call | flops 1 | bytes 1 | tf_op jit(solution)/shard_map/scattered/pallas_call | solution.py:256
  43.4 1.2 %tested_even.1 = bf16[4,256,128]{2,1,0:T(8,128)(2,1)S(1)} custom-call(bf16[512,1024]{1,0:T(8,128)(2,1)S(1)} %get-tuple-element.45.refs_0_, bf16[2,512,512]{2,1,0:T(8,128)(2,1)S(1)} %copy-done, bf16[768,512]{1,0:T(8,128)(2,1)S(1)} %lists.1.pick_ref.refs_2_, f32[2,768,256]{2,1,0:T(8,128)S(1)} %get-tuple-element.28.mom_cos.refs_3_, ...), custom_call_target="tpu_custom_call" | custom-call | flops 1 | bytes 1 | tf_op jit(solution)/shard_map/tested_even/pallas_call | solution.py:256
  44.6 0.1 collective-permute-start.10
  44.7 3.1 %collective-permute-start.11 = (bf16[4,256,128]{2,1,0:T(8,128)(2,1)S(1)}, bf16[4,256,128]{2,1,0:T(8,128)(2,1)S(1)}, u32[]{:S(2)}, u32[]{:S(2)}) collective-permute-start(bf16[4,256,128]{2,1,0:T(8,128)(2,1)S(1)} %get-tuple-element.44), channel_id=1, source_target_pairs={{4,8},{8,4},{12,16},{16,12},{20,24},{24,20},{28,32},{32,28},{36,40... | collective-permute-start | bytes 786440 | tf_op jit(solution)/shard_map/ppermute | solution.py:278
  47.8 1.2 %tested_own.1.own_ref = f32[4,256,128]{2,1,0:T(8,128)S(1)} custom-call(bf16[512,1024]{1,0:T(8,128)(2,1)S(1)} %get-tuple-element.45.refs_0_, bf16[2,512,512]{2,1,0:T(8,128)(2,1)S(1)} %copy-done, bf16[768,512]{1,0:T(8,128)(2,1)S(1)} %lists.1.pick_ref.refs_2_, f32[2,768,256]{2,1,0:T(8,128)S(1)} %get-tuple-element.28.mom_cos.refs_3_, ...), custom_call_target="tpu_custom_call" | custom-call | flops 1 | bytes 1 | tf_op jit(solution)/shard_map/tested_own/pallas_call | solution.py:256
  49.1 0.0 collective-permute-done.10.even_ref
  49.1 5.4 %collective-permute-done.11.odd_ref = bf16[4,256,128]{2,1,0:T(8,128)(2,1)S(1)} collective-permute-done((bf16[4,256,128]{2,1,0:T(8,128)(2,1)S(1)}, bf16[4,256,128]{2,1,0:T(8,128)(2,1)S(1)}, u32[]{:S(2)}, u32[]{:S(2)}) %collective-permute-start.11) | collective-permute-done | bytes 262176 | tf_op jit(solution)/shard_map/ppermute | solution.py:278
  54.5 0.1 merged.1
  54.6 0.1 collective-permute-start.12
  54.7 2.6 %collective-permute-start.13 = (bf16[256,128]{1,0:T(8,128)(2,1)S(1)}, bf16[256,128]{1,0:T(8,128)(2,1)S(1)}, u32[]{:S(2)}, u32[]{:S(2)}) collective-permute-start(bf16[256,128]{1,0:T(8,128)(2,1)S(1)} %get-tuple-element.48), channel_id=1, source_target_pairs={{0,2},{1,3},{2,0},{3,1},{4,6},{5,7},{6,4},{7,5},{8,10},{9,11},{10,... | collective-permute-start | bytes 196616 | tf_op jit(solution)/shard_map/ppermute | solution.py:270
  57.2 0.7 %collective-permute-start.14 = (bf16[256,128]{1,0:T(8,128)(2,1)S(1)}, bf16[256,128]{1,0:T(8,128)(2,1)S(1)}, u32[]{:S(2)}, u32[]{:S(2)}) collective-permute-start(bf16[256,128]{1,0:T(8,128)(2,1)S(1)} %get-tuple-element.49), channel_id=1, source_target_pairs={{0,3},{1,0},{2,1},{3,2},{4,7},{5,4},{6,5},{7,6},{8,11},{9,8},{10,9... | collective-permute-start | bytes 196616 | tf_op jit(solution)/shard_map/ppermute | solution.py:270
  57.9 2.9 %collective-permute-done.12 = bf16[256,128]{1,0:T(8,128)(2,1)S(1)} collective-permute-done((bf16[256,128]{1,0:T(8,128)(2,1)S(1)}, bf16[256,128]{1,0:T(8,128)(2,1)S(1)}, u32[]{:S(2)}, u32[]{:S(2)}) %collective-permute-start.12) | collective-permute-done | bytes 65568 | tf_op jit(solution)/shard_map/ppermute | solution.py:270
  60.8 0.0 collective-permute-done.13
  60.8 0.9 %collective-permute-done.14 = bf16[256,128]{1,0:T(8,128)(2,1)S(1)} collective-permute-done((bf16[256,128]{1,0:T(8,128)(2,1)S(1)}, bf16[256,128]{1,0:T(8,128)(2,1)S(1)}, u32[]{:S(2)}, u32[]{:S(2)}) %collective-permute-start.14) | collective-permute-done | bytes 65568 | tf_op jit(solution)/shard_map/ppermute | solution.py:270
  61.7 0.7 %convert_add_fusion = f32[256,128]{1,0:T(8,128)} fusion(bf16[256,128]{1,0:T(8,128)(2,1)S(1)} %collective-permute-done.14, bf16[256,128]{1,0:T(8,128)(2,1)S(1)} %collective-permute-done.13, f32[256,128]{1,0:T(8,128)S(1)} %get-tuple-element.46, bf16[256,128]{1,0:T(8,128)(2,1)S(1)} %collective-permute-done.12), kind=kLoop, calls=%fused_computation.1 | loop fusion | flops 196608 | bytes 458752 | tf_op jit(solution)/shard_map/add | solution.py:353
  (4 shorter events, 0.0 us)
Async XLA Ops:
  0.6 13.7 %copy-start.1 = (bf16[2,512,512]{2,1,0:T(8,128)(2,1)S(1)}, bf16[2,512,512]{2,1,0:T(8,128)(2,1)}, u32[]{:S(2)}) copy-start(bf16[2,512,512]{2,1,0:T(8,128)(2,1)} %radiate_ref.2) | copy-start | bytes 3145732
  0.6 13.7 %copy-start.2 = (bf16[2,512,512]{2,1,0:T(8,128)(2,1)S(1)}, bf16[2,512,512]{2,1,0:T(8,128)(2,1)}, u32[]{:S(2)}) copy-start(bf16[2,512,512]{2,1,0:T(8,128)(2,1)} %receive_ref.4) | copy-start | bytes 3145732
  0.7 13.7 %copy-start.5 = (s32[2,512]{1,0:T(2,128)S(1)}, s32[2,512]{1,0:T(2,128)}, u32[]{:S(2)}) copy-start(s32[2,512]{1,0:T(2,128)} %lit_ref.1) | copy-start | bytes 12292
  0.7 13.6 %collective-permute-start = (bf16[256,512]{1,0:T(8,128)(2,1)}, bf16[256,512]{1,0:T(8,128)(2,1)S(1)}, u32[]{:S(2)}, u32[]{:S(2)}) collective-permute-start(bf16[256,512]{1,0:T(8,128)(2,1)} %current_hbm.1), channel_id=1, source_target_pairs={{4,8},{8,4},{12,16},{16,12},{20,24},{24,20},{28,32},{32,28},{36,40... | collective-permute-start | bytes 786440 | tf_op jit(solution)/shard_map/ppermute | solution.py:278
  8.3 6.0 %collective-permute-start.1 = (bf16[256,512]{1,0:T(8,128)(2,1)}, bf16[256,512]{1,0:T(8,128)(2,1)S(1)}, u32[]{:S(2)}, u32[]{:S(2)}) collective-permute-start(bf16[256,512]{1,0:T(8,128)(2,1)} %current_hbm.1), channel_id=1, source_target_pairs={{0,4},{4,0},{8,12},{12,8},{16,20},{20,16},{24,28},{28,24},{32,36},... | collective-permute-start | bytes 786440 | tf_op jit(solution)/shard_map/ppermute | solution.py:274
  17.4 14.0 %collective-permute-start.2 = (bf16[512,128]{1,0:T(8,128)(2,1)S(1)}, bf16[512,128]{1,0:T(8,128)(2,1)S(1)}, u32[]{:S(2)}, u32[]{:S(2)}) collective-permute-start(bf16[512,128]{1,0:T(8,128)(2,1)S(1)} %get-tuple-element.36), channel_id=1, source_target_pairs={{0,1},{1,2},{2,3},{3,0},{4,5},{5,6},{6,7},{7,4},{8,9},{9,10},{10,1... | collective-permute-start | bytes 393224 | tf_op jit(solution)/shard_map/ppermute | solution.py:270
  19.0 22.5 %copy-start = (bf16[2,512,512]{2,1,0:T(8,128)(2,1)S(1)}, bf16[2,512,512]{2,1,0:T(8,128)(2,1)}, u32[]{:S(2)}) copy-start(bf16[2,512,512]{2,1,0:T(8,128)(2,1)} %refs_1_.3) | copy-start | bytes 3145732
  19.0 22.5 %copy-start.3 = (bf16[2,512,512]{2,1,0:T(8,128)(2,1)S(1)}, bf16[2,512,512]{2,1,0:T(8,128)(2,1)}, u32[]{:S(2)}) copy-start(bf16[2,512,512]{2,1,0:T(8,128)(2,1)} %radiate_ref.3) | copy-start | bytes 3145732
  19.9 11.5 %collective-permute-start.5 = (bf16[512,128]{1,0:T(8,128)(2,1)S(1)}, bf16[512,128]{1,0:T(8,128)(2,1)S(1)}, u32[]{:S(2)}, u32[]{:S(2)}) collective-permute-start(bf16[512,128]{1,0:T(8,128)(2,1)S(1)} %get-tuple-element.39), channel_id=1, source_target_pairs={{0,2},{1,3},{2,0},{3,1},{4,6},{5,7},{6,4},{7,5},{8,10},{9,11},{10,... | collective-permute-start | bytes 393224 | tf_op jit(solution)/shard_map/ppermute | solution.py:270
  22.9 8.5 %collective-permute-start.6 = (bf16[512,128]{1,0:T(8,128)(2,1)S(1)}, bf16[512,128]{1,0:T(8,128)(2,1)S(1)}, u32[]{:S(2)}, u32[]{:S(2)}) collective-permute-start(bf16[512,128]{1,0:T(8,128)(2,1)S(1)} %get-tuple-element.40), channel_id=1, source_target_pairs={{0,3},{1,0},{2,1},{3,2},{4,7},{5,4},{6,5},{7,6},{8,11},{9,8},{10,9... | collective-permute-start | bytes 393224 | tf_op jit(solution)/shard_map/ppermute | solution.py:270
  24.2 7.2 %collective-permute-start.4 = (f32[16,256]{1,0:T(8,128)S(1)}, f32[16,256]{1,0:T(8,128)S(1)}, u32[]{:S(2)}, u32[]{:S(2)}) collective-permute-start(f32[16,256]{1,0:T(8,128)S(1)} %get-tuple-element.37.own_ref), channel_id=1, source_target_pairs={{4,8},{8,4},{12,16},{16,12},{20,24},{24,20},{28,32},{32,28},{36,40... | collective-permute-start | bytes 49160 | tf_op jit(solution)/shard_map/ppermute | solution.py:278
  27.3 4.0 %collective-permute-start.3 = (f32[16,256]{1,0:T(8,128)S(1)}, f32[16,256]{1,0:T(8,128)S(1)}, u32[]{:S(2)}, u32[]{:S(2)}) collective-permute-start(f32[16,256]{1,0:T(8,128)S(1)} %get-tuple-element.37.own_ref), channel_id=1, source_target_pairs={{0,4},{4,0},{8,12},{12,8},{16,20},{20,16},{24,28},{28,24},{32,36},... | collective-permute-start | bytes 49160 | tf_op jit(solution)/shard_map/ppermute | solution.py:274
  31.5 11.9 %copy-start.4 = (bf16[512,128]{1,0:T(8,128)(2,1)}, bf16[512,128]{1,0:T(8,128)(2,1)S(1)}, u32[]{:S(2)}) copy-start(bf16[512,128]{1,0:T(8,128)(2,1)S(1)} %add_convert_fusion.p0_ref) | copy-start | bytes 393220
  31.5 7.7 %collective-permute-start.9 = (bf16[512,128]{1,0:T(8,128)(2,1)S(1)}, bf16[512,128]{1,0:T(8,128)(2,1)S(1)}, u32[]{:S(2)}, u32[]{:S(2)}) collective-permute-start(bf16[512,128]{1,0:T(8,128)(2,1)S(1)} %add_convert_fusion.p0_ref), channel_id=1, source_target_pairs={{0,1},{1,2},{2,3},{3,0},{4,5},{5,6},{6,7},{7,4},{8,9},{9,10},{10,1... | collective-permute-start | bytes 393224 | tf_op jit(solution)/shard_map/ppermute | solution.py:270
  32.4 6.8 %collective-permute-start.8 = (bf16[512,128]{1,0:T(8,128)(2,1)S(1)}, bf16[512,128]{1,0:T(8,128)(2,1)S(1)}, u32[]{:S(2)}, u32[]{:S(2)}) collective-permute-start(bf16[512,128]{1,0:T(8,128)(2,1)S(1)} %add_convert_fusion.p0_ref), channel_id=1, source_target_pairs={{0,3},{1,0},{2,1},{3,2},{4,7},{5,4},{6,5},{7,6},{8,11},{9,8},{10,9... | collective-permute-start | bytes 393224 | tf_op jit(solution)/shard_map/ppermute | solution.py:270
  35.0 6.5 %collective-permute-start.7 = (bf16[512,128]{1,0:T(8,128)(2,1)S(1)}, bf16[512,128]{1,0:T(8,128)(2,1)S(1)}, u32[]{:S(2)}, u32[]{:S(2)}) collective-permute-start(bf16[512,128]{1,0:T(8,128)(2,1)S(1)} %add_convert_fusion.p0_ref), channel_id=1, source_target_pairs={{0,2},{1,3},{2,0},{3,1},{4,6},{5,7},{6,4},{7,5},{8,10},{9,11},{10,... | collective-permute-start | bytes 393224 | tf_op jit(solution)/shard_map/ppermute | solution.py:270
  44.6 4.5 %collective-permute-start.10 = (bf16[4,256,128]{2,1,0:T(8,128)(2,1)S(1)}, bf16[4,256,128]{2,1,0:T(8,128)(2,1)S(1)}, u32[]{:S(2)}, u32[]{:S(2)}) collective-permute-start(bf16[4,256,128]{2,1,0:T(8,128)(2,1)S(1)} %tested_even.1), channel_id=1, source_target_pairs={{0,4},{4,0},{8,12},{12,8},{16,20},{20,16},{24,28},{28,24},{32,36},... | collective-permute-start | bytes 786440 | tf_op jit(solution)/shard_map/ppermute | solution.py:274
  44.7 9.8 %collective-permute-start.11 = (bf16[4,256,128]{2,1,0:T(8,128)(2,1)S(1)}, bf16[4,256,128]{2,1,0:T(8,128)(2,1)S(1)}, u32[]{:S(2)}, u32[]{:S(2)}) collective-permute-start(bf16[4,256,128]{2,1,0:T(8,128)(2,1)S(1)} %get-tuple-element.44), channel_id=1, source_target_pairs={{4,8},{8,4},{12,16},{16,12},{20,24},{24,20},{28,32},{32,28},{36,40... | collective-permute-start | bytes 786440 | tf_op jit(solution)/shard_map/ppermute | solution.py:278
  54.6 6.3 %collective-permute-start.12 = (bf16[256,128]{1,0:T(8,128)(2,1)S(1)}, bf16[256,128]{1,0:T(8,128)(2,1)S(1)}, u32[]{:S(2)}, u32[]{:S(2)}) collective-permute-start(bf16[256,128]{1,0:T(8,128)(2,1)S(1)} %get-tuple-element.47), channel_id=1, source_target_pairs={{0,1},{1,2},{2,3},{3,0},{4,5},{5,6},{6,7},{7,4},{8,9},{9,10},{10,1... | collective-permute-start | bytes 196616 | tf_op jit(solution)/shard_map/ppermute | solution.py:270
  54.7 6.2 %collective-permute-start.13 = (bf16[256,128]{1,0:T(8,128)(2,1)S(1)}, bf16[256,128]{1,0:T(8,128)(2,1)S(1)}, u32[]{:S(2)}, u32[]{:S(2)}) collective-permute-start(bf16[256,128]{1,0:T(8,128)(2,1)S(1)} %get-tuple-element.48), channel_id=1, source_target_pairs={{0,2},{1,3},{2,0},{3,1},{4,6},{5,7},{6,4},{7,5},{8,10},{9,11},{10,... | collective-permute-start | bytes 196616 | tf_op jit(solution)/shard_map/ppermute | solution.py:270
  57.2 4.5 %collective-permute-start.14 = (bf16[256,128]{1,0:T(8,128)(2,1)S(1)}, bf16[256,128]{1,0:T(8,128)(2,1)S(1)}, u32[]{:S(2)}, u32[]{:S(2)}) collective-permute-start(bf16[256,128]{1,0:T(8,128)(2,1)S(1)} %get-tuple-element.49), channel_id=1, source_target_pairs={{0,3},{1,0},{2,1},{3,2},{4,7},{5,4},{6,5},{7,6},{8,11},{9,8},{10,9... | collective-permute-start | bytes 196616 | tf_op jit(solution)/shard_map/ppermute | solution.py:270

commit v5 on v4

--- a/solution.py
+++ b/solution.py
@@ -95,10 +95,28 @@
     return [slice(r, r + TILE) for r in range(0, rows, TILE)]
 
 
+def packed(current_hbm, src_hbm, weight_hbm, out_ref, src_ref, weight_ref, sems):
+    m = current_hbm.shape[0]
+    slots = src_ref.shape[0]
+    pairs = ((src_hbm, src_ref), (weight_hbm, weight_ref), (current_hbm, out_ref.at[pl.ds(0, m)]))
+    copies = [pltpu.make_async_copy(here, there, sems.at[i]) for i, (here, there) in enumerate(pairs)]
+    for copy in copies:
+        copy.start()
+    copies[0].wait()
+    copies[1].wait()
+    offsets = src_ref[...] - (lax.axis_index("box") - 1) * (2 * m)
+    high, low = offsets >> 4, offsets & 15
+    weight = weight_ref[...]
+    left = jnp.concatenate([high.astype(F32), weight], axis=0).astype(BF)
+    right = jnp.concatenate([low.astype(F32), jnp.zeros_like(weight)], axis=0).astype(BF)
+    out_ref[m : m + 2 * slots] = jnp.concatenate([left, right], axis=1)
+    copies[2].wait()
+
+
 def prepare(
-    current_hbm, radiate_hbm, dirs_hbm, mom_center_hbm, po_center_hbm, src_hbm, weight_hbm, mom_src_hbm, mom_weight_hbm,
-    mom_cos, mom_sin, po_cos, po_sin, pick_ref, wave_ref, list_ref,
-    current_ref, radiate_ref, dirs_ref, src_ref, weight_ref, mom_src_ref, mom_weight_ref, mom_c, po_c, sems,
+    current_hbm, radiate_hbm, dirs_hbm, mom_center_hbm, po_center_hbm, src_hbm, weight_hbm,
+    mom_cos, mom_sin, po_cos, po_sin, pick_ref, wave_ref,
+    current_ref, radiate_ref, dirs_ref, src_ref, weight_ref, mom_c, po_c, sems,
 ):
     box = lax.axis_index("box")
     boxes = lax.axis_size("box")
@@ -110,7 +128,7 @@
         pairs.append((mom_center_hbm.at[:, pl.ds(at, m)], mom_c.at[:, pl.ds(i * m, m)]))
     at = pl.multiple_of(box * q, 128)
     pairs.append((po_center_hbm.at[:, pl.ds(at, q)], po_c))
-    pairs += [(current_hbm, current_ref), (radiate_hbm, radiate_ref), (mom_src_hbm, mom_src_ref), (mom_weight_hbm, mom_weight_ref)]
+    pairs += [(current_hbm, current_ref), (radiate_hbm, radiate_ref)]
     copies = [pltpu.make_async_copy(here, there, sems.at[i]) for i, (here, there) in enumerate(pairs)]
     for copy in copies:
         copy.start()
@@ -124,8 +142,6 @@
         fill(pick_ref, at, r * m // q, (r + step - 1) * m // q + 2 * m + 1, src_col[at], w_col[at])
     for copy in copies[2:]:
         copy.wait()
-    list_ref[0:8] = mom_src_ref[...].astype(F32)
-    list_ref[8:16] = mom_weight_ref[...]
     trig(mom_c[...], dirs_ref, mom_cos, mom_sin)
     for at in tiles(m):
         radiated(current_ref, at, radiate_ref, mom_cos, mom_sin, wave_ref, 0, m)
@@ -140,7 +156,7 @@
     cone = lax.axis_index("cone")
     count = lax.axis_size("cone")
     box = lax.axis_index("box")
-    m = even_ref.shape[0]
+    m = wave_ref.shape[0]
     q, share = first_ref.shape
     cones, _, k2 = radiate_ref.shape
     k = k2 // 2
@@ -177,18 +193,29 @@
     s3_ref[...] = chunks[3].astype(BF)
 
 
-def lists(even_ref, own_ref, odd_ref, pick_ref):
+def summed(a_ref, b_ref, own_ref, out_ref):
+    total = own_ref[...] + a_ref[...].astype(F32) + b_ref[...].astype(F32)
+    out_ref[...] = total.astype(out_ref.dtype)
+
+
+def lists(even_ref, odd_ref, src_ref, weight_ref, pick_ref):
     box = lax.axis_index("box")
     even = lax.rem(box, 2) == 0
-    e, o = even_ref[...], odd_ref[...]
-    entries = (jnp.where(even, o, e), own_ref[...], jnp.where(even, e, o))
-    m = own_ref.shape[1]
+    m = src_ref.shape[1]
     q = pick_ref.shape[1]
     ratio = q // m
-    first = (box * q).astype(F32)
-    for i, value in enumerate(entries):
-        src_col = (value[0:8] - first).astype(jnp.int32).T
-        w_col = value[8:16].T
+    slots = src_ref.shape[0]
+
+    def entries(after):
+        rows = [jnp.where(even == after, e_o[0], e_o[1]) for e_o in zip(*(
+            (ref[m : m + slots].astype(F32), ref[m + slots : m + 2 * slots].astype(F32)) for ref in (even_ref, odd_ref)
+        ))]
+        there = rows[0][:, :m].astype(jnp.int32) * 16 + rows[0][:, m:].astype(jnp.int32)
+        return there + ((0 if after else -2) * q), rows[1][:, :m]
+
+    sides = (entries(False), (src_ref[...] - box * q, weight_ref[...]), entries(True))
+    for i, (src, weight) in enumerate(sides):
+        src_col, w_col = src.T, weight.T
         step = 32
         for r in range(0, m, step):
             middle = (i - 1) * q + r * ratio
@@ -205,7 +232,7 @@
 
 
 def scattered(
-    p0_ref, p2_ref, p3_ref, p1_ref, radiate_ref, receive_ref, pick_ref, po_cos, po_sin, mom_cos, mom_sin,
+    p0_ref, p1_ref, p3_ref, p2_ref, radiate_ref, receive_ref, pick_ref, po_cos, po_sin, mom_cos, mom_sin,
     waves_ref, out_ref,
     whole,
 ):
@@ -244,10 +271,13 @@
     tested(1, *refs)
 
 
-def merged(even_ref, odd_ref, own_ref, *outs):
+def added(new_ref, own_ref, out_ref):
+    out_ref[...] = own_ref[...] + new_ref[...].astype(F32)
+
+
+def merged(even_ref, own_ref, *outs):
     for slot, out in enumerate(outs):
-        total = own_ref[slot] + odd_ref[slot].astype(F32) + even_ref[slot].astype(F32)
-        out[...] = total.astype(out.dtype)
+        out[...] = (own_ref[slot] + even_ref[slot].astype(F32)).astype(out.dtype)
 
 
 def call(body, outs, ins, scratch=(), space=pltpu.VMEM, vmem=24):
@@ -291,19 +321,27 @@
     share = n // count
     width = cones * k2
 
-    odd = swapped_odd(mom_current)
-    even = swapped_even(mom_current)
+    slots = mom_src.shape[0]
+    payload = call(
+        packed,
+        shape((m + 2 * slots, n), BF),
+        (mom_current, mom_src, mom_weight),
+        (pltpu.VMEM((slots, m), jnp.int32), pltpu.VMEM((slots, m), F32), pltpu.SemaphoreType.DMA((3,))),
+        pltpu.HBM,
+    )
+    odd = swapped_odd(payload)
+    even = swapped_even(payload)
     waves3 = jnp.transpose(dirs, (1, 0, 2))
-    staged = (mom_current, mom_radiate, waves3, po_src, po_weight, mom_src, mom_weight)
-    mom_cos, mom_sin, po_cos, po_sin, pick, wave, entries = call(
+    staged = (mom_current, mom_radiate, waves3, po_src, po_weight)
+    mom_cos, mom_sin, po_cos, po_sin, pick, wave = call(
         prepare,
         (
             shape((cones, 3 * m, k), F32), shape((cones, 3 * m, k), F32), shape((cones, q, k), F32), shape((cones, q, k), F32),
-            shape((q, 3 * m), BF), shape((m, width), BF), shape((16, m), F32),
+            shape((q, 3 * m), BF), shape((m, width), BF),
         ),
-        (mom_current, mom_radiate, waves3, mom_center, po_center, po_src, po_weight, mom_src, mom_weight),
+        (mom_current, mom_radiate, waves3, mom_center, po_center, po_src, po_weight),
         tuple(pltpu.VMEM(value.shape, value.dtype) for value in staged)
-        + (pltpu.VMEM((3, 3 * m), F32), pltpu.VMEM((3, q), F32), pltpu.SemaphoreType.DMA((11,))),
+        + (pltpu.VMEM((3, 3 * m), F32), pltpu.VMEM((3, q), F32), pltpu.SemaphoreType.DMA((9,))),
         pltpu.HBM,
     )
     s1, po_lit = call(
@@ -321,19 +359,16 @@
     )
     s2 = turned(s2, 2)
     s3 = turned(s3, 3)
-    own, entries = lax.optimization_barrier((own, entries))
-    odd_list = swapped_odd(entries)
-    even_list = swapped_even(entries)
-    s1, even_list, odd_list = lax.optimization_barrier((s1, even_list, odd_list))
-    back = call(lists, shape((3 * m, q), BF), (even_list, entries, odd_list))
-    po_share = (own + s1.astype(F32) + s2.astype(F32) + s3.astype(F32)).astype(BF)
+    back = call(lists, shape((3 * m, q), BF), (even, odd, mom_src, mom_weight))
+    own = call(added, shape((q, share), F32), (s1, own))
+    po_share = call(summed, shape((q, share), BF), (s3, s2, own))
     p2 = turned(po_share, 2)
     p1 = turned(po_share, 1)
     p3 = turned(po_share, 3)
     waves, for_odd = call(
         scattered,
         (shape((q, width), BF), shape((count, m, share), BF)),
-        (po_share, p2, p3, p1, po_radiate, mom_receive, back, po_cos, po_sin, mom_cos, mom_sin),
+        (po_share, p1, p3, p2, po_radiate, mom_receive, back, po_cos, po_sin, mom_cos, mom_sin),
         (pltpu.VMEM((q, n), BF),),
     )
     rest = (mom_receive, back, mom_cos, mom_sin)
@@ -342,10 +377,11 @@
     from_even = swapped_even(for_even)
     for_even, own_waves = lax.optimization_barrier((for_even, waves))
     field = call(tested_own, shape((count, m, share), F32), (own_waves,) + rest)
+    field = call(added, shape((count, m, share), F32), (from_odd, field))
     f0, f1, f2, f3 = call(
         merged,
         (shape((m, share), F32),) + (shape((m, share), BF),) * 3,
-        (from_even, from_odd, field),
+        (from_even, field),
     )
     f2 = turned(f2, 2)
     f1 = turned(f1, 1)

time: 62.6 us -> 61.9 us (0.989)
  starting transfers between devices: 26.9 us -> 23.9 us
  Pallas kernels: 16.8 us -> 18.1 us
  local copies, waits for them, and re-layouts: 0.03 us -> 0.94 us
    ppermute x9, waiting for transfers between devices: 7.69 us -> 12.4 us  [turned(): lax.ppermute(value, 'cone', [(i, (i + shift) % count) for i in range(coun...]
    ppermute x3 -> x2, waiting for transfers between devices: 9.33 us -> 4.87 us  [swapped_odd(): lax.ppermute(value, 'box', [(i, (i + 1 ^ 1) - 1) for i in range(1, lax.ax...]
    ppermute x3 -> x2, starting transfers between devices: 13.9 us -> 9.88 us  [swapped_odd(): lax.ppermute(value, 'box', [(i, (i + 1 ^ 1) - 1) for i in range(1, lax.ax...]
    pallas_call x8 -> x12, Pallas kernels: 16.8 us -> 18.1 us  [call(): pl.pallas_call(body, out_shape=outs, in_specs=[pl.BlockSpec(memory_space=...]
    ppermute x9, starting transfers between devices: 12.8 us -> 13.8 us  [turned(): lax.ppermute(value, 'cone', [(i, (i + shift) % count) for i in range(coun...]
    unnamed x12 -> x16, local copies, waits for them, and re-layouts: 0.03 us -> 0.94 us
  transfers between devices with their start and end apart: 15 -> 13, of which waited for: 6 -> 10; matrix products, arithmetic and copies ran while one was open for 0% -> 0% of each run, Pallas kernels for 17% -> 19%
where the time goes in v5:
time: 61.9 us; the launch traced here: 61.7 us
  starting transfers between devices  23.9 us (39%)
  Pallas kernels  18.1 us (29%)
  waiting for transfers between devices  17.2 us (28%)
  local copies, waits for them, and re-layouts  0.94 us (2%)
  between operations  0.84 us (1%)
  other arithmetic  0.68 us (1%)
    pallas_call x12, Pallas kernels, call(): pl.pallas_call(body, out_shape=outs, in_specs=[pl.BlockSpec(memory_space=...  18.1 us
    ppermute x9, starting transfers between devices, turned(): lax.ppermute(value, 'cone', [(i, (i + shift) % count) for i in range(coun...  13.8 us
    ppermute x9, waiting for transfers between devices, turned(): lax.ppermute(value, 'cone', [(i, (i + shift) % count) for i in range(coun...  12.4 us
    ppermute x2, starting transfers between devices, swapped_odd(): lax.ppermute(value, 'box', [(i, (i + 1 ^ 1) - 1) for i in range(1, lax.ax...  9.88 us
    ppermute x2, waiting for transfers between devices, swapped_odd(): lax.ppermute(value, 'box', [(i, (i + 1 ^ 1) - 1) for i in range(1, lax.ax...  4.87 us
  transfers between devices with their start and end apart: 13, of which 10 were waited for; matrix products, arithmetic and copies ran while one was open for 0% of the time, Pallas kernels for 19%

profile of v5, /device:TPU:6, one launch (start us, length us, event | category | flops | bytes accessed | tf_op | source)
XLA Modules:
  0.0 61.7 jit_solution(7047325867288884986)
XLA Ops:
  0.6 0.0 copy-start.1
  0.6 0.0 copy-start.2
  0.7 0.0 copy-start.7
  0.7 1.2 %packed.1 = bf16[272,512]{1,0:T(8,128)(2,1)S(1)} custom-call(bf16[256,512]{1,0:T(8,128)(2,1)} %current_hbm.3, s32[8,256]{1,0:T(8,128)} %src_ref.1, f32[8,256]{1,0:T(8,128)} %weight_ref.1), custom_call_target="tpu_custom_call" | custom-call | flops 1 | bytes 1 | tf_op jit(solution)/shard_map/packed/pallas_call | solution.py:286
  1.8 7.5 %collective-permute-start = (bf16[272,512]{1,0:T(8,128)(2,1)S(1)}, bf16[272,512]{1,0:T(8,128)(2,1)S(1)}, u32[]{:S(2)}, u32[]{:S(2)}) collective-permute-start(bf16[272,512]{1,0:T(8,128)(2,1)S(1)} %packed.1), channel_id=1, source_target_pairs={{4,8},{8,4},{12,16},{16,12},{20,24},{24,20},{28,32},{32,28},{36,40... | collective-permute-start | bytes 835592 | tf_op jit(solution)/shard_map/ppermute | solution.py:308
  9.3 0.1 collective-permute-start.1
  9.4 5.9 %prepare.1 = (f32[2,768,256]{2,1,0:T(8,128)S(1)}, f32[2,768,256]{2,1,0:T(8,128)S(1)}, f32[2,512,256]{2,1,0:T(8,128)S(1)}, f32[2,512,256]{2,1,0:T(8,128)S(1)}, bf...) custom-call(bf16[256,512]{1,0:T(8,128)(2,1)} %current_hbm.3, bf16[2,512,512]{2,1,0:T(8,128)(2,1)} %radiate_ref.2, ...), custom_call_target="tpu_custom_call" | custom-call | flops 1 | bytes 1 | tf_op jit(solution)/shard_map/prepare/pallas_call | solution.py:286
  15.3 0.0 collective-permute-done.odd_ref
  15.3 0.0 collective-permute-done.1.even_ref
  15.3 0.0 copy-done.1
  15.3 0.0 copy-done.2
  15.3 0.0 copy-done.7
  15.3 2.9 %incident.1 = (bf16[512,128]{1,0:T(8,128)(2,1)S(1)}, bf16[512,1024]{1,0:T(8,128)(2,1)S(1)}) custom-call(bf16[272,512]{1,0:T(8,128)(2,1)S(1)} %collective-permute-done.odd_ref, bf16[272,512]{1,0:T(8,128)(2,1)S(1)} %collective-permute-done.1.even_ref, bf16[256,1024]{1,0:T(8,128)(2,1)S(1)} %get-tuple-element.20.wave_ref, ...), custom_call_target="tpu_custom_call" | custom-call | flops 1 | bytes 1 | tf_op jit(solution)/shard_map/incident/pallas_call | solution.py:286
  18.3 1.6 %collective-permute-start.4 = (bf16[512,128]{1,0:T(8,128)(2,1)S(1)}, bf16[512,128]{1,0:T(8,128)(2,1)S(1)}, u32[]{:S(2)}, u32[]{:S(2)}) collective-permute-start(bf16[512,128]{1,0:T(8,128)(2,1)S(1)} %get-tuple-element.29), channel_id=1, source_target_pairs={{0,1},{1,2},{2,3},{3,0},{4,5},{5,6},{6,7},{7,4},{8,9},{9,10},{10,1... | collective-permute-start | bytes 393224 | tf_op jit(solution)/shard_map/ppermute | solution.py:300
  19.9 0.8 %received.1 = (f32[512,128]{1,0:T(8,128)S(1)}, bf16[512,128]{1,0:T(8,128)(2,1)S(1)}, bf16[512,128]{1,0:T(8,128)(2,1)S(1)}) custom-call(bf16[512,1024]{1,0:T(8,128)(2,1)S(1)} %get-tuple-element.26.po_lit_ref, bf16[2,512,512]{2,1,0:T(8,128)(2,1)S(1)} %copy-done.2), custom_call_target="tpu_custom_call" | custom-call | flops 1 | bytes 1 | tf_op jit(solution)/shard_map/received/pallas_call | solution.py:286
  20.8 0.0 copy-start
  20.8 0.0 copy-start.3
  20.8 1.8 %collective-permute-start.2 = (bf16[512,128]{1,0:T(8,128)(2,1)S(1)}, bf16[512,128]{1,0:T(8,128)(2,1)S(1)}, u32[]{:S(2)}, u32[]{:S(2)}) collective-permute-start(bf16[512,128]{1,0:T(8,128)(2,1)S(1)} %get-tuple-element.27), channel_id=1, source_target_pairs={{0,3},{1,0},{2,1},{3,2},{4,7},{5,4},{6,5},{7,6},{8,11},{9,8},{10,9... | collective-permute-start | bytes 393224 | tf_op jit(solution)/shard_map/ppermute | solution.py:300
  22.5 2.0 %collective-permute-start.3 = (bf16[512,128]{1,0:T(8,128)(2,1)S(1)}, bf16[512,128]{1,0:T(8,128)(2,1)S(1)}, u32[]{:S(2)}, u32[]{:S(2)}) collective-permute-start(bf16[512,128]{1,0:T(8,128)(2,1)S(1)} %get-tuple-element.28), channel_id=1, source_target_pairs={{0,2},{1,3},{2,0},{3,1},{4,6},{5,7},{6,4},{7,5},{8,10},{9,11},{10,... | collective-permute-start | bytes 393224 | tf_op jit(solution)/shard_map/ppermute | solution.py:300
  24.5 0.9 %collective-permute-done.4.new_ref = bf16[512,128]{1,0:T(8,128)(2,1)S(1)} collective-permute-done((bf16[512,128]{1,0:T(8,128)(2,1)S(1)}, bf16[512,128]{1,0:T(8,128)(2,1)S(1)}, u32[]{:S(2)}, u32[]{:S(2)}) %collective-permute-start.4) | collective-permute-done | bytes 131104 | tf_op jit(solution)/shard_map/ppermute | solution.py:300
  25.5 3.1 %collective-permute-done.2.a_ref = bf16[512,128]{1,0:T(8,128)(2,1)S(1)} collective-permute-done((bf16[512,128]{1,0:T(8,128)(2,1)S(1)}, bf16[512,128]{1,0:T(8,128)(2,1)S(1)}, u32[]{:S(2)}, u32[]{:S(2)}) %collective-permute-start.2) | collective-permute-done | bytes 131104 | tf_op jit(solution)/shard_map/ppermute | solution.py:300
  28.6 0.9 %collective-permute-done.3.b_ref = bf16[512,128]{1,0:T(8,128)(2,1)S(1)} collective-permute-done((bf16[512,128]{1,0:T(8,128)(2,1)S(1)}, bf16[512,128]{1,0:T(8,128)(2,1)S(1)}, u32[]{:S(2)}, u32[]{:S(2)}) %collective-permute-start.3) | collective-permute-done | bytes 131104 | tf_op jit(solution)/shard_map/ppermute | solution.py:300
  29.5 0.7 %summed.1.p0_ref = bf16[512,128]{1,0:T(8,128)(2,1)} custom-call(bf16[512,128]{1,0:T(8,128)(2,1)S(1)} %collective-permute-done.2.a_ref, bf16[512,128]{1,0:T(8,128)(2,1)S(1)} %collective-permute-done.3.b_ref, f32[512,128]{1,0:T(8,128)S(1)} %added.2.own_ref), custom_call_target="tpu_custom_call" | custom-call | flops 1 | bytes 1 | tf_op jit(solution)/shard_map/summed/pallas_call | solution.py:286
  30.2 2.1 %collective-permute-start.5 = (bf16[512,128]{1,0:T(8,128)(2,1)}, bf16[512,128]{1,0:T(8,128)(2,1)S(1)}, u32[]{:S(2)}, u32[]{:S(2)}) collective-permute-start(bf16[512,128]{1,0:T(8,128)(2,1)} %summed.1.p0_ref), channel_id=1, source_target_pairs={{0,1},{1,2},{2,3},{3,0},{4,5},{5,6},{6,7},{7,4},{8,9},{9,10},{10,1... | collective-permute-start | bytes 393224 | tf_op jit(solution)/shard_map/ppermute | solution.py:300
  32.3 1.1 %collective-permute-start.6 = (bf16[512,128]{1,0:T(8,128)(2,1)}, bf16[512,128]{1,0:T(8,128)(2,1)S(1)}, u32[]{:S(2)}, u32[]{:S(2)}) collective-permute-start(bf16[512,128]{1,0:T(8,128)(2,1)} %summed.1.p0_ref), channel_id=1, source_target_pairs={{0,3},{1,0},{2,1},{3,2},{4,7},{5,4},{6,5},{7,6},{8,11},{9,8},{10,9... | collective-permute-start | bytes 393224 | tf_op jit(solution)/shard_map/ppermute | solution.py:300
  33.4 1.0 %collective-permute-start.7 = (bf16[512,128]{1,0:T(8,128)(2,1)}, bf16[512,128]{1,0:T(8,128)(2,1)S(1)}, u32[]{:S(2)}, u32[]{:S(2)}) collective-permute-start(bf16[512,128]{1,0:T(8,128)(2,1)} %summed.1.p0_ref), channel_id=1, source_target_pairs={{0,2},{1,3},{2,0},{3,1},{4,6},{5,7},{6,4},{7,5},{8,10},{9,11},{10,... | collective-permute-start | bytes 393224 | tf_op jit(solution)/shard_map/ppermute | solution.py:300
  34.4 0.0 copy-done.5
  34.4 0.0 copy-done.6
  34.4 2.3 %lists.1.pick_ref.refs_2_ = bf16[768,512]{1,0:T(8,128)(2,1)S(1)} custom-call(bf16[272,512]{1,0:T(8,128)(2,1)S(1)} %collective-permute-done.1.even_ref, bf16[272,512]{1,0:T(8,128)(2,1)S(1)} %collective-permute-done.odd_ref, s32[8,256]{1,0:T(8,128)S(1)} %copy-done.5, f32[8,256]{1,0:T(8,128)S(1)} %copy-done.6), custom_call_target="tpu_custom_call" | custom-call | flops 1 | bytes 1 | tf_op jit(solution)/shard_map/lists/pallas_call | solution.py:286
  36.7 0.1 collective-permute-done.5.p1_ref
  36.8 1.6 %collective-permute-done.6.p3_ref = bf16[512,128]{1,0:T(8,128)(2,1)S(1)} collective-permute-done((bf16[512,128]{1,0:T(8,128)(2,1)}, bf16[512,128]{1,0:T(8,128)(2,1)S(1)}, u32[]{:S(2)}, u32[]{:S(2)}) %collective-permute-start.6) | collective-permute-done | bytes 131104 | tf_op jit(solution)/shard_map/ppermute | solution.py:300
  38.4 2.0 %collective-permute-done.7.p2_ref = bf16[512,128]{1,0:T(8,128)(2,1)S(1)} collective-permute-done((bf16[512,128]{1,0:T(8,128)(2,1)}, bf16[512,128]{1,0:T(8,128)(2,1)S(1)}, u32[]{:S(2)}, u32[]{:S(2)}) %collective-permute-start.7) | collective-permute-done | bytes 131104 | tf_op jit(solution)/shard_map/ppermute | solution.py:300
  40.4 0.0 copy-done
  40.4 0.9 %copy-done.4 = bf16[512,128]{1,0:T(8,128)(2,1)S(1)} copy-done((bf16[512,128]{1,0:T(8,128)(2,1)S(1)}, bf16[512,128]{1,0:T(8,128)(2,1)}, u32[]{:S(2)}) %copy-start.4) | copy-done | bytes 131096
  41.3 1.8 %scattered.1 = (bf16[512,1024]{1,0:T(8,128)(2,1)S(1)}, bf16[4,256,128]{2,1,0:T(8,128)(2,1)S(1)}) custom-call(bf16[512,128]{1,0:T(8,128)(2,1)S(1)} %copy-done.4, bf16[512,128]{1,0:T(8,128)(2,1)S(1)} %collective-permute-done.5.p1_ref, bf16[512,128]{1,0:T(8,128)(2,1)S(1)} %collective-permute-done.6.p3_ref, bf16[512,128]{1,0:T(8,128)(2,1)S(1)} %collective-permute-done.7.p2_ref, ...), custom_call_target="tpu_custom_call" | custom-call | flops 1 | bytes 1 | tf_op jit(solution)/shard_map/scattered/pallas_call | solution.py:286
  43.1 2.4 %collective-permute-start.9 = (bf16[4,256,128]{2,1,0:T(8,128)(2,1)S(1)}, bf16[4,256,128]{2,1,0:T(8,128)(2,1)S(1)}, u32[]{:S(2)}, u32[]{:S(2)}) collective-permute-start(bf16[4,256,128]{2,1,0:T(8,128)(2,1)S(1)} %get-tuple-element.32), channel_id=1, source_target_pairs={{4,8},{8,4},{12,16},{16,12},{20,24},{24,20},{28,32},{32,28},{36,40... | collective-permute-start | bytes 786440 | tf_op jit(solution)/shard_map/ppermute | solution.py:308
  45.5 1.2 %tested_even.1 = bf16[4,256,128]{2,1,0:T(8,128)(2,1)S(1)} custom-call(bf16[512,1024]{1,0:T(8,128)(2,1)S(1)} %get-tuple-element.33.refs_0_, bf16[2,512,512]{2,1,0:T(8,128)(2,1)S(1)} %copy-done, bf16[768,512]{1,0:T(8,128)(2,1)S(1)} %lists.1.pick_ref.refs_2_, f32[2,768,256]{2,1,0:T(8,128)S(1)} %get-tuple-element.22.mom_cos.refs_3_, ...), custom_call_target="tpu_custom_call" | custom-call | flops 1 | bytes 1 | tf_op jit(solution)/shard_map/tested_even/pallas_call | solution.py:286
  46.8 0.1 collective-permute-start.8
  46.9 1.2 %tested_own.1.own_ref = f32[4,256,128]{2,1,0:T(8,128)S(1)} custom-call(bf16[512,1024]{1,0:T(8,128)(2,1)S(1)} %get-tuple-element.33.refs_0_, bf16[2,512,512]{2,1,0:T(8,128)(2,1)S(1)} %copy-done, bf16[768,512]{1,0:T(8,128)(2,1)S(1)} %lists.1.pick_ref.refs_2_, f32[2,768,256]{2,1,0:T(8,128)S(1)} %get-tuple-element.22.mom_cos.refs_3_, ...), custom_call_target="tpu_custom_call" | custom-call | flops 1 | bytes 1 | tf_op jit(solution)/shard_map/tested_own/pallas_call | solution.py:286
  48.1 4.9 %collective-permute-done.9.new_ref = bf16[4,256,128]{2,1,0:T(8,128)(2,1)S(1)} collective-permute-done((bf16[4,256,128]{2,1,0:T(8,128)(2,1)S(1)}, bf16[4,256,128]{2,1,0:T(8,128)(2,1)S(1)}, u32[]{:S(2)}, u32[]{:S(2)}) %collective-permute-start.9) | collective-permute-done | bytes 262176 | tf_op jit(solution)/shard_map/ppermute | solution.py:308
  53.0 0.0 collective-permute-done.8.even_ref
  53.0 1.4 %collective-permute-start.10 = (bf16[256,128]{1,0:T(8,128)(2,1)S(1)}, bf16[256,128]{1,0:T(8,128)(2,1)S(1)}, u32[]{:S(2)}, u32[]{:S(2)}) collective-permute-start(bf16[256,128]{1,0:T(8,128)(2,1)S(1)} %get-tuple-element.35), channel_id=1, source_target_pairs={{0,1},{1,2},{2,3},{3,0},{4,5},{5,6},{6,7},{7,4},{8,9},{9,10},{10,1... | collective-permute-start | bytes 196616 | tf_op jit(solution)/shard_map/ppermute | solution.py:300
  54.4 2.3 %collective-permute-start.11 = (bf16[256,128]{1,0:T(8,128)(2,1)S(1)}, bf16[256,128]{1,0:T(8,128)(2,1)S(1)}, u32[]{:S(2)}, u32[]{:S(2)}) collective-permute-start(bf16[256,128]{1,0:T(8,128)(2,1)S(1)} %get-tuple-element.36), channel_id=1, source_target_pairs={{0,2},{1,3},{2,0},{3,1},{4,6},{5,7},{6,4},{7,5},{8,10},{9,11},{10,... | collective-permute-start | bytes 196616 | tf_op jit(solution)/shard_map/ppermute | solution.py:300
  56.7 0.5 collective-permute-start.12
  57.2 1.4 %collective-permute-done.10 = bf16[256,128]{1,0:T(8,128)(2,1)S(1)} collective-permute-done((bf16[256,128]{1,0:T(8,128)(2,1)S(1)}, bf16[256,128]{1,0:T(8,128)(2,1)S(1)}, u32[]{:S(2)}, u32[]{:S(2)}) %collective-permute-start.10) | collective-permute-done | bytes 65568 | tf_op jit(solution)/shard_map/ppermute | solution.py:300
  58.6 1.6 %collective-permute-done.11 = bf16[256,128]{1,0:T(8,128)(2,1)S(1)} collective-permute-done((bf16[256,128]{1,0:T(8,128)(2,1)S(1)}, bf16[256,128]{1,0:T(8,128)(2,1)S(1)}, u32[]{:S(2)}, u32[]{:S(2)}) %collective-permute-start.11) | collective-permute-done | bytes 65568 | tf_op jit(solution)/shard_map/ppermute | solution.py:300
  60.2 0.8 %collective-permute-done.12 = bf16[256,128]{1,0:T(8,128)(2,1)S(1)} collective-permute-done((bf16[256,128]{1,0:T(8,128)(2,1)S(1)}, bf16[256,128]{1,0:T(8,128)(2,1)S(1)}, u32[]{:S(2)}, u32[]{:S(2)}) %collective-permute-start.12) | collective-permute-done | bytes 65568 | tf_op jit(solution)/shard_map/ppermute | solution.py:300
  61.0 0.7 %convert_add_fusion = f32[256,128]{1,0:T(8,128)} fusion(bf16[256,128]{1,0:T(8,128)(2,1)S(1)} %collective-permute-done.12, bf16[256,128]{1,0:T(8,128)(2,1)S(1)} %collective-permute-done.11, f32[256,128]{1,0:T(8,128)S(1)} %get-tuple-element.34, bf16[256,128]{1,0:T(8,128)(2,1)S(1)} %collective-permute-done.10), kind=kLoop, calls=%fused_computation | loop fusion | flops 196608 | bytes 458752 | tf_op jit(solution)/shard_map/add | solution.py:389
  (7 shorter events, 0.1 us)
Async XLA Ops:
  0.6 14.7 %copy-start.1 = (bf16[2,512,512]{2,1,0:T(8,128)(2,1)S(1)}, bf16[2,512,512]{2,1,0:T(8,128)(2,1)}, u32[]{:S(2)}) copy-start(bf16[2,512,512]{2,1,0:T(8,128)(2,1)} %radiate_ref.2) | copy-start | bytes 3145732
  0.6 14.7 %copy-start.2 = (bf16[2,512,512]{2,1,0:T(8,128)(2,1)S(1)}, bf16[2,512,512]{2,1,0:T(8,128)(2,1)}, u32[]{:S(2)}) copy-start(bf16[2,512,512]{2,1,0:T(8,128)(2,1)} %receive_ref.4) | copy-start | bytes 3145732
  0.7 14.7 %copy-start.7 = (s32[2,512]{1,0:T(2,128)S(1)}, s32[2,512]{1,0:T(2,128)}, u32[]{:S(2)}) copy-start(s32[2,512]{1,0:T(2,128)} %lit_ref.1) | copy-start | bytes 12292
  1.8 13.5 %collective-permute-start = (bf16[272,512]{1,0:T(8,128)(2,1)S(1)}, bf16[272,512]{1,0:T(8,128)(2,1)S(1)}, u32[]{:S(2)}, u32[]{:S(2)}) collective-permute-start(bf16[272,512]{1,0:T(8,128)(2,1)S(1)} %packed.1), channel_id=1, source_target_pairs={{4,8},{8,4},{12,16},{16,12},{20,24},{24,20},{28,32},{32,28},{36,40... | collective-permute-start | bytes 835592 | tf_op jit(solution)/shard_map/ppermute | solution.py:308
  9.3 6.0 %collective-permute-start.1 = (bf16[272,512]{1,0:T(8,128)(2,1)S(1)}, bf16[272,512]{1,0:T(8,128)(2,1)S(1)}, u32[]{:S(2)}, u32[]{:S(2)}) collective-permute-start(bf16[272,512]{1,0:T(8,128)(2,1)S(1)} %packed.1), channel_id=1, source_target_pairs={{0,4},{4,0},{8,12},{12,8},{16,20},{20,16},{24,28},{28,24},{32,36},... | collective-permute-start | bytes 835592 | tf_op jit(solution)/shard_map/ppermute | solution.py:304
  18.3 7.2 %collective-permute-start.4 = (bf16[512,128]{1,0:T(8,128)(2,1)S(1)}, bf16[512,128]{1,0:T(8,128)(2,1)S(1)}, u32[]{:S(2)}, u32[]{:S(2)}) collective-permute-start(bf16[512,128]{1,0:T(8,128)(2,1)S(1)} %get-tuple-element.29), channel_id=1, source_target_pairs={{0,1},{1,2},{2,3},{3,0},{4,5},{5,6},{6,7},{7,4},{8,9},{9,10},{10,1... | collective-permute-start | bytes 393224 | tf_op jit(solution)/shard_map/ppermute | solution.py:300
  19.9 14.5 %copy-start.5 = (s32[8,256]{1,0:T(8,128)S(1)}, s32[8,256]{1,0:T(8,128)}, u32[]{:S(2)}) copy-start(s32[8,256]{1,0:T(8,128)} %src_ref.1) | copy-start | bytes 24580
  19.9 14.5 %copy-start.6 = (f32[8,256]{1,0:T(8,128)S(1)}, f32[8,256]{1,0:T(8,128)}, u32[]{:S(2)}) copy-start(f32[8,256]{1,0:T(8,128)} %weight_ref.1) | copy-start | bytes 24580
  20.8 19.6 %copy-start = (bf16[2,512,512]{2,1,0:T(8,128)(2,1)S(1)}, bf16[2,512,512]{2,1,0:T(8,128)(2,1)}, u32[]{:S(2)}) copy-start(bf16[2,512,512]{2,1,0:T(8,128)(2,1)} %refs_1_.3) | copy-start | bytes 3145732
  20.8 19.6 %copy-start.3 = (bf16[2,512,512]{2,1,0:T(8,128)(2,1)S(1)}, bf16[2,512,512]{2,1,0:T(8,128)(2,1)}, u32[]{:S(2)}) copy-start(bf16[2,512,512]{2,1,0:T(8,128)(2,1)} %radiate_ref.3) | copy-start | bytes 3145732
  20.8 7.8 %collective-permute-start.2 = (bf16[512,128]{1,0:T(8,128)(2,1)S(1)}, bf16[512,128]{1,0:T(8,128)(2,1)S(1)}, u32[]{:S(2)}, u32[]{:S(2)}) collective-permute-start(bf16[512,128]{1,0:T(8,128)(2,1)S(1)} %get-tuple-element.27), channel_id=1, source_target_pairs={{0,3},{1,0},{2,1},{3,2},{4,7},{5,4},{6,5},{7,6},{8,11},{9,8},{10,9... | collective-permute-start | bytes 393224 | tf_op jit(solution)/shard_map/ppermute | solution.py:300
  22.5 6.9 %collective-permute-start.3 = (bf16[512,128]{1,0:T(8,128)(2,1)S(1)}, bf16[512,128]{1,0:T(8,128)(2,1)S(1)}, u32[]{:S(2)}, u32[]{:S(2)}) collective-permute-start(bf16[512,128]{1,0:T(8,128)(2,1)S(1)} %get-tuple-element.28), channel_id=1, source_target_pairs={{0,2},{1,3},{2,0},{3,1},{4,6},{5,7},{6,4},{7,5},{8,10},{9,11},{10,... | collective-permute-start | bytes 393224 | tf_op jit(solution)/shard_map/ppermute | solution.py:300
  30.2 6.6 %collective-permute-start.5 = (bf16[512,128]{1,0:T(8,128)(2,1)}, bf16[512,128]{1,0:T(8,128)(2,1)S(1)}, u32[]{:S(2)}, u32[]{:S(2)}) collective-permute-start(bf16[512,128]{1,0:T(8,128)(2,1)} %summed.1.p0_ref), channel_id=1, source_target_pairs={{0,1},{1,2},{2,3},{3,0},{4,5},{5,6},{6,7},{7,4},{8,9},{9,10},{10,1... | collective-permute-start | bytes 393224 | tf_op jit(solution)/shard_map/ppermute | solution.py:300
  32.3 6.1 %collective-permute-start.6 = (bf16[512,128]{1,0:T(8,128)(2,1)}, bf16[512,128]{1,0:T(8,128)(2,1)S(1)}, u32[]{:S(2)}, u32[]{:S(2)}) collective-permute-start(bf16[512,128]{1,0:T(8,128)(2,1)} %summed.1.p0_ref), channel_id=1, source_target_pairs={{0,3},{1,0},{2,1},{3,2},{4,7},{5,4},{6,5},{7,6},{8,11},{9,8},{10,9... | collective-permute-start | bytes 393224 | tf_op jit(solution)/shard_map/ppermute | solution.py:300
  33.4 7.0 %collective-permute-start.7 = (bf16[512,128]{1,0:T(8,128)(2,1)}, bf16[512,128]{1,0:T(8,128)(2,1)S(1)}, u32[]{:S(2)}, u32[]{:S(2)}) collective-permute-start(bf16[512,128]{1,0:T(8,128)(2,1)} %summed.1.p0_ref), channel_id=1, source_target_pairs={{0,2},{1,3},{2,0},{3,1},{4,6},{5,7},{6,4},{7,5},{8,10},{9,11},{10,... | collective-permute-start | bytes 393224 | tf_op jit(solution)/shard_map/ppermute | solution.py:300
  40.4 0.9 %copy-start.4 = (bf16[512,128]{1,0:T(8,128)(2,1)S(1)}, bf16[512,128]{1,0:T(8,128)(2,1)}, u32[]{:S(2)}) copy-start(bf16[512,128]{1,0:T(8,128)(2,1)} %summed.1.p0_ref) | copy-start | bytes 393220
  43.1 9.8 %collective-permute-start.9 = (bf16[4,256,128]{2,1,0:T(8,128)(2,1)S(1)}, bf16[4,256,128]{2,1,0:T(8,128)(2,1)S(1)}, u32[]{:S(2)}, u32[]{:S(2)}) collective-permute-start(bf16[4,256,128]{2,1,0:T(8,128)(2,1)S(1)} %get-tuple-element.32), channel_id=1, source_target_pairs={{4,8},{8,4},{12,16},{16,12},{20,24},{24,20},{28,32},{32,28},{36,40... | collective-permute-start | bytes 786440 | tf_op jit(solution)/shard_map/ppermute | solution.py:308
  46.8 6.2 %collective-permute-start.8 = (bf16[4,256,128]{2,1,0:T(8,128)(2,1)S(1)}, bf16[4,256,128]{2,1,0:T(8,128)(2,1)S(1)}, u32[]{:S(2)}, u32[]{:S(2)}) collective-permute-start(bf16[4,256,128]{2,1,0:T(8,128)(2,1)S(1)} %tested_even.1), channel_id=1, source_target_pairs={{0,4},{4,0},{8,12},{12,8},{16,20},{20,16},{24,28},{28,24},{32,36},... | collective-permute-start | bytes 786440 | tf_op jit(solution)/shard_map/ppermute | solution.py:304
  53.0 5.6 %collective-permute-start.10 = (bf16[256,128]{1,0:T(8,128)(2,1)S(1)}, bf16[256,128]{1,0:T(8,128)(2,1)S(1)}, u32[]{:S(2)}, u32[]{:S(2)}) collective-permute-start(bf16[256,128]{1,0:T(8,128)(2,1)S(1)} %get-tuple-element.35), channel_id=1, source_target_pairs={{0,1},{1,2},{2,3},{3,0},{4,5},{5,6},{6,7},{7,4},{8,9},{9,10},{10,1... | collective-permute-start | bytes 196616 | tf_op jit(solution)/shard_map/ppermute | solution.py:300
  54.4 5.8 %collective-permute-start.11 = (bf16[256,128]{1,0:T(8,128)(2,1)S(1)}, bf16[256,128]{1,0:T(8,128)(2,1)S(1)}, u32[]{:S(2)}, u32[]{:S(2)}) collective-permute-start(bf16[256,128]{1,0:T(8,128)(2,1)S(1)} %get-tuple-element.36), channel_id=1, source_target_pairs={{0,2},{1,3},{2,0},{3,1},{4,6},{5,7},{6,4},{7,5},{8,10},{9,11},{10,... | collective-permute-start | bytes 196616 | tf_op jit(solution)/shard_map/ppermute | solution.py:300
  56.7 4.3 %collective-permute-start.12 = (bf16[256,128]{1,0:T(8,128)(2,1)S(1)}, bf16[256,128]{1,0:T(8,128)(2,1)S(1)}, u32[]{:S(2)}, u32[]{:S(2)}) collective-permute-start(bf16[256,128]{1,0:T(8,128)(2,1)S(1)} %get-tuple-element.37), channel_id=1, source_target_pairs={{0,3},{1,0},{2,1},{3,2},{4,7},{5,4},{6,5},{7,6},{8,11},{9,8},{10,9... | collective-permute-start | bytes 196616 | tf_op jit(solution)/shard_map/ppermute | solution.py:300

commit v6 on v5

--- a/solution.py
+++ b/solution.py
@@ -193,11 +193,6 @@
     s3_ref[...] = chunks[3].astype(BF)
 
 
-def summed(a_ref, b_ref, own_ref, out_ref):
-    total = own_ref[...] + a_ref[...].astype(F32) + b_ref[...].astype(F32)
-    out_ref[...] = total.astype(out_ref.dtype)
-
-
 def lists(even_ref, odd_ref, src_ref, weight_ref, pick_ref):
     box = lax.axis_index("box")
     even = lax.rem(box, 2) == 0
@@ -361,7 +356,7 @@
     s3 = turned(s3, 3)
     back = call(lists, shape((3 * m, q), BF), (even, odd, mom_src, mom_weight))
     own = call(added, shape((q, share), F32), (s1, own))
-    po_share = call(summed, shape((q, share), BF), (s3, s2, own))
+    po_share = (own + s3.astype(F32) + s2.astype(F32)).astype(BF)
     p2 = turned(po_share, 2)
     p1 = turned(po_share, 1)
     p3 = turned(po_share, 3)

time: 61.9 us -> 60.4 us (0.976)
  local copies, waits for them, and re-layouts: 0.94 us -> 0.04 us
    unnamed x16, local copies, waits for them, and re-layouts: 0.94 us -> 0.04 us
    pallas_call x12 -> x11, Pallas kernels: 18.1 us -> 17.7 us  [call(): pl.pallas_call(body, out_shape=outs, in_specs=[pl.BlockSpec(memory_space=...]
  transfers between devices with their start and end apart: 13 -> 13, of which waited for: 10 -> 9; matrix products, arithmetic and copies ran while one was open for 0% -> 0% of each run, Pallas kernels for 19% -> 19%
where the time goes in v6:
time: 60.4 us; the launch traced here: 60.2 us
  starting transfers between devices  24.1 us (40%)
  Pallas kernels  17.7 us (29%)
  waiting for transfers between devices  16.8 us (28%)
  between operations  0.86 us (1%)
  other arithmetic  0.73 us (1%)
    pallas_call x11, Pallas kernels, call(): pl.pallas_call(body, out_shape=outs, in_specs=[pl.BlockSpec(memory_space=...  17.7 us
    ppermute x9, starting transfers between devices, turned(): lax.ppermute(value, 'cone', [(i, (i + shift) % count) for i in range(coun...  14.1 us
    ppermute x9, waiting for transfers between devices, turned(): lax.ppermute(value, 'cone', [(i, (i + shift) % count) for i in range(coun...  11.9 us
    ppermute x2, starting transfers between devices, swapped_odd(): lax.ppermute(value, 'box', [(i, (i + 1 ^ 1) - 1) for i in range(1, lax.ax...  9.83 us
    ppermute x2, waiting for transfers between devices, swapped_odd(): lax.ppermute(value, 'box', [(i, (i + 1 ^ 1) - 1) for i in range(1, lax.ax...  4.88 us
  transfers between devices with their start and end apart: 13, of which 9 were waited for; matrix products, arithmetic and copies ran while one was open for 0% of the time, Pallas kernels for 19%

profile of v6, /device:TPU:6, one launch (start us, length us, event | category | flops | bytes accessed | tf_op | source)
XLA Modules:
  0.0 60.2 jit_solution(17862231219096513277)
XLA Ops:
  0.6 0.0 copy-start.1
  0.6 0.0 copy-start.2
  0.7 0.0 copy-start.7
  0.7 1.2 %packed.1 = bf16[272,512]{1,0:T(8,128)(2,1)S(1)} custom-call(bf16[256,512]{1,0:T(8,128)(2,1)} %current_hbm.3, s32[8,256]{1,0:T(8,128)} %src_ref.1, f32[8,256]{1,0:T(8,128)} %weight_ref.1), custom_call_target="tpu_custom_call" | custom-call | flops 1 | bytes 1 | tf_op jit(solution)/shard_map/packed/pallas_call | solution.py:281
  1.8 7.5 %collective-permute-start = (bf16[272,512]{1,0:T(8,128)(2,1)S(1)}, bf16[272,512]{1,0:T(8,128)(2,1)S(1)}, u32[]{:S(2)}, u32[]{:S(2)}) collective-permute-start(bf16[272,512]{1,0:T(8,128)(2,1)S(1)} %packed.1), channel_id=1, source_target_pairs={{4,8},{8,4},{12,16},{16,12},{20,24},{24,20},{28,32},{32,28},{36,40... | collective-permute-start | bytes 835592 | tf_op jit(solution)/shard_map/ppermute | solution.py:303
  9.3 0.1 collective-permute-start.1
  9.4 5.9 %prepare.1 = (f32[2,768,256]{2,1,0:T(8,128)S(1)}, f32[2,768,256]{2,1,0:T(8,128)S(1)}, f32[2,512,256]{2,1,0:T(8,128)S(1)}, f32[2,512,256]{2,1,0:T(8,128)S(1)}, bf...) custom-call(bf16[256,512]{1,0:T(8,128)(2,1)} %current_hbm.3, bf16[2,512,512]{2,1,0:T(8,128)(2,1)} %radiate_ref.2, ...), custom_call_target="tpu_custom_call" | custom-call | flops 1 | bytes 1 | tf_op jit(solution)/shard_map/prepare/pallas_call | solution.py:281
  15.3 0.0 collective-permute-done.odd_ref
  15.3 0.0 collective-permute-done.1.even_ref
  15.3 0.0 copy-done.1
  15.3 0.0 copy-done.2
  15.3 0.0 copy-done.7
  15.3 3.0 %incident.1 = (bf16[512,128]{1,0:T(8,128)(2,1)S(1)}, bf16[512,1024]{1,0:T(8,128)(2,1)S(1)}) custom-call(bf16[272,512]{1,0:T(8,128)(2,1)S(1)} %collective-permute-done.odd_ref, bf16[272,512]{1,0:T(8,128)(2,1)S(1)} %collective-permute-done.1.even_ref, bf16[256,1024]{1,0:T(8,128)(2,1)S(1)} %get-tuple-element.20.wave_ref, ...), custom_call_target="tpu_custom_call" | custom-call | flops 1 | bytes 1 | tf_op jit(solution)/shard_map/incident/pallas_call | solution.py:281
  18.4 1.7 %collective-permute-start.2 = (bf16[512,128]{1,0:T(8,128)(2,1)S(1)}, bf16[512,128]{1,0:T(8,128)(2,1)S(1)}, u32[]{:S(2)}, u32[]{:S(2)}) collective-permute-start(bf16[512,128]{1,0:T(8,128)(2,1)S(1)} %get-tuple-element.26), channel_id=1, source_target_pairs={{0,1},{1,2},{2,3},{3,0},{4,5},{5,6},{6,7},{7,4},{8,9},{9,10},{10,1... | collective-permute-start | bytes 393224 | tf_op jit(solution)/shard_map/ppermute | solution.py:295
  20.0 0.9 %received.1 = (f32[512,128]{1,0:T(8,128)S(1)}, bf16[512,128]{1,0:T(8,128)(2,1)S(1)}, bf16[512,128]{1,0:T(8,128)(2,1)S(1)}) custom-call(bf16[512,1024]{1,0:T(8,128)(2,1)S(1)} %get-tuple-element.27.po_lit_ref, bf16[2,512,512]{2,1,0:T(8,128)(2,1)S(1)} %copy-done.2), custom_call_target="tpu_custom_call" | custom-call | flops 1 | bytes 1 | tf_op jit(solution)/shard_map/received/pallas_call | solution.py:281
  20.9 0.0 copy-start
  20.9 0.0 copy-start.3
  21.0 1.7 %collective-permute-start.3 = (bf16[512,128]{1,0:T(8,128)(2,1)S(1)}, bf16[512,128]{1,0:T(8,128)(2,1)S(1)}, u32[]{:S(2)}, u32[]{:S(2)}) collective-permute-start(bf16[512,128]{1,0:T(8,128)(2,1)S(1)} %get-tuple-element.29), channel_id=1, source_target_pairs={{0,3},{1,0},{2,1},{3,2},{4,7},{5,4},{6,5},{7,6},{8,11},{9,8},{10,9... | collective-permute-start | bytes 393224 | tf_op jit(solution)/shard_map/ppermute | solution.py:295
  22.7 2.0 %collective-permute-start.4 = (bf16[512,128]{1,0:T(8,128)(2,1)S(1)}, bf16[512,128]{1,0:T(8,128)(2,1)S(1)}, u32[]{:S(2)}, u32[]{:S(2)}) collective-permute-start(bf16[512,128]{1,0:T(8,128)(2,1)S(1)} %get-tuple-element.30), channel_id=1, source_target_pairs={{0,2},{1,3},{2,0},{3,1},{4,6},{5,7},{6,4},{7,5},{8,10},{9,11},{10,... | collective-permute-start | bytes 393224 | tf_op jit(solution)/shard_map/ppermute | solution.py:295
  24.7 0.9 %collective-permute-done.2.new_ref = bf16[512,128]{1,0:T(8,128)(2,1)S(1)} collective-permute-done((bf16[512,128]{1,0:T(8,128)(2,1)S(1)}, bf16[512,128]{1,0:T(8,128)(2,1)S(1)}, u32[]{:S(2)}, u32[]{:S(2)}) %collective-permute-start.2) | collective-permute-done | bytes 131104 | tf_op jit(solution)/shard_map/ppermute | solution.py:295
  25.6 3.1 %collective-permute-done.3 = bf16[512,128]{1,0:T(8,128)(2,1)S(1)} collective-permute-done((bf16[512,128]{1,0:T(8,128)(2,1)S(1)}, bf16[512,128]{1,0:T(8,128)(2,1)S(1)}, u32[]{:S(2)}, u32[]{:S(2)}) %collective-permute-start.3) | collective-permute-done | bytes 131104 | tf_op jit(solution)/shard_map/ppermute | solution.py:295
  28.8 0.9 %collective-permute-done.4 = bf16[512,128]{1,0:T(8,128)(2,1)S(1)} collective-permute-done((bf16[512,128]{1,0:T(8,128)(2,1)S(1)}, bf16[512,128]{1,0:T(8,128)(2,1)S(1)}, u32[]{:S(2)}, u32[]{:S(2)}) %collective-permute-start.4) | collective-permute-done | bytes 131104 | tf_op jit(solution)/shard_map/ppermute | solution.py:295
  29.7 0.0 copy-start.4
  29.7 2.2 %collective-permute-start.5 = (bf16[512,128]{1,0:T(8,128)(2,1)S(1)}, bf16[512,128]{1,0:T(8,128)(2,1)S(1)}, u32[]{:S(2)}, u32[]{:S(2)}) collective-permute-start(bf16[512,128]{1,0:T(8,128)(2,1)S(1)} %add_convert_fusion.p0_ref), channel_id=1, source_target_pairs={{0,1},{1,2},{2,3},{3,0},{4,5},{5,6},{6,7},{7,4},{8,9},{9,10},{10,1... | collective-permute-start | bytes 393224 | tf_op jit(solution)/shard_map/ppermute | solution.py:295
  31.9 1.1 %collective-permute-start.6 = (bf16[512,128]{1,0:T(8,128)(2,1)S(1)}, bf16[512,128]{1,0:T(8,128)(2,1)S(1)}, u32[]{:S(2)}, u32[]{:S(2)}) collective-permute-start(bf16[512,128]{1,0:T(8,128)(2,1)S(1)} %add_convert_fusion.p0_ref), channel_id=1, source_target_pairs={{0,3},{1,0},{2,1},{3,2},{4,7},{5,4},{6,5},{7,6},{8,11},{9,8},{10,9... | collective-permute-start | bytes 393224 | tf_op jit(solution)/shard_map/ppermute | solution.py:295
  33.0 1.2 %collective-permute-start.7 = (bf16[512,128]{1,0:T(8,128)(2,1)S(1)}, bf16[512,128]{1,0:T(8,128)(2,1)S(1)}, u32[]{:S(2)}, u32[]{:S(2)}) collective-permute-start(bf16[512,128]{1,0:T(8,128)(2,1)S(1)} %add_convert_fusion.p0_ref), channel_id=1, source_target_pairs={{0,2},{1,3},{2,0},{3,1},{4,6},{5,7},{6,4},{7,5},{8,10},{9,11},{10,... | collective-permute-start | bytes 393224 | tf_op jit(solution)/shard_map/ppermute | solution.py:295
  34.2 0.0 copy-done.5
  34.2 0.0 copy-done.6
  34.2 2.3 %lists.1.pick_ref.refs_2_ = bf16[768,512]{1,0:T(8,128)(2,1)S(1)} custom-call(bf16[272,512]{1,0:T(8,128)(2,1)S(1)} %collective-permute-done.1.even_ref, bf16[272,512]{1,0:T(8,128)(2,1)S(1)} %collective-permute-done.odd_ref, s32[8,256]{1,0:T(8,128)S(1)} %copy-done.5, f32[8,256]{1,0:T(8,128)S(1)} %copy-done.6), custom_call_target="tpu_custom_call" | custom-call | flops 1 | bytes 1 | tf_op jit(solution)/shard_map/lists/pallas_call | solution.py:281
  36.5 0.0 collective-permute-done.5.p1_ref
  36.5 1.3 %collective-permute-done.6.p3_ref = bf16[512,128]{1,0:T(8,128)(2,1)S(1)} collective-permute-done((bf16[512,128]{1,0:T(8,128)(2,1)S(1)}, bf16[512,128]{1,0:T(8,128)(2,1)S(1)}, u32[]{:S(2)}, u32[]{:S(2)}) %collective-permute-start.6) | collective-permute-done | bytes 131104 | tf_op jit(solution)/shard_map/ppermute | solution.py:295
  37.8 2.0 %collective-permute-done.7.p2_ref = bf16[512,128]{1,0:T(8,128)(2,1)S(1)} collective-permute-done((bf16[512,128]{1,0:T(8,128)(2,1)S(1)}, bf16[512,128]{1,0:T(8,128)(2,1)S(1)}, u32[]{:S(2)}, u32[]{:S(2)}) %collective-permute-start.7) | collective-permute-done | bytes 131104 | tf_op jit(solution)/shard_map/ppermute | solution.py:295
  39.8 0.0 copy-done
  39.8 0.0 copy-done.3
  39.8 1.9 %scattered.1 = (bf16[512,1024]{1,0:T(8,128)(2,1)S(1)}, bf16[4,256,128]{2,1,0:T(8,128)(2,1)S(1)}) custom-call(bf16[512,128]{1,0:T(8,128)(2,1)S(1)} %add_convert_fusion.p0_ref, bf16[512,128]{1,0:T(8,128)(2,1)S(1)} %collective-permute-done.5.p1_ref, bf16[512,128]{1,0:T(8,128)(2,1)S(1)} %collective-permute-done.6.p3_ref, ...), custom_call_target="tpu_custom_call" | custom-call | flops 1 | bytes 1 | tf_op jit(solution)/shard_map/scattered/pallas_call | solution.py:281
  41.7 2.4 %collective-permute-start.9 = (bf16[4,256,128]{2,1,0:T(8,128)(2,1)S(1)}, bf16[4,256,128]{2,1,0:T(8,128)(2,1)S(1)}, u32[]{:S(2)}, u32[]{:S(2)}) collective-permute-start(bf16[4,256,128]{2,1,0:T(8,128)(2,1)S(1)} %get-tuple-element.32), channel_id=1, source_target_pairs={{4,8},{8,4},{12,16},{16,12},{20,24},{24,20},{28,32},{32,28},{36,40... | collective-permute-start | bytes 786440 | tf_op jit(solution)/shard_map/ppermute | solution.py:303
  44.1 1.2 %tested_even.1 = bf16[4,256,128]{2,1,0:T(8,128)(2,1)S(1)} custom-call(bf16[512,1024]{1,0:T(8,128)(2,1)S(1)} %get-tuple-element.33.refs_0_, bf16[2,512,512]{2,1,0:T(8,128)(2,1)S(1)} %copy-done, bf16[768,512]{1,0:T(8,128)(2,1)S(1)} %lists.1.pick_ref.refs_2_, f32[2,768,256]{2,1,0:T(8,128)S(1)} %get-tuple-element.22.mom_cos.refs_3_, ...), custom_call_target="tpu_custom_call" | custom-call | flops 1 | bytes 1 | tf_op jit(solution)/shard_map/tested_even/pallas_call | solution.py:281
  45.3 0.1 collective-permute-start.8
  45.4 1.2 %tested_own.1.own_ref = f32[4,256,128]{2,1,0:T(8,128)S(1)} custom-call(bf16[512,1024]{1,0:T(8,128)(2,1)S(1)} %get-tuple-element.33.refs_0_, bf16[2,512,512]{2,1,0:T(8,128)(2,1)S(1)} %copy-done, bf16[768,512]{1,0:T(8,128)(2,1)S(1)} %lists.1.pick_ref.refs_2_, f32[2,768,256]{2,1,0:T(8,128)S(1)} %get-tuple-element.22.mom_cos.refs_3_, ...), custom_call_target="tpu_custom_call" | custom-call | flops 1 | bytes 1 | tf_op jit(solution)/shard_map/tested_own/pallas_call | solution.py:281
  46.6 4.9 %collective-permute-done.9.new_ref = bf16[4,256,128]{2,1,0:T(8,128)(2,1)S(1)} collective-permute-done((bf16[4,256,128]{2,1,0:T(8,128)(2,1)S(1)}, bf16[4,256,128]{2,1,0:T(8,128)(2,1)S(1)}, u32[]{:S(2)}, u32[]{:S(2)}) %collective-permute-start.9) | collective-permute-done | bytes 262176 | tf_op jit(solution)/shard_map/ppermute | solution.py:303
  51.6 0.0 collective-permute-done.8.even_ref
  51.6 1.3 %collective-permute-start.10 = (bf16[256,128]{1,0:T(8,128)(2,1)S(1)}, bf16[256,128]{1,0:T(8,128)(2,1)S(1)}, u32[]{:S(2)}, u32[]{:S(2)}) collective-permute-start(bf16[256,128]{1,0:T(8,128)(2,1)S(1)} %get-tuple-element.35), channel_id=1, source_target_pairs={{0,1},{1,2},{2,3},{3,0},{4,5},{5,6},{6,7},{7,4},{8,9},{9,10},{10,1... | collective-permute-start | bytes 196616 | tf_op jit(solution)/shard_map/ppermute | solution.py:295
  53.0 2.3 %collective-permute-start.11 = (bf16[256,128]{1,0:T(8,128)(2,1)S(1)}, bf16[256,128]{1,0:T(8,128)(2,1)S(1)}, u32[]{:S(2)}, u32[]{:S(2)}) collective-permute-start(bf16[256,128]{1,0:T(8,128)(2,1)S(1)} %get-tuple-element.36), channel_id=1, source_target_pairs={{0,2},{1,3},{2,0},{3,1},{4,6},{5,7},{6,4},{7,5},{8,10},{9,11},{10,... | collective-permute-start | bytes 196616 | tf_op jit(solution)/shard_map/ppermute | solution.py:295
  55.3 0.5 collective-permute-start.12
  55.7 1.4 %collective-permute-done.10 = bf16[256,128]{1,0:T(8,128)(2,1)S(1)} collective-permute-done((bf16[256,128]{1,0:T(8,128)(2,1)S(1)}, bf16[256,128]{1,0:T(8,128)(2,1)S(1)}, u32[]{:S(2)}, u32[]{:S(2)}) %collective-permute-start.10) | collective-permute-done | bytes 65568 | tf_op jit(solution)/shard_map/ppermute | solution.py:295
  57.2 1.5 %collective-permute-done.11 = bf16[256,128]{1,0:T(8,128)(2,1)S(1)} collective-permute-done((bf16[256,128]{1,0:T(8,128)(2,1)S(1)}, bf16[256,128]{1,0:T(8,128)(2,1)S(1)}, u32[]{:S(2)}, u32[]{:S(2)}) %collective-permute-start.11) | collective-permute-done | bytes 65568 | tf_op jit(solution)/shard_map/ppermute | solution.py:295
  58.7 0.8 %collective-permute-done.12 = bf16[256,128]{1,0:T(8,128)(2,1)S(1)} collective-permute-done((bf16[256,128]{1,0:T(8,128)(2,1)S(1)}, bf16[256,128]{1,0:T(8,128)(2,1)S(1)}, u32[]{:S(2)}, u32[]{:S(2)}) %collective-permute-start.12) | collective-permute-done | bytes 65568 | tf_op jit(solution)/shard_map/ppermute | solution.py:295
  59.5 0.7 %convert_add_fusion = f32[256,128]{1,0:T(8,128)} fusion(bf16[256,128]{1,0:T(8,128)(2,1)S(1)} %collective-permute-done.12, bf16[256,128]{1,0:T(8,128)(2,1)S(1)} %collective-permute-done.11, f32[256,128]{1,0:T(8,128)S(1)} %get-tuple-element.34, bf16[256,128]{1,0:T(8,128)(2,1)S(1)} %collective-permute-done.10), kind=kLoop, calls=%fused_computation.1 | loop fusion | flops 196608 | bytes 458752 | tf_op jit(solution)/shard_map/add | solution.py:384
  (7 shorter events, 0.2 us)
Async XLA Ops:
  0.6 14.7 %copy-start.1 = (bf16[2,512,512]{2,1,0:T(8,128)(2,1)S(1)}, bf16[2,512,512]{2,1,0:T(8,128)(2,1)}, u32[]{:S(2)}) copy-start(bf16[2,512,512]{2,1,0:T(8,128)(2,1)} %radiate_ref.2) | copy-start | bytes 3145732
  0.6 14.7 %copy-start.2 = (bf16[2,512,512]{2,1,0:T(8,128)(2,1)S(1)}, bf16[2,512,512]{2,1,0:T(8,128)(2,1)}, u32[]{:S(2)}) copy-start(bf16[2,512,512]{2,1,0:T(8,128)(2,1)} %receive_ref.4) | copy-start | bytes 3145732
  0.7 14.7 %copy-start.7 = (s32[2,512]{1,0:T(2,128)S(1)}, s32[2,512]{1,0:T(2,128)}, u32[]{:S(2)}) copy-start(s32[2,512]{1,0:T(2,128)} %lit_ref.1) | copy-start | bytes 12292
  1.8 13.5 %collective-permute-start = (bf16[272,512]{1,0:T(8,128)(2,1)S(1)}, bf16[272,512]{1,0:T(8,128)(2,1)S(1)}, u32[]{:S(2)}, u32[]{:S(2)}) collective-permute-start(bf16[272,512]{1,0:T(8,128)(2,1)S(1)} %packed.1), channel_id=1, source_target_pairs={{4,8},{8,4},{12,16},{16,12},{20,24},{24,20},{28,32},{32,28},{36,40... | collective-permute-start | bytes 835592 | tf_op jit(solution)/shard_map/ppermute | solution.py:303
  9.3 6.0 %collective-permute-start.1 = (bf16[272,512]{1,0:T(8,128)(2,1)S(1)}, bf16[272,512]{1,0:T(8,128)(2,1)S(1)}, u32[]{:S(2)}, u32[]{:S(2)}) collective-permute-start(bf16[272,512]{1,0:T(8,128)(2,1)S(1)} %packed.1), channel_id=1, source_target_pairs={{0,4},{4,0},{8,12},{12,8},{16,20},{20,16},{24,28},{28,24},{32,36},... | collective-permute-start | bytes 835592 | tf_op jit(solution)/shard_map/ppermute | solution.py:299
  18.4 7.3 %collective-permute-start.2 = (bf16[512,128]{1,0:T(8,128)(2,1)S(1)}, bf16[512,128]{1,0:T(8,128)(2,1)S(1)}, u32[]{:S(2)}, u32[]{:S(2)}) collective-permute-start(bf16[512,128]{1,0:T(8,128)(2,1)S(1)} %get-tuple-element.26), channel_id=1, source_target_pairs={{0,1},{1,2},{2,3},{3,0},{4,5},{5,6},{6,7},{7,4},{8,9},{9,10},{10,1... | collective-permute-start | bytes 393224 | tf_op jit(solution)/shard_map/ppermute | solution.py:295
  20.0 14.2 %copy-start.5 = (s32[8,256]{1,0:T(8,128)S(1)}, s32[8,256]{1,0:T(8,128)}, u32[]{:S(2)}) copy-start(s32[8,256]{1,0:T(8,128)} %src_ref.1) | copy-start | bytes 24580
  20.0 14.2 %copy-start.6 = (f32[8,256]{1,0:T(8,128)S(1)}, f32[8,256]{1,0:T(8,128)}, u32[]{:S(2)}) copy-start(f32[8,256]{1,0:T(8,128)} %weight_ref.1) | copy-start | bytes 24580
  20.9 18.8 %copy-start = (bf16[2,512,512]{2,1,0:T(8,128)(2,1)S(1)}, bf16[2,512,512]{2,1,0:T(8,128)(2,1)}, u32[]{:S(2)}) copy-start(bf16[2,512,512]{2,1,0:T(8,128)(2,1)} %refs_1_.3) | copy-start | bytes 3145732
  20.9 18.8 %copy-start.3 = (bf16[2,512,512]{2,1,0:T(8,128)(2,1)S(1)}, bf16[2,512,512]{2,1,0:T(8,128)(2,1)}, u32[]{:S(2)}) copy-start(bf16[2,512,512]{2,1,0:T(8,128)(2,1)} %radiate_ref.3) | copy-start | bytes 3145732
  21.0 7.8 %collective-permute-start.3 = (bf16[512,128]{1,0:T(8,128)(2,1)S(1)}, bf16[512,128]{1,0:T(8,128)(2,1)S(1)}, u32[]{:S(2)}, u32[]{:S(2)}) collective-permute-start(bf16[512,128]{1,0:T(8,128)(2,1)S(1)} %get-tuple-element.29), channel_id=1, source_target_pairs={{0,3},{1,0},{2,1},{3,2},{4,7},{5,4},{6,5},{7,6},{8,11},{9,8},{10,9... | collective-permute-start | bytes 393224 | tf_op jit(solution)/shard_map/ppermute | solution.py:295
  22.7 6.9 %collective-permute-start.4 = (bf16[512,128]{1,0:T(8,128)(2,1)S(1)}, bf16[512,128]{1,0:T(8,128)(2,1)S(1)}, u32[]{:S(2)}, u32[]{:S(2)}) collective-permute-start(bf16[512,128]{1,0:T(8,128)(2,1)S(1)} %get-tuple-element.30), channel_id=1, source_target_pairs={{0,2},{1,3},{2,0},{3,1},{4,6},{5,7},{6,4},{7,5},{8,10},{9,11},{10,... | collective-permute-start | bytes 393224 | tf_op jit(solution)/shard_map/ppermute | solution.py:295
  29.7 12.0 %copy-start.4 = (bf16[512,128]{1,0:T(8,128)(2,1)}, bf16[512,128]{1,0:T(8,128)(2,1)S(1)}, u32[]{:S(2)}) copy-start(bf16[512,128]{1,0:T(8,128)(2,1)S(1)} %add_convert_fusion.p0_ref) | copy-start | bytes 393220
  29.7 6.8 %collective-permute-start.5 = (bf16[512,128]{1,0:T(8,128)(2,1)S(1)}, bf16[512,128]{1,0:T(8,128)(2,1)S(1)}, u32[]{:S(2)}, u32[]{:S(2)}) collective-permute-start(bf16[512,128]{1,0:T(8,128)(2,1)S(1)} %add_convert_fusion.p0_ref), channel_id=1, source_target_pairs={{0,1},{1,2},{2,3},{3,0},{4,5},{5,6},{6,7},{7,4},{8,9},{9,10},{10,1... | collective-permute-start | bytes 393224 | tf_op jit(solution)/shard_map/ppermute | solution.py:295
  31.9 5.9 %collective-permute-start.6 = (bf16[512,128]{1,0:T(8,128)(2,1)S(1)}, bf16[512,128]{1,0:T(8,128)(2,1)S(1)}, u32[]{:S(2)}, u32[]{:S(2)}) collective-permute-start(bf16[512,128]{1,0:T(8,128)(2,1)S(1)} %add_convert_fusion.p0_ref), channel_id=1, source_target_pairs={{0,3},{1,0},{2,1},{3,2},{4,7},{5,4},{6,5},{7,6},{8,11},{9,8},{10,9... | collective-permute-start | bytes 393224 | tf_op jit(solution)/shard_map/ppermute | solution.py:295
  33.0 6.8 %collective-permute-start.7 = (bf16[512,128]{1,0:T(8,128)(2,1)S(1)}, bf16[512,128]{1,0:T(8,128)(2,1)S(1)}, u32[]{:S(2)}, u32[]{:S(2)}) collective-permute-start(bf16[512,128]{1,0:T(8,128)(2,1)S(1)} %add_convert_fusion.p0_ref), channel_id=1, source_target_pairs={{0,2},{1,3},{2,0},{3,1},{4,6},{5,7},{6,4},{7,5},{8,10},{9,11},{10,... | collective-permute-start | bytes 393224 | tf_op jit(solution)/shard_map/ppermute | solution.py:295
  41.7 9.8 %collective-permute-start.9 = (bf16[4,256,128]{2,1,0:T(8,128)(2,1)S(1)}, bf16[4,256,128]{2,1,0:T(8,128)(2,1)S(1)}, u32[]{:S(2)}, u32[]{:S(2)}) collective-permute-start(bf16[4,256,128]{2,1,0:T(8,128)(2,1)S(1)} %get-tuple-element.32), channel_id=1, source_target_pairs={{4,8},{8,4},{12,16},{16,12},{20,24},{24,20},{28,32},{32,28},{36,40... | collective-permute-start | bytes 786440 | tf_op jit(solution)/shard_map/ppermute | solution.py:303
  45.3 6.3 %collective-permute-start.8 = (bf16[4,256,128]{2,1,0:T(8,128)(2,1)S(1)}, bf16[4,256,128]{2,1,0:T(8,128)(2,1)S(1)}, u32[]{:S(2)}, u32[]{:S(2)}) collective-permute-start(bf16[4,256,128]{2,1,0:T(8,128)(2,1)S(1)} %tested_even.1), channel_id=1, source_target_pairs={{0,4},{4,0},{8,12},{12,8},{16,20},{20,16},{24,28},{28,24},{32,36},... | collective-permute-start | bytes 786440 | tf_op jit(solution)/shard_map/ppermute | solution.py:299
  51.6 5.6 %collective-permute-start.10 = (bf16[256,128]{1,0:T(8,128)(2,1)S(1)}, bf16[256,128]{1,0:T(8,128)(2,1)S(1)}, u32[]{:S(2)}, u32[]{:S(2)}) collective-permute-start(bf16[256,128]{1,0:T(8,128)(2,1)S(1)} %get-tuple-element.35), channel_id=1, source_target_pairs={{0,1},{1,2},{2,3},{3,0},{4,5},{5,6},{6,7},{7,4},{8,9},{9,10},{10,1... | collective-permute-start | bytes 196616 | tf_op jit(solution)/shard_map/ppermute | solution.py:295
  53.0 5.8 %collective-permute-start.11 = (bf16[256,128]{1,0:T(8,128)(2,1)S(1)}, bf16[256,128]{1,0:T(8,128)(2,1)S(1)}, u32[]{:S(2)}, u32[]{:S(2)}) collective-permute-start(bf16[256,128]{1,0:T(8,128)(2,1)S(1)} %get-tuple-element.36), channel_id=1, source_target_pairs={{0,2},{1,3},{2,0},{3,1},{4,6},{5,7},{6,4},{7,5},{8,10},{9,11},{10,... | collective-permute-start | bytes 196616 | tf_op jit(solution)/shard_map/ppermute | solution.py:295
  55.3 4.3 %collective-permute-start.12 = (bf16[256,128]{1,0:T(8,128)(2,1)S(1)}, bf16[256,128]{1,0:T(8,128)(2,1)S(1)}, u32[]{:S(2)}, u32[]{:S(2)}) collective-permute-start(bf16[256,128]{1,0:T(8,128)(2,1)S(1)} %get-tuple-element.37), channel_id=1, source_target_pairs={{0,3},{1,0},{2,1},{3,2},{4,7},{5,4},{6,5},{7,6},{8,11},{9,8},{10,9... | collective-permute-start | bytes 196616 | tf_op jit(solution)/shard_map/ppermute | solution.py:295

commit v7 on v4

--- a/solution.py
+++ b/solution.py
@@ -35,11 +35,20 @@
 
 
 def hot(src_col, w_col, first, width):
-    lanes = lax.broadcasted_iota(jnp.int32, (src_col.shape[0], width), 1) + first
-    total = jnp.zeros((src_col.shape[0], width), F32)
-    for slot in range(src_col.shape[1]):
-        total = total + jnp.where(lanes == src_col[:, slot : slot + 1], w_col[:, slot : slot + 1], 0.0)
-    return total.astype(BF)
+    rows, slots = src_col.shape
+    shape = (rows, 128)
+    lanes = (lax.broadcasted_iota(jnp.int32, shape, 1) + first).astype(jnp.int16)
+    sources = [jnp.broadcast_to(src_col[:, i : i + 1], shape).astype(jnp.int16) for i in range(slots)]
+    weights = [jnp.broadcast_to(w_col[:, i : i + 1], shape).astype(BF) for i in range(slots)]
+    zero = jnp.zeros(shape, BF)
+    parts = []
+    for low in range(0, width, 128):
+        here = lanes + jnp.int16(low)
+        terms = [jnp.where(here == source, weight, zero) for source, weight in zip(sources, weights)]
+        while len(terms) > 1:
+            terms = [a + b for a, b in zip(terms[::2], terms[1::2])] + terms[len(terms) // 2 * 2 :]
+        parts.append(terms[0])
+    return jnp.concatenate(parts, axis=1)
 
 
 def fill(pick_ref, at, low, high, src_col, w_col):
@@ -52,18 +61,28 @@
             pick_ref[at, a:b] = jnp.zeros((at.stop - at.start, b - a), BF)
 
 
+def split(value):
+    first = value.astype(BF)
+    rest = value - first.astype(F32)
+    second = rest.astype(BF)
+    return first, second, (rest - second.astype(F32)).astype(BF)
+
+
 def trig(center, dirs_ref, cos_ref, sin_ref):
     rows = center.shape[1]
-    columns = jnp.concatenate([center, jnp.zeros((5, rows), F32)], axis=0).T
+    pad = jnp.zeros((5, rows), F32)
+    a, b, c = (part.astype(F32) for part in split(jnp.concatenate([center, pad], axis=0)))
+    left = jnp.concatenate([a, a, b, b, a, c], axis=0).T.astype(BF)
     step = 64
-    for c in range(dirs_ref.shape[1]):
-        waves = [dirs_ref[i, c : c + 1] * (0.5 / math.pi) for i in range(3)]
+    for cone in range(dirs_ref.shape[1]):
+        waves = jnp.concatenate([dirs_ref[i, cone : cone + 1] for i in range(3)], axis=0) * (0.5 / math.pi)
+        waves = jnp.concatenate([waves, jnp.zeros((5, waves.shape[1]), F32)], axis=0)
+        d, e, f = (part.astype(F32) for part in split(waves))
+        right = jnp.concatenate([d, e, d, e, f, d], axis=0).astype(BF)
         for r in range(0, rows, step):
-            part = columns[r : r + step]
-            turns = part[:, 0:1] * waves[0] + part[:, 1:2] * waves[1] + part[:, 2:3] * waves[2]
-            cosine, sine = turn(turns)
-            cos_ref[c, r : r + step] = cosine
-            sin_ref[c, r : r + step] = sine
+            cosine, sine = turn(mm(left[r : r + step], right))
+            cos_ref[cone, r : r + step] = cosine
+            sin_ref[cone, r : r + step] = sine
 
 
 def rotated(value, cosine, sine, orient):
@@ -140,14 +159,15 @@
     cone = lax.axis_index("cone")
     count = lax.axis_size("cone")
     box = lax.axis_index("box")
-    m = even_ref.shape[0]
+    m = wave_ref.shape[0]
     q, share = first_ref.shape
     cones, _, k2 = radiate_ref.shape
     k = k2 // 2
-    table[m : 2 * m] = wave_ref[...]
+    side = lax.rem(box, 2) * 2 * m
     for at in tiles(m):
-        for rows_ref, after in ((even_ref, 1 - lax.rem(box, 2)), (odd_ref, lax.rem(box, 2))):
-            radiated(rows_ref, at, radiate_ref, mom_cos, mom_sin, table, after * 2 * m, after * 2 * m)
+        table[rows_at(m, at)] = wave_ref[at]
+        radiated(even_ref, at, radiate_ref, mom_cos, mom_sin, table, 2 * m - side, 2 * m - side)
+        radiated(odd_ref, at, radiate_ref, mom_cos, mom_sin, table, side, side)
     lit_col = jnp.concatenate([lit_ref[...].astype(F32), jnp.zeros((8 - cones, q), F32)], axis=0).T
     columns = pl.ds(pl.multiple_of(lax.rem(cone + 1, count) * share, share), share)
     for at in tiles(q):
@@ -244,13 +264,16 @@
     tested(1, *refs)
 
 
-def merged(even_ref, odd_ref, own_ref, *outs):
+def added(new_ref, own_ref, out_ref):
+    out_ref[...] = own_ref[...] + new_ref[...].astype(F32)
+
+
+def merged(even_ref, own_ref, *outs):
     for slot, out in enumerate(outs):
-        total = own_ref[slot] + odd_ref[slot].astype(F32) + even_ref[slot].astype(F32)
-        out[...] = total.astype(out.dtype)
-
-
-def call(body, outs, ins, scratch=(), space=pltpu.VMEM, vmem=24):
+        out[...] = (own_ref[slot] + even_ref[slot].astype(F32)).astype(out.dtype)
+
+
+def call(body, outs, ins, scratch=(), space=pltpu.VMEM, vmem=24, flops=1):
     if space is pltpu.HBM:
         ins = [pltpu.with_memory_space_constraint(value, space) for value in ins]
     return pl.pallas_call(
@@ -260,7 +283,7 @@
         out_specs=jax.tree.map(lambda _: pl.BlockSpec(memory_space=pltpu.VMEM), outs),
         scratch_shapes=list(scratch),
         compiler_params=pltpu.CompilerParams(vmem_limit_bytes=vmem * MIB),
-        cost_estimate=pl.CostEstimate(flops=1, bytes_accessed=1, transcendentals=0),
+        cost_estimate=pl.CostEstimate(flops=flops, bytes_accessed=1, transcendentals=0),
         name=body.__name__,
     )(*ins)
 
@@ -324,9 +347,9 @@
     own, entries = lax.optimization_barrier((own, entries))
     odd_list = swapped_odd(entries)
     even_list = swapped_even(entries)
-    s1, even_list, odd_list = lax.optimization_barrier((s1, even_list, odd_list))
-    back = call(lists, shape((3 * m, q), BF), (even_list, entries, odd_list))
-    po_share = (own + s1.astype(F32) + s2.astype(F32) + s3.astype(F32)).astype(BF)
+    back = call(lists, shape((3 * m, q), BF), (even_list, entries, odd_list), flops=4_000_000_000)
+    own = call(added, shape((q, share), F32), (s1, own))
+    po_share = (own + s3.astype(F32) + s2.astype(F32)).astype(BF)
     p2 = turned(po_share, 2)
     p1 = turned(po_share, 1)
     p3 = turned(po_share, 3)
@@ -342,10 +365,11 @@
     from_even = swapped_even(for_even)
     for_even, own_waves = lax.optimization_barrier((for_even, waves))
     field = call(tested_own, shape((count, m, share), F32), (own_waves,) + rest)
+    field = call(added, shape((count, m, share), F32), (from_odd, field))
     f0, f1, f2, f3 = call(
         merged,
         (shape((m, share), F32),) + (shape((m, share), BF),) * 3,
-        (from_even, from_odd, field),
+        (from_even, field),
     )
     f2 = turned(f2, 2)
     f1 = turned(f1, 1)

time: 62.6 us -> 58.6 us (0.936)
  waiting for transfers between devices: 17 us -> 12.1 us
  starting transfers between devices: 26.9 us -> 29 us
  Pallas kernels: 16.8 us -> 15.5 us
    ppermute x3, waiting for transfers between devices: 9.33 us -> 3.99 us  [swapped_odd(): lax.ppermute(value, 'box', [(i, (i + 1 ^ 1) - 1) for i in range(1, lax.ax...]
    pallas_call x8 -> x10, Pallas kernels: 16.8 us -> 15.5 us  [call(): pl.pallas_call(body, out_shape=outs, in_specs=[pl.BlockSpec(memory_space=...]
    ppermute x9, starting transfers between devices: 12.8 us -> 13.9 us  [turned(): lax.ppermute(value, 'cone', [(i, (i + shift) % count) for i in range(coun...]
    ppermute x3, starting transfers between devices: 13.9 us -> 14.9 us  [swapped_odd(): lax.ppermute(value, 'box', [(i, (i + 1 ^ 1) - 1) for i in range(1, lax.ax...]
  transfers between devices with their start and end apart: 15 -> 15, of which waited for: 6 -> 7; matrix products, arithmetic and copies ran while one was open for 0% -> 0% of each run, Pallas kernels for 17% -> 18%
where the time goes in v7:
time: 58.6 us; the launch traced here: 58.3 us
  starting transfers between devices  29 us (49%)
  Pallas kernels  15.5 us (26%)
  waiting for transfers between devices  12.1 us (21%)
  between operations  0.89 us (2%)
  other arithmetic  0.73 us (1%)
    pallas_call x10, Pallas kernels, call(): pl.pallas_call(body, out_shape=outs, in_specs=[pl.BlockSpec(memory_space=...  15.5 us
    ppermute x3, starting transfers between devices, swapped_odd(): lax.ppermute(value, 'box', [(i, (i + 1 ^ 1) - 1) for i in range(1, lax.ax...  14.9 us
    ppermute x9, starting transfers between devices, turned(): lax.ppermute(value, 'cone', [(i, (i + shift) % count) for i in range(coun...  13.9 us
    ppermute x9, waiting for transfers between devices, turned(): lax.ppermute(value, 'cone', [(i, (i + shift) % count) for i in range(coun...  8.14 us
    ppermute x3, waiting for transfers between devices, swapped_odd(): lax.ppermute(value, 'box', [(i, (i + 1 ^ 1) - 1) for i in range(1, lax.ax...  3.99 us
  transfers between devices with their start and end apart: 15, of which 7 were waited for; matrix products, arithmetic and copies ran while one was open for 0% of the time, Pallas kernels for 18%

profile of v7, /device:TPU:6, one launch (start us, length us, event | category | flops | bytes accessed | tf_op | source)
XLA Modules:
  0.0 58.3 jit_solution(7277957201655185255)
XLA Ops:
  0.6 0.0 copy-start.1
  0.6 0.0 copy-start.2
  0.7 0.0 copy-start.5
  0.7 7.6 %collective-permute-start = (bf16[256,512]{1,0:T(8,128)(2,1)}, bf16[256,512]{1,0:T(8,128)(2,1)S(1)}, u32[]{:S(2)}, u32[]{:S(2)}) collective-permute-start(bf16[256,512]{1,0:T(8,128)(2,1)} %current_hbm.1), channel_id=1, source_target_pairs={{4,8},{8,4},{12,16},{16,12},{20,24},{24,20},{28,32},{32,28},{36,40... | collective-permute-start | bytes 786440 | tf_op jit(solution)/shard_map/ppermute | solution.py:301
  8.3 0.1 collective-permute-start.1
  8.4 5.0 %prepare.1 = (f32[2,768,256]{2,1,0:T(8,128)S(1)}, f32[2,768,256]{2,1,0:T(8,128)S(1)}, f32[2,512,256]{2,1,0:T(8,128)S(1)}, f32[2,512,256]{2,1,0:T(8,128)S(1)}, bf...) custom-call(bf16[256,512]{1,0:T(8,128)(2,1)} %current_hbm.1, ...), custom_call_target="tpu_custom_call" | custom-call | flops 1 | bytes 1 | tf_op jit(solution)/shard_map/prepare/pallas_call | solution.py:279
  13.4 0.0 collective-permute-done.odd_ref
  13.4 0.0 collective-permute-done.1.even_ref
  13.4 0.0 copy-done.1
  13.4 0.0 copy-done.2
  13.4 0.0 copy-done.5
  13.4 3.0 %incident.1 = (bf16[512,128]{1,0:T(8,128)(2,1)S(1)}, bf16[512,1024]{1,0:T(8,128)(2,1)S(1)}) custom-call(bf16[256,512]{1,0:T(8,128)(2,1)S(1)} %collective-permute-done.odd_ref, bf16[256,512]{1,0:T(8,128)(2,1)S(1)} %collective-permute-done.1.even_ref, bf16[256,1024]{1,0:T(8,128)(2,1)S(1)} %get-tuple-element.23.wave_ref, ...), custom_call_target="tpu_custom_call" | custom-call | flops 1 | bytes 1 | tf_op jit(solution)/shard_map/incident/pallas_call | solution.py:279
  16.5 1.7 %collective-permute-start.2 = (bf16[512,128]{1,0:T(8,128)(2,1)S(1)}, bf16[512,128]{1,0:T(8,128)(2,1)S(1)}, u32[]{:S(2)}, u32[]{:S(2)}) collective-permute-start(bf16[512,128]{1,0:T(8,128)(2,1)S(1)} %get-tuple-element.29), channel_id=1, source_target_pairs={{0,1},{1,2},{2,3},{3,0},{4,5},{5,6},{6,7},{7,4},{8,9},{9,10},{10,1... | collective-permute-start | bytes 393224 | tf_op jit(solution)/shard_map/ppermute | solution.py:293
  18.1 0.9 %received.1 = (f32[512,128]{1,0:T(8,128)S(1)}, bf16[512,128]{1,0:T(8,128)(2,1)S(1)}, bf16[512,128]{1,0:T(8,128)(2,1)S(1)}) custom-call(bf16[512,1024]{1,0:T(8,128)(2,1)S(1)} %get-tuple-element.30.po_lit_ref, bf16[2,512,512]{2,1,0:T(8,128)(2,1)S(1)} %copy-done.2), custom_call_target="tpu_custom_call" | custom-call | flops 1 | bytes 1 | tf_op jit(solution)/shard_map/received/pallas_call | solution.py:279
  19.0 1.7 %collective-permute-start.3 = (bf16[512,128]{1,0:T(8,128)(2,1)S(1)}, bf16[512,128]{1,0:T(8,128)(2,1)S(1)}, u32[]{:S(2)}, u32[]{:S(2)}) collective-permute-start(bf16[512,128]{1,0:T(8,128)(2,1)S(1)} %get-tuple-element.34), channel_id=1, source_target_pairs={{0,3},{1,0},{2,1},{3,2},{4,7},{5,4},{6,5},{7,6},{8,11},{9,8},{10,9... | collective-permute-start | bytes 393224 | tf_op jit(solution)/shard_map/ppermute | solution.py:293
  20.8 2.0 %collective-permute-start.4 = (bf16[512,128]{1,0:T(8,128)(2,1)S(1)}, bf16[512,128]{1,0:T(8,128)(2,1)S(1)}, u32[]{:S(2)}, u32[]{:S(2)}) collective-permute-start(bf16[512,128]{1,0:T(8,128)(2,1)S(1)} %get-tuple-element.35), channel_id=1, source_target_pairs={{0,2},{1,3},{2,0},{3,1},{4,6},{5,7},{6,4},{7,5},{8,10},{9,11},{10,... | collective-permute-start | bytes 393224 | tf_op jit(solution)/shard_map/ppermute | solution.py:293
  22.8 4.0 %collective-permute-start.9 = (f32[16,256]{1,0:T(8,128)S(1)}, f32[16,256]{1,0:T(8,128)S(1)}, u32[]{:S(2)}, u32[]{:S(2)}) collective-permute-start(f32[16,256]{1,0:T(8,128)S(1)} %get-tuple-element.36.own_ref), channel_id=1, source_target_pairs={{4,8},{8,4},{12,16},{16,12},{20,24},{24,20},{28,32},{32,28},{36,40... | collective-permute-start | bytes 49160 | tf_op jit(solution)/shard_map/ppermute | solution.py:301
  26.8 0.1 collective-permute-start.8
  26.9 0.0 collective-permute-done.2.new_ref
  26.9 0.0 collective-permute-done.3
  26.9 0.8 %collective-permute-done.4 = bf16[512,128]{1,0:T(8,128)(2,1)S(1)} collective-permute-done((bf16[512,128]{1,0:T(8,128)(2,1)S(1)}, bf16[512,128]{1,0:T(8,128)(2,1)S(1)}, u32[]{:S(2)}, u32[]{:S(2)}) %collective-permute-start.4) | collective-permute-done | bytes 131104 | tf_op jit(solution)/shard_map/ppermute | solution.py:293
  27.7 0.0 copy-start.4
  27.7 0.0 copy-start
  27.8 0.0 copy-start.3
  27.8 2.2 %collective-permute-start.7 = (bf16[512,128]{1,0:T(8,128)(2,1)S(1)}, bf16[512,128]{1,0:T(8,128)(2,1)S(1)}, u32[]{:S(2)}, u32[]{:S(2)}) collective-permute-start(bf16[512,128]{1,0:T(8,128)(2,1)S(1)} %add_convert_fusion.p0_ref), channel_id=1, source_target_pairs={{0,1},{1,2},{2,3},{3,0},{4,5},{5,6},{6,7},{7,4},{8,9},{9,10},{10,1... | collective-permute-start | bytes 393224 | tf_op jit(solution)/shard_map/ppermute | solution.py:293
  30.0 1.1 %collective-permute-start.6 = (bf16[512,128]{1,0:T(8,128)(2,1)S(1)}, bf16[512,128]{1,0:T(8,128)(2,1)S(1)}, u32[]{:S(2)}, u32[]{:S(2)}) collective-permute-start(bf16[512,128]{1,0:T(8,128)(2,1)S(1)} %add_convert_fusion.p0_ref), channel_id=1, source_target_pairs={{0,3},{1,0},{2,1},{3,2},{4,7},{5,4},{6,5},{7,6},{8,11},{9,8},{10,9... | collective-permute-start | bytes 393224 | tf_op jit(solution)/shard_map/ppermute | solution.py:293
  31.1 1.0 %collective-permute-start.5 = (bf16[512,128]{1,0:T(8,128)(2,1)S(1)}, bf16[512,128]{1,0:T(8,128)(2,1)S(1)}, u32[]{:S(2)}, u32[]{:S(2)}) collective-permute-start(bf16[512,128]{1,0:T(8,128)(2,1)S(1)} %add_convert_fusion.p0_ref), channel_id=1, source_target_pairs={{0,2},{1,3},{2,0},{3,1},{4,6},{5,7},{6,4},{7,5},{8,10},{9,11},{10,... | collective-permute-start | bytes 393224 | tf_op jit(solution)/shard_map/ppermute | solution.py:293
  32.1 0.0 collective-permute-done.9.odd_ref
  32.1 0.0 collective-permute-done.8.even_ref
  32.1 2.1 %lists.1.pick_ref.refs_2_ = bf16[768,512]{1,0:T(8,128)(2,1)S(1)} custom-call(f32[16,256]{1,0:T(8,128)S(1)} %collective-permute-done.8.even_ref, f32[16,256]{1,0:T(8,128)S(1)} %get-tuple-element.36.own_ref, f32[16,256]{1,0:T(8,128)S(1)} %collective-permute-done.9.odd_ref), custom_call_target="tpu_custom_call" | custom-call | flops 4000000000 | bytes 1 | tf_op jit(solution)/shard_map/lists/pallas_call | solution.py:279
  34.2 0.0 collective-permute-done.7.p1_ref
  34.3 1.6 %collective-permute-done.6.p3_ref = bf16[512,128]{1,0:T(8,128)(2,1)S(1)} collective-permute-done((bf16[512,128]{1,0:T(8,128)(2,1)S(1)}, bf16[512,128]{1,0:T(8,128)(2,1)S(1)}, u32[]{:S(2)}, u32[]{:S(2)}) %collective-permute-start.6) | collective-permute-done | bytes 131104 | tf_op jit(solution)/shard_map/ppermute | solution.py:293
  35.9 1.9 %collective-permute-done.5.p2_ref = bf16[512,128]{1,0:T(8,128)(2,1)S(1)} collective-permute-done((bf16[512,128]{1,0:T(8,128)(2,1)S(1)}, bf16[512,128]{1,0:T(8,128)(2,1)S(1)}, u32[]{:S(2)}, u32[]{:S(2)}) %collective-permute-start.5) | collective-permute-done | bytes 131104 | tf_op jit(solution)/shard_map/ppermute | solution.py:293
  37.8 0.0 copy-done.4
  37.8 1.9 %scattered.1 = (bf16[512,1024]{1,0:T(8,128)(2,1)S(1)}, bf16[4,256,128]{2,1,0:T(8,128)(2,1)S(1)}) custom-call(bf16[512,128]{1,0:T(8,128)(2,1)S(1)} %add_convert_fusion.p0_ref, bf16[512,128]{1,0:T(8,128)(2,1)S(1)} %collective-permute-done.5.p2_ref, bf16[512,128]{1,0:T(8,128)(2,1)S(1)} %collective-permute-done.6.p3_ref, ...), custom_call_target="tpu_custom_call" | custom-call | flops 1 | bytes 1 | tf_op jit(solution)/shard_map/scattered/pallas_call | solution.py:279
  39.8 3.2 %collective-permute-start.11 = (bf16[4,256,128]{2,1,0:T(8,128)(2,1)S(1)}, bf16[4,256,128]{2,1,0:T(8,128)(2,1)S(1)}, u32[]{:S(2)}, u32[]{:S(2)}) collective-permute-start(bf16[4,256,128]{2,1,0:T(8,128)(2,1)S(1)} %get-tuple-element.38), channel_id=1, source_target_pairs={{4,8},{8,4},{12,16},{16,12},{20,24},{24,20},{28,32},{32,28},{36,40... | collective-permute-start | bytes 786440 | tf_op jit(solution)/shard_map/ppermute | solution.py:301
  43.0 1.2 %tested_even.1 = bf16[4,256,128]{2,1,0:T(8,128)(2,1)S(1)} custom-call(bf16[512,1024]{1,0:T(8,128)(2,1)S(1)} %get-tuple-element.39.refs_0_, bf16[2,512,512]{2,1,0:T(8,128)(2,1)S(1)} %copy-done, bf16[768,512]{1,0:T(8,128)(2,1)S(1)} %lists.1.pick_ref.refs_2_, f32[2,768,256]{2,1,0:T(8,128)S(1)} %get-tuple-element.25.mom_cos.refs_3_, ...), custom_call_target="tpu_custom_call" | custom-call | flops 1 | bytes 1 | tf_op jit(solution)/shard_map/tested_even/pallas_call | solution.py:279
  44.2 0.1 collective-permute-start.10
  44.3 1.2 %tested_own.1.own_ref = f32[4,256,128]{2,1,0:T(8,128)S(1)} custom-call(bf16[512,1024]{1,0:T(8,128)(2,1)S(1)} %get-tuple-element.39.refs_0_, bf16[2,512,512]{2,1,0:T(8,128)(2,1)S(1)} %copy-done, bf16[768,512]{1,0:T(8,128)(2,1)S(1)} %lists.1.pick_ref.refs_2_, f32[2,768,256]{2,1,0:T(8,128)S(1)} %get-tuple-element.25.mom_cos.refs_3_, ...), custom_call_target="tpu_custom_call" | custom-call | flops 1 | bytes 1 | tf_op jit(solution)/shard_map/tested_own/pallas_call | solution.py:279
  45.6 4.0 %collective-permute-done.11.new_ref = bf16[4,256,128]{2,1,0:T(8,128)(2,1)S(1)} collective-permute-done((bf16[4,256,128]{2,1,0:T(8,128)(2,1)S(1)}, bf16[4,256,128]{2,1,0:T(8,128)(2,1)S(1)}, u32[]{:S(2)}, u32[]{:S(2)}) %collective-permute-start.11) | collective-permute-done | bytes 262176 | tf_op jit(solution)/shard_map/ppermute | solution.py:301
  49.6 0.0 collective-permute-done.10.even_ref
  49.7 1.4 %collective-permute-start.12 = (bf16[256,128]{1,0:T(8,128)(2,1)S(1)}, bf16[256,128]{1,0:T(8,128)(2,1)S(1)}, u32[]{:S(2)}, u32[]{:S(2)}) collective-permute-start(bf16[256,128]{1,0:T(8,128)(2,1)S(1)} %get-tuple-element.41), channel_id=1, source_target_pairs={{0,1},{1,2},{2,3},{3,0},{4,5},{5,6},{6,7},{7,4},{8,9},{9,10},{10,1... | collective-permute-start | bytes 196616 | tf_op jit(solution)/shard_map/ppermute | solution.py:293
  51.1 2.3 %collective-permute-start.13 = (bf16[256,128]{1,0:T(8,128)(2,1)S(1)}, bf16[256,128]{1,0:T(8,128)(2,1)S(1)}, u32[]{:S(2)}, u32[]{:S(2)}) collective-permute-start(bf16[256,128]{1,0:T(8,128)(2,1)S(1)} %get-tuple-element.42), channel_id=1, source_target_pairs={{0,2},{1,3},{2,0},{3,1},{4,6},{5,7},{6,4},{7,5},{8,10},{9,11},{10,... | collective-permute-start | bytes 196616 | tf_op jit(solution)/shard_map/ppermute | solution.py:293
  53.4 0.5 collective-permute-start.14
  53.8 1.4 %collective-permute-done.12 = bf16[256,128]{1,0:T(8,128)(2,1)S(1)} collective-permute-done((bf16[256,128]{1,0:T(8,128)(2,1)S(1)}, bf16[256,128]{1,0:T(8,128)(2,1)S(1)}, u32[]{:S(2)}, u32[]{:S(2)}) %collective-permute-start.12) | collective-permute-done | bytes 65568 | tf_op jit(solution)/shard_map/ppermute | solution.py:293
  55.2 1.6 %collective-permute-done.13 = bf16[256,128]{1,0:T(8,128)(2,1)S(1)} collective-permute-done((bf16[256,128]{1,0:T(8,128)(2,1)S(1)}, bf16[256,128]{1,0:T(8,128)(2,1)S(1)}, u32[]{:S(2)}, u32[]{:S(2)}) %collective-permute-start.13) | collective-permute-done | bytes 65568 | tf_op jit(solution)/shard_map/ppermute | solution.py:293
  56.8 0.8 %collective-permute-done.14 = bf16[256,128]{1,0:T(8,128)(2,1)S(1)} collective-permute-done((bf16[256,128]{1,0:T(8,128)(2,1)S(1)}, bf16[256,128]{1,0:T(8,128)(2,1)S(1)}, u32[]{:S(2)}, u32[]{:S(2)}) %collective-permute-start.14) | collective-permute-done | bytes 65568 | tf_op jit(solution)/shard_map/ppermute | solution.py:293
  57.6 0.7 %convert_add_fusion = f32[256,128]{1,0:T(8,128)} fusion(bf16[256,128]{1,0:T(8,128)(2,1)S(1)} %collective-permute-done.14, bf16[256,128]{1,0:T(8,128)(2,1)S(1)} %collective-permute-done.13, f32[256,128]{1,0:T(8,128)S(1)} %get-tuple-element.40, bf16[256,128]{1,0:T(8,128)(2,1)S(1)} %collective-permute-done.12), kind=kLoop, calls=%fused_computation.1 | loop fusion | flops 196608 | bytes 458752 | tf_op jit(solution)/shard_map/add | solution.py:377
  (6 shorter events, 0.2 us)
Async XLA Ops:
  0.6 12.8 %copy-start.1 = (bf16[2,512,512]{2,1,0:T(8,128)(2,1)S(1)}, bf16[2,512,512]{2,1,0:T(8,128)(2,1)}, u32[]{:S(2)}) copy-start(bf16[2,512,512]{2,1,0:T(8,128)(2,1)} %radiate_ref.2) | copy-start | bytes 3145732
  0.6 12.8 %copy-start.2 = (bf16[2,512,512]{2,1,0:T(8,128)(2,1)S(1)}, bf16[2,512,512]{2,1,0:T(8,128)(2,1)}, u32[]{:S(2)}) copy-start(bf16[2,512,512]{2,1,0:T(8,128)(2,1)} %receive_ref.4) | copy-start | bytes 3145732
  0.7 12.8 %copy-start.5 = (s32[2,512]{1,0:T(2,128)S(1)}, s32[2,512]{1,0:T(2,128)}, u32[]{:S(2)}) copy-start(s32[2,512]{1,0:T(2,128)} %lit_ref.1) | copy-start | bytes 12292
  0.7 12.7 %collective-permute-start = (bf16[256,512]{1,0:T(8,128)(2,1)}, bf16[256,512]{1,0:T(8,128)(2,1)S(1)}, u32[]{:S(2)}, u32[]{:S(2)}) collective-permute-start(bf16[256,512]{1,0:T(8,128)(2,1)} %current_hbm.1), channel_id=1, source_target_pairs={{4,8},{8,4},{12,16},{16,12},{20,24},{24,20},{28,32},{32,28},{36,40... | collective-permute-start | bytes 786440 | tf_op jit(solution)/shard_map/ppermute | solution.py:301
  8.3 5.1 %collective-permute-start.1 = (bf16[256,512]{1,0:T(8,128)(2,1)}, bf16[256,512]{1,0:T(8,128)(2,1)S(1)}, u32[]{:S(2)}, u32[]{:S(2)}) collective-permute-start(bf16[256,512]{1,0:T(8,128)(2,1)} %current_hbm.1), channel_id=1, source_target_pairs={{0,4},{4,0},{8,12},{12,8},{16,20},{20,16},{24,28},{28,24},{32,36},... | collective-permute-start | bytes 786440 | tf_op jit(solution)/shard_map/ppermute | solution.py:297
  16.5 10.4 %collective-permute-start.2 = (bf16[512,128]{1,0:T(8,128)(2,1)S(1)}, bf16[512,128]{1,0:T(8,128)(2,1)S(1)}, u32[]{:S(2)}, u32[]{:S(2)}) collective-permute-start(bf16[512,128]{1,0:T(8,128)(2,1)S(1)} %get-tuple-element.29), channel_id=1, source_target_pairs={{0,1},{1,2},{2,3},{3,0},{4,5},{5,6},{6,7},{7,4},{8,9},{9,10},{10,1... | collective-permute-start | bytes 393224 | tf_op jit(solution)/shard_map/ppermute | solution.py:293
  19.0 7.9 %collective-permute-start.3 = (bf16[512,128]{1,0:T(8,128)(2,1)S(1)}, bf16[512,128]{1,0:T(8,128)(2,1)S(1)}, u32[]{:S(2)}, u32[]{:S(2)}) collective-permute-start(bf16[512,128]{1,0:T(8,128)(2,1)S(1)} %get-tuple-element.34), channel_id=1, source_target_pairs={{0,3},{1,0},{2,1},{3,2},{4,7},{5,4},{6,5},{7,6},{8,11},{9,8},{10,9... | collective-permute-start | bytes 393224 | tf_op jit(solution)/shard_map/ppermute | solution.py:293
  20.8 6.9 %collective-permute-start.4 = (bf16[512,128]{1,0:T(8,128)(2,1)S(1)}, bf16[512,128]{1,0:T(8,128)(2,1)S(1)}, u32[]{:S(2)}, u32[]{:S(2)}) collective-permute-start(bf16[512,128]{1,0:T(8,128)(2,1)S(1)} %get-tuple-element.35), channel_id=1, source_target_pairs={{0,2},{1,3},{2,0},{3,1},{4,6},{5,7},{6,4},{7,5},{8,10},{9,11},{10,... | collective-permute-start | bytes 393224 | tf_op jit(solution)/shard_map/ppermute | solution.py:293
  22.8 9.4 %collective-permute-start.9 = (f32[16,256]{1,0:T(8,128)S(1)}, f32[16,256]{1,0:T(8,128)S(1)}, u32[]{:S(2)}, u32[]{:S(2)}) collective-permute-start(f32[16,256]{1,0:T(8,128)S(1)} %get-tuple-element.36.own_ref), channel_id=1, source_target_pairs={{4,8},{8,4},{12,16},{16,12},{20,24},{24,20},{28,32},{32,28},{36,40... | collective-permute-start | bytes 49160 | tf_op jit(solution)/shard_map/ppermute | solution.py:301
  26.8 5.4 %collective-permute-start.8 = (f32[16,256]{1,0:T(8,128)S(1)}, f32[16,256]{1,0:T(8,128)S(1)}, u32[]{:S(2)}, u32[]{:S(2)}) collective-permute-start(f32[16,256]{1,0:T(8,128)S(1)} %get-tuple-element.36.own_ref), channel_id=1, source_target_pairs={{0,4},{4,0},{8,12},{12,8},{16,20},{20,16},{24,28},{28,24},{32,36},... | collective-permute-start | bytes 49160 | tf_op jit(solution)/shard_map/ppermute | solution.py:297
  27.7 10.1 %copy-start.4 = (bf16[512,128]{1,0:T(8,128)(2,1)}, bf16[512,128]{1,0:T(8,128)(2,1)S(1)}, u32[]{:S(2)}) copy-start(bf16[512,128]{1,0:T(8,128)(2,1)S(1)} %add_convert_fusion.p0_ref) | copy-start | bytes 393220
  27.7 10.1 %copy-start = (bf16[2,512,512]{2,1,0:T(8,128)(2,1)S(1)}, bf16[2,512,512]{2,1,0:T(8,128)(2,1)}, u32[]{:S(2)}) copy-start(bf16[2,512,512]{2,1,0:T(8,128)(2,1)} %refs_1_.3) | copy-start | bytes 3145732
  27.8 10.1 %copy-start.3 = (bf16[2,512,512]{2,1,0:T(8,128)(2,1)S(1)}, bf16[2,512,512]{2,1,0:T(8,128)(2,1)}, u32[]{:S(2)}) copy-start(bf16[2,512,512]{2,1,0:T(8,128)(2,1)} %radiate_ref.3) | copy-start | bytes 3145732
  27.8 6.5 %collective-permute-start.7 = (bf16[512,128]{1,0:T(8,128)(2,1)S(1)}, bf16[512,128]{1,0:T(8,128)(2,1)S(1)}, u32[]{:S(2)}, u32[]{:S(2)}) collective-permute-start(bf16[512,128]{1,0:T(8,128)(2,1)S(1)} %add_convert_fusion.p0_ref), channel_id=1, source_target_pairs={{0,1},{1,2},{2,3},{3,0},{4,5},{5,6},{6,7},{7,4},{8,9},{9,10},{10,1... | collective-permute-start | bytes 393224 | tf_op jit(solution)/shard_map/ppermute | solution.py:293
  30.0 5.9 %collective-permute-start.6 = (bf16[512,128]{1,0:T(8,128)(2,1)S(1)}, bf16[512,128]{1,0:T(8,128)(2,1)S(1)}, u32[]{:S(2)}, u32[]{:S(2)}) collective-permute-start(bf16[512,128]{1,0:T(8,128)(2,1)S(1)} %add_convert_fusion.p0_ref), channel_id=1, source_target_pairs={{0,3},{1,0},{2,1},{3,2},{4,7},{5,4},{6,5},{7,6},{8,11},{9,8},{10,9... | collective-permute-start | bytes 393224 | tf_op jit(solution)/shard_map/ppermute | solution.py:293
  31.1 6.7 %collective-permute-start.5 = (bf16[512,128]{1,0:T(8,128)(2,1)S(1)}, bf16[512,128]{1,0:T(8,128)(2,1)S(1)}, u32[]{:S(2)}, u32[]{:S(2)}) collective-permute-start(bf16[512,128]{1,0:T(8,128)(2,1)S(1)} %add_convert_fusion.p0_ref), channel_id=1, source_target_pairs={{0,2},{1,3},{2,0},{3,1},{4,6},{5,7},{6,4},{7,5},{8,10},{9,11},{10,... | collective-permute-start | bytes 393224 | tf_op jit(solution)/shard_map/ppermute | solution.py:293
  39.8 9.8 %collective-permute-start.11 = (bf16[4,256,128]{2,1,0:T(8,128)(2,1)S(1)}, bf16[4,256,128]{2,1,0:T(8,128)(2,1)S(1)}, u32[]{:S(2)}, u32[]{:S(2)}) collective-permute-start(bf16[4,256,128]{2,1,0:T(8,128)(2,1)S(1)} %get-tuple-element.38), channel_id=1, source_target_pairs={{4,8},{8,4},{12,16},{16,12},{20,24},{24,20},{28,32},{32,28},{36,40... | collective-permute-start | bytes 786440 | tf_op jit(solution)/shard_map/ppermute | solution.py:301
  44.2 5.4 %collective-permute-start.10 = (bf16[4,256,128]{2,1,0:T(8,128)(2,1)S(1)}, bf16[4,256,128]{2,1,0:T(8,128)(2,1)S(1)}, u32[]{:S(2)}, u32[]{:S(2)}) collective-permute-start(bf16[4,256,128]{2,1,0:T(8,128)(2,1)S(1)} %tested_even.1), channel_id=1, source_target_pairs={{0,4},{4,0},{8,12},{12,8},{16,20},{20,16},{24,28},{28,24},{32,36},... | collective-permute-start | bytes 786440 | tf_op jit(solution)/shard_map/ppermute | solution.py:297
  49.7 5.6 %collective-permute-start.12 = (bf16[256,128]{1,0:T(8,128)(2,1)S(1)}, bf16[256,128]{1,0:T(8,128)(2,1)S(1)}, u32[]{:S(2)}, u32[]{:S(2)}) collective-permute-start(bf16[256,128]{1,0:T(8,128)(2,1)S(1)} %get-tuple-element.41), channel_id=1, source_target_pairs={{0,1},{1,2},{2,3},{3,0},{4,5},{5,6},{6,7},{7,4},{8,9},{9,10},{10,1... | collective-permute-start | bytes 196616 | tf_op jit(solution)/shard_map/ppermute | solution.py:293
  51.1 5.8 %collective-permute-start.13 = (bf16[256,128]{1,0:T(8,128)(2,1)S(1)}, bf16[256,128]{1,0:T(8,128)(2,1)S(1)}, u32[]{:S(2)}, u32[]{:S(2)}) collective-permute-start(bf16[256,128]{1,0:T(8,128)(2,1)S(1)} %get-tuple-element.42), channel_id=1, source_target_pairs={{0,2},{1,3},{2,0},{3,1},{4,6},{5,7},{6,4},{7,5},{8,10},{9,11},{10,... | collective-permute-start | bytes 196616 | tf_op jit(solution)/shard_map/ppermute | solution.py:293
  53.4 4.3 %collective-permute-start.14 = (bf16[256,128]{1,0:T(8,128)(2,1)S(1)}, bf16[256,128]{1,0:T(8,128)(2,1)S(1)}, u32[]{:S(2)}, u32[]{:S(2)}) collective-permute-start(bf16[256,128]{1,0:T(8,128)(2,1)S(1)} %get-tuple-element.43), channel_id=1, source_target_pairs={{0,3},{1,0},{2,1},{3,2},{4,7},{5,4},{6,5},{7,6},{8,11},{9,8},{10,9... | collective-permute-start | bytes 196616 | tf_op jit(solution)/shard_map/ppermute | solution.py:293

commit v8 on v7

--- a/solution.py
+++ b/solution.py
@@ -114,25 +114,67 @@
     return [slice(r, r + TILE) for r in range(0, rows, TILE)]
 
 
-def prepare(
-    current_hbm, radiate_hbm, dirs_hbm, mom_center_hbm, po_center_hbm, src_hbm, weight_hbm, mom_src_hbm, mom_weight_hbm,
-    mom_cos, mom_sin, po_cos, po_sin, pick_ref, wave_ref, list_ref,
-    current_ref, radiate_ref, dirs_ref, src_ref, weight_ref, mom_src_ref, mom_weight_ref, mom_c, po_c, sems,
-):
-    box = lax.axis_index("box")
-    boxes = lax.axis_size("box")
-    m = current_ref.shape[0]
-    q = src_ref.shape[1]
-    pairs = [(src_hbm, src_ref), (weight_hbm, weight_ref), (dirs_hbm, dirs_ref)]
-    for i, other in enumerate((jnp.maximum(box - 1, 0), box, jnp.minimum(box + 1, boxes - 1))):
-        at = pl.multiple_of(other * m, 128)
-        pairs.append((mom_center_hbm.at[:, pl.ds(at, m)], mom_c.at[:, pl.ds(i * m, m)]))
-    at = pl.multiple_of(box * q, 128)
-    pairs.append((po_center_hbm.at[:, pl.ds(at, q)], po_c))
-    pairs += [(current_hbm, current_ref), (radiate_hbm, radiate_ref), (mom_src_hbm, mom_src_ref), (mom_weight_hbm, mom_weight_ref)]
+def start_all(pairs, sems):
     copies = [pltpu.make_async_copy(here, there, sems.at[i]) for i, (here, there) in enumerate(pairs)]
     for copy in copies:
         copy.start()
+    return copies
+
+
+def centers_of(center_hbm, box, rows):
+    return center_hbm.at[:, pl.ds(pl.multiple_of(box * rows, 128), rows)]
+
+
+def neighbour(after):
+    return jnp.clip(lax.axis_index("box") - 1 + 2 * after, 0, lax.axis_size("box") - 1)
+
+
+def parity():
+    return lax.rem(lax.axis_index("box"), 2)
+
+
+def own_waves(
+    current_hbm, radiate_hbm, dirs_hbm, mom_center_hbm,
+    own_cos, own_sin, *refs,
+):
+    outs, (current_ref, radiate_ref, dirs_ref, center, sems) = refs[:-5], refs[-5:]
+    m = current_ref.shape[0]
+    there = centers_of(mom_center_hbm, lax.axis_index("box"), m)
+    copies = start_all(
+        ((dirs_hbm, dirs_ref), (there, center), (current_hbm, current_ref), (radiate_hbm, radiate_ref)), sems
+    )
+    for copy in copies[:2]:
+        copy.wait()
+    trig(center[...], dirs_ref, own_cos, own_sin)
+    for copy in copies[2:]:
+        copy.wait()
+    for at in tiles(m):
+        for c in range(radiate_ref.shape[0]):
+            re, im = rotated(mm(current_ref[at], radiate_ref[c]), own_cos[c, at], own_sin[c, at], -1)
+            outs[2 * c][at] = re.astype(BF)
+            outs[2 * c + 1][at] = im.astype(BF)
+
+
+def prepare(
+    dirs_hbm, mom_center_hbm, po_center_hbm, src_hbm, weight_hbm, mom_src_hbm, mom_weight_hbm,
+    odd_cos, odd_sin, po_cos, po_sin, pick_ref, list_ref,
+    dirs_ref, src_ref, weight_ref, mom_src_ref, mom_weight_ref, mom_c, po_c, sems,
+):
+    box = lax.axis_index("box")
+    m = mom_c.shape[1]
+    q = src_ref.shape[1]
+    copies = start_all(
+        (
+            (src_hbm, src_ref),
+            (weight_hbm, weight_ref),
+            (dirs_hbm, dirs_ref),
+            (centers_of(mom_center_hbm, neighbour(parity()), m), mom_c),
+            (centers_of(po_center_hbm, box, q), po_c),
+            (mom_src_hbm, mom_src_ref),
+            (mom_weight_hbm, mom_weight_ref),
+        ),
+        sems,
+    )
     for copy in copies[:2]:
         copy.wait()
     src_col = (src_ref[...] - (box - 1) * m).T
@@ -145,29 +187,27 @@
         copy.wait()
     list_ref[0:8] = mom_src_ref[...].astype(F32)
     list_ref[8:16] = mom_weight_ref[...]
-    trig(mom_c[...], dirs_ref, mom_cos, mom_sin)
-    for at in tiles(m):
-        radiated(current_ref, at, radiate_ref, mom_cos, mom_sin, wave_ref, 0, m)
+    trig(mom_c[...], dirs_ref, odd_cos, odd_sin)
     trig(po_c[...], dirs_ref, po_cos, po_sin)
 
 
 def incident(
-    odd_ref, even_ref, wave_ref, pick_ref, radiate_ref, receive_ref, mom_cos, mom_sin, po_cos, po_sin, lit_ref,
+    odd_ref, e0, e1, e2, e3, w0, w1, w2, w3, pick_ref, radiate_ref, receive_ref, odd_cos, odd_sin, po_cos, po_sin, lit_ref,
     first_ref, po_lit_ref,
     table,
 ):
     cone = lax.axis_index("cone")
     count = lax.axis_size("cone")
-    box = lax.axis_index("box")
-    m = wave_ref.shape[0]
+    m = odd_ref.shape[0]
     q, share = first_ref.shape
     cones, _, k2 = radiate_ref.shape
     k = k2 // 2
-    side = lax.rem(box, 2) * 2 * m
+    side = parity() * 2 * m
     for at in tiles(m):
-        table[rows_at(m, at)] = wave_ref[at]
-        radiated(even_ref, at, radiate_ref, mom_cos, mom_sin, table, 2 * m - side, 2 * m - side)
-        radiated(odd_ref, at, radiate_ref, mom_cos, mom_sin, table, side, side)
+        for i, (e_ref, w_ref) in enumerate(((e0, w0), (e1, w1), (e2, w2), (e3, w3))):
+            table[rows_at(m, at), i * k : (i + 1) * k] = w_ref[at]
+            table[rows_at(2 * m - side, at), i * k : (i + 1) * k] = e_ref[at]
+        radiated(odd_ref, at, radiate_ref, odd_cos, odd_sin, table, side, 0)
     lit_col = jnp.concatenate([lit_ref[...].astype(F32), jnp.zeros((8 - cones, q), F32)], axis=0).T
     columns = pl.ds(pl.multiple_of(lax.rem(cone + 1, count) * share, share), share)
     for at in tiles(q):
@@ -197,13 +237,14 @@
     s3_ref[...] = chunks[3].astype(BF)
 
 
-def lists(even_ref, own_ref, odd_ref, pick_ref):
+def lists(even_ref, own_ref, odd_ref, dirs_ref, mom_center_hbm, pick_ref, even_cos, even_sin, mom_c, sems):
     box = lax.axis_index("box")
+    m = own_ref.shape[1]
+    q = pick_ref.shape[1]
+    copies = start_all(((centers_of(mom_center_hbm, neighbour(1 - parity()), m), mom_c),), sems)
     even = lax.rem(box, 2) == 0
     e, o = even_ref[...], odd_ref[...]
     entries = (jnp.where(even, o, e), own_ref[...], jnp.where(even, e, o))
-    m = own_ref.shape[1]
-    q = pick_ref.shape[1]
     ratio = q // m
     first = (box * q).astype(F32)
     for i, value in enumerate(entries):
@@ -214,6 +255,8 @@
             middle = (i - 1) * q + r * ratio
             at = slice(i * m + r, i * m + r + step)
             fill(pick_ref, at, middle - q, middle + (step - 1) * ratio + q + 1, src_col[r : r + step], w_col[r : r + step])
+    copies[0].wait()
+    trig(mom_c[...], dirs_ref, even_cos, even_sin)
 
 
 def put_chunks(out, at, total):
@@ -237,8 +280,7 @@
         whole[:, pl.ds(pl.multiple_of(owner * share, share), share)] = ref[...]
     for at in tiles(q):
         radiated(whole, at, radiate_ref, po_cos, po_sin, waves_ref, 0, 0)
-    after = lax.rem(lax.axis_index("box"), 2)
-    tested(2 * after, waves_ref, receive_ref, pick_ref, mom_cos, mom_sin, out_ref)
+    tested(2 * parity(), waves_ref, receive_ref, pick_ref, mom_cos, mom_sin, out_ref)
 
 
 def tested(part, waves_ref, receive_ref, pick_ref, mom_cos, mom_sin, out_ref):
@@ -250,14 +292,14 @@
         total = None
         for c in range(cones):
             value = mm(pick_ref[here], waves_ref[:, c * k2 : (c + 1) * k2])
-            re, im = rotated(value, mom_cos[c, here], mom_sin[c, here], 1)
+            re, im = rotated(value, mom_cos[c, at], mom_sin[c, at], 1)
             piece = mm(re.astype(BF), receive_ref[c, :k]) + mm(im.astype(BF), receive_ref[c, k:])
             total = piece if total is None else total + piece
         put_chunks(out_ref, at, total)
 
 
 def tested_even(*refs):
-    tested(2 - 2 * lax.rem(lax.axis_index("box"), 2), *refs)
+    tested(2 - 2 * parity(), *refs)
 
 
 def tested_own(*refs):
@@ -274,12 +316,12 @@
 
 
 def call(body, outs, ins, scratch=(), space=pltpu.VMEM, vmem=24, flops=1):
-    if space is pltpu.HBM:
-        ins = [pltpu.with_memory_space_constraint(value, space) for value in ins]
+    spaces = space if isinstance(space, tuple) else (space,) * len(ins)
+    ins = [pltpu.with_memory_space_constraint(value, at) if at is pltpu.HBM else value for value, at in zip(ins, spaces)]
     return pl.pallas_call(
         body,
         out_shape=outs,
-        in_specs=[pl.BlockSpec(memory_space=space) for _ in ins],
+        in_specs=[pl.BlockSpec(memory_space=at) for at in spaces],
         out_specs=jax.tree.map(lambda _: pl.BlockSpec(memory_space=pltpu.VMEM), outs),
         scratch_shapes=list(scratch),
         compiler_params=pltpu.CompilerParams(vmem_limit_bytes=vmem * MIB),
@@ -315,24 +357,32 @@
     width = cones * k2
 
     odd = swapped_odd(mom_current)
-    even = swapped_even(mom_current)
     waves3 = jnp.transpose(dirs, (1, 0, 2))
-    staged = (mom_current, mom_radiate, waves3, po_src, po_weight, mom_src, mom_weight)
-    mom_cos, mom_sin, po_cos, po_sin, pick, wave, entries = call(
+
+    def scratch(*values):
+        return tuple(pltpu.VMEM(value.shape, value.dtype) for value in values)
+
+    angles = (shape((cones, m, k), F32),) * 2
+    own_cos, own_sin, *own_parts = call(
+        own_waves,
+        angles + (shape((m, k), BF),) * (2 * cones),
+        (mom_current, mom_radiate, waves3, mom_center),
+        scratch(mom_current, mom_radiate, waves3) + (pltpu.VMEM((3, m), F32), pltpu.SemaphoreType.DMA((4,))),
+        pltpu.HBM,
+    )
+    even_parts = [swapped_even(part) for part in own_parts]
+    odd_cos, odd_sin, po_cos, po_sin, pick, entries = call(
         prepare,
-        (
-            shape((cones, 3 * m, k), F32), shape((cones, 3 * m, k), F32), shape((cones, q, k), F32), shape((cones, q, k), F32),
-            shape((q, 3 * m), BF), shape((m, width), BF), shape((16, m), F32),
-        ),
-        (mom_current, mom_radiate, waves3, mom_center, po_center, po_src, po_weight, mom_src, mom_weight),
-        tuple(pltpu.VMEM(value.shape, value.dtype) for value in staged)
-        + (pltpu.VMEM((3, 3 * m), F32), pltpu.VMEM((3, q), F32), pltpu.SemaphoreType.DMA((11,))),
+        angles + (shape((cones, q, k), F32),) * 2 + (shape((q, 3 * m), BF), shape((16, m), F32)),
+        (waves3, mom_center, po_center, po_src, po_weight, mom_src, mom_weight),
+        scratch(waves3, po_src, po_weight, mom_src, mom_weight)
+        + (pltpu.VMEM((3, m), F32), pltpu.VMEM((3, q), F32), pltpu.SemaphoreType.DMA((7,))),
         pltpu.HBM,
     )
     s1, po_lit = call(
         incident,
         (shape((q, share), BF), shape((q, width), BF)),
-        (odd, even, wave, pick, mom_radiate, po_receive, mom_cos, mom_sin, po_cos, po_sin, lit),
+        (odd, *even_parts, *own_parts, pick, mom_radiate, po_receive, odd_cos, odd_sin, po_cos, po_sin, lit),
         (pltpu.VMEM((3 * m, width), BF),),
     )
     s1 = turned(s1, 1)
@@ -347,7 +397,14 @@
     own, entries = lax.optimization_barrier((own, entries))
     odd_list = swapped_odd(entries)
     even_list = swapped_even(entries)
-    back = call(lists, shape((3 * m, q), BF), (even_list, entries, odd_list), flops=4_000_000_000)
+    back, even_cos, even_sin = call(
+        lists,
+        (shape((3 * m, q), BF),) + angles,
+        (even_list, entries, odd_list, waves3, mom_center),
+        (pltpu.VMEM((3, m), F32), pltpu.SemaphoreType.DMA((1,))),
+        (pltpu.VMEM,) * 4 + (pltpu.HBM,),
+        flops=4_000_000_000,
+    )
     own = call(added, shape((q, share), F32), (s1, own))
     po_share = (own + s3.astype(F32) + s2.astype(F32)).astype(BF)
     p2 = turned(po_share, 2)
@@ -356,15 +413,15 @@
     waves, for_odd = call(
         scattered,
         (shape((q, width), BF), shape((count, m, share), BF)),
-        (po_share, p2, p3, p1, po_radiate, mom_receive, back, po_cos, po_sin, mom_cos, mom_sin),
+        (po_share, p2, p3, p1, po_radiate, mom_receive, back, po_cos, po_sin, odd_cos, odd_sin),
         (pltpu.VMEM((q, n), BF),),
     )
-    rest = (mom_receive, back, mom_cos, mom_sin)
+    rest = (mom_receive, back)
     from_odd = swapped_odd(for_odd)
-    for_even = call(tested_even, shape((count, m, share), BF), (waves,) + rest)
+    for_even = call(tested_even, shape((count, m, share), BF), (waves,) + rest + (even_cos, even_sin))
     from_even = swapped_even(for_even)
-    for_even, own_waves = lax.optimization_barrier((for_even, waves))
-    field = call(tested_own, shape((count, m, share), F32), (own_waves,) + rest)
+    for_even, last_waves = lax.optimization_barrier((for_even, waves))
+    field = call(tested_own, shape((count, m, share), F32), (last_waves,) + rest + (own_cos, own_sin))
     field = call(added, shape((count, m, share), F32), (from_odd, field))
     f0, f1, f2, f3 = call(
         merged,

time: 58.6 us -> 59.8 us (1.020)
  starting transfers between devices: 29 us -> 26.8 us
  waiting for transfers between devices: 12.1 us -> 13.9 us
  Pallas kernels: 15.5 us -> 16.4 us
  local copies, waits for them, and re-layouts: 0.03 us -> 0.7 us
    ppermute x3, starting transfers between devices: 14.9 us -> 11.5 us  [swapped_odd(): lax.ppermute(value, 'box', [(i, (i + 1 ^ 1) - 1) for i in range(1, lax.ax...]
    ppermute x3, waiting for transfers between devices: 3.99 us -> 5.36 us  [swapped_odd(): lax.ppermute(value, 'box', [(i, (i + 1 ^ 1) - 1) for i in range(1, lax.ax...]
    ppermute x3 -> x6, starting transfers between devices: 0.28 us -> 1.28 us  [swapped_even(): lax.ppermute(value, 'box', [(i, i ^ 1) for i in range(lax.axis_size('box'...]
    pallas_call x10 -> x11, Pallas kernels: 15.5 us -> 16.4 us  [call(): pl.pallas_call(body, out_shape=outs, in_specs=[pl.BlockSpec(memory_space=...]
    unnamed x12 -> x14, local copies, waits for them, and re-layouts: 0.03 us -> 0.7 us
  transfers between devices with their start and end apart: 15 -> 18, of which waited for: 7 -> 8; matrix products, arithmetic and copies ran while one was open for 0% -> 0% of each run, Pallas kernels for 18% -> 20%
where the time goes in v8:
time: 59.8 us; the launch traced here: 59.5 us
  starting transfers between devices  26.8 us (45%)
  Pallas kernels  16.4 us (27%)
  waiting for transfers between devices  13.9 us (23%)
  between operations  0.91 us (2%)
  other arithmetic  0.74 us (1%)
  local copies, waits for them, and re-layouts  0.7 us (1%)
    pallas_call x11, Pallas kernels, call(): pl.pallas_call(body, out_shape=outs, in_specs=[pl.BlockSpec(memory_space=...  16.4 us
    ppermute x9, starting transfers between devices, turned(): lax.ppermute(value, 'cone', [(i, (i + shift) % count) for i in range(coun...  14 us
    ppermute x3, starting transfers between devices, swapped_odd(): lax.ppermute(value, 'box', [(i, (i + 1 ^ 1) - 1) for i in range(1, lax.ax...  11.5 us
    ppermute x9, waiting for transfers between devices, turned(): lax.ppermute(value, 'cone', [(i, (i + shift) % count) for i in range(coun...  8.56 us
    ppermute x3, waiting for transfers between devices, swapped_odd(): lax.ppermute(value, 'box', [(i, (i + 1 ^ 1) - 1) for i in range(1, lax.ax...  5.36 us
    ppermute x6, starting transfers between devices, swapped_even(): lax.ppermute(value, 'box', [(i, i ^ 1) for i in range(lax.axis_size('box'...  1.28 us
  transfers between devices with their start and end apart: 18, of which 8 were waited for; matrix products, arithmetic and copies ran while one was open for 0% of the time, Pallas kernels for 20%

profile of v8, /device:TPU:6, one launch (start us, length us, event | category | flops | bytes accessed | tf_op | source)
XLA Modules:
  0.0 59.5 jit_solution(2644729650437028981)
XLA Ops:
  0.6 7.5 %collective-permute-start = (bf16[256,512]{1,0:T(8,128)(2,1)}, bf16[256,512]{1,0:T(8,128)(2,1)S(1)}, u32[]{:S(2)}, u32[]{:S(2)}) collective-permute-start(bf16[256,512]{1,0:T(8,128)(2,1)} %current_hbm.1), channel_id=1, source_target_pairs={{4,8},{8,4},{12,16},{16,12},{20,24},{24,20},{28,32},{32,28},{36,40... | collective-permute-start | bytes 786440 | tf_op jit(solution)/shard_map/ppermute | solution.py:343
  8.1 2.0 %own_waves.1 = (f32[2,256,256]{2,1,0:T(8,128)S(1)}, f32[2,256,256]{2,1,0:T(8,128)S(1)}, bf16[256,256]{1,0:T(8,128)(2,1)S(1)}, bf16[256,256]{1,0:T(8,128)(2,1)S(1...) custom-call(bf16[256,512]{1,0:T(8,128)(2,1)} %current_hbm.1, bf16[2,512,512]{2,1,0:T(8,128)(2,1)} %radiate_ref.2, ...), custom_call_target="tpu_custom_call" | custom-call | flops 1 | bytes 1 | tf_op jit(solution)/shard_map/own_waves/pallas_call | solution.py:321
  10.1 0.1 collective-permute-start.1
  10.2 0.5 collective-permute-start.2
  10.7 0.1 collective-permute-start.3
  10.8 0.4 collective-permute-start.4
  11.2 3.8 %prepare.1 = (f32[2,256,256]{2,1,0:T(8,128)S(1)}, f32[2,256,256]{2,1,0:T(8,128)S(1)}, f32[2,512,256]{2,1,0:T(8,128)S(1)}, f32[2,512,256]{2,1,0:T(8,128)S(1)}, bf...) custom-call(f32[3,2,256]{2,1,0:T(2,128)} %bitcast.2, f32[3,16384]{1,0:T(4,128)} %mom_center_hbm.5, ...), custom_call_target="tpu_custom_call" | custom-call | flops 1 | bytes 1 | tf_op jit(solution)/shard_map/prepare/pallas_call | solution.py:321
  15.0 0.0 collective-permute-done.1.e0
  15.0 0.0 collective-permute-done.2.e1
  15.1 0.0 collective-permute-done.4.e3
  15.1 0.0 collective-permute-done.odd_ref
  15.1 0.0 copy-start.6
  15.1 0.7 %copy-done.6 = s32[2,512]{1,0:T(2,128)S(1)} copy-done((s32[2,512]{1,0:T(2,128)S(1)}, s32[2,512]{1,0:T(2,128)}, u32[]{:S(2)}) %copy-start.6) | copy-done | bytes 4120
  15.8 2.7 %incident.1 = (bf16[512,128]{1,0:T(8,128)(2,1)S(1)}, bf16[512,1024]{1,0:T(8,128)(2,1)S(1)}) custom-call(bf16[256,512]{1,0:T(8,128)(2,1)S(1)} %collective-permute-done.odd_ref, bf16[256,256]{1,0:T(8,128)(2,1)S(1)} %collective-permute-done.1.e0, bf16[256,256]{1,0:T(8,128)(2,1)S(1)} %collective-permute-done.2.e1, ...), custom_call_target="tpu_custom_call" | custom-call | flops 1 | bytes 1 | tf_op jit(solution)/shard_map/incident/pallas_call | solution.py:321
  18.5 1.7 %collective-permute-start.5 = (bf16[512,128]{1,0:T(8,128)(2,1)S(1)}, bf16[512,128]{1,0:T(8,128)(2,1)S(1)}, u32[]{:S(2)}, u32[]{:S(2)}) collective-permute-start(bf16[512,128]{1,0:T(8,128)(2,1)S(1)} %get-tuple-element.40), channel_id=1, source_target_pairs={{0,1},{1,2},{2,3},{3,0},{4,5},{5,6},{6,7},{7,4},{8,9},{9,10},{10,1... | collective-permute-start | bytes 393224 | tf_op jit(solution)/shard_map/ppermute | solution.py:335
  20.1 0.9 %received.1 = (f32[512,128]{1,0:T(8,128)S(1)}, bf16[512,128]{1,0:T(8,128)(2,1)S(1)}, bf16[512,128]{1,0:T(8,128)(2,1)S(1)}) custom-call(bf16[512,1024]{1,0:T(8,128)(2,1)S(1)} %get-tuple-element.41.po_lit_ref, bf16[2,512,512]{2,1,0:T(8,128)(2,1)S(1)} %copy-done.2), custom_call_target="tpu_custom_call" | custom-call | flops 1 | bytes 1 | tf_op jit(solution)/shard_map/received/pallas_call | solution.py:321
  21.0 1.7 %collective-permute-start.6 = (bf16[512,128]{1,0:T(8,128)(2,1)S(1)}, bf16[512,128]{1,0:T(8,128)(2,1)S(1)}, u32[]{:S(2)}, u32[]{:S(2)}) collective-permute-start(bf16[512,128]{1,0:T(8,128)(2,1)S(1)} %get-tuple-element.45), channel_id=1, source_target_pairs={{0,3},{1,0},{2,1},{3,2},{4,7},{5,4},{6,5},{7,6},{8,11},{9,8},{10,9... | collective-permute-start | bytes 393224 | tf_op jit(solution)/shard_map/ppermute | solution.py:335
  22.7 2.0 %collective-permute-start.7 = (bf16[512,128]{1,0:T(8,128)(2,1)S(1)}, bf16[512,128]{1,0:T(8,128)(2,1)S(1)}, u32[]{:S(2)}, u32[]{:S(2)}) collective-permute-start(bf16[512,128]{1,0:T(8,128)(2,1)S(1)} %get-tuple-element.46), channel_id=1, source_target_pairs={{0,2},{1,3},{2,0},{3,1},{4,6},{5,7},{6,4},{7,5},{8,10},{9,11},{10,... | collective-permute-start | bytes 393224 | tf_op jit(solution)/shard_map/ppermute | solution.py:335
  24.7 2.2 %collective-permute-start.12 = (f32[16,256]{1,0:T(8,128)S(1)}, f32[16,256]{1,0:T(8,128)S(1)}, u32[]{:S(2)}, u32[]{:S(2)}) collective-permute-start(f32[16,256]{1,0:T(8,128)S(1)} %get-tuple-element.47.own_ref), channel_id=1, source_target_pairs={{4,8},{8,4},{12,16},{16,12},{20,24},{24,20},{28,32},{32,28},{36,40... | collective-permute-start | bytes 49160 | tf_op jit(solution)/shard_map/ppermute | solution.py:343
  26.9 0.1 collective-permute-start.11
  27.0 0.0 collective-permute-done.5.new_ref
  27.0 0.0 copy-start.5
  27.0 1.3 %collective-permute-done.6 = bf16[512,128]{1,0:T(8,128)(2,1)S(1)} collective-permute-done((bf16[512,128]{1,0:T(8,128)(2,1)S(1)}, bf16[512,128]{1,0:T(8,128)(2,1)S(1)}, u32[]{:S(2)}, u32[]{:S(2)}) %collective-permute-start.6) | collective-permute-done | bytes 131104 | tf_op jit(solution)/shard_map/ppermute | solution.py:335
  28.4 0.9 %collective-permute-done.7 = bf16[512,128]{1,0:T(8,128)(2,1)S(1)} collective-permute-done((bf16[512,128]{1,0:T(8,128)(2,1)S(1)}, bf16[512,128]{1,0:T(8,128)(2,1)S(1)}, u32[]{:S(2)}, u32[]{:S(2)}) %collective-permute-start.7) | collective-permute-done | bytes 131104 | tf_op jit(solution)/shard_map/ppermute | solution.py:335
  29.3 0.0 copy-start.4
  29.4 0.0 copy-start
  29.4 0.0 copy-start.3
  29.4 2.3 %collective-permute-start.10 = (bf16[512,128]{1,0:T(8,128)(2,1)S(1)}, bf16[512,128]{1,0:T(8,128)(2,1)S(1)}, u32[]{:S(2)}, u32[]{:S(2)}) collective-permute-start(bf16[512,128]{1,0:T(8,128)(2,1)S(1)} %add_convert_fusion.p0_ref), channel_id=1, source_target_pairs={{0,1},{1,2},{2,3},{3,0},{4,5},{5,6},{6,7},{7,4},{8,9},{9,10},{10,1... | collective-permute-start | bytes 393224 | tf_op jit(solution)/shard_map/ppermute | solution.py:335
  31.7 1.2 %collective-permute-start.9 = (bf16[512,128]{1,0:T(8,128)(2,1)S(1)}, bf16[512,128]{1,0:T(8,128)(2,1)S(1)}, u32[]{:S(2)}, u32[]{:S(2)}) collective-permute-start(bf16[512,128]{1,0:T(8,128)(2,1)S(1)} %add_convert_fusion.p0_ref), channel_id=1, source_target_pairs={{0,3},{1,0},{2,1},{3,2},{4,7},{5,4},{6,5},{7,6},{8,11},{9,8},{10,9... | collective-permute-start | bytes 393224 | tf_op jit(solution)/shard_map/ppermute | solution.py:335
  32.9 1.0 %collective-permute-start.8 = (bf16[512,128]{1,0:T(8,128)(2,1)S(1)}, bf16[512,128]{1,0:T(8,128)(2,1)S(1)}, u32[]{:S(2)}, u32[]{:S(2)}) collective-permute-start(bf16[512,128]{1,0:T(8,128)(2,1)S(1)} %add_convert_fusion.p0_ref), channel_id=1, source_target_pairs={{0,2},{1,3},{2,0},{3,1},{4,6},{5,7},{6,4},{7,5},{8,10},{9,11},{10,... | collective-permute-start | bytes 393224 | tf_op jit(solution)/shard_map/ppermute | solution.py:335
  33.9 0.0 collective-permute-done.12.odd_ref
  33.9 0.0 collective-permute-done.11.even_ref
  33.9 2.8 %lists.1 = (bf16[768,512]{1,0:T(8,128)(2,1)S(1)}, f32[2,256,256]{2,1,0:T(8,128)S(1)}, f32[2,256,256]{2,1,0:T(8,128)S(1)}) custom-call(f32[16,256]{1,0:T(8,128)S(1)} %collective-permute-done.11.even_ref, f32[16,256]{1,0:T(8,128)S(1)} %get-tuple-element.47.own_ref, f32[16,256]{1,0:T(8,128)S(1)} %collective-permute-done.12.odd_ref, f32[3,2,256]{2,1,0:T(2,128)S(1)} %bitcast.3, ...), custom_call_target="tpu_custom_call" | custom-call | flops 4000000000 | bytes 1 | tf_op jit(solution)/shard_map/lists/pallas_call | solution.py:321
  36.7 0.5 collective-permute-done.9.p3_ref
  37.2 2.3 %collective-permute-done.8.p2_ref = bf16[512,128]{1,0:T(8,128)(2,1)S(1)} collective-permute-done((bf16[512,128]{1,0:T(8,128)(2,1)S(1)}, bf16[512,128]{1,0:T(8,128)(2,1)S(1)}, u32[]{:S(2)}, u32[]{:S(2)}) %collective-permute-start.8) | collective-permute-done | bytes 131104 | tf_op jit(solution)/shard_map/ppermute | solution.py:335
  39.5 1.8 %scattered.1 = (bf16[512,1024]{1,0:T(8,128)(2,1)S(1)}, bf16[4,256,128]{2,1,0:T(8,128)(2,1)S(1)}) custom-call(bf16[512,128]{1,0:T(8,128)(2,1)S(1)} %add_convert_fusion.p0_ref, bf16[512,128]{1,0:T(8,128)(2,1)S(1)} %collective-permute-done.8.p2_ref, bf16[512,128]{1,0:T(8,128)(2,1)S(1)} %collective-permute-done.9.p3_ref, ...), custom_call_target="tpu_custom_call" | custom-call | flops 1 | bytes 1 | tf_op jit(solution)/shard_map/scattered/pallas_call | solution.py:321
  41.4 1.9 %collective-permute-start.14 = (bf16[4,256,128]{2,1,0:T(8,128)(2,1)S(1)}, bf16[4,256,128]{2,1,0:T(8,128)(2,1)S(1)}, u32[]{:S(2)}, u32[]{:S(2)}) collective-permute-start(bf16[4,256,128]{2,1,0:T(8,128)(2,1)S(1)} %get-tuple-element.52), channel_id=1, source_target_pairs={{4,8},{8,4},{12,16},{16,12},{20,24},{24,20},{28,32},{32,28},{36,40... | collective-permute-start | bytes 786440 | tf_op jit(solution)/shard_map/ppermute | solution.py:343
  43.3 1.2 %tested_even.1 = bf16[4,256,128]{2,1,0:T(8,128)(2,1)S(1)} custom-call(bf16[512,1024]{1,0:T(8,128)(2,1)S(1)} %get-tuple-element.53.refs_0_, bf16[2,512,512]{2,1,0:T(8,128)(2,1)S(1)} %copy-done, bf16[768,512]{1,0:T(8,128)(2,1)S(1)} %get-tuple-element.48.pick_ref.refs_2_, f32[2,256,256]{2,1,0:T(8,128)S(1)} %get-tuple-element.50.refs_3_, ...), custom_call_target="tpu_custom_call" | custom-call | flops 1 | bytes 1 | tf_op jit(solution)/shard_map/tested_even/pallas_call | solution.py:321
  44.5 0.1 collective-permute-start.13
  44.6 1.2 %tested_own.1.own_ref = f32[4,256,128]{2,1,0:T(8,128)S(1)} custom-call(bf16[512,1024]{1,0:T(8,128)(2,1)S(1)} %get-tuple-element.53.refs_0_, bf16[2,512,512]{2,1,0:T(8,128)(2,1)S(1)} %copy-done, bf16[768,512]{1,0:T(8,128)(2,1)S(1)} %get-tuple-element.48.pick_ref.refs_2_, f32[2,256,256]{2,1,0:T(8,128)S(1)} %get-tuple-element.54.refs_3_, ...), custom_call_target="tpu_custom_call" | custom-call | flops 1 | bytes 1 | tf_op jit(solution)/shard_map/tested_own/pallas_call | solution.py:321
  45.8 5.4 %collective-permute-done.14.new_ref = bf16[4,256,128]{2,1,0:T(8,128)(2,1)S(1)} collective-permute-done((bf16[4,256,128]{2,1,0:T(8,128)(2,1)S(1)}, bf16[4,256,128]{2,1,0:T(8,128)(2,1)S(1)}, u32[]{:S(2)}, u32[]{:S(2)}) %collective-permute-start.14) | collective-permute-done | bytes 262176 | tf_op jit(solution)/shard_map/ppermute | solution.py:343
  51.3 1.0 %collective-permute-start.15 = (bf16[256,128]{1,0:T(8,128)(2,1)S(1)}, bf16[256,128]{1,0:T(8,128)(2,1)S(1)}, u32[]{:S(2)}, u32[]{:S(2)}) collective-permute-start(bf16[256,128]{1,0:T(8,128)(2,1)S(1)} %get-tuple-element.57), channel_id=1, source_target_pairs={{0,1},{1,2},{2,3},{3,0},{4,5},{5,6},{6,7},{7,4},{8,9},{9,10},{10,1... | collective-permute-start | bytes 196616 | tf_op jit(solution)/shard_map/ppermute | solution.py:335
  52.2 2.3 %collective-permute-start.16 = (bf16[256,128]{1,0:T(8,128)(2,1)S(1)}, bf16[256,128]{1,0:T(8,128)(2,1)S(1)}, u32[]{:S(2)}, u32[]{:S(2)}) collective-permute-start(bf16[256,128]{1,0:T(8,128)(2,1)S(1)} %get-tuple-element.58), channel_id=1, source_target_pairs={{0,2},{1,3},{2,0},{3,1},{4,6},{5,7},{6,4},{7,5},{8,10},{9,11},{10,... | collective-permute-start | bytes 196616 | tf_op jit(solution)/shard_map/ppermute | solution.py:335
  54.6 0.8 %collective-permute-start.17 = (bf16[256,128]{1,0:T(8,128)(2,1)S(1)}, bf16[256,128]{1,0:T(8,128)(2,1)S(1)}, u32[]{:S(2)}, u32[]{:S(2)}) collective-permute-start(bf16[256,128]{1,0:T(8,128)(2,1)S(1)} %get-tuple-element.59), channel_id=1, source_target_pairs={{0,3},{1,0},{2,1},{3,2},{4,7},{5,4},{6,5},{7,6},{8,11},{9,8},{10,9... | collective-permute-start | bytes 196616 | tf_op jit(solution)/shard_map/ppermute | solution.py:335
  55.4 1.5 %collective-permute-done.15 = bf16[256,128]{1,0:T(8,128)(2,1)S(1)} collective-permute-done((bf16[256,128]{1,0:T(8,128)(2,1)S(1)}, bf16[256,128]{1,0:T(8,128)(2,1)S(1)}, u32[]{:S(2)}, u32[]{:S(2)}) %collective-permute-start.15) | collective-permute-done | bytes 65568 | tf_op jit(solution)/shard_map/ppermute | solution.py:335
  56.8 1.2 %collective-permute-done.16 = bf16[256,128]{1,0:T(8,128)(2,1)S(1)} collective-permute-done((bf16[256,128]{1,0:T(8,128)(2,1)S(1)}, bf16[256,128]{1,0:T(8,128)(2,1)S(1)}, u32[]{:S(2)}, u32[]{:S(2)}) %collective-permute-start.16) | collective-permute-done | bytes 65568 | tf_op jit(solution)/shard_map/ppermute | solution.py:335
  58.0 0.8 %collective-permute-done.17 = bf16[256,128]{1,0:T(8,128)(2,1)S(1)} collective-permute-done((bf16[256,128]{1,0:T(8,128)(2,1)S(1)}, bf16[256,128]{1,0:T(8,128)(2,1)S(1)}, u32[]{:S(2)}, u32[]{:S(2)}) %collective-permute-start.17) | collective-permute-done | bytes 65568 | tf_op jit(solution)/shard_map/ppermute | solution.py:335
  58.8 0.7 %convert_add_fusion = f32[256,128]{1,0:T(8,128)} fusion(bf16[256,128]{1,0:T(8,128)(2,1)S(1)} %collective-permute-done.17, bf16[256,128]{1,0:T(8,128)(2,1)S(1)} %collective-permute-done.16, f32[256,128]{1,0:T(8,128)S(1)} %get-tuple-element.56, bf16[256,128]{1,0:T(8,128)(2,1)S(1)} %collective-permute-done.15), kind=kLoop, calls=%fused_computation.1 | loop fusion | flops 196608 | bytes 458752 | tf_op jit(solution)/shard_map/add | solution.py:434
  (15 shorter events, 0.2 us)
Async XLA Ops:
  0.6 14.5 %collective-permute-start = (bf16[256,512]{1,0:T(8,128)(2,1)}, bf16[256,512]{1,0:T(8,128)(2,1)S(1)}, u32[]{:S(2)}, u32[]{:S(2)}) collective-permute-start(bf16[256,512]{1,0:T(8,128)(2,1)} %current_hbm.1), channel_id=1, source_target_pairs={{4,8},{8,4},{12,16},{16,12},{20,24},{24,20},{28,32},{32,28},{36,40... | collective-permute-start | bytes 786440 | tf_op jit(solution)/shard_map/ppermute | solution.py:343
  8.1 7.0 %copy-start.1 = (bf16[2,512,512]{2,1,0:T(8,128)(2,1)S(1)}, bf16[2,512,512]{2,1,0:T(8,128)(2,1)}, u32[]{:S(2)}) copy-start(bf16[2,512,512]{2,1,0:T(8,128)(2,1)} %radiate_ref.2) | copy-start | bytes 3145732
  8.1 7.0 %copy-start.2 = (bf16[2,512,512]{2,1,0:T(8,128)(2,1)S(1)}, bf16[2,512,512]{2,1,0:T(8,128)(2,1)}, u32[]{:S(2)}) copy-start(bf16[2,512,512]{2,1,0:T(8,128)(2,1)} %receive_ref.4) | copy-start | bytes 3145732
  10.1 4.9 %collective-permute-start.1 = (bf16[256,256]{1,0:T(8,128)(2,1)S(1)}, bf16[256,256]{1,0:T(8,128)(2,1)S(1)}, u32[]{:S(2)}, u32[]{:S(2)}) collective-permute-start(bf16[256,256]{1,0:T(8,128)(2,1)S(1)} %get-tuple-element.31.w0), channel_id=1, source_target_pairs={{0,4},{4,0},{8,12},{12,8},{16,20},{20,16},{24,28},{28,24},{32,36},... | collective-permute-start | bytes 393224 | tf_op jit(solution)/shard_map/ppermute | solution.py:339
  10.2 4.8 %collective-permute-start.2 = (bf16[256,256]{1,0:T(8,128)(2,1)S(1)}, bf16[256,256]{1,0:T(8,128)(2,1)S(1)}, u32[]{:S(2)}, u32[]{:S(2)}) collective-permute-start(bf16[256,256]{1,0:T(8,128)(2,1)S(1)} %get-tuple-element.32.w1), channel_id=1, source_target_pairs={{0,4},{4,0},{8,12},{12,8},{16,20},{20,16},{24,28},{28,24},{32,36},... | collective-permute-start | bytes 393224 | tf_op jit(solution)/shard_map/ppermute | solution.py:339
  10.7 4.4 %collective-permute-start.3 = (bf16[256,256]{1,0:T(8,128)(2,1)S(1)}, bf16[256,256]{1,0:T(8,128)(2,1)S(1)}, u32[]{:S(2)}, u32[]{:S(2)}) collective-permute-start(bf16[256,256]{1,0:T(8,128)(2,1)S(1)} %get-tuple-element.33.w2), channel_id=1, source_target_pairs={{0,4},{4,0},{8,12},{12,8},{16,20},{20,16},{24,28},{28,24},{32,36},... | collective-permute-start | bytes 393224 | tf_op jit(solution)/shard_map/ppermute | solution.py:339
  10.8 4.3 %collective-permute-start.4 = (bf16[256,256]{1,0:T(8,128)(2,1)S(1)}, bf16[256,256]{1,0:T(8,128)(2,1)S(1)}, u32[]{:S(2)}, u32[]{:S(2)}) collective-permute-start(bf16[256,256]{1,0:T(8,128)(2,1)S(1)} %get-tuple-element.34.w3), channel_id=1, source_target_pairs={{0,4},{4,0},{8,12},{12,8},{16,20},{20,16},{24,28},{28,24},{32,36},... | collective-permute-start | bytes 393224 | tf_op jit(solution)/shard_map/ppermute | solution.py:339
  15.1 0.7 %copy-start.6 = (s32[2,512]{1,0:T(2,128)S(1)}, s32[2,512]{1,0:T(2,128)}, u32[]{:S(2)}) copy-start(s32[2,512]{1,0:T(2,128)} %lit_ref.1) | copy-start | bytes 12292
  18.5 8.5 %collective-permute-start.5 = (bf16[512,128]{1,0:T(8,128)(2,1)S(1)}, bf16[512,128]{1,0:T(8,128)(2,1)S(1)}, u32[]{:S(2)}, u32[]{:S(2)}) collective-permute-start(bf16[512,128]{1,0:T(8,128)(2,1)S(1)} %get-tuple-element.40), channel_id=1, source_target_pairs={{0,1},{1,2},{2,3},{3,0},{4,5},{5,6},{6,7},{7,4},{8,9},{9,10},{10,1... | collective-permute-start | bytes 393224 | tf_op jit(solution)/shard_map/ppermute | solution.py:335
  21.0 7.4 %collective-permute-start.6 = (bf16[512,128]{1,0:T(8,128)(2,1)S(1)}, bf16[512,128]{1,0:T(8,128)(2,1)S(1)}, u32[]{:S(2)}, u32[]{:S(2)}) collective-permute-start(bf16[512,128]{1,0:T(8,128)(2,1)S(1)} %get-tuple-element.45), channel_id=1, source_target_pairs={{0,3},{1,0},{2,1},{3,2},{4,7},{5,4},{6,5},{7,6},{8,11},{9,8},{10,9... | collective-permute-start | bytes 393224 | tf_op jit(solution)/shard_map/ppermute | solution.py:335
  22.7 6.6 %collective-permute-start.7 = (bf16[512,128]{1,0:T(8,128)(2,1)S(1)}, bf16[512,128]{1,0:T(8,128)(2,1)S(1)}, u32[]{:S(2)}, u32[]{:S(2)}) collective-permute-start(bf16[512,128]{1,0:T(8,128)(2,1)S(1)} %get-tuple-element.46), channel_id=1, source_target_pairs={{0,2},{1,3},{2,0},{3,1},{4,6},{5,7},{6,4},{7,5},{8,10},{9,11},{10,... | collective-permute-start | bytes 393224 | tf_op jit(solution)/shard_map/ppermute | solution.py:335
  24.7 9.1 %collective-permute-start.12 = (f32[16,256]{1,0:T(8,128)S(1)}, f32[16,256]{1,0:T(8,128)S(1)}, u32[]{:S(2)}, u32[]{:S(2)}) collective-permute-start(f32[16,256]{1,0:T(8,128)S(1)} %get-tuple-element.47.own_ref), channel_id=1, source_target_pairs={{4,8},{8,4},{12,16},{16,12},{20,24},{24,20},{28,32},{32,28},{36,40... | collective-permute-start | bytes 49160 | tf_op jit(solution)/shard_map/ppermute | solution.py:343
  26.9 7.0 %collective-permute-start.11 = (f32[16,256]{1,0:T(8,128)S(1)}, f32[16,256]{1,0:T(8,128)S(1)}, u32[]{:S(2)}, u32[]{:S(2)}) collective-permute-start(f32[16,256]{1,0:T(8,128)S(1)} %get-tuple-element.47.own_ref), channel_id=1, source_target_pairs={{0,4},{4,0},{8,12},{12,8},{16,20},{20,16},{24,28},{28,24},{32,36},... | collective-permute-start | bytes 49160 | tf_op jit(solution)/shard_map/ppermute | solution.py:339
  27.0 6.8 %copy-start.5 = (f32[2,3,256]{2,0,1:T(2,128)S(1)}, f32[2,3,256]{2,0,1:T(2,128)}, u32[]{:S(2)}) copy-start(f32[2,3,256]{2,0,1:T(2,128)} %param.18) | copy-start | bytes 18436
  29.3 10.2 %copy-start.4 = (bf16[512,128]{1,0:T(8,128)(2,1)}, bf16[512,128]{1,0:T(8,128)(2,1)S(1)}, u32[]{:S(2)}) copy-start(bf16[512,128]{1,0:T(8,128)(2,1)S(1)} %add_convert_fusion.p0_ref) | copy-start | bytes 393220
  29.4 10.2 %copy-start = (bf16[2,512,512]{2,1,0:T(8,128)(2,1)S(1)}, bf16[2,512,512]{2,1,0:T(8,128)(2,1)}, u32[]{:S(2)}) copy-start(bf16[2,512,512]{2,1,0:T(8,128)(2,1)} %refs_1_.3) | copy-start | bytes 3145732
  29.4 10.1 %copy-start.3 = (bf16[2,512,512]{2,1,0:T(8,128)(2,1)S(1)}, bf16[2,512,512]{2,1,0:T(8,128)(2,1)}, u32[]{:S(2)}) copy-start(bf16[2,512,512]{2,1,0:T(8,128)(2,1)} %radiate_ref.3) | copy-start | bytes 3145732
  29.4 7.3 %collective-permute-start.10 = (bf16[512,128]{1,0:T(8,128)(2,1)S(1)}, bf16[512,128]{1,0:T(8,128)(2,1)S(1)}, u32[]{:S(2)}, u32[]{:S(2)}) collective-permute-start(bf16[512,128]{1,0:T(8,128)(2,1)S(1)} %add_convert_fusion.p0_ref), channel_id=1, source_target_pairs={{0,1},{1,2},{2,3},{3,0},{4,5},{5,6},{6,7},{7,4},{8,9},{9,10},{10,1... | collective-permute-start | bytes 393224 | tf_op jit(solution)/shard_map/ppermute | solution.py:335
  31.7 5.4 %collective-permute-start.9 = (bf16[512,128]{1,0:T(8,128)(2,1)S(1)}, bf16[512,128]{1,0:T(8,128)(2,1)S(1)}, u32[]{:S(2)}, u32[]{:S(2)}) collective-permute-start(bf16[512,128]{1,0:T(8,128)(2,1)S(1)} %add_convert_fusion.p0_ref), channel_id=1, source_target_pairs={{0,3},{1,0},{2,1},{3,2},{4,7},{5,4},{6,5},{7,6},{8,11},{9,8},{10,9... | collective-permute-start | bytes 393224 | tf_op jit(solution)/shard_map/ppermute | solution.py:335
  32.9 6.6 %collective-permute-start.8 = (bf16[512,128]{1,0:T(8,128)(2,1)S(1)}, bf16[512,128]{1,0:T(8,128)(2,1)S(1)}, u32[]{:S(2)}, u32[]{:S(2)}) collective-permute-start(bf16[512,128]{1,0:T(8,128)(2,1)S(1)} %add_convert_fusion.p0_ref), channel_id=1, source_target_pairs={{0,2},{1,3},{2,0},{3,1},{4,6},{5,7},{6,4},{7,5},{8,10},{9,11},{10,... | collective-permute-start | bytes 393224 | tf_op jit(solution)/shard_map/ppermute | solution.py:335
  41.4 9.8 %collective-permute-start.14 = (bf16[4,256,128]{2,1,0:T(8,128)(2,1)S(1)}, bf16[4,256,128]{2,1,0:T(8,128)(2,1)S(1)}, u32[]{:S(2)}, u32[]{:S(2)}) collective-permute-start(bf16[4,256,128]{2,1,0:T(8,128)(2,1)S(1)} %get-tuple-element.52), channel_id=1, source_target_pairs={{4,8},{8,4},{12,16},{16,12},{20,24},{24,20},{28,32},{32,28},{36,40... | collective-permute-start | bytes 786440 | tf_op jit(solution)/shard_map/ppermute | solution.py:343
  44.5 6.7 %collective-permute-start.13 = (bf16[4,256,128]{2,1,0:T(8,128)(2,1)S(1)}, bf16[4,256,128]{2,1,0:T(8,128)(2,1)S(1)}, u32[]{:S(2)}, u32[]{:S(2)}) collective-permute-start(bf16[4,256,128]{2,1,0:T(8,128)(2,1)S(1)} %tested_even.1), channel_id=1, source_target_pairs={{0,4},{4,0},{8,12},{12,8},{16,20},{20,16},{24,28},{28,24},{32,36},... | collective-permute-start | bytes 786440 | tf_op jit(solution)/shard_map/ppermute | solution.py:339
  51.3 5.6 %collective-permute-start.15 = (bf16[256,128]{1,0:T(8,128)(2,1)S(1)}, bf16[256,128]{1,0:T(8,128)(2,1)S(1)}, u32[]{:S(2)}, u32[]{:S(2)}) collective-permute-start(bf16[256,128]{1,0:T(8,128)(2,1)S(1)} %get-tuple-element.57), channel_id=1, source_target_pairs={{0,1},{1,2},{2,3},{3,0},{4,5},{5,6},{6,7},{7,4},{8,9},{9,10},{10,1... | collective-permute-start | bytes 196616 | tf_op jit(solution)/shard_map/ppermute | solution.py:335
  52.2 5.8 %collective-permute-start.16 = (bf16[256,128]{1,0:T(8,128)(2,1)S(1)}, bf16[256,128]{1,0:T(8,128)(2,1)S(1)}, u32[]{:S(2)}, u32[]{:S(2)}) collective-permute-start(bf16[256,128]{1,0:T(8,128)(2,1)S(1)} %get-tuple-element.58), channel_id=1, source_target_pairs={{0,2},{1,3},{2,0},{3,1},{4,6},{5,7},{6,4},{7,5},{8,10},{9,11},{10,... | collective-permute-start | bytes 196616 | tf_op jit(solution)/shard_map/ppermute | solution.py:335
  54.6 4.3 %collective-permute-start.17 = (bf16[256,128]{1,0:T(8,128)(2,1)S(1)}, bf16[256,128]{1,0:T(8,128)(2,1)S(1)}, u32[]{:S(2)}, u32[]{:S(2)}) collective-permute-start(bf16[256,128]{1,0:T(8,128)(2,1)S(1)} %get-tuple-element.59), channel_id=1, source_target_pairs={{0,3},{1,0},{2,1},{3,2},{4,7},{5,4},{6,5},{7,6},{8,11},{9,8},{10,9... | collective-permute-start | bytes 196616 | tf_op jit(solution)/shard_map/ppermute | solution.py:335

commit v9 on v8

--- a/solution.py
+++ b/solution.py
@@ -134,20 +134,36 @@
 
 
 def own_waves(
-    current_hbm, radiate_hbm, dirs_hbm, mom_center_hbm,
-    own_cos, own_sin, *refs,
+    current_hbm, radiate_hbm, dirs_hbm, mom_center_hbm, po_center_hbm, src_hbm, weight_hbm, mom_src_hbm, mom_weight_hbm, lit_hbm,
+    own_cos, own_sin, dirs_ref, odd_c, po_c, src_ref, weight_ref, lit_ref, list_ref, *refs,
 ):
-    outs, (current_ref, radiate_ref, dirs_ref, center, sems) = refs[:-5], refs[-5:]
+    outs, (current_ref, radiate_ref, center, mom_src_ref, sems) = refs[:-5], refs[-5:]
+    box = lax.axis_index("box")
     m = current_ref.shape[0]
-    there = centers_of(mom_center_hbm, lax.axis_index("box"), m)
+    q = src_ref.shape[1]
+    slots = mom_src_ref.shape[0]
     copies = start_all(
-        ((dirs_hbm, dirs_ref), (there, center), (current_hbm, current_ref), (radiate_hbm, radiate_ref)), sems
+        (
+            (dirs_hbm, dirs_ref),
+            (centers_of(mom_center_hbm, box, m), center),
+            (current_hbm, current_ref),
+            (radiate_hbm, radiate_ref),
+            (centers_of(mom_center_hbm, neighbour(parity()), m), odd_c),
+            (centers_of(po_center_hbm, box, q), po_c),
+            (src_hbm, src_ref),
+            (weight_hbm, weight_ref),
+            (lit_hbm, lit_ref),
+            (mom_src_hbm, mom_src_ref),
+            (mom_weight_hbm, list_ref.at[pl.ds(slots, slots)]),
+        ),
+        sems,
     )
     for copy in copies[:2]:
         copy.wait()
     trig(center[...], dirs_ref, own_cos, own_sin)
     for copy in copies[2:]:
         copy.wait()
+    list_ref[:slots] = mom_src_ref[...].astype(F32)
     for at in tiles(m):
         for c in range(radiate_ref.shape[0]):
             re, im = rotated(mm(current_ref[at], radiate_ref[c]), own_cos[c, at], own_sin[c, at], -1)
@@ -155,38 +171,16 @@
             outs[2 * c + 1][at] = im.astype(BF)
 
 
-def prepare(
-    dirs_hbm, mom_center_hbm, po_center_hbm, src_hbm, weight_hbm, mom_src_hbm, mom_weight_hbm,
-    odd_cos, odd_sin, po_cos, po_sin, pick_ref, list_ref,
-    dirs_ref, src_ref, weight_ref, mom_src_ref, mom_weight_ref, mom_c, po_c, sems,
-):
+def prepare(dirs_ref, mom_c, po_c, src_ref, weight_ref, odd_cos, odd_sin, po_cos, po_sin, pick_ref):
     box = lax.axis_index("box")
     m = mom_c.shape[1]
     q = src_ref.shape[1]
-    copies = start_all(
-        (
-            (src_hbm, src_ref),
-            (weight_hbm, weight_ref),
-            (dirs_hbm, dirs_ref),
-            (centers_of(mom_center_hbm, neighbour(parity()), m), mom_c),
-            (centers_of(po_center_hbm, box, q), po_c),
-            (mom_src_hbm, mom_src_ref),
-            (mom_weight_hbm, mom_weight_ref),
-        ),
-        sems,
-    )
-    for copy in copies[:2]:
-        copy.wait()
     src_col = (src_ref[...] - (box - 1) * m).T
     w_col = weight_ref[...].T
     step = 32
     for r in range(0, q, step):
         at = slice(r, r + step)
         fill(pick_ref, at, r * m // q, (r + step - 1) * m // q + 2 * m + 1, src_col[at], w_col[at])
-    for copy in copies[2:]:
-        copy.wait()
-    list_ref[0:8] = mom_src_ref[...].astype(F32)
-    list_ref[8:16] = mom_weight_ref[...]
     trig(mom_c[...], dirs_ref, odd_cos, odd_sin)
     trig(po_c[...], dirs_ref, po_cos, po_sin)
 
@@ -363,21 +357,22 @@
         return tuple(pltpu.VMEM(value.shape, value.dtype) for value in values)
 
     angles = (shape((cones, m, k), F32),) * 2
-    own_cos, own_sin, *own_parts = call(
+    own_cos, own_sin, waves3, odd_c, po_c, src, weight, lit, entries, *own_parts = call(
         own_waves,
-        angles + (shape((m, k), BF),) * (2 * cones),
-        (mom_current, mom_radiate, waves3, mom_center),
-        scratch(mom_current, mom_radiate, waves3) + (pltpu.VMEM((3, m), F32), pltpu.SemaphoreType.DMA((4,))),
+        angles
+        + (shape(waves3.shape, F32), shape((3, m), F32), shape((3, q), F32), shape(po_src.shape, po_src.dtype))
+        + (shape(po_weight.shape, F32), shape(lit.shape, lit.dtype), shape((16, m), F32))
+        + (shape((m, k), BF),) * (2 * cones),
+        (mom_current, mom_radiate, waves3, mom_center, po_center, po_src, po_weight, mom_src, mom_weight, lit),
+        scratch(mom_current, mom_radiate)
+        + (pltpu.VMEM((3, m), F32), pltpu.VMEM(mom_src.shape, mom_src.dtype), pltpu.SemaphoreType.DMA((11,))),
         pltpu.HBM,
     )
     even_parts = [swapped_even(part) for part in own_parts]
-    odd_cos, odd_sin, po_cos, po_sin, pick, entries = call(
+    odd_cos, odd_sin, po_cos, po_sin, pick = call(
         prepare,
-        angles + (shape((cones, q, k), F32),) * 2 + (shape((q, 3 * m), BF), shape((16, m), F32)),
-        (waves3, mom_center, po_center, po_src, po_weight, mom_src, mom_weight),
-        scratch(waves3, po_src, po_weight, mom_src, mom_weight)
-        + (pltpu.VMEM((3, m), F32), pltpu.VMEM((3, q), F32), pltpu.SemaphoreType.DMA((7,))),
-        pltpu.HBM,
+        angles + (shape((cones, q, k), F32),) * 2 + (shape((q, 3 * m), BF),),
+        (waves3, odd_c, po_c, src, weight),
     )
     s1, po_lit = call(
         incident,

time: 59.8 us -> 58.2 us (0.973)
  starting transfers between devices: 26.8 us -> 28.6 us
  waiting for transfers between devices: 13.9 us -> 12.3 us
  Pallas kernels: 16.4 us -> 15.5 us
  local copies, waits for them, and re-layouts: 0.7 us -> 0.03 us
    ppermute x3, starting transfers between devices: 11.5 us -> 13.4 us  [swapped_odd(): lax.ppermute(value, 'box', [(i, (i + 1 ^ 1) - 1) for i in range(1, lax.ax...]
    pallas_call x11, Pallas kernels: 16.4 us -> 15.5 us  [call(): pl.pallas_call(body, out_shape=outs, in_specs=[pl.BlockSpec(memory_space=...]
    ppermute x3, waiting for transfers between devices: 5.36 us -> 4.51 us  [swapped_odd(): lax.ppermute(value, 'box', [(i, (i + 1 ^ 1) - 1) for i in range(1, lax.ax...]
    ppermute x9, waiting for transfers between devices: 8.56 us -> 7.74 us  [turned(): lax.ppermute(value, 'cone', [(i, (i + shift) % count) for i in range(coun...]
    unnamed x14 -> x10, local copies, waits for them, and re-layouts: 0.7 us -> 0.03 us
  transfers between devices with their start and end apart: 18 -> 18, of which waited for: 8 -> 8; matrix products, arithmetic and copies ran while one was open for 0% -> 0% of each run, Pallas kernels for 20% -> 19%
where the time goes in v9:
time: 58.2 us; the launch traced here: 58 us
  starting transfers between devices  28.6 us (49%)
  Pallas kernels  15.5 us (27%)
  waiting for transfers between devices  12.3 us (21%)
  between operations  0.9 us (2%)
  other arithmetic  0.74 us (1%)
    pallas_call x11, Pallas kernels, call(): pl.pallas_call(body, out_shape=outs, in_specs=[pl.BlockSpec(memory_space=...  15.5 us
    ppermute x9, starting transfers between devices, turned(): lax.ppermute(value, 'cone', [(i, (i + shift) % count) for i in range(coun...  13.9 us
    ppermute x3, starting transfers between devices, swapped_odd(): lax.ppermute(value, 'box', [(i, (i + 1 ^ 1) - 1) for i in range(1, lax.ax...  13.4 us
    ppermute x9, waiting for transfers between devices, turned(): lax.ppermute(value, 'cone', [(i, (i + shift) % count) for i in range(coun...  7.74 us
    ppermute x3, waiting for transfers between devices, swapped_odd(): lax.ppermute(value, 'box', [(i, (i + 1 ^ 1) - 1) for i in range(1, lax.ax...  4.51 us
    ppermute x6, starting transfers between devices, swapped_even(): lax.ppermute(value, 'box', [(i, i ^ 1) for i in range(lax.axis_size('box'...  1.28 us
  transfers between devices with their start and end apart: 18, of which 8 were waited for; matrix products, arithmetic and copies ran while one was open for 0% of the time, Pallas kernels for 19%

profile of v9, /device:TPU:6, one launch (start us, length us, event | category | flops | bytes accessed | tf_op | source)
XLA Modules:
  0.0 58.0 jit_solution(736488779076058708)
XLA Ops:
  0.6 7.5 %collective-permute-start = (bf16[256,512]{1,0:T(8,128)(2,1)}, bf16[256,512]{1,0:T(8,128)(2,1)S(1)}, u32[]{:S(2)}, u32[]{:S(2)}) collective-permute-start(bf16[256,512]{1,0:T(8,128)(2,1)} %current_hbm.1), channel_id=1, source_target_pairs={{4,8},{8,4},{12,16},{16,12},{20,24},{24,20},{28,32},{32,28},{36,40... | collective-permute-start | bytes 786440 | tf_op jit(solution)/shard_map/ppermute | solution.py:337
  8.1 2.1 %own_waves.1 = (f32[2,256,256]{2,1,0:T(8,128)S(1)}, f32[2,256,256]{2,1,0:T(8,128)S(1)}, f32[3,2,256]{2,1,0:T(2,128)S(1)}, f32[3,256]{1,0:T(4,128)S(1)}, f32[3,51...) custom-call(bf16[256,512]{1,0:T(8,128)(2,1)} %current_hbm.1, ...), custom_call_target="tpu_custom_call" | custom-call | flops 1 | bytes 1 | tf_op jit(solution)/shard_map/own_waves/pallas_call | solution.py:315
  10.2 0.1 collective-permute-start.1
  10.3 0.5 collective-permute-start.2
  10.8 0.1 collective-permute-start.3
  10.9 0.4 collective-permute-start.4
  11.3 2.7 %prepare.1 = (f32[2,256,256]{2,1,0:T(8,128)S(1)}, f32[2,256,256]{2,1,0:T(8,128)S(1)}, f32[2,512,256]{2,1,0:T(8,128)S(1)}, f32[2,512,256]{2,1,0:T(8,128)S(1)}, bf16[512,768]{1,0:T(8,128)(2,1)S(1)}) custom-call(f32[3,2,256]{2,1,0:T(2,128)S(1)} %get-tuple-element.41.dirs_ref, f32[3,256]{1,0:T(4,128)S(1)} %get-tuple-element.42.mom_c, ...), custom_call_target="tpu_custom_call" | custom-call | flops 1 | bytes 1 | tf_op jit(solution)/shard_map/prepare/pallas_call | solution.py:315
  14.0 0.0 collective-permute-done.1.e0
  14.0 0.0 collective-permute-done.2.e1
  14.1 0.0 collective-permute-done.3.e2
  14.1 0.0 collective-permute-done.4.e3
  14.1 0.0 collective-permute-done.odd_ref
  14.1 2.7 %incident.1 = (bf16[512,128]{1,0:T(8,128)(2,1)S(1)}, bf16[512,1024]{1,0:T(8,128)(2,1)S(1)}) custom-call(bf16[256,512]{1,0:T(8,128)(2,1)S(1)} %collective-permute-done.odd_ref, bf16[256,256]{1,0:T(8,128)(2,1)S(1)} %collective-permute-done.1.e0, bf16[256,256]{1,0:T(8,128)(2,1)S(1)} %collective-permute-done.2.e1, ...), custom_call_target="tpu_custom_call" | custom-call | flops 1 | bytes 1 | tf_op jit(solution)/shard_map/incident/pallas_call | solution.py:315
  16.8 1.6 %collective-permute-start.5 = (bf16[512,128]{1,0:T(8,128)(2,1)S(1)}, bf16[512,128]{1,0:T(8,128)(2,1)S(1)}, u32[]{:S(2)}, u32[]{:S(2)}) collective-permute-start(bf16[512,128]{1,0:T(8,128)(2,1)S(1)} %get-tuple-element.52), channel_id=1, source_target_pairs={{0,1},{1,2},{2,3},{3,0},{4,5},{5,6},{6,7},{7,4},{8,9},{9,10},{10,1... | collective-permute-start | bytes 393224 | tf_op jit(solution)/shard_map/ppermute | solution.py:329
  18.4 0.9 %received.1 = (f32[512,128]{1,0:T(8,128)S(1)}, bf16[512,128]{1,0:T(8,128)(2,1)S(1)}, bf16[512,128]{1,0:T(8,128)(2,1)S(1)}) custom-call(bf16[512,1024]{1,0:T(8,128)(2,1)S(1)} %get-tuple-element.53.po_lit_ref, bf16[2,512,512]{2,1,0:T(8,128)(2,1)S(1)} %copy-done.2), custom_call_target="tpu_custom_call" | custom-call | flops 1 | bytes 1 | tf_op jit(solution)/shard_map/received/pallas_call | solution.py:315
  19.3 1.8 %collective-permute-start.6 = (bf16[512,128]{1,0:T(8,128)(2,1)S(1)}, bf16[512,128]{1,0:T(8,128)(2,1)S(1)}, u32[]{:S(2)}, u32[]{:S(2)}) collective-permute-start(bf16[512,128]{1,0:T(8,128)(2,1)S(1)} %get-tuple-element.57), channel_id=1, source_target_pairs={{0,3},{1,0},{2,1},{3,2},{4,7},{5,4},{6,5},{7,6},{8,11},{9,8},{10,9... | collective-permute-start | bytes 393224 | tf_op jit(solution)/shard_map/ppermute | solution.py:329
  21.1 2.0 %collective-permute-start.7 = (bf16[512,128]{1,0:T(8,128)(2,1)S(1)}, bf16[512,128]{1,0:T(8,128)(2,1)S(1)}, u32[]{:S(2)}, u32[]{:S(2)}) collective-permute-start(bf16[512,128]{1,0:T(8,128)(2,1)S(1)} %get-tuple-element.58), channel_id=1, source_target_pairs={{0,2},{1,3},{2,0},{3,1},{4,6},{5,7},{6,4},{7,5},{8,10},{9,11},{10,... | collective-permute-start | bytes 393224 | tf_op jit(solution)/shard_map/ppermute | solution.py:329
  23.1 3.1 %collective-permute-start.12 = (f32[16,256]{1,0:T(8,128)S(1)}, f32[16,256]{1,0:T(8,128)S(1)}, u32[]{:S(2)}, u32[]{:S(2)}) collective-permute-start(f32[16,256]{1,0:T(8,128)S(1)} %get-tuple-element.59.own_ref), channel_id=1, source_target_pairs={{4,8},{8,4},{12,16},{16,12},{20,24},{24,20},{28,32},{32,28},{36,40... | collective-permute-start | bytes 49160 | tf_op jit(solution)/shard_map/ppermute | solution.py:337
  26.2 0.1 collective-permute-start.11
  26.3 0.0 collective-permute-done.5.new_ref
  26.4 0.4 collective-permute-done.6
  26.8 0.9 %collective-permute-done.7 = bf16[512,128]{1,0:T(8,128)(2,1)S(1)} collective-permute-done((bf16[512,128]{1,0:T(8,128)(2,1)S(1)}, bf16[512,128]{1,0:T(8,128)(2,1)S(1)}, u32[]{:S(2)}, u32[]{:S(2)}) %collective-permute-start.7) | collective-permute-done | bytes 131104 | tf_op jit(solution)/shard_map/ppermute | solution.py:329
  27.7 0.0 copy-start.4
  27.7 0.0 copy-start
  27.8 0.0 copy-start.3
  27.8 2.4 %collective-permute-start.10 = (bf16[512,128]{1,0:T(8,128)(2,1)S(1)}, bf16[512,128]{1,0:T(8,128)(2,1)S(1)}, u32[]{:S(2)}, u32[]{:S(2)}) collective-permute-start(bf16[512,128]{1,0:T(8,128)(2,1)S(1)} %add_convert_fusion.p0_ref), channel_id=1, source_target_pairs={{0,1},{1,2},{2,3},{3,0},{4,5},{5,6},{6,7},{7,4},{8,9},{9,10},{10,1... | collective-permute-start | bytes 393224 | tf_op jit(solution)/shard_map/ppermute | solution.py:329
  30.1 1.1 %collective-permute-start.9 = (bf16[512,128]{1,0:T(8,128)(2,1)S(1)}, bf16[512,128]{1,0:T(8,128)(2,1)S(1)}, u32[]{:S(2)}, u32[]{:S(2)}) collective-permute-start(bf16[512,128]{1,0:T(8,128)(2,1)S(1)} %add_convert_fusion.p0_ref), channel_id=1, source_target_pairs={{0,3},{1,0},{2,1},{3,2},{4,7},{5,4},{6,5},{7,6},{8,11},{9,8},{10,9... | collective-permute-start | bytes 393224 | tf_op jit(solution)/shard_map/ppermute | solution.py:329
  31.3 1.0 %collective-permute-start.8 = (bf16[512,128]{1,0:T(8,128)(2,1)S(1)}, bf16[512,128]{1,0:T(8,128)(2,1)S(1)}, u32[]{:S(2)}, u32[]{:S(2)}) collective-permute-start(bf16[512,128]{1,0:T(8,128)(2,1)S(1)} %add_convert_fusion.p0_ref), channel_id=1, source_target_pairs={{0,2},{1,3},{2,0},{3,1},{4,6},{5,7},{6,4},{7,5},{8,10},{9,11},{10,... | collective-permute-start | bytes 393224 | tf_op jit(solution)/shard_map/ppermute | solution.py:329
  32.3 0.0 collective-permute-done.12.odd_ref
  32.3 0.0 collective-permute-done.11.even_ref
  32.3 2.8 %lists.1 = (bf16[768,512]{1,0:T(8,128)(2,1)S(1)}, f32[2,256,256]{2,1,0:T(8,128)S(1)}, f32[2,256,256]{2,1,0:T(8,128)S(1)}) custom-call(f32[16,256]{1,0:T(8,128)S(1)} %collective-permute-done.11.even_ref, f32[16,256]{1,0:T(8,128)S(1)} %get-tuple-element.59.own_ref, f32[16,256]{1,0:T(8,128)S(1)} %collective-permute-done.12.odd_ref, ...), custom_call_target="tpu_custom_call" | custom-call | flops 4000000000 | bytes 1 | tf_op jit(solution)/shard_map/lists/pallas_call | solution.py:315
  35.1 0.0 collective-permute-done.10.p1_ref
  35.1 0.6 collective-permute-done.9.p3_ref
  35.6 2.4 %collective-permute-done.8.p2_ref = bf16[512,128]{1,0:T(8,128)(2,1)S(1)} collective-permute-done((bf16[512,128]{1,0:T(8,128)(2,1)S(1)}, bf16[512,128]{1,0:T(8,128)(2,1)S(1)}, u32[]{:S(2)}, u32[]{:S(2)}) %collective-permute-start.8) | collective-permute-done | bytes 131104 | tf_op jit(solution)/shard_map/ppermute | solution.py:329
  38.0 1.8 %scattered.1 = (bf16[512,1024]{1,0:T(8,128)(2,1)S(1)}, bf16[4,256,128]{2,1,0:T(8,128)(2,1)S(1)}) custom-call(bf16[512,128]{1,0:T(8,128)(2,1)S(1)} %add_convert_fusion.p0_ref, bf16[512,128]{1,0:T(8,128)(2,1)S(1)} %collective-permute-done.8.p2_ref, bf16[512,128]{1,0:T(8,128)(2,1)S(1)} %collective-permute-done.9.p3_ref, ...), custom_call_target="tpu_custom_call" | custom-call | flops 1 | bytes 1 | tf_op jit(solution)/shard_map/scattered/pallas_call | solution.py:315
  39.9 2.8 %collective-permute-start.14 = (bf16[4,256,128]{2,1,0:T(8,128)(2,1)S(1)}, bf16[4,256,128]{2,1,0:T(8,128)(2,1)S(1)}, u32[]{:S(2)}, u32[]{:S(2)}) collective-permute-start(bf16[4,256,128]{2,1,0:T(8,128)(2,1)S(1)} %get-tuple-element.64), channel_id=1, source_target_pairs={{4,8},{8,4},{12,16},{16,12},{20,24},{24,20},{28,32},{32,28},{36,40... | collective-permute-start | bytes 786440 | tf_op jit(solution)/shard_map/ppermute | solution.py:337
  42.6 1.2 %tested_even.1 = bf16[4,256,128]{2,1,0:T(8,128)(2,1)S(1)} custom-call(bf16[512,1024]{1,0:T(8,128)(2,1)S(1)} %get-tuple-element.65.refs_0_, bf16[2,512,512]{2,1,0:T(8,128)(2,1)S(1)} %copy-done, bf16[768,512]{1,0:T(8,128)(2,1)S(1)} %get-tuple-element.60.pick_ref.refs_2_, f32[2,256,256]{2,1,0:T(8,128)S(1)} %get-tuple-element.62.refs_3_, ...), custom_call_target="tpu_custom_call" | custom-call | flops 1 | bytes 1 | tf_op jit(solution)/shard_map/tested_even/pallas_call | solution.py:315
  43.8 0.1 collective-permute-start.13
  43.9 1.2 %tested_own.1.own_ref = f32[4,256,128]{2,1,0:T(8,128)S(1)} custom-call(bf16[512,1024]{1,0:T(8,128)(2,1)S(1)} %get-tuple-element.65.refs_0_, bf16[2,512,512]{2,1,0:T(8,128)(2,1)S(1)} %copy-done, bf16[768,512]{1,0:T(8,128)(2,1)S(1)} %get-tuple-element.60.pick_ref.refs_2_, f32[2,256,256]{2,1,0:T(8,128)S(1)} %get-tuple-element.66.refs_3_, ...), custom_call_target="tpu_custom_call" | custom-call | flops 1 | bytes 1 | tf_op jit(solution)/shard_map/tested_own/pallas_call | solution.py:315
  45.2 4.5 %collective-permute-done.14.new_ref = bf16[4,256,128]{2,1,0:T(8,128)(2,1)S(1)} collective-permute-done((bf16[4,256,128]{2,1,0:T(8,128)(2,1)S(1)}, bf16[4,256,128]{2,1,0:T(8,128)(2,1)S(1)}, u32[]{:S(2)}, u32[]{:S(2)}) %collective-permute-start.14) | collective-permute-done | bytes 262176 | tf_op jit(solution)/shard_map/ppermute | solution.py:337
  49.7 0.0 collective-permute-done.13.even_ref
  49.8 1.0 %collective-permute-start.15 = (bf16[256,128]{1,0:T(8,128)(2,1)S(1)}, bf16[256,128]{1,0:T(8,128)(2,1)S(1)}, u32[]{:S(2)}, u32[]{:S(2)}) collective-permute-start(bf16[256,128]{1,0:T(8,128)(2,1)S(1)} %get-tuple-element.69), channel_id=1, source_target_pairs={{0,1},{1,2},{2,3},{3,0},{4,5},{5,6},{6,7},{7,4},{8,9},{9,10},{10,1... | collective-permute-start | bytes 196616 | tf_op jit(solution)/shard_map/ppermute | solution.py:329
  50.7 2.3 %collective-permute-start.16 = (bf16[256,128]{1,0:T(8,128)(2,1)S(1)}, bf16[256,128]{1,0:T(8,128)(2,1)S(1)}, u32[]{:S(2)}, u32[]{:S(2)}) collective-permute-start(bf16[256,128]{1,0:T(8,128)(2,1)S(1)} %get-tuple-element.70), channel_id=1, source_target_pairs={{0,2},{1,3},{2,0},{3,1},{4,6},{5,7},{6,4},{7,5},{8,10},{9,11},{10,... | collective-permute-start | bytes 196616 | tf_op jit(solution)/shard_map/ppermute | solution.py:329
  53.1 0.7 %collective-permute-start.17 = (bf16[256,128]{1,0:T(8,128)(2,1)S(1)}, bf16[256,128]{1,0:T(8,128)(2,1)S(1)}, u32[]{:S(2)}, u32[]{:S(2)}) collective-permute-start(bf16[256,128]{1,0:T(8,128)(2,1)S(1)} %get-tuple-element.71), channel_id=1, source_target_pairs={{0,3},{1,0},{2,1},{3,2},{4,7},{5,4},{6,5},{7,6},{8,11},{9,8},{10,9... | collective-permute-start | bytes 196616 | tf_op jit(solution)/shard_map/ppermute | solution.py:329
  53.8 1.5 %collective-permute-done.15 = bf16[256,128]{1,0:T(8,128)(2,1)S(1)} collective-permute-done((bf16[256,128]{1,0:T(8,128)(2,1)S(1)}, bf16[256,128]{1,0:T(8,128)(2,1)S(1)}, u32[]{:S(2)}, u32[]{:S(2)}) %collective-permute-start.15) | collective-permute-done | bytes 65568 | tf_op jit(solution)/shard_map/ppermute | solution.py:329
  55.3 1.2 %collective-permute-done.16 = bf16[256,128]{1,0:T(8,128)(2,1)S(1)} collective-permute-done((bf16[256,128]{1,0:T(8,128)(2,1)S(1)}, bf16[256,128]{1,0:T(8,128)(2,1)S(1)}, u32[]{:S(2)}, u32[]{:S(2)}) %collective-permute-start.16) | collective-permute-done | bytes 65568 | tf_op jit(solution)/shard_map/ppermute | solution.py:329
  56.5 0.8 %collective-permute-done.17 = bf16[256,128]{1,0:T(8,128)(2,1)S(1)} collective-permute-done((bf16[256,128]{1,0:T(8,128)(2,1)S(1)}, bf16[256,128]{1,0:T(8,128)(2,1)S(1)}, u32[]{:S(2)}, u32[]{:S(2)}) %collective-permute-start.17) | collective-permute-done | bytes 65568 | tf_op jit(solution)/shard_map/ppermute | solution.py:329
  57.3 0.7 %convert_add_fusion = f32[256,128]{1,0:T(8,128)} fusion(bf16[256,128]{1,0:T(8,128)(2,1)S(1)} %collective-permute-done.17, bf16[256,128]{1,0:T(8,128)(2,1)S(1)} %collective-permute-done.16, f32[256,128]{1,0:T(8,128)S(1)} %get-tuple-element.68, bf16[256,128]{1,0:T(8,128)(2,1)S(1)} %collective-permute-done.15), kind=kLoop, calls=%fused_computation.1 | loop fusion | flops 196608 | bytes 458752 | tf_op jit(solution)/shard_map/add | solution.py:429
  (11 shorter events, 0.2 us)
Async XLA Ops:
  0.6 13.5 %collective-permute-start = (bf16[256,512]{1,0:T(8,128)(2,1)}, bf16[256,512]{1,0:T(8,128)(2,1)S(1)}, u32[]{:S(2)}, u32[]{:S(2)}) collective-permute-start(bf16[256,512]{1,0:T(8,128)(2,1)} %current_hbm.1), channel_id=1, source_target_pairs={{4,8},{8,4},{12,16},{16,12},{20,24},{24,20},{28,32},{32,28},{36,40... | collective-permute-start | bytes 786440 | tf_op jit(solution)/shard_map/ppermute | solution.py:337
  8.1 6.0 %copy-start.1 = (bf16[2,512,512]{2,1,0:T(8,128)(2,1)S(1)}, bf16[2,512,512]{2,1,0:T(8,128)(2,1)}, u32[]{:S(2)}) copy-start(bf16[2,512,512]{2,1,0:T(8,128)(2,1)} %radiate_ref.2) | copy-start | bytes 3145732
  8.1 6.0 %copy-start.2 = (bf16[2,512,512]{2,1,0:T(8,128)(2,1)S(1)}, bf16[2,512,512]{2,1,0:T(8,128)(2,1)}, u32[]{:S(2)}) copy-start(bf16[2,512,512]{2,1,0:T(8,128)(2,1)} %receive_ref.4) | copy-start | bytes 3145732
  10.2 3.8 %collective-permute-start.1 = (bf16[256,256]{1,0:T(8,128)(2,1)S(1)}, bf16[256,256]{1,0:T(8,128)(2,1)S(1)}, u32[]{:S(2)}, u32[]{:S(2)}) collective-permute-start(bf16[256,256]{1,0:T(8,128)(2,1)S(1)} %get-tuple-element.37.w0), channel_id=1, source_target_pairs={{0,4},{4,0},{8,12},{12,8},{16,20},{20,16},{24,28},{28,24},{32,36},... | collective-permute-start | bytes 393224 | tf_op jit(solution)/shard_map/ppermute | solution.py:333
  10.3 3.8 %collective-permute-start.2 = (bf16[256,256]{1,0:T(8,128)(2,1)S(1)}, bf16[256,256]{1,0:T(8,128)(2,1)S(1)}, u32[]{:S(2)}, u32[]{:S(2)}) collective-permute-start(bf16[256,256]{1,0:T(8,128)(2,1)S(1)} %get-tuple-element.38.w1), channel_id=1, source_target_pairs={{0,4},{4,0},{8,12},{12,8},{16,20},{20,16},{24,28},{28,24},{32,36},... | collective-permute-start | bytes 393224 | tf_op jit(solution)/shard_map/ppermute | solution.py:333
  10.8 3.3 %collective-permute-start.3 = (bf16[256,256]{1,0:T(8,128)(2,1)S(1)}, bf16[256,256]{1,0:T(8,128)(2,1)S(1)}, u32[]{:S(2)}, u32[]{:S(2)}) collective-permute-start(bf16[256,256]{1,0:T(8,128)(2,1)S(1)} %get-tuple-element.39.w2), channel_id=1, source_target_pairs={{0,4},{4,0},{8,12},{12,8},{16,20},{20,16},{24,28},{28,24},{32,36},... | collective-permute-start | bytes 393224 | tf_op jit(solution)/shard_map/ppermute | solution.py:333
  10.9 3.2 %collective-permute-start.4 = (bf16[256,256]{1,0:T(8,128)(2,1)S(1)}, bf16[256,256]{1,0:T(8,128)(2,1)S(1)}, u32[]{:S(2)}, u32[]{:S(2)}) collective-permute-start(bf16[256,256]{1,0:T(8,128)(2,1)S(1)} %get-tuple-element.40.w3), channel_id=1, source_target_pairs={{0,4},{4,0},{8,12},{12,8},{16,20},{20,16},{24,28},{28,24},{32,36},... | collective-permute-start | bytes 393224 | tf_op jit(solution)/shard_map/ppermute | solution.py:333
  16.8 9.5 %collective-permute-start.5 = (bf16[512,128]{1,0:T(8,128)(2,1)S(1)}, bf16[512,128]{1,0:T(8,128)(2,1)S(1)}, u32[]{:S(2)}, u32[]{:S(2)}) collective-permute-start(bf16[512,128]{1,0:T(8,128)(2,1)S(1)} %get-tuple-element.52), channel_id=1, source_target_pairs={{0,1},{1,2},{2,3},{3,0},{4,5},{5,6},{6,7},{7,4},{8,9},{9,10},{10,1... | collective-permute-start | bytes 393224 | tf_op jit(solution)/shard_map/ppermute | solution.py:329
  19.3 7.4 %collective-permute-start.6 = (bf16[512,128]{1,0:T(8,128)(2,1)S(1)}, bf16[512,128]{1,0:T(8,128)(2,1)S(1)}, u32[]{:S(2)}, u32[]{:S(2)}) collective-permute-start(bf16[512,128]{1,0:T(8,128)(2,1)S(1)} %get-tuple-element.57), channel_id=1, source_target_pairs={{0,3},{1,0},{2,1},{3,2},{4,7},{5,4},{6,5},{7,6},{8,11},{9,8},{10,9... | collective-permute-start | bytes 393224 | tf_op jit(solution)/shard_map/ppermute | solution.py:329
  21.1 6.5 %collective-permute-start.7 = (bf16[512,128]{1,0:T(8,128)(2,1)S(1)}, bf16[512,128]{1,0:T(8,128)(2,1)S(1)}, u32[]{:S(2)}, u32[]{:S(2)}) collective-permute-start(bf16[512,128]{1,0:T(8,128)(2,1)S(1)} %get-tuple-element.58), channel_id=1, source_target_pairs={{0,2},{1,3},{2,0},{3,1},{4,6},{5,7},{6,4},{7,5},{8,10},{9,11},{10,... | collective-permute-start | bytes 393224 | tf_op jit(solution)/shard_map/ppermute | solution.py:329
  23.1 9.2 %collective-permute-start.12 = (f32[16,256]{1,0:T(8,128)S(1)}, f32[16,256]{1,0:T(8,128)S(1)}, u32[]{:S(2)}, u32[]{:S(2)}) collective-permute-start(f32[16,256]{1,0:T(8,128)S(1)} %get-tuple-element.59.own_ref), channel_id=1, source_target_pairs={{4,8},{8,4},{12,16},{16,12},{20,24},{24,20},{28,32},{32,28},{36,40... | collective-permute-start | bytes 49160 | tf_op jit(solution)/shard_map/ppermute | solution.py:337
  26.2 6.1 %collective-permute-start.11 = (f32[16,256]{1,0:T(8,128)S(1)}, f32[16,256]{1,0:T(8,128)S(1)}, u32[]{:S(2)}, u32[]{:S(2)}) collective-permute-start(f32[16,256]{1,0:T(8,128)S(1)} %get-tuple-element.59.own_ref), channel_id=1, source_target_pairs={{0,4},{4,0},{8,12},{12,8},{16,20},{20,16},{24,28},{28,24},{32,36},... | collective-permute-start | bytes 49160 | tf_op jit(solution)/shard_map/ppermute | solution.py:333
  27.7 10.3 %copy-start.4 = (bf16[512,128]{1,0:T(8,128)(2,1)}, bf16[512,128]{1,0:T(8,128)(2,1)S(1)}, u32[]{:S(2)}) copy-start(bf16[512,128]{1,0:T(8,128)(2,1)S(1)} %add_convert_fusion.p0_ref) | copy-start | bytes 393220
  27.7 10.3 %copy-start = (bf16[2,512,512]{2,1,0:T(8,128)(2,1)S(1)}, bf16[2,512,512]{2,1,0:T(8,128)(2,1)}, u32[]{:S(2)}) copy-start(bf16[2,512,512]{2,1,0:T(8,128)(2,1)} %refs_1_.3) | copy-start | bytes 3145732
  27.8 10.3 %copy-start.3 = (bf16[2,512,512]{2,1,0:T(8,128)(2,1)S(1)}, bf16[2,512,512]{2,1,0:T(8,128)(2,1)}, u32[]{:S(2)}) copy-start(bf16[2,512,512]{2,1,0:T(8,128)(2,1)} %radiate_ref.3) | copy-start | bytes 3145732
  27.8 7.3 %collective-permute-start.10 = (bf16[512,128]{1,0:T(8,128)(2,1)S(1)}, bf16[512,128]{1,0:T(8,128)(2,1)S(1)}, u32[]{:S(2)}, u32[]{:S(2)}) collective-permute-start(bf16[512,128]{1,0:T(8,128)(2,1)S(1)} %add_convert_fusion.p0_ref), channel_id=1, source_target_pairs={{0,1},{1,2},{2,3},{3,0},{4,5},{5,6},{6,7},{7,4},{8,9},{9,10},{10,1... | collective-permute-start | bytes 393224 | tf_op jit(solution)/shard_map/ppermute | solution.py:329
  30.1 5.5 %collective-permute-start.9 = (bf16[512,128]{1,0:T(8,128)(2,1)S(1)}, bf16[512,128]{1,0:T(8,128)(2,1)S(1)}, u32[]{:S(2)}, u32[]{:S(2)}) collective-permute-start(bf16[512,128]{1,0:T(8,128)(2,1)S(1)} %add_convert_fusion.p0_ref), channel_id=1, source_target_pairs={{0,3},{1,0},{2,1},{3,2},{4,7},{5,4},{6,5},{7,6},{8,11},{9,8},{10,9... | collective-permute-start | bytes 393224 | tf_op jit(solution)/shard_map/ppermute | solution.py:329
  31.3 6.7 %collective-permute-start.8 = (bf16[512,128]{1,0:T(8,128)(2,1)S(1)}, bf16[512,128]{1,0:T(8,128)(2,1)S(1)}, u32[]{:S(2)}, u32[]{:S(2)}) collective-permute-start(bf16[512,128]{1,0:T(8,128)(2,1)S(1)} %add_convert_fusion.p0_ref), channel_id=1, source_target_pairs={{0,2},{1,3},{2,0},{3,1},{4,6},{5,7},{6,4},{7,5},{8,10},{9,11},{10,... | collective-permute-start | bytes 393224 | tf_op jit(solution)/shard_map/ppermute | solution.py:329
  39.9 9.8 %collective-permute-start.14 = (bf16[4,256,128]{2,1,0:T(8,128)(2,1)S(1)}, bf16[4,256,128]{2,1,0:T(8,128)(2,1)S(1)}, u32[]{:S(2)}, u32[]{:S(2)}) collective-permute-start(bf16[4,256,128]{2,1,0:T(8,128)(2,1)S(1)} %get-tuple-element.64), channel_id=1, source_target_pairs={{4,8},{8,4},{12,16},{16,12},{20,24},{24,20},{28,32},{32,28},{36,40... | collective-permute-start | bytes 786440 | tf_op jit(solution)/shard_map/ppermute | solution.py:337
  43.8 5.9 %collective-permute-start.13 = (bf16[4,256,128]{2,1,0:T(8,128)(2,1)S(1)}, bf16[4,256,128]{2,1,0:T(8,128)(2,1)S(1)}, u32[]{:S(2)}, u32[]{:S(2)}) collective-permute-start(bf16[4,256,128]{2,1,0:T(8,128)(2,1)S(1)} %tested_even.1), channel_id=1, source_target_pairs={{0,4},{4,0},{8,12},{12,8},{16,20},{20,16},{24,28},{28,24},{32,36},... | collective-permute-start | bytes 786440 | tf_op jit(solution)/shard_map/ppermute | solution.py:333
  49.8 5.6 %collective-permute-start.15 = (bf16[256,128]{1,0:T(8,128)(2,1)S(1)}, bf16[256,128]{1,0:T(8,128)(2,1)S(1)}, u32[]{:S(2)}, u32[]{:S(2)}) collective-permute-start(bf16[256,128]{1,0:T(8,128)(2,1)S(1)} %get-tuple-element.69), channel_id=1, source_target_pairs={{0,1},{1,2},{2,3},{3,0},{4,5},{5,6},{6,7},{7,4},{8,9},{9,10},{10,1... | collective-permute-start | bytes 196616 | tf_op jit(solution)/shard_map/ppermute | solution.py:329
  50.7 5.8 %collective-permute-start.16 = (bf16[256,128]{1,0:T(8,128)(2,1)S(1)}, bf16[256,128]{1,0:T(8,128)(2,1)S(1)}, u32[]{:S(2)}, u32[]{:S(2)}) collective-permute-start(bf16[256,128]{1,0:T(8,128)(2,1)S(1)} %get-tuple-element.70), channel_id=1, source_target_pairs={{0,2},{1,3},{2,0},{3,1},{4,6},{5,7},{6,4},{7,5},{8,10},{9,11},{10,... | collective-permute-start | bytes 196616 | tf_op jit(solution)/shard_map/ppermute | solution.py:329
  53.1 4.3 %collective-permute-start.17 = (bf16[256,128]{1,0:T(8,128)(2,1)S(1)}, bf16[256,128]{1,0:T(8,128)(2,1)S(1)}, u32[]{:S(2)}, u32[]{:S(2)}) collective-permute-start(bf16[256,128]{1,0:T(8,128)(2,1)S(1)} %get-tuple-element.71), channel_id=1, source_target_pairs={{0,3},{1,0},{2,1},{3,2},{4,7},{5,4},{6,5},{7,6},{8,11},{9,8},{10,9... | collective-permute-start | bytes 196616 | tf_op jit(solution)/shard_map/ppermute | solution.py:329

commit v10 on v9

--- a/solution.py
+++ b/solution.py
@@ -187,13 +187,11 @@
 
 def incident(
     odd_ref, e0, e1, e2, e3, w0, w1, w2, w3, pick_ref, radiate_ref, receive_ref, odd_cos, odd_sin, po_cos, po_sin, lit_ref,
-    first_ref, po_lit_ref,
-    table,
+    own_ref, s1_ref, s2_ref, s3_ref,
+    table, chunks,
 ):
-    cone = lax.axis_index("cone")
-    count = lax.axis_size("cone")
     m = odd_ref.shape[0]
-    q, share = first_ref.shape
+    q = own_ref.shape[0]
     cones, _, k2 = radiate_ref.shape
     k = k2 // 2
     side = parity() * 2 * m
@@ -203,30 +201,17 @@
             table[rows_at(2 * m - side, at), i * k : (i + 1) * k] = e_ref[at]
         radiated(odd_ref, at, radiate_ref, odd_cos, odd_sin, table, side, 0)
     lit_col = jnp.concatenate([lit_ref[...].astype(F32), jnp.zeros((8 - cones, q), F32)], axis=0).T
-    columns = pl.ds(pl.multiple_of(lax.rem(cone + 1, count) * share, share), share)
     for at in tiles(q):
         total = None
         for c in range(cones):
             value = mm(pick_ref[at], table[:, c * k2 : (c + 1) * k2])
             mask = lit_col[at, c : c + 1]
             re, im = rotated(value, po_cos[c, at] * mask, po_sin[c, at] * mask, 1)
-            re, im = re.astype(BF), im.astype(BF)
-            po_lit_ref[at, c * k2 : c * k2 + k] = re
-            po_lit_ref[at, c * k2 + k : (c + 1) * k2] = im
-            part = mm(re, receive_ref[c, :k, columns]) + mm(im, receive_ref[c, k:, columns])
-            total = part if total is None else total + part
-        first_ref[at] = total.astype(BF)
-
-
-def received(po_lit_ref, receive_ref, own_ref, s2_ref, s3_ref, chunks):
-    cones, k2, n = receive_ref.shape
-    for at in tiles(po_lit_ref.shape[0]):
-        total = None
-        for c in range(cones):
-            part = mm(po_lit_ref[at, c * k2 : (c + 1) * k2], receive_ref[c])
+            part = mm(re.astype(BF), receive_ref[c, :k]) + mm(im.astype(BF), receive_ref[c, k:])
             total = part if total is None else total + part
         put_chunks(chunks, at, total)
     own_ref[...] = chunks[0]
+    s1_ref[...] = chunks[1].astype(BF)
     s2_ref[...] = chunks[2].astype(BF)
     s3_ref[...] = chunks[3].astype(BF)
 
@@ -374,19 +359,13 @@
         angles + (shape((cones, q, k), F32),) * 2 + (shape((q, 3 * m), BF),),
         (waves3, odd_c, po_c, src, weight),
     )
-    s1, po_lit = call(
+    own, s1, s2, s3 = call(
         incident,
-        (shape((q, share), BF), shape((q, width), BF)),
+        (shape((q, share), F32),) + (shape((q, share), BF),) * 3,
         (odd, *even_parts, *own_parts, pick, mom_radiate, po_receive, odd_cos, odd_sin, po_cos, po_sin, lit),
-        (pltpu.VMEM((3 * m, width), BF),),
+        (pltpu.VMEM((3 * m, width), BF), pltpu.VMEM((count, q, share), F32)),
     )
     s1 = turned(s1, 1)
-    own, s2, s3 = call(
-        received,
-        (shape((q, share), F32), shape((q, share), BF), shape((q, share), BF)),
-        (po_lit, po_receive),
-        (pltpu.VMEM((count, q, share), F32),),
-    )
     s2 = turned(s2, 2)
     s3 = turned(s3, 3)
     own, entries = lax.optimization_barrier((own, entries))

time: 58.2 us -> 58.3 us (level)
  waiting for transfers between devices: 12.3 us -> 15.2 us
  starting transfers between devices: 28.6 us -> 26.3 us
    ppermute x9, waiting for transfers between devices: 7.74 us -> 9.95 us  [turned(): lax.ppermute(value, 'cone', [(i, (i + shift) % count) for i in range(coun...]
    ppermute x9, starting transfers between devices: 13.9 us -> 12.4 us  [turned(): lax.ppermute(value, 'cone', [(i, (i + shift) % count) for i in range(coun...]
    ppermute x3, starting transfers between devices: 13.4 us -> 12.6 us  [swapped_odd(): lax.ppermute(value, 'box', [(i, (i + 1 ^ 1) - 1) for i in range(1, lax.ax...]
    ppermute x3, waiting for transfers between devices: 4.51 us -> 5.27 us  [swapped_odd(): lax.ppermute(value, 'box', [(i, (i + 1 ^ 1) - 1) for i in range(1, lax.ax...]
    pallas_call x11 -> x10, Pallas kernels: 15.5 us -> 15 us  [call(): pl.pallas_call(body, out_shape=outs, in_specs=[pl.BlockSpec(memory_space=...]
  transfers between devices with their start and end apart: 18 -> 18, of which waited for: 8 -> 8; matrix products, arithmetic and copies ran while one was open for 0% -> 0% of each run, Pallas kernels for 19% -> 17%
where the time goes in v10:
time: 58.3 us; the launch traced here: 58.2 us
  starting transfers between devices  26.3 us (45%)
  waiting for transfers between devices  15.2 us (26%)
  Pallas kernels  15 us (26%)
  between operations  0.88 us (2%)
  other arithmetic  0.74 us (1%)
    pallas_call x10, Pallas kernels, call(): pl.pallas_call(body, out_shape=outs, in_specs=[pl.BlockSpec(memory_space=...  15 us
    ppermute x3, starting transfers between devices, swapped_odd(): lax.ppermute(value, 'box', [(i, (i + 1 ^ 1) - 1) for i in range(1, lax.ax...  12.6 us
    ppermute x9, starting transfers between devices, turned(): lax.ppermute(value, 'cone', [(i, (i + shift) % count) for i in range(coun...  12.4 us
    ppermute x9, waiting for transfers between devices, turned(): lax.ppermute(value, 'cone', [(i, (i + shift) % count) for i in range(coun...  9.95 us
    ppermute x3, waiting for transfers between devices, swapped_odd(): lax.ppermute(value, 'box', [(i, (i + 1 ^ 1) - 1) for i in range(1, lax.ax...  5.27 us
    ppermute x6, starting transfers between devices, swapped_even(): lax.ppermute(value, 'box', [(i, i ^ 1) for i in range(lax.axis_size('box'...  1.28 us
  transfers between devices with their start and end apart: 18, of which 8 were waited for; matrix products, arithmetic and copies ran while one was open for 0% of the time, Pallas kernels for 17%

profile of v10, /device:TPU:6, one launch (start us, length us, event | category | flops | bytes accessed | tf_op | source)
XLA Modules:
  0.0 58.2 jit_solution(14415103920247195955)
XLA Ops:
  0.6 7.5 %collective-permute-start = (bf16[256,512]{1,0:T(8,128)(2,1)}, bf16[256,512]{1,0:T(8,128)(2,1)S(1)}, u32[]{:S(2)}, u32[]{:S(2)}) collective-permute-start(bf16[256,512]{1,0:T(8,128)(2,1)} %current_hbm.1), channel_id=1, source_target_pairs={{4,8},{8,4},{12,16},{16,12},{20,24},{24,20},{28,32},{32,28},{36,40... | collective-permute-start | bytes 786440 | tf_op jit(solution)/shard_map/ppermute | solution.py:322
  8.1 2.1 %own_waves.1 = (f32[2,256,256]{2,1,0:T(8,128)S(1)}, f32[2,256,256]{2,1,0:T(8,128)S(1)}, f32[3,2,256]{2,1,0:T(2,128)S(1)}, f32[3,256]{1,0:T(4,128)S(1)}, f32[3,51...) custom-call(bf16[256,512]{1,0:T(8,128)(2,1)} %current_hbm.1, ...), custom_call_target="tpu_custom_call" | custom-call | flops 1 | bytes 1 | tf_op jit(solution)/shard_map/own_waves/pallas_call | solution.py:300
  10.2 0.1 collective-permute-start.1
  10.3 0.5 collective-permute-start.2
  10.8 0.1 collective-permute-start.3
  10.9 0.4 collective-permute-start.4
  11.3 2.7 %prepare.1 = (f32[2,256,256]{2,1,0:T(8,128)S(1)}, f32[2,256,256]{2,1,0:T(8,128)S(1)}, f32[2,512,256]{2,1,0:T(8,128)S(1)}, f32[2,512,256]{2,1,0:T(8,128)S(1)}, bf16[512,768]{1,0:T(8,128)(2,1)S(1)}) custom-call(f32[3,2,256]{2,1,0:T(2,128)S(1)} %get-tuple-element.40.dirs_ref, f32[3,256]{1,0:T(4,128)S(1)} %get-tuple-element.41.mom_c, ...), custom_call_target="tpu_custom_call" | custom-call | flops 1 | bytes 1 | tf_op jit(solution)/shard_map/prepare/pallas_call | solution.py:300
  14.0 0.0 collective-permute-done.1.e0
  14.0 0.0 collective-permute-done.2.e1
  14.1 0.0 collective-permute-done.3.e2
  14.1 0.0 collective-permute-done.4.e3
  14.1 0.0 collective-permute-done.odd_ref
  14.1 0.0 copy-done.1
  14.1 3.1 %incident.1 = (f32[512,128]{1,0:T(8,128)S(1)}, bf16[512,128]{1,0:T(8,128)(2,1)S(1)}, bf16[512,128]{1,0:T(8,128)(2,1)S(1)}, bf16[512,128]{1,0:T(8,128)(2,1)S(1)}) custom-call(bf16[256,512]{1,0:T(8,128)(2,1)S(1)} %collective-permute-done.odd_ref, bf16[256,256]{1,0:T(8,128)(2,1)S(1)} %collective-permute-done.1.e0, ...), custom_call_target="tpu_custom_call" | custom-call | flops 1 | bytes 1 | tf_op jit(solution)/shard_map/incident/pallas_call | solution.py:300
  17.2 1.7 %collective-permute-start.5 = (bf16[512,128]{1,0:T(8,128)(2,1)S(1)}, bf16[512,128]{1,0:T(8,128)(2,1)S(1)}, u32[]{:S(2)}, u32[]{:S(2)}) collective-permute-start(bf16[512,128]{1,0:T(8,128)(2,1)S(1)} %get-tuple-element.51), channel_id=1, source_target_pairs={{0,1},{1,2},{2,3},{3,0},{4,5},{5,6},{6,7},{7,4},{8,9},{9,10},{10,1... | collective-permute-start | bytes 393224 | tf_op jit(solution)/shard_map/ppermute | solution.py:314
  18.9 1.6 %collective-permute-start.6 = (bf16[512,128]{1,0:T(8,128)(2,1)S(1)}, bf16[512,128]{1,0:T(8,128)(2,1)S(1)}, u32[]{:S(2)}, u32[]{:S(2)}) collective-permute-start(bf16[512,128]{1,0:T(8,128)(2,1)S(1)} %get-tuple-element.55), channel_id=1, source_target_pairs={{0,3},{1,0},{2,1},{3,2},{4,7},{5,4},{6,5},{7,6},{8,11},{9,8},{10,9... | collective-permute-start | bytes 393224 | tf_op jit(solution)/shard_map/ppermute | solution.py:314
  20.5 2.0 %collective-permute-start.7 = (bf16[512,128]{1,0:T(8,128)(2,1)S(1)}, bf16[512,128]{1,0:T(8,128)(2,1)S(1)}, u32[]{:S(2)}, u32[]{:S(2)}) collective-permute-start(bf16[512,128]{1,0:T(8,128)(2,1)S(1)} %get-tuple-element.56), channel_id=1, source_target_pairs={{0,2},{1,3},{2,0},{3,1},{4,6},{5,7},{6,4},{7,5},{8,10},{9,11},{10,... | collective-permute-start | bytes 393224 | tf_op jit(solution)/shard_map/ppermute | solution.py:314
  22.6 3.1 %collective-permute-start.12 = (f32[16,256]{1,0:T(8,128)S(1)}, f32[16,256]{1,0:T(8,128)S(1)}, u32[]{:S(2)}, u32[]{:S(2)}) collective-permute-start(f32[16,256]{1,0:T(8,128)S(1)} %get-tuple-element.57.own_ref), channel_id=1, source_target_pairs={{4,8},{8,4},{12,16},{16,12},{20,24},{24,20},{28,32},{32,28},{36,40... | collective-permute-start | bytes 49160 | tf_op jit(solution)/shard_map/ppermute | solution.py:322
  25.7 0.1 collective-permute-start.11
  25.8 0.0 collective-permute-done.5.new_ref
  25.9 0.4 collective-permute-done.6
  26.3 1.8 %collective-permute-done.7 = bf16[512,128]{1,0:T(8,128)(2,1)S(1)} collective-permute-done((bf16[512,128]{1,0:T(8,128)(2,1)S(1)}, bf16[512,128]{1,0:T(8,128)(2,1)S(1)}, u32[]{:S(2)}, u32[]{:S(2)}) %collective-permute-start.7) | collective-permute-done | bytes 131104 | tf_op jit(solution)/shard_map/ppermute | solution.py:314
  28.2 0.0 copy-start.4
  28.2 0.0 copy-start
  28.2 0.0 copy-start.3
  28.2 1.2 %collective-permute-start.10 = (bf16[512,128]{1,0:T(8,128)(2,1)S(1)}, bf16[512,128]{1,0:T(8,128)(2,1)S(1)}, u32[]{:S(2)}, u32[]{:S(2)}) collective-permute-start(bf16[512,128]{1,0:T(8,128)(2,1)S(1)} %add_convert_fusion.p0_ref), channel_id=1, source_target_pairs={{0,1},{1,2},{2,3},{3,0},{4,5},{5,6},{6,7},{7,4},{8,9},{9,10},{10,1... | collective-permute-start | bytes 393224 | tf_op jit(solution)/shard_map/ppermute | solution.py:314
  29.4 2.1 %collective-permute-start.9 = (bf16[512,128]{1,0:T(8,128)(2,1)S(1)}, bf16[512,128]{1,0:T(8,128)(2,1)S(1)}, u32[]{:S(2)}, u32[]{:S(2)}) collective-permute-start(bf16[512,128]{1,0:T(8,128)(2,1)S(1)} %add_convert_fusion.p0_ref), channel_id=1, source_target_pairs={{0,3},{1,0},{2,1},{3,2},{4,7},{5,4},{6,5},{7,6},{8,11},{9,8},{10,9... | collective-permute-start | bytes 393224 | tf_op jit(solution)/shard_map/ppermute | solution.py:314
  31.5 0.2 collective-permute-start.8
  31.7 0.0 collective-permute-done.12.odd_ref
  31.8 0.0 collective-permute-done.11.even_ref
  31.8 2.8 %lists.1 = (bf16[768,512]{1,0:T(8,128)(2,1)S(1)}, f32[2,256,256]{2,1,0:T(8,128)S(1)}, f32[2,256,256]{2,1,0:T(8,128)S(1)}) custom-call(f32[16,256]{1,0:T(8,128)S(1)} %collective-permute-done.11.even_ref, f32[16,256]{1,0:T(8,128)S(1)} %get-tuple-element.57.own_ref, f32[16,256]{1,0:T(8,128)S(1)} %collective-permute-done.12.odd_ref, ...), custom_call_target="tpu_custom_call" | custom-call | flops 4000000000 | bytes 1 | tf_op jit(solution)/shard_map/lists/pallas_call | solution.py:300
  34.5 0.0 collective-permute-done.10.p1_ref
  34.6 1.7 %collective-permute-done.9.p3_ref = bf16[512,128]{1,0:T(8,128)(2,1)S(1)} collective-permute-done((bf16[512,128]{1,0:T(8,128)(2,1)S(1)}, bf16[512,128]{1,0:T(8,128)(2,1)S(1)}, u32[]{:S(2)}, u32[]{:S(2)}) %collective-permute-start.9) | collective-permute-done | bytes 131104 | tf_op jit(solution)/shard_map/ppermute | solution.py:314
  36.2 1.7 %collective-permute-done.8.p2_ref = bf16[512,128]{1,0:T(8,128)(2,1)S(1)} collective-permute-done((bf16[512,128]{1,0:T(8,128)(2,1)S(1)}, bf16[512,128]{1,0:T(8,128)(2,1)S(1)}, u32[]{:S(2)}, u32[]{:S(2)}) %collective-permute-start.8) | collective-permute-done | bytes 131104 | tf_op jit(solution)/shard_map/ppermute | solution.py:314
  38.0 1.8 %scattered.1 = (bf16[512,1024]{1,0:T(8,128)(2,1)S(1)}, bf16[4,256,128]{2,1,0:T(8,128)(2,1)S(1)}) custom-call(bf16[512,128]{1,0:T(8,128)(2,1)S(1)} %add_convert_fusion.p0_ref, bf16[512,128]{1,0:T(8,128)(2,1)S(1)} %collective-permute-done.8.p2_ref, bf16[512,128]{1,0:T(8,128)(2,1)S(1)} %collective-permute-done.9.p3_ref, ...), custom_call_target="tpu_custom_call" | custom-call | flops 1 | bytes 1 | tf_op jit(solution)/shard_map/scattered/pallas_call | solution.py:300
  39.8 2.0 %collective-permute-start.14 = (bf16[4,256,128]{2,1,0:T(8,128)(2,1)S(1)}, bf16[4,256,128]{2,1,0:T(8,128)(2,1)S(1)}, u32[]{:S(2)}, u32[]{:S(2)}) collective-permute-start(bf16[4,256,128]{2,1,0:T(8,128)(2,1)S(1)} %get-tuple-element.62), channel_id=1, source_target_pairs={{4,8},{8,4},{12,16},{16,12},{20,24},{24,20},{28,32},{32,28},{36,40... | collective-permute-start | bytes 786440 | tf_op jit(solution)/shard_map/ppermute | solution.py:322
  41.9 1.2 %tested_even.1 = bf16[4,256,128]{2,1,0:T(8,128)(2,1)S(1)} custom-call(bf16[512,1024]{1,0:T(8,128)(2,1)S(1)} %get-tuple-element.63.refs_0_, bf16[2,512,512]{2,1,0:T(8,128)(2,1)S(1)} %copy-done, bf16[768,512]{1,0:T(8,128)(2,1)S(1)} %get-tuple-element.58.pick_ref.refs_2_, f32[2,256,256]{2,1,0:T(8,128)S(1)} %get-tuple-element.60.refs_3_, ...), custom_call_target="tpu_custom_call" | custom-call | flops 1 | bytes 1 | tf_op jit(solution)/shard_map/tested_even/pallas_call | solution.py:300
  43.1 0.1 collective-permute-start.13
  43.2 1.2 %tested_own.1.own_ref = f32[4,256,128]{2,1,0:T(8,128)S(1)} custom-call(bf16[512,1024]{1,0:T(8,128)(2,1)S(1)} %get-tuple-element.63.refs_0_, bf16[2,512,512]{2,1,0:T(8,128)(2,1)S(1)} %copy-done, bf16[768,512]{1,0:T(8,128)(2,1)S(1)} %get-tuple-element.58.pick_ref.refs_2_, f32[2,256,256]{2,1,0:T(8,128)S(1)} %get-tuple-element.64.refs_3_, ...), custom_call_target="tpu_custom_call" | custom-call | flops 1 | bytes 1 | tf_op jit(solution)/shard_map/tested_own/pallas_call | solution.py:300
  44.4 5.3 %collective-permute-done.14.new_ref = bf16[4,256,128]{2,1,0:T(8,128)(2,1)S(1)} collective-permute-done((bf16[4,256,128]{2,1,0:T(8,128)(2,1)S(1)}, bf16[4,256,128]{2,1,0:T(8,128)(2,1)S(1)}, u32[]{:S(2)}, u32[]{:S(2)}) %collective-permute-start.14) | collective-permute-done | bytes 262176 | tf_op jit(solution)/shard_map/ppermute | solution.py:322
  49.7 0.0 collective-permute-done.13.even_ref
  49.8 0.2 collective-permute-start.15
  50.0 3.3 %collective-permute-start.16 = (bf16[256,128]{1,0:T(8,128)(2,1)S(1)}, bf16[256,128]{1,0:T(8,128)(2,1)S(1)}, u32[]{:S(2)}, u32[]{:S(2)}) collective-permute-start(bf16[256,128]{1,0:T(8,128)(2,1)S(1)} %get-tuple-element.68), channel_id=1, source_target_pairs={{0,2},{1,3},{2,0},{3,1},{4,6},{5,7},{6,4},{7,5},{8,10},{9,11},{10,... | collective-permute-start | bytes 196616 | tf_op jit(solution)/shard_map/ppermute | solution.py:314
  53.2 0.0 collective-permute-start.17
  53.2 2.1 %collective-permute-done.15 = bf16[256,128]{1,0:T(8,128)(2,1)S(1)} collective-permute-done((bf16[256,128]{1,0:T(8,128)(2,1)S(1)}, bf16[256,128]{1,0:T(8,128)(2,1)S(1)}, u32[]{:S(2)}, u32[]{:S(2)}) %collective-permute-start.15) | collective-permute-done | bytes 65568 | tf_op jit(solution)/shard_map/ppermute | solution.py:314
  55.3 0.8 %collective-permute-done.16 = bf16[256,128]{1,0:T(8,128)(2,1)S(1)} collective-permute-done((bf16[256,128]{1,0:T(8,128)(2,1)S(1)}, bf16[256,128]{1,0:T(8,128)(2,1)S(1)}, u32[]{:S(2)}, u32[]{:S(2)}) %collective-permute-start.16) | collective-permute-done | bytes 65568 | tf_op jit(solution)/shard_map/ppermute | solution.py:314
  56.2 1.3 %collective-permute-done.17 = bf16[256,128]{1,0:T(8,128)(2,1)S(1)} collective-permute-done((bf16[256,128]{1,0:T(8,128)(2,1)S(1)}, bf16[256,128]{1,0:T(8,128)(2,1)S(1)}, u32[]{:S(2)}, u32[]{:S(2)}) %collective-permute-start.17) | collective-permute-done | bytes 65568 | tf_op jit(solution)/shard_map/ppermute | solution.py:314
  57.5 0.7 %convert_add_fusion = f32[256,128]{1,0:T(8,128)} fusion(bf16[256,128]{1,0:T(8,128)(2,1)S(1)} %collective-permute-done.17, bf16[256,128]{1,0:T(8,128)(2,1)S(1)} %collective-permute-done.16, f32[256,128]{1,0:T(8,128)S(1)} %get-tuple-element.66, bf16[256,128]{1,0:T(8,128)(2,1)S(1)} %collective-permute-done.15), kind=kLoop, calls=%fused_computation.1 | loop fusion | flops 196608 | bytes 458752 | tf_op jit(solution)/shard_map/add | solution.py:408
  (10 shorter events, 0.2 us)
Async XLA Ops:
  0.6 13.5 %collective-permute-start = (bf16[256,512]{1,0:T(8,128)(2,1)}, bf16[256,512]{1,0:T(8,128)(2,1)S(1)}, u32[]{:S(2)}, u32[]{:S(2)}) collective-permute-start(bf16[256,512]{1,0:T(8,128)(2,1)} %current_hbm.1), channel_id=1, source_target_pairs={{4,8},{8,4},{12,16},{16,12},{20,24},{24,20},{28,32},{32,28},{36,40... | collective-permute-start | bytes 786440 | tf_op jit(solution)/shard_map/ppermute | solution.py:322
  8.1 6.0 %copy-start.1 = (bf16[2,512,512]{2,1,0:T(8,128)(2,1)S(1)}, bf16[2,512,512]{2,1,0:T(8,128)(2,1)}, u32[]{:S(2)}) copy-start(bf16[2,512,512]{2,1,0:T(8,128)(2,1)} %radiate_ref.2) | copy-start | bytes 3145732
  8.1 6.0 %copy-start.2 = (bf16[2,512,512]{2,1,0:T(8,128)(2,1)S(1)}, bf16[2,512,512]{2,1,0:T(8,128)(2,1)}, u32[]{:S(2)}) copy-start(bf16[2,512,512]{2,1,0:T(8,128)(2,1)} %receive_ref.2) | copy-start | bytes 3145732
  10.2 3.8 %collective-permute-start.1 = (bf16[256,256]{1,0:T(8,128)(2,1)S(1)}, bf16[256,256]{1,0:T(8,128)(2,1)S(1)}, u32[]{:S(2)}, u32[]{:S(2)}) collective-permute-start(bf16[256,256]{1,0:T(8,128)(2,1)S(1)} %get-tuple-element.36.w0), channel_id=1, source_target_pairs={{0,4},{4,0},{8,12},{12,8},{16,20},{20,16},{24,28},{28,24},{32,36},... | collective-permute-start | bytes 393224 | tf_op jit(solution)/shard_map/ppermute | solution.py:318
  10.3 3.8 %collective-permute-start.2 = (bf16[256,256]{1,0:T(8,128)(2,1)S(1)}, bf16[256,256]{1,0:T(8,128)(2,1)S(1)}, u32[]{:S(2)}, u32[]{:S(2)}) collective-permute-start(bf16[256,256]{1,0:T(8,128)(2,1)S(1)} %get-tuple-element.37.w1), channel_id=1, source_target_pairs={{0,4},{4,0},{8,12},{12,8},{16,20},{20,16},{24,28},{28,24},{32,36},... | collective-permute-start | bytes 393224 | tf_op jit(solution)/shard_map/ppermute | solution.py:318
  10.8 3.3 %collective-permute-start.3 = (bf16[256,256]{1,0:T(8,128)(2,1)S(1)}, bf16[256,256]{1,0:T(8,128)(2,1)S(1)}, u32[]{:S(2)}, u32[]{:S(2)}) collective-permute-start(bf16[256,256]{1,0:T(8,128)(2,1)S(1)} %get-tuple-element.38.w2), channel_id=1, source_target_pairs={{0,4},{4,0},{8,12},{12,8},{16,20},{20,16},{24,28},{28,24},{32,36},... | collective-permute-start | bytes 393224 | tf_op jit(solution)/shard_map/ppermute | solution.py:318
  10.9 3.2 %collective-permute-start.4 = (bf16[256,256]{1,0:T(8,128)(2,1)S(1)}, bf16[256,256]{1,0:T(8,128)(2,1)S(1)}, u32[]{:S(2)}, u32[]{:S(2)}) collective-permute-start(bf16[256,256]{1,0:T(8,128)(2,1)S(1)} %get-tuple-element.39.w3), channel_id=1, source_target_pairs={{0,4},{4,0},{8,12},{12,8},{16,20},{20,16},{24,28},{28,24},{32,36},... | collective-permute-start | bytes 393224 | tf_op jit(solution)/shard_map/ppermute | solution.py:318
  17.2 8.6 %collective-permute-start.5 = (bf16[512,128]{1,0:T(8,128)(2,1)S(1)}, bf16[512,128]{1,0:T(8,128)(2,1)S(1)}, u32[]{:S(2)}, u32[]{:S(2)}) collective-permute-start(bf16[512,128]{1,0:T(8,128)(2,1)S(1)} %get-tuple-element.51), channel_id=1, source_target_pairs={{0,1},{1,2},{2,3},{3,0},{4,5},{5,6},{6,7},{7,4},{8,9},{9,10},{10,1... | collective-permute-start | bytes 393224 | tf_op jit(solution)/shard_map/ppermute | solution.py:314
  18.9 7.4 %collective-permute-start.6 = (bf16[512,128]{1,0:T(8,128)(2,1)S(1)}, bf16[512,128]{1,0:T(8,128)(2,1)S(1)}, u32[]{:S(2)}, u32[]{:S(2)}) collective-permute-start(bf16[512,128]{1,0:T(8,128)(2,1)S(1)} %get-tuple-element.55), channel_id=1, source_target_pairs={{0,3},{1,0},{2,1},{3,2},{4,7},{5,4},{6,5},{7,6},{8,11},{9,8},{10,9... | collective-permute-start | bytes 393224 | tf_op jit(solution)/shard_map/ppermute | solution.py:314
  20.5 7.6 %collective-permute-start.7 = (bf16[512,128]{1,0:T(8,128)(2,1)S(1)}, bf16[512,128]{1,0:T(8,128)(2,1)S(1)}, u32[]{:S(2)}, u32[]{:S(2)}) collective-permute-start(bf16[512,128]{1,0:T(8,128)(2,1)S(1)} %get-tuple-element.56), channel_id=1, source_target_pairs={{0,2},{1,3},{2,0},{3,1},{4,6},{5,7},{6,4},{7,5},{8,10},{9,11},{10,... | collective-permute-start | bytes 393224 | tf_op jit(solution)/shard_map/ppermute | solution.py:314
  22.6 9.2 %collective-permute-start.12 = (f32[16,256]{1,0:T(8,128)S(1)}, f32[16,256]{1,0:T(8,128)S(1)}, u32[]{:S(2)}, u32[]{:S(2)}) collective-permute-start(f32[16,256]{1,0:T(8,128)S(1)} %get-tuple-element.57.own_ref), channel_id=1, source_target_pairs={{4,8},{8,4},{12,16},{16,12},{20,24},{24,20},{28,32},{32,28},{36,40... | collective-permute-start | bytes 49160 | tf_op jit(solution)/shard_map/ppermute | solution.py:322
  25.7 6.0 %collective-permute-start.11 = (f32[16,256]{1,0:T(8,128)S(1)}, f32[16,256]{1,0:T(8,128)S(1)}, u32[]{:S(2)}, u32[]{:S(2)}) collective-permute-start(f32[16,256]{1,0:T(8,128)S(1)} %get-tuple-element.57.own_ref), channel_id=1, source_target_pairs={{0,4},{4,0},{8,12},{12,8},{16,20},{20,16},{24,28},{28,24},{32,36},... | collective-permute-start | bytes 49160 | tf_op jit(solution)/shard_map/ppermute | solution.py:318
  28.2 9.8 %copy-start.4 = (bf16[512,128]{1,0:T(8,128)(2,1)}, bf16[512,128]{1,0:T(8,128)(2,1)S(1)}, u32[]{:S(2)}) copy-start(bf16[512,128]{1,0:T(8,128)(2,1)S(1)} %add_convert_fusion.p0_ref) | copy-start | bytes 393220
  28.2 9.8 %copy-start = (bf16[2,512,512]{2,1,0:T(8,128)(2,1)S(1)}, bf16[2,512,512]{2,1,0:T(8,128)(2,1)}, u32[]{:S(2)}) copy-start(bf16[2,512,512]{2,1,0:T(8,128)(2,1)} %refs_1_.3) | copy-start | bytes 3145732
  28.2 9.8 %copy-start.3 = (bf16[2,512,512]{2,1,0:T(8,128)(2,1)S(1)}, bf16[2,512,512]{2,1,0:T(8,128)(2,1)}, u32[]{:S(2)}) copy-start(bf16[2,512,512]{2,1,0:T(8,128)(2,1)} %radiate_ref.3) | copy-start | bytes 3145732
  28.2 6.4 %collective-permute-start.10 = (bf16[512,128]{1,0:T(8,128)(2,1)S(1)}, bf16[512,128]{1,0:T(8,128)(2,1)S(1)}, u32[]{:S(2)}, u32[]{:S(2)}) collective-permute-start(bf16[512,128]{1,0:T(8,128)(2,1)S(1)} %add_convert_fusion.p0_ref), channel_id=1, source_target_pairs={{0,1},{1,2},{2,3},{3,0},{4,5},{5,6},{6,7},{7,4},{8,9},{9,10},{10,1... | collective-permute-start | bytes 393224 | tf_op jit(solution)/shard_map/ppermute | solution.py:314
  29.4 6.8 %collective-permute-start.9 = (bf16[512,128]{1,0:T(8,128)(2,1)S(1)}, bf16[512,128]{1,0:T(8,128)(2,1)S(1)}, u32[]{:S(2)}, u32[]{:S(2)}) collective-permute-start(bf16[512,128]{1,0:T(8,128)(2,1)S(1)} %add_convert_fusion.p0_ref), channel_id=1, source_target_pairs={{0,3},{1,0},{2,1},{3,2},{4,7},{5,4},{6,5},{7,6},{8,11},{9,8},{10,9... | collective-permute-start | bytes 393224 | tf_op jit(solution)/shard_map/ppermute | solution.py:314
  31.5 6.5 %collective-permute-start.8 = (bf16[512,128]{1,0:T(8,128)(2,1)S(1)}, bf16[512,128]{1,0:T(8,128)(2,1)S(1)}, u32[]{:S(2)}, u32[]{:S(2)}) collective-permute-start(bf16[512,128]{1,0:T(8,128)(2,1)S(1)} %add_convert_fusion.p0_ref), channel_id=1, source_target_pairs={{0,2},{1,3},{2,0},{3,1},{4,6},{5,7},{6,4},{7,5},{8,10},{9,11},{10,... | collective-permute-start | bytes 393224 | tf_op jit(solution)/shard_map/ppermute | solution.py:314
  39.8 9.8 %collective-permute-start.14 = (bf16[4,256,128]{2,1,0:T(8,128)(2,1)S(1)}, bf16[4,256,128]{2,1,0:T(8,128)(2,1)S(1)}, u32[]{:S(2)}, u32[]{:S(2)}) collective-permute-start(bf16[4,256,128]{2,1,0:T(8,128)(2,1)S(1)} %get-tuple-element.62), channel_id=1, source_target_pairs={{4,8},{8,4},{12,16},{16,12},{20,24},{24,20},{28,32},{32,28},{36,40... | collective-permute-start | bytes 786440 | tf_op jit(solution)/shard_map/ppermute | solution.py:322
  43.1 6.6 %collective-permute-start.13 = (bf16[4,256,128]{2,1,0:T(8,128)(2,1)S(1)}, bf16[4,256,128]{2,1,0:T(8,128)(2,1)S(1)}, u32[]{:S(2)}, u32[]{:S(2)}) collective-permute-start(bf16[4,256,128]{2,1,0:T(8,128)(2,1)S(1)} %tested_even.1), channel_id=1, source_target_pairs={{0,4},{4,0},{8,12},{12,8},{16,20},{20,16},{24,28},{28,24},{32,36},... | collective-permute-start | bytes 786440 | tf_op jit(solution)/shard_map/ppermute | solution.py:318
  49.8 5.6 %collective-permute-start.15 = (bf16[256,128]{1,0:T(8,128)(2,1)S(1)}, bf16[256,128]{1,0:T(8,128)(2,1)S(1)}, u32[]{:S(2)}, u32[]{:S(2)}) collective-permute-start(bf16[256,128]{1,0:T(8,128)(2,1)S(1)} %get-tuple-element.67), channel_id=1, source_target_pairs={{0,1},{1,2},{2,3},{3,0},{4,5},{5,6},{6,7},{7,4},{8,9},{9,10},{10,1... | collective-permute-start | bytes 196616 | tf_op jit(solution)/shard_map/ppermute | solution.py:314
  50.0 6.2 %collective-permute-start.16 = (bf16[256,128]{1,0:T(8,128)(2,1)S(1)}, bf16[256,128]{1,0:T(8,128)(2,1)S(1)}, u32[]{:S(2)}, u32[]{:S(2)}) collective-permute-start(bf16[256,128]{1,0:T(8,128)(2,1)S(1)} %get-tuple-element.68), channel_id=1, source_target_pairs={{0,2},{1,3},{2,0},{3,1},{4,6},{5,7},{6,4},{7,5},{8,10},{9,11},{10,... | collective-permute-start | bytes 196616 | tf_op jit(solution)/shard_map/ppermute | solution.py:314
  53.2 4.3 %collective-permute-start.17 = (bf16[256,128]{1,0:T(8,128)(2,1)S(1)}, bf16[256,128]{1,0:T(8,128)(2,1)S(1)}, u32[]{:S(2)}, u32[]{:S(2)}) collective-permute-start(bf16[256,128]{1,0:T(8,128)(2,1)S(1)} %get-tuple-element.69), channel_id=1, source_target_pairs={{0,3},{1,0},{2,1},{3,2},{4,7},{5,4},{6,5},{7,6},{8,11},{9,8},{10,9... | collective-permute-start | bytes 196616 | tf_op jit(solution)/shard_map/ppermute | solution.py:314

commit v11 on v10

--- a/solution.py
+++ b/solution.py
@@ -185,8 +185,17 @@
     trig(po_c[...], dirs_ref, po_cos, po_sin)
 
 
+def partial(e0, e1, e2, e3, w0, w1, w2, w3, pick_ref, out_ref):
+    m, k = w0.shape
+    beside = pl.ds(pl.multiple_of(2 * m - parity() * 2 * m, 128), m)
+    for at in tiles(pick_ref.shape[0]):
+        for i, (e_ref, w_ref) in enumerate(((e0, w0), (e1, w1), (e2, w2), (e3, w3))):
+            total = mm(pick_ref[at, m : 2 * m], w_ref[...]) + mm(pick_ref[at, beside], e_ref[...])
+            out_ref[at, i * k : (i + 1) * k] = total
+
+
 def incident(
-    odd_ref, e0, e1, e2, e3, w0, w1, w2, w3, pick_ref, radiate_ref, receive_ref, odd_cos, odd_sin, po_cos, po_sin, lit_ref,
+    odd_ref, partial_ref, pick_ref, radiate_ref, receive_ref, odd_cos, odd_sin, po_cos, po_sin, lit_ref,
     own_ref, s1_ref, s2_ref, s3_ref,
     table, chunks,
 ):
@@ -194,17 +203,15 @@
     q = own_ref.shape[0]
     cones, _, k2 = radiate_ref.shape
     k = k2 // 2
-    side = parity() * 2 * m
+    beside = pl.ds(pl.multiple_of(parity() * 2 * m, 128), m)
     for at in tiles(m):
-        for i, (e_ref, w_ref) in enumerate(((e0, w0), (e1, w1), (e2, w2), (e3, w3))):
-            table[rows_at(m, at), i * k : (i + 1) * k] = w_ref[at]
-            table[rows_at(2 * m - side, at), i * k : (i + 1) * k] = e_ref[at]
-        radiated(odd_ref, at, radiate_ref, odd_cos, odd_sin, table, side, 0)
+        radiated(odd_ref, at, radiate_ref, odd_cos, odd_sin, table, 0, 0)
     lit_col = jnp.concatenate([lit_ref[...].astype(F32), jnp.zeros((8 - cones, q), F32)], axis=0).T
     for at in tiles(q):
         total = None
         for c in range(cones):
-            value = mm(pick_ref[at], table[:, c * k2 : (c + 1) * k2])
+            columns = slice(c * k2, (c + 1) * k2)
+            value = partial_ref[at, columns] + mm(pick_ref[at, beside], table[:, columns])
             mask = lit_col[at, c : c + 1]
             re, im = rotated(value, po_cos[c, at] * mask, po_sin[c, at] * mask, 1)
             part = mm(re.astype(BF), receive_ref[c, :k]) + mm(im.astype(BF), receive_ref[c, k:])
@@ -359,11 +366,12 @@
         angles + (shape((cones, q, k), F32),) * 2 + (shape((q, 3 * m), BF),),
         (waves3, odd_c, po_c, src, weight),
     )
+    nearer = call(partial, shape((q, width), F32), (*even_parts, *own_parts, pick))
     own, s1, s2, s3 = call(
         incident,
         (shape((q, share), F32),) + (shape((q, share), BF),) * 3,
-        (odd, *even_parts, *own_parts, pick, mom_radiate, po_receive, odd_cos, odd_sin, po_cos, po_sin, lit),
-        (pltpu.VMEM((3 * m, width), BF), pltpu.VMEM((count, q, share), F32)),
+        (odd, nearer, pick, mom_radiate, po_receive, odd_cos, odd_sin, po_cos, po_sin, lit),
+        (pltpu.VMEM((m, width), BF), pltpu.VMEM((count, q, share), F32)),
     )
     s1 = turned(s1, 1)
     s2 = turned(s2, 2)

time: 58.3 us -> 58.9 us (1.010)
  starting transfers between devices: 26.3 us -> 28.2 us
  waiting for transfers between devices: 15.2 us -> 13.6 us
    ppermute x9, starting transfers between devices: 12.4 us -> 13.7 us  [turned(): lax.ppermute(value, 'cone', [(i, (i + shift) % count) for i in range(coun...]
    ppermute x9, waiting for transfers between devices: 9.95 us -> 9.12 us  [turned(): lax.ppermute(value, 'cone', [(i, (i + shift) % count) for i in range(coun...]
    ppermute x3, waiting for transfers between devices: 5.27 us -> 4.46 us  [swapped_odd(): lax.ppermute(value, 'box', [(i, (i + 1 ^ 1) - 1) for i in range(1, lax.ax...]
    ppermute x3, starting transfers between devices: 12.6 us -> 13.3 us  [swapped_odd(): lax.ppermute(value, 'box', [(i, (i + 1 ^ 1) - 1) for i in range(1, lax.ax...]
    pallas_call x10 -> x11, Pallas kernels: 15 us -> 15.3 us  [call(): pl.pallas_call(body, out_shape=outs, in_specs=[pl.BlockSpec(memory_space=...]
  transfers between devices with their start and end apart: 18 -> 18, of which waited for: 8 -> 8; matrix products, arithmetic and copies ran while one was open for 0% -> 0% of each run, Pallas kernels for 17% -> 18%
where the time goes in v11:
time: 58.9 us; the launch traced here: 58.7 us
  starting transfers between devices  28.2 us (48%)
  Pallas kernels  15.3 us (26%)
  waiting for transfers between devices  13.6 us (23%)
  between operations  0.88 us (1%)
  other arithmetic  0.74 us (1%)
    pallas_call x11, Pallas kernels, call(): pl.pallas_call(body, out_shape=outs, in_specs=[pl.BlockSpec(memory_space=...  15.3 us
    ppermute x9, starting transfers between devices, turned(): lax.ppermute(value, 'cone', [(i, (i + shift) % count) for i in range(coun...  13.7 us
    ppermute x3, starting transfers between devices, swapped_odd(): lax.ppermute(value, 'box', [(i, (i + 1 ^ 1) - 1) for i in range(1, lax.ax...  13.3 us
    ppermute x9, waiting for transfers between devices, turned(): lax.ppermute(value, 'cone', [(i, (i + shift) % count) for i in range(coun...  9.12 us
    ppermute x3, waiting for transfers between devices, swapped_odd(): lax.ppermute(value, 'box', [(i, (i + 1 ^ 1) - 1) for i in range(1, lax.ax...  4.46 us
    ppermute x6, starting transfers between devices, swapped_even(): lax.ppermute(value, 'box', [(i, i ^ 1) for i in range(lax.axis_size('box'...  1.19 us
  transfers between devices with their start and end apart: 18, of which 8 were waited for; matrix products, arithmetic and copies ran while one was open for 0% of the time, Pallas kernels for 18%

profile of v11, /device:TPU:6, one launch (start us, length us, event | category | flops | bytes accessed | tf_op | source)
XLA Modules:
  0.0 58.7 jit_solution(213308791579207677)
XLA Ops:
  0.6 7.5 %collective-permute-start = (bf16[256,512]{1,0:T(8,128)(2,1)}, bf16[256,512]{1,0:T(8,128)(2,1)S(1)}, u32[]{:S(2)}, u32[]{:S(2)}) collective-permute-start(bf16[256,512]{1,0:T(8,128)(2,1)} %current_hbm.1), channel_id=1, source_target_pairs={{4,8},{8,4},{12,16},{16,12},{20,24},{24,20},{28,32},{32,28},{36,40... | collective-permute-start | bytes 786440 | tf_op jit(solution)/shard_map/ppermute | solution.py:329
  8.1 1.9 %own_waves.1 = (f32[2,256,256]{2,1,0:T(8,128)S(1)}, f32[2,256,256]{2,1,0:T(8,128)S(1)}, f32[3,2,256]{2,1,0:T(2,128)S(1)}, f32[3,256]{1,0:T(4,128)S(1)}, f32[3,51...) custom-call(bf16[256,512]{1,0:T(8,128)(2,1)} %current_hbm.1, ...), custom_call_target="tpu_custom_call" | custom-call | flops 1 | bytes 1 | tf_op jit(solution)/shard_map/own_waves/pallas_call | solution.py:307
  10.1 0.0 copy-start.1
  10.1 0.0 copy-start.3
  10.1 0.1 collective-permute-start.1
  10.2 0.5 collective-permute-start.2
  10.7 0.1 collective-permute-start.3
  10.8 0.4 collective-permute-start.4
  11.2 2.7 %prepare.1 = (f32[2,256,256]{2,1,0:T(8,128)S(1)}, f32[2,256,256]{2,1,0:T(8,128)S(1)}, f32[2,512,256]{2,1,0:T(8,128)S(1)}, f32[2,512,256]{2,1,0:T(8,128)S(1)}, bf16[512,768]{1,0:T(8,128)(2,1)S(1)}) custom-call(f32[3,2,256]{2,1,0:T(2,128)S(1)} %get-tuple-element.40.dirs_ref, f32[3,256]{1,0:T(4,128)S(1)} %get-tuple-element.41.mom_c, ...), custom_call_target="tpu_custom_call" | custom-call | flops 1 | bytes 1 | tf_op jit(solution)/shard_map/prepare/pallas_call | solution.py:307
  13.9 0.0 collective-permute-done.1.e0
  13.9 0.0 collective-permute-done.2.e1
  13.9 0.0 collective-permute-done.3.e2
  14.0 0.0 collective-permute-done.4.e3
  14.0 0.7 %partial.1.partial_ref = f32[512,1024]{1,0:T(8,128)S(1)} custom-call(bf16[256,256]{1,0:T(8,128)(2,1)S(1)} %collective-permute-done.1.e0, bf16[256,256]{1,0:T(8,128)(2,1)S(1)} %collective-permute-done.2.e1, bf16[256,256]{1,0:T(8,128)(2,1)S(1)} %collective-permute-done.3.e2, bf16[256,256]{1,0:T(8,128)(2,1)S(1)} %collective-permute-done.4.e3, ...), custom_call_target="tpu_custom_call" | custom-call | flops 1 | bytes 1 | tf_op jit(solution)/shard_map/partial/pallas_call | solution.py:307
  14.7 0.0 collective-permute-done.odd_ref
  14.7 2.6 %incident.1 = (f32[512,128]{1,0:T(8,128)S(1)}, bf16[512,128]{1,0:T(8,128)(2,1)S(1)}, bf16[512,128]{1,0:T(8,128)(2,1)S(1)}, bf16[512,128]{1,0:T(8,128)(2,1)S(1)}) custom-call(bf16[256,512]{1,0:T(8,128)(2,1)S(1)} %collective-permute-done.odd_ref, f32[512,1024]{1,0:T(8,128)S(1)} %partial.1.partial_ref, bf16[512,768]{1,0:T(8,128)(2,1)S(1)} %get-tuple-element.45.pick_ref, ...), custom_call_target="tpu_custom_call" | custom-call | flops 1 | bytes 1 | tf_op jit(solution)/shard_map/incident/pallas_call | solution.py:307
  17.4 1.7 %collective-permute-start.5 = (bf16[512,128]{1,0:T(8,128)(2,1)S(1)}, bf16[512,128]{1,0:T(8,128)(2,1)S(1)}, u32[]{:S(2)}, u32[]{:S(2)}) collective-permute-start(bf16[512,128]{1,0:T(8,128)(2,1)S(1)} %get-tuple-element.51), channel_id=1, source_target_pairs={{0,1},{1,2},{2,3},{3,0},{4,5},{5,6},{6,7},{7,4},{8,9},{9,10},{10,1... | collective-permute-start | bytes 393224 | tf_op jit(solution)/shard_map/ppermute | solution.py:321
  19.0 1.7 %collective-permute-start.6 = (bf16[512,128]{1,0:T(8,128)(2,1)S(1)}, bf16[512,128]{1,0:T(8,128)(2,1)S(1)}, u32[]{:S(2)}, u32[]{:S(2)}) collective-permute-start(bf16[512,128]{1,0:T(8,128)(2,1)S(1)} %get-tuple-element.55), channel_id=1, source_target_pairs={{0,3},{1,0},{2,1},{3,2},{4,7},{5,4},{6,5},{7,6},{8,11},{9,8},{10,9... | collective-permute-start | bytes 393224 | tf_op jit(solution)/shard_map/ppermute | solution.py:321
  20.7 2.0 %collective-permute-start.7 = (bf16[512,128]{1,0:T(8,128)(2,1)S(1)}, bf16[512,128]{1,0:T(8,128)(2,1)S(1)}, u32[]{:S(2)}, u32[]{:S(2)}) collective-permute-start(bf16[512,128]{1,0:T(8,128)(2,1)S(1)} %get-tuple-element.56), channel_id=1, source_target_pairs={{0,2},{1,3},{2,0},{3,1},{4,6},{5,7},{6,4},{7,5},{8,10},{9,11},{10,... | collective-permute-start | bytes 393224 | tf_op jit(solution)/shard_map/ppermute | solution.py:321
  22.7 0.0 collective-permute-start.11
  22.7 3.0 %collective-permute-start.12 = (f32[16,256]{1,0:T(8,128)S(1)}, f32[16,256]{1,0:T(8,128)S(1)}, u32[]{:S(2)}, u32[]{:S(2)}) collective-permute-start(f32[16,256]{1,0:T(8,128)S(1)} %get-tuple-element.57.own_ref), channel_id=1, source_target_pairs={{4,8},{8,4},{12,16},{16,12},{20,24},{24,20},{28,32},{32,28},{36,40... | collective-permute-start | bytes 49160 | tf_op jit(solution)/shard_map/ppermute | solution.py:329
  25.7 0.0 collective-permute-done.5.new_ref
  25.7 0.7 %collective-permute-done.6 = bf16[512,128]{1,0:T(8,128)(2,1)S(1)} collective-permute-done((bf16[512,128]{1,0:T(8,128)(2,1)S(1)}, bf16[512,128]{1,0:T(8,128)(2,1)S(1)}, u32[]{:S(2)}, u32[]{:S(2)}) %collective-permute-start.6) | collective-permute-done | bytes 131104 | tf_op jit(solution)/shard_map/ppermute | solution.py:321
  26.4 1.8 %collective-permute-done.7 = bf16[512,128]{1,0:T(8,128)(2,1)S(1)} collective-permute-done((bf16[512,128]{1,0:T(8,128)(2,1)S(1)}, bf16[512,128]{1,0:T(8,128)(2,1)S(1)}, u32[]{:S(2)}, u32[]{:S(2)}) %collective-permute-start.7) | collective-permute-done | bytes 131104 | tf_op jit(solution)/shard_map/ppermute | solution.py:321
  28.2 0.0 copy-start.4
  28.3 0.0 copy-start
  28.3 0.0 copy-start.2
  28.3 1.2 %collective-permute-start.10 = (bf16[512,128]{1,0:T(8,128)(2,1)S(1)}, bf16[512,128]{1,0:T(8,128)(2,1)S(1)}, u32[]{:S(2)}, u32[]{:S(2)}) collective-permute-start(bf16[512,128]{1,0:T(8,128)(2,1)S(1)} %add_convert_fusion.p0_ref), channel_id=1, source_target_pairs={{0,1},{1,2},{2,3},{3,0},{4,5},{5,6},{6,7},{7,4},{8,9},{9,10},{10,1... | collective-permute-start | bytes 393224 | tf_op jit(solution)/shard_map/ppermute | solution.py:321
  29.5 2.2 %collective-permute-start.8 = (bf16[512,128]{1,0:T(8,128)(2,1)S(1)}, bf16[512,128]{1,0:T(8,128)(2,1)S(1)}, u32[]{:S(2)}, u32[]{:S(2)}) collective-permute-start(bf16[512,128]{1,0:T(8,128)(2,1)S(1)} %add_convert_fusion.p0_ref), channel_id=1, source_target_pairs={{0,2},{1,3},{2,0},{3,1},{4,6},{5,7},{6,4},{7,5},{8,10},{9,11},{10,... | collective-permute-start | bytes 393224 | tf_op jit(solution)/shard_map/ppermute | solution.py:321
  31.7 0.8 %collective-permute-start.9 = (bf16[512,128]{1,0:T(8,128)(2,1)S(1)}, bf16[512,128]{1,0:T(8,128)(2,1)S(1)}, u32[]{:S(2)}, u32[]{:S(2)}) collective-permute-start(bf16[512,128]{1,0:T(8,128)(2,1)S(1)} %add_convert_fusion.p0_ref), channel_id=1, source_target_pairs={{0,3},{1,0},{2,1},{3,2},{4,7},{5,4},{6,5},{7,6},{8,11},{9,8},{10,9... | collective-permute-start | bytes 393224 | tf_op jit(solution)/shard_map/ppermute | solution.py:321
  32.5 0.0 collective-permute-done.11.even_ref
  32.5 2.8 %lists.1 = (bf16[768,512]{1,0:T(8,128)(2,1)S(1)}, f32[2,256,256]{2,1,0:T(8,128)S(1)}, f32[2,256,256]{2,1,0:T(8,128)S(1)}) custom-call(f32[16,256]{1,0:T(8,128)S(1)} %collective-permute-done.11.even_ref, f32[16,256]{1,0:T(8,128)S(1)} %get-tuple-element.57.own_ref, f32[16,256]{1,0:T(8,128)S(1)} %collective-permute-done.12.odd_ref, ...), custom_call_target="tpu_custom_call" | custom-call | flops 4000000000 | bytes 1 | tf_op jit(solution)/shard_map/lists/pallas_call | solution.py:307
  35.2 1.8 %collective-permute-done.10.p1_ref = bf16[512,128]{1,0:T(8,128)(2,1)S(1)} collective-permute-done((bf16[512,128]{1,0:T(8,128)(2,1)S(1)}, bf16[512,128]{1,0:T(8,128)(2,1)S(1)}, u32[]{:S(2)}, u32[]{:S(2)}) %collective-permute-start.10) | collective-permute-done | bytes 131104 | tf_op jit(solution)/shard_map/ppermute | solution.py:321
  37.1 0.6 collective-permute-done.9.p3_ref
  37.6 2.0 %scattered.1 = (bf16[512,1024]{1,0:T(8,128)(2,1)S(1)}, bf16[4,256,128]{2,1,0:T(8,128)(2,1)S(1)}) custom-call(bf16[512,128]{1,0:T(8,128)(2,1)S(1)} %add_convert_fusion.p0_ref, bf16[512,128]{1,0:T(8,128)(2,1)S(1)} %collective-permute-done.8.p2_ref, bf16[512,128]{1,0:T(8,128)(2,1)S(1)} %collective-permute-done.9.p3_ref, ...), custom_call_target="tpu_custom_call" | custom-call | flops 1 | bytes 1 | tf_op jit(solution)/shard_map/scattered/pallas_call | solution.py:307
  39.6 2.8 %collective-permute-start.14 = (bf16[4,256,128]{2,1,0:T(8,128)(2,1)S(1)}, bf16[4,256,128]{2,1,0:T(8,128)(2,1)S(1)}, u32[]{:S(2)}, u32[]{:S(2)}) collective-permute-start(bf16[4,256,128]{2,1,0:T(8,128)(2,1)S(1)} %get-tuple-element.62), channel_id=1, source_target_pairs={{4,8},{8,4},{12,16},{16,12},{20,24},{24,20},{28,32},{32,28},{36,40... | collective-permute-start | bytes 786440 | tf_op jit(solution)/shard_map/ppermute | solution.py:329
  42.4 1.2 %tested_even.1 = bf16[4,256,128]{2,1,0:T(8,128)(2,1)S(1)} custom-call(bf16[512,1024]{1,0:T(8,128)(2,1)S(1)} %get-tuple-element.63.refs_0_, bf16[2,512,512]{2,1,0:T(8,128)(2,1)S(1)} %copy-done, bf16[768,512]{1,0:T(8,128)(2,1)S(1)} %get-tuple-element.58.pick_ref.refs_2_, f32[2,256,256]{2,1,0:T(8,128)S(1)} %get-tuple-element.60.refs_3_, ...), custom_call_target="tpu_custom_call" | custom-call | flops 1 | bytes 1 | tf_op jit(solution)/shard_map/tested_even/pallas_call | solution.py:307
  43.6 0.1 collective-permute-start.13
  43.7 1.2 %tested_own.1.own_ref = f32[4,256,128]{2,1,0:T(8,128)S(1)} custom-call(bf16[512,1024]{1,0:T(8,128)(2,1)S(1)} %get-tuple-element.63.refs_0_, bf16[2,512,512]{2,1,0:T(8,128)(2,1)S(1)} %copy-done, bf16[768,512]{1,0:T(8,128)(2,1)S(1)} %get-tuple-element.58.pick_ref.refs_2_, f32[2,256,256]{2,1,0:T(8,128)S(1)} %get-tuple-element.64.refs_3_, ...), custom_call_target="tpu_custom_call" | custom-call | flops 1 | bytes 1 | tf_op jit(solution)/shard_map/tested_own/pallas_call | solution.py:307
  45.0 4.5 %collective-permute-done.14.new_ref = bf16[4,256,128]{2,1,0:T(8,128)(2,1)S(1)} collective-permute-done((bf16[4,256,128]{2,1,0:T(8,128)(2,1)S(1)}, bf16[4,256,128]{2,1,0:T(8,128)(2,1)S(1)}, u32[]{:S(2)}, u32[]{:S(2)}) %collective-permute-start.14) | collective-permute-done | bytes 262176 | tf_op jit(solution)/shard_map/ppermute | solution.py:329
  49.5 0.0 collective-permute-done.13.even_ref
  49.6 0.9 %collective-permute-start.15 = (bf16[256,128]{1,0:T(8,128)(2,1)S(1)}, bf16[256,128]{1,0:T(8,128)(2,1)S(1)}, u32[]{:S(2)}, u32[]{:S(2)}) collective-permute-start(bf16[256,128]{1,0:T(8,128)(2,1)S(1)} %get-tuple-element.67), channel_id=1, source_target_pairs={{0,1},{1,2},{2,3},{3,0},{4,5},{5,6},{6,7},{7,4},{8,9},{9,10},{10,1... | collective-permute-start | bytes 196616 | tf_op jit(solution)/shard_map/ppermute | solution.py:321
  50.4 3.3 %collective-permute-start.16 = (bf16[256,128]{1,0:T(8,128)(2,1)S(1)}, bf16[256,128]{1,0:T(8,128)(2,1)S(1)}, u32[]{:S(2)}, u32[]{:S(2)}) collective-permute-start(bf16[256,128]{1,0:T(8,128)(2,1)S(1)} %get-tuple-element.68), channel_id=1, source_target_pairs={{0,2},{1,3},{2,0},{3,1},{4,6},{5,7},{6,4},{7,5},{8,10},{9,11},{10,... | collective-permute-start | bytes 196616 | tf_op jit(solution)/shard_map/ppermute | solution.py:321
  53.8 0.0 collective-permute-start.17
  53.8 1.3 %collective-permute-done.15 = bf16[256,128]{1,0:T(8,128)(2,1)S(1)} collective-permute-done((bf16[256,128]{1,0:T(8,128)(2,1)S(1)}, bf16[256,128]{1,0:T(8,128)(2,1)S(1)}, u32[]{:S(2)}, u32[]{:S(2)}) %collective-permute-start.15) | collective-permute-done | bytes 65568 | tf_op jit(solution)/shard_map/ppermute | solution.py:321
  55.1 1.6 %collective-permute-done.16 = bf16[256,128]{1,0:T(8,128)(2,1)S(1)} collective-permute-done((bf16[256,128]{1,0:T(8,128)(2,1)S(1)}, bf16[256,128]{1,0:T(8,128)(2,1)S(1)}, u32[]{:S(2)}, u32[]{:S(2)}) %collective-permute-start.16) | collective-permute-done | bytes 65568 | tf_op jit(solution)/shard_map/ppermute | solution.py:321
  56.7 1.3 %collective-permute-done.17 = bf16[256,128]{1,0:T(8,128)(2,1)S(1)} collective-permute-done((bf16[256,128]{1,0:T(8,128)(2,1)S(1)}, bf16[256,128]{1,0:T(8,128)(2,1)S(1)}, u32[]{:S(2)}, u32[]{:S(2)}) %collective-permute-start.17) | collective-permute-done | bytes 65568 | tf_op jit(solution)/shard_map/ppermute | solution.py:321
  58.0 0.7 %convert_add_fusion = f32[256,128]{1,0:T(8,128)} fusion(bf16[256,128]{1,0:T(8,128)(2,1)S(1)} %collective-permute-done.17, bf16[256,128]{1,0:T(8,128)(2,1)S(1)} %collective-permute-done.16, f32[256,128]{1,0:T(8,128)S(1)} %get-tuple-element.66, bf16[256,128]{1,0:T(8,128)(2,1)S(1)} %collective-permute-done.15), kind=kLoop, calls=%fused_computation.1 | loop fusion | flops 196608 | bytes 458752 | tf_op jit(solution)/shard_map/add | solution.py:416
  (11 shorter events, 0.2 us)
Async XLA Ops:
  0.6 14.1 %collective-permute-start = (bf16[256,512]{1,0:T(8,128)(2,1)}, bf16[256,512]{1,0:T(8,128)(2,1)S(1)}, u32[]{:S(2)}, u32[]{:S(2)}) collective-permute-start(bf16[256,512]{1,0:T(8,128)(2,1)} %current_hbm.1), channel_id=1, source_target_pairs={{4,8},{8,4},{12,16},{16,12},{20,24},{24,20},{28,32},{32,28},{36,40... | collective-permute-start | bytes 786440 | tf_op jit(solution)/shard_map/ppermute | solution.py:329
  10.1 4.7 %copy-start.1 = (bf16[2,512,512]{2,1,0:T(8,128)(2,1)S(1)}, bf16[2,512,512]{2,1,0:T(8,128)(2,1)}, u32[]{:S(2)}) copy-start(bf16[2,512,512]{2,1,0:T(8,128)(2,1)} %radiate_ref.2) | copy-start | bytes 3145732
  10.1 4.7 %copy-start.3 = (bf16[2,512,512]{2,1,0:T(8,128)(2,1)S(1)}, bf16[2,512,512]{2,1,0:T(8,128)(2,1)}, u32[]{:S(2)}) copy-start(bf16[2,512,512]{2,1,0:T(8,128)(2,1)} %receive_ref.2) | copy-start | bytes 3145732
  10.1 3.8 %collective-permute-start.1 = (bf16[256,256]{1,0:T(8,128)(2,1)S(1)}, bf16[256,256]{1,0:T(8,128)(2,1)S(1)}, u32[]{:S(2)}, u32[]{:S(2)}) collective-permute-start(bf16[256,256]{1,0:T(8,128)(2,1)S(1)} %get-tuple-element.36.w0), channel_id=1, source_target_pairs={{0,4},{4,0},{8,12},{12,8},{16,20},{20,16},{24,28},{28,24},{32,36},... | collective-permute-start | bytes 393224 | tf_op jit(solution)/shard_map/ppermute | solution.py:325
  10.2 3.8 %collective-permute-start.2 = (bf16[256,256]{1,0:T(8,128)(2,1)S(1)}, bf16[256,256]{1,0:T(8,128)(2,1)S(1)}, u32[]{:S(2)}, u32[]{:S(2)}) collective-permute-start(bf16[256,256]{1,0:T(8,128)(2,1)S(1)} %get-tuple-element.37.w1), channel_id=1, source_target_pairs={{0,4},{4,0},{8,12},{12,8},{16,20},{20,16},{24,28},{28,24},{32,36},... | collective-permute-start | bytes 393224 | tf_op jit(solution)/shard_map/ppermute | solution.py:325
  10.7 3.3 %collective-permute-start.3 = (bf16[256,256]{1,0:T(8,128)(2,1)S(1)}, bf16[256,256]{1,0:T(8,128)(2,1)S(1)}, u32[]{:S(2)}, u32[]{:S(2)}) collective-permute-start(bf16[256,256]{1,0:T(8,128)(2,1)S(1)} %get-tuple-element.38.w2), channel_id=1, source_target_pairs={{0,4},{4,0},{8,12},{12,8},{16,20},{20,16},{24,28},{28,24},{32,36},... | collective-permute-start | bytes 393224 | tf_op jit(solution)/shard_map/ppermute | solution.py:325
  10.8 3.2 %collective-permute-start.4 = (bf16[256,256]{1,0:T(8,128)(2,1)S(1)}, bf16[256,256]{1,0:T(8,128)(2,1)S(1)}, u32[]{:S(2)}, u32[]{:S(2)}) collective-permute-start(bf16[256,256]{1,0:T(8,128)(2,1)S(1)} %get-tuple-element.39.w3), channel_id=1, source_target_pairs={{0,4},{4,0},{8,12},{12,8},{16,20},{20,16},{24,28},{28,24},{32,36},... | collective-permute-start | bytes 393224 | tf_op jit(solution)/shard_map/ppermute | solution.py:325
  17.4 8.3 %collective-permute-start.5 = (bf16[512,128]{1,0:T(8,128)(2,1)S(1)}, bf16[512,128]{1,0:T(8,128)(2,1)S(1)}, u32[]{:S(2)}, u32[]{:S(2)}) collective-permute-start(bf16[512,128]{1,0:T(8,128)(2,1)S(1)} %get-tuple-element.51), channel_id=1, source_target_pairs={{0,1},{1,2},{2,3},{3,0},{4,5},{5,6},{6,7},{7,4},{8,9},{9,10},{10,1... | collective-permute-start | bytes 393224 | tf_op jit(solution)/shard_map/ppermute | solution.py:321
  19.0 7.4 %collective-permute-start.6 = (bf16[512,128]{1,0:T(8,128)(2,1)S(1)}, bf16[512,128]{1,0:T(8,128)(2,1)S(1)}, u32[]{:S(2)}, u32[]{:S(2)}) collective-permute-start(bf16[512,128]{1,0:T(8,128)(2,1)S(1)} %get-tuple-element.55), channel_id=1, source_target_pairs={{0,3},{1,0},{2,1},{3,2},{4,7},{5,4},{6,5},{7,6},{8,11},{9,8},{10,9... | collective-permute-start | bytes 393224 | tf_op jit(solution)/shard_map/ppermute | solution.py:321
  20.7 7.5 %collective-permute-start.7 = (bf16[512,128]{1,0:T(8,128)(2,1)S(1)}, bf16[512,128]{1,0:T(8,128)(2,1)S(1)}, u32[]{:S(2)}, u32[]{:S(2)}) collective-permute-start(bf16[512,128]{1,0:T(8,128)(2,1)S(1)} %get-tuple-element.56), channel_id=1, source_target_pairs={{0,2},{1,3},{2,0},{3,1},{4,6},{5,7},{6,4},{7,5},{8,10},{9,11},{10,... | collective-permute-start | bytes 393224 | tf_op jit(solution)/shard_map/ppermute | solution.py:321
  22.7 9.8 %collective-permute-start.11 = (f32[16,256]{1,0:T(8,128)S(1)}, f32[16,256]{1,0:T(8,128)S(1)}, u32[]{:S(2)}, u32[]{:S(2)}) collective-permute-start(f32[16,256]{1,0:T(8,128)S(1)} %get-tuple-element.57.own_ref), channel_id=1, source_target_pairs={{0,4},{4,0},{8,12},{12,8},{16,20},{20,16},{24,28},{28,24},{32,36},... | collective-permute-start | bytes 49160 | tf_op jit(solution)/shard_map/ppermute | solution.py:325
  22.7 9.8 %collective-permute-start.12 = (f32[16,256]{1,0:T(8,128)S(1)}, f32[16,256]{1,0:T(8,128)S(1)}, u32[]{:S(2)}, u32[]{:S(2)}) collective-permute-start(f32[16,256]{1,0:T(8,128)S(1)} %get-tuple-element.57.own_ref), channel_id=1, source_target_pairs={{4,8},{8,4},{12,16},{16,12},{20,24},{24,20},{28,32},{32,28},{36,40... | collective-permute-start | bytes 49160 | tf_op jit(solution)/shard_map/ppermute | solution.py:329
  28.2 9.4 %copy-start.4 = (bf16[512,128]{1,0:T(8,128)(2,1)}, bf16[512,128]{1,0:T(8,128)(2,1)S(1)}, u32[]{:S(2)}) copy-start(bf16[512,128]{1,0:T(8,128)(2,1)S(1)} %add_convert_fusion.p0_ref) | copy-start | bytes 393220
  28.3 9.4 %copy-start = (bf16[2,512,512]{2,1,0:T(8,128)(2,1)S(1)}, bf16[2,512,512]{2,1,0:T(8,128)(2,1)}, u32[]{:S(2)}) copy-start(bf16[2,512,512]{2,1,0:T(8,128)(2,1)} %refs_1_.3) | copy-start | bytes 3145732
  28.3 9.4 %copy-start.2 = (bf16[2,512,512]{2,1,0:T(8,128)(2,1)S(1)}, bf16[2,512,512]{2,1,0:T(8,128)(2,1)}, u32[]{:S(2)}) copy-start(bf16[2,512,512]{2,1,0:T(8,128)(2,1)} %radiate_ref.3) | copy-start | bytes 3145732
  28.3 8.8 %collective-permute-start.10 = (bf16[512,128]{1,0:T(8,128)(2,1)S(1)}, bf16[512,128]{1,0:T(8,128)(2,1)S(1)}, u32[]{:S(2)}, u32[]{:S(2)}) collective-permute-start(bf16[512,128]{1,0:T(8,128)(2,1)S(1)} %add_convert_fusion.p0_ref), channel_id=1, source_target_pairs={{0,1},{1,2},{2,3},{3,0},{4,5},{5,6},{6,7},{7,4},{8,9},{9,10},{10,1... | collective-permute-start | bytes 393224 | tf_op jit(solution)/shard_map/ppermute | solution.py:321
  29.5 7.6 %collective-permute-start.8 = (bf16[512,128]{1,0:T(8,128)(2,1)S(1)}, bf16[512,128]{1,0:T(8,128)(2,1)S(1)}, u32[]{:S(2)}, u32[]{:S(2)}) collective-permute-start(bf16[512,128]{1,0:T(8,128)(2,1)S(1)} %add_convert_fusion.p0_ref), channel_id=1, source_target_pairs={{0,2},{1,3},{2,0},{3,1},{4,6},{5,7},{6,4},{7,5},{8,10},{9,11},{10,... | collective-permute-start | bytes 393224 | tf_op jit(solution)/shard_map/ppermute | solution.py:321
  31.7 5.9 %collective-permute-start.9 = (bf16[512,128]{1,0:T(8,128)(2,1)S(1)}, bf16[512,128]{1,0:T(8,128)(2,1)S(1)}, u32[]{:S(2)}, u32[]{:S(2)}) collective-permute-start(bf16[512,128]{1,0:T(8,128)(2,1)S(1)} %add_convert_fusion.p0_ref), channel_id=1, source_target_pairs={{0,3},{1,0},{2,1},{3,2},{4,7},{5,4},{6,5},{7,6},{8,11},{9,8},{10,9... | collective-permute-start | bytes 393224 | tf_op jit(solution)/shard_map/ppermute | solution.py:321
  39.6 9.8 %collective-permute-start.14 = (bf16[4,256,128]{2,1,0:T(8,128)(2,1)S(1)}, bf16[4,256,128]{2,1,0:T(8,128)(2,1)S(1)}, u32[]{:S(2)}, u32[]{:S(2)}) collective-permute-start(bf16[4,256,128]{2,1,0:T(8,128)(2,1)S(1)} %get-tuple-element.62), channel_id=1, source_target_pairs={{4,8},{8,4},{12,16},{16,12},{20,24},{24,20},{28,32},{32,28},{36,40... | collective-permute-start | bytes 786440 | tf_op jit(solution)/shard_map/ppermute | solution.py:329
  43.6 5.8 %collective-permute-start.13 = (bf16[4,256,128]{2,1,0:T(8,128)(2,1)S(1)}, bf16[4,256,128]{2,1,0:T(8,128)(2,1)S(1)}, u32[]{:S(2)}, u32[]{:S(2)}) collective-permute-start(bf16[4,256,128]{2,1,0:T(8,128)(2,1)S(1)} %tested_even.1), channel_id=1, source_target_pairs={{0,4},{4,0},{8,12},{12,8},{16,20},{20,16},{24,28},{28,24},{32,36},... | collective-permute-start | bytes 786440 | tf_op jit(solution)/shard_map/ppermute | solution.py:325
  49.6 5.6 %collective-permute-start.15 = (bf16[256,128]{1,0:T(8,128)(2,1)S(1)}, bf16[256,128]{1,0:T(8,128)(2,1)S(1)}, u32[]{:S(2)}, u32[]{:S(2)}) collective-permute-start(bf16[256,128]{1,0:T(8,128)(2,1)S(1)} %get-tuple-element.67), channel_id=1, source_target_pairs={{0,1},{1,2},{2,3},{3,0},{4,5},{5,6},{6,7},{7,4},{8,9},{9,10},{10,1... | collective-permute-start | bytes 196616 | tf_op jit(solution)/shard_map/ppermute | solution.py:321
  50.4 6.3 %collective-permute-start.16 = (bf16[256,128]{1,0:T(8,128)(2,1)S(1)}, bf16[256,128]{1,0:T(8,128)(2,1)S(1)}, u32[]{:S(2)}, u32[]{:S(2)}) collective-permute-start(bf16[256,128]{1,0:T(8,128)(2,1)S(1)} %get-tuple-element.68), channel_id=1, source_target_pairs={{0,2},{1,3},{2,0},{3,1},{4,6},{5,7},{6,4},{7,5},{8,10},{9,11},{10,... | collective-permute-start | bytes 196616 | tf_op jit(solution)/shard_map/ppermute | solution.py:321
  53.8 4.3 %collective-permute-start.17 = (bf16[256,128]{1,0:T(8,128)(2,1)S(1)}, bf16[256,128]{1,0:T(8,128)(2,1)S(1)}, u32[]{:S(2)}, u32[]{:S(2)}) collective-permute-start(bf16[256,128]{1,0:T(8,128)(2,1)S(1)} %get-tuple-element.69), channel_id=1, source_target_pairs={{0,3},{1,0},{2,1},{3,2},{4,7},{5,4},{6,5},{7,6},{8,11},{9,8},{10,9... | collective-permute-start | bytes 196616 | tf_op jit(solution)/shard_map/ppermute | solution.py:321

commit v12 on v10

--- a/solution.py
+++ b/solution.py
@@ -167,8 +167,7 @@
     for at in tiles(m):
         for c in range(radiate_ref.shape[0]):
             re, im = rotated(mm(current_ref[at], radiate_ref[c]), own_cos[c, at], own_sin[c, at], -1)
-            outs[2 * c][at] = re.astype(BF)
-            outs[2 * c + 1][at] = im.astype(BF)
+            outs[c][at] = jnp.concatenate([re, im], axis=1).astype(BF)
 
 
 def prepare(dirs_ref, mom_c, po_c, src_ref, weight_ref, odd_cos, odd_sin, po_cos, po_sin, pick_ref):
@@ -186,7 +185,7 @@
 
 
 def incident(
-    odd_ref, e0, e1, e2, e3, w0, w1, w2, w3, pick_ref, radiate_ref, receive_ref, odd_cos, odd_sin, po_cos, po_sin, lit_ref,
+    odd_ref, e0, e1, w0, w1, pick_ref, radiate_ref, receive_ref, odd_cos, odd_sin, po_cos, po_sin, lit_ref,
     own_ref, s1_ref, s2_ref, s3_ref,
     table, chunks,
 ):
@@ -196,9 +195,9 @@
     k = k2 // 2
     side = parity() * 2 * m
     for at in tiles(m):
-        for i, (e_ref, w_ref) in enumerate(((e0, w0), (e1, w1), (e2, w2), (e3, w3))):
-            table[rows_at(m, at), i * k : (i + 1) * k] = w_ref[at]
-            table[rows_at(2 * m - side, at), i * k : (i + 1) * k] = e_ref[at]
+        for c, (e_ref, w_ref) in enumerate(((e0, w0), (e1, w1))):
+            table[rows_at(m, at), c * k2 : (c + 1) * k2] = w_ref[at]
+            table[rows_at(2 * m - side, at), c * k2 : (c + 1) * k2] = e_ref[at]
         radiated(odd_ref, at, radiate_ref, odd_cos, odd_sin, table, side, 0)
     lit_col = jnp.concatenate([lit_ref[...].astype(F32), jnp.zeros((8 - cones, q), F32)], axis=0).T
     for at in tiles(q):
@@ -347,7 +346,7 @@
         angles
         + (shape(waves3.shape, F32), shape((3, m), F32), shape((3, q), F32), shape(po_src.shape, po_src.dtype))
         + (shape(po_weight.shape, F32), shape(lit.shape, lit.dtype), shape((16, m), F32))
-        + (shape((m, k), BF),) * (2 * cones),
+        + (shape((m, k2), BF),) * cones,
         (mom_current, mom_radiate, waves3, mom_center, po_center, po_src, po_weight, mom_src, mom_weight, lit),
         scratch(mom_current, mom_radiate)
         + (pltpu.VMEM((3, m), F32), pltpu.VMEM(mom_src.shape, mom_src.dtype), pltpu.SemaphoreType.DMA((11,))),

time: 58.3 us -> 57.8 us (level)
    ppermute x3, starting transfers between devices: 12.6 us -> 13.3 us  [swapped_odd(): lax.ppermute(value, 'box', [(i, (i + 1 ^ 1) - 1) for i in range(1, lax.ax...]
    ppermute x6 -> x4, starting transfers between devices: 1.28 us -> 0.77 us  [swapped_even(): lax.ppermute(value, 'box', [(i, i ^ 1) for i in range(lax.axis_size('box'...]
  transfers between devices with their start and end apart: 18 -> 16, of which waited for: 8 -> 8; matrix products, arithmetic and copies ran while one was open for 0% -> 0% of each run, Pallas kernels for 17% -> 17%
where the time goes in v12:
time: 57.8 us; the launch traced here: 57.7 us
  starting transfers between devices  26.3 us (46%)
  Pallas kernels  15 us (26%)
  waiting for transfers between devices  14.7 us (25%)
  between operations  0.87 us (2%)
  other arithmetic  0.74 us (1%)
    pallas_call x10, Pallas kernels, call(): pl.pallas_call(body, out_shape=outs, in_specs=[pl.BlockSpec(memory_space=...  15 us
    ppermute x3, starting transfers between devices, swapped_odd(): lax.ppermute(value, 'box', [(i, (i + 1 ^ 1) - 1) for i in range(1, lax.ax...  13.3 us
    ppermute x9, starting transfers between devices, turned(): lax.ppermute(value, 'cone', [(i, (i + shift) % count) for i in range(coun...  12.2 us
    ppermute x9, waiting for transfers between devices, turned(): lax.ppermute(value, 'cone', [(i, (i + shift) % count) for i in range(coun...  9.56 us
    ppermute x3, waiting for transfers between devices, swapped_odd(): lax.ppermute(value, 'box', [(i, (i + 1 ^ 1) - 1) for i in range(1, lax.ax...  5.13 us
  transfers between devices with their start and end apart: 16, of which 8 were waited for; matrix products, arithmetic and copies ran while one was open for 0% of the time, Pallas kernels for 17%

profile of v12, /device:TPU:6, one launch (start us, length us, event | category | flops | bytes accessed | tf_op | source)
XLA Modules:
  0.0 57.7 jit_solution(9037527705178465053)
XLA Ops:
  0.6 7.5 %collective-permute-start = (bf16[256,512]{1,0:T(8,128)(2,1)}, bf16[256,512]{1,0:T(8,128)(2,1)S(1)}, u32[]{:S(2)}, u32[]{:S(2)}) collective-permute-start(bf16[256,512]{1,0:T(8,128)(2,1)} %current_hbm.1), channel_id=1, source_target_pairs={{4,8},{8,4},{12,16},{16,12},{20,24},{24,20},{28,32},{32,28},{36,40... | collective-permute-start | bytes 786440 | tf_op jit(solution)/shard_map/ppermute | solution.py:321
  8.1 0.0 copy-start.1
  8.1 0.0 copy-start.2
  8.1 2.1 %own_waves.1 = (f32[2,256,256]{2,1,0:T(8,128)S(1)}, f32[2,256,256]{2,1,0:T(8,128)S(1)}, f32[3,2,256]{2,1,0:T(2,128)S(1)}, f32[3,256]{1,0:T(4,128)S(1)}, f32[3,51...) custom-call(bf16[256,512]{1,0:T(8,128)(2,1)} %current_hbm.1, ...), custom_call_target="tpu_custom_call" | custom-call | flops 1 | bytes 1 | tf_op jit(solution)/shard_map/own_waves/pallas_call | solution.py:299
  10.2 0.1 collective-permute-start.1
  10.3 0.5 collective-permute-start.2
  10.8 2.7 %prepare.1 = (f32[2,256,256]{2,1,0:T(8,128)S(1)}, f32[2,256,256]{2,1,0:T(8,128)S(1)}, f32[2,512,256]{2,1,0:T(8,128)S(1)}, f32[2,512,256]{2,1,0:T(8,128)S(1)}, bf16[512,768]{1,0:T(8,128)(2,1)S(1)}) custom-call(f32[3,2,256]{2,1,0:T(2,128)S(1)} %get-tuple-element.36.dirs_ref, f32[3,256]{1,0:T(4,128)S(1)} %get-tuple-element.37.mom_c, ...), custom_call_target="tpu_custom_call" | custom-call | flops 1 | bytes 1 | tf_op jit(solution)/shard_map/prepare/pallas_call | solution.py:299
  13.5 0.0 collective-permute-done.odd_ref
  13.5 0.0 collective-permute-done.1.e0
  13.5 0.0 collective-permute-done.2.e1
  13.6 0.0 copy-done.1
  13.6 0.0 copy-done.2
  13.6 3.1 %incident.1 = (f32[512,128]{1,0:T(8,128)S(1)}, bf16[512,128]{1,0:T(8,128)(2,1)S(1)}, bf16[512,128]{1,0:T(8,128)(2,1)S(1)}, bf16[512,128]{1,0:T(8,128)(2,1)S(1)}) custom-call(bf16[256,512]{1,0:T(8,128)(2,1)S(1)} %collective-permute-done.odd_ref, bf16[256,512]{1,0:T(8,128)(2,1)S(1)} %collective-permute-done.1.e0, ...), custom_call_target="tpu_custom_call" | custom-call | flops 1 | bytes 1 | tf_op jit(solution)/shard_map/incident/pallas_call | solution.py:299
  16.7 1.7 %collective-permute-start.3 = (bf16[512,128]{1,0:T(8,128)(2,1)S(1)}, bf16[512,128]{1,0:T(8,128)(2,1)S(1)}, u32[]{:S(2)}, u32[]{:S(2)}) collective-permute-start(bf16[512,128]{1,0:T(8,128)(2,1)S(1)} %get-tuple-element.47), channel_id=1, source_target_pairs={{0,1},{1,2},{2,3},{3,0},{4,5},{5,6},{6,7},{7,4},{8,9},{9,10},{10,1... | collective-permute-start | bytes 393224 | tf_op jit(solution)/shard_map/ppermute | solution.py:313
  18.4 1.6 %collective-permute-start.4 = (bf16[512,128]{1,0:T(8,128)(2,1)S(1)}, bf16[512,128]{1,0:T(8,128)(2,1)S(1)}, u32[]{:S(2)}, u32[]{:S(2)}) collective-permute-start(bf16[512,128]{1,0:T(8,128)(2,1)S(1)} %get-tuple-element.51), channel_id=1, source_target_pairs={{0,3},{1,0},{2,1},{3,2},{4,7},{5,4},{6,5},{7,6},{8,11},{9,8},{10,9... | collective-permute-start | bytes 393224 | tf_op jit(solution)/shard_map/ppermute | solution.py:313
  20.0 2.0 %collective-permute-start.5 = (bf16[512,128]{1,0:T(8,128)(2,1)S(1)}, bf16[512,128]{1,0:T(8,128)(2,1)S(1)}, u32[]{:S(2)}, u32[]{:S(2)}) collective-permute-start(bf16[512,128]{1,0:T(8,128)(2,1)S(1)} %get-tuple-element.52), channel_id=1, source_target_pairs={{0,2},{1,3},{2,0},{3,1},{4,6},{5,7},{6,4},{7,5},{8,10},{9,11},{10,... | collective-permute-start | bytes 393224 | tf_op jit(solution)/shard_map/ppermute | solution.py:313
  22.0 3.7 %collective-permute-start.10 = (f32[16,256]{1,0:T(8,128)S(1)}, f32[16,256]{1,0:T(8,128)S(1)}, u32[]{:S(2)}, u32[]{:S(2)}) collective-permute-start(f32[16,256]{1,0:T(8,128)S(1)} %get-tuple-element.53.own_ref), channel_id=1, source_target_pairs={{4,8},{8,4},{12,16},{16,12},{20,24},{24,20},{28,32},{32,28},{36,40... | collective-permute-start | bytes 49160 | tf_op jit(solution)/shard_map/ppermute | solution.py:321
  25.7 0.1 collective-permute-start.9
  25.8 0.0 collective-permute-done.3.new_ref
  25.9 0.0 collective-permute-done.4
  25.9 1.7 %collective-permute-done.5 = bf16[512,128]{1,0:T(8,128)(2,1)S(1)} collective-permute-done((bf16[512,128]{1,0:T(8,128)(2,1)S(1)}, bf16[512,128]{1,0:T(8,128)(2,1)S(1)}, u32[]{:S(2)}, u32[]{:S(2)}) %collective-permute-start.5) | collective-permute-done | bytes 131104 | tf_op jit(solution)/shard_map/ppermute | solution.py:313
  27.6 0.1 add_convert_fusion.p0_ref
  27.6 0.0 copy-start.4
  27.6 0.0 copy-start
  27.6 0.0 copy-start.3
  27.6 1.2 %collective-permute-start.8 = (bf16[512,128]{1,0:T(8,128)(2,1)S(1)}, bf16[512,128]{1,0:T(8,128)(2,1)S(1)}, u32[]{:S(2)}, u32[]{:S(2)}) collective-permute-start(bf16[512,128]{1,0:T(8,128)(2,1)S(1)} %add_convert_fusion.p0_ref), channel_id=1, source_target_pairs={{0,1},{1,2},{2,3},{3,0},{4,5},{5,6},{6,7},{7,4},{8,9},{9,10},{10,1... | collective-permute-start | bytes 393224 | tf_op jit(solution)/shard_map/ppermute | solution.py:313
  28.9 2.1 %collective-permute-start.7 = (bf16[512,128]{1,0:T(8,128)(2,1)S(1)}, bf16[512,128]{1,0:T(8,128)(2,1)S(1)}, u32[]{:S(2)}, u32[]{:S(2)}) collective-permute-start(bf16[512,128]{1,0:T(8,128)(2,1)S(1)} %add_convert_fusion.p0_ref), channel_id=1, source_target_pairs={{0,3},{1,0},{2,1},{3,2},{4,7},{5,4},{6,5},{7,6},{8,11},{9,8},{10,9... | collective-permute-start | bytes 393224 | tf_op jit(solution)/shard_map/ppermute | solution.py:313
  31.0 0.1 collective-permute-start.6
  31.1 0.0 collective-permute-done.10.odd_ref
  31.1 0.0 collective-permute-done.9.even_ref
  31.1 2.8 %lists.1 = (bf16[768,512]{1,0:T(8,128)(2,1)S(1)}, f32[2,256,256]{2,1,0:T(8,128)S(1)}, f32[2,256,256]{2,1,0:T(8,128)S(1)}) custom-call(f32[16,256]{1,0:T(8,128)S(1)} %collective-permute-done.9.even_ref, f32[16,256]{1,0:T(8,128)S(1)} %get-tuple-element.53.own_ref, f32[16,256]{1,0:T(8,128)S(1)} %collective-permute-done.10.odd_ref, ...), custom_call_target="tpu_custom_call" | custom-call | flops 4000000000 | bytes 1 | tf_op jit(solution)/shard_map/lists/pallas_call | solution.py:299
  33.8 0.2 collective-permute-done.8.p1_ref
  34.0 1.7 %collective-permute-done.7.p3_ref = bf16[512,128]{1,0:T(8,128)(2,1)S(1)} collective-permute-done((bf16[512,128]{1,0:T(8,128)(2,1)S(1)}, bf16[512,128]{1,0:T(8,128)(2,1)S(1)}, u32[]{:S(2)}, u32[]{:S(2)}) %collective-permute-start.7) | collective-permute-done | bytes 131104 | tf_op jit(solution)/shard_map/ppermute | solution.py:313
  35.7 1.7 %collective-permute-done.6.p2_ref = bf16[512,128]{1,0:T(8,128)(2,1)S(1)} collective-permute-done((bf16[512,128]{1,0:T(8,128)(2,1)S(1)}, bf16[512,128]{1,0:T(8,128)(2,1)S(1)}, u32[]{:S(2)}, u32[]{:S(2)}) %collective-permute-start.6) | collective-permute-done | bytes 131104 | tf_op jit(solution)/shard_map/ppermute | solution.py:313
  37.4 1.8 %scattered.1 = (bf16[512,1024]{1,0:T(8,128)(2,1)S(1)}, bf16[4,256,128]{2,1,0:T(8,128)(2,1)S(1)}) custom-call(bf16[512,128]{1,0:T(8,128)(2,1)S(1)} %add_convert_fusion.p0_ref, bf16[512,128]{1,0:T(8,128)(2,1)S(1)} %collective-permute-done.6.p2_ref, bf16[512,128]{1,0:T(8,128)(2,1)S(1)} %collective-permute-done.7.p3_ref, ...), custom_call_target="tpu_custom_call" | custom-call | flops 1 | bytes 1 | tf_op jit(solution)/shard_map/scattered/pallas_call | solution.py:299
  39.3 2.1 %collective-permute-start.12 = (bf16[4,256,128]{2,1,0:T(8,128)(2,1)S(1)}, bf16[4,256,128]{2,1,0:T(8,128)(2,1)S(1)}, u32[]{:S(2)}, u32[]{:S(2)}) collective-permute-start(bf16[4,256,128]{2,1,0:T(8,128)(2,1)S(1)} %get-tuple-element.58), channel_id=1, source_target_pairs={{4,8},{8,4},{12,16},{16,12},{20,24},{24,20},{28,32},{32,28},{36,40... | collective-permute-start | bytes 786440 | tf_op jit(solution)/shard_map/ppermute | solution.py:321
  41.5 1.2 %tested_even.1 = bf16[4,256,128]{2,1,0:T(8,128)(2,1)S(1)} custom-call(bf16[512,1024]{1,0:T(8,128)(2,1)S(1)} %get-tuple-element.59.refs_0_, bf16[2,512,512]{2,1,0:T(8,128)(2,1)S(1)} %copy-done, bf16[768,512]{1,0:T(8,128)(2,1)S(1)} %get-tuple-element.54.pick_ref.refs_2_, f32[2,256,256]{2,1,0:T(8,128)S(1)} %get-tuple-element.56.refs_3_, ...), custom_call_target="tpu_custom_call" | custom-call | flops 1 | bytes 1 | tf_op jit(solution)/shard_map/tested_even/pallas_call | solution.py:299
  42.7 0.1 collective-permute-start.11
  42.8 1.2 %tested_own.1.own_ref = f32[4,256,128]{2,1,0:T(8,128)S(1)} custom-call(bf16[512,1024]{1,0:T(8,128)(2,1)S(1)} %get-tuple-element.59.refs_0_, bf16[2,512,512]{2,1,0:T(8,128)(2,1)S(1)} %copy-done, bf16[768,512]{1,0:T(8,128)(2,1)S(1)} %get-tuple-element.54.pick_ref.refs_2_, f32[2,256,256]{2,1,0:T(8,128)S(1)} %get-tuple-element.60.refs_3_, ...), custom_call_target="tpu_custom_call" | custom-call | flops 1 | bytes 1 | tf_op jit(solution)/shard_map/tested_own/pallas_call | solution.py:299
  44.0 5.1 %collective-permute-done.12.new_ref = bf16[4,256,128]{2,1,0:T(8,128)(2,1)S(1)} collective-permute-done((bf16[4,256,128]{2,1,0:T(8,128)(2,1)S(1)}, bf16[4,256,128]{2,1,0:T(8,128)(2,1)S(1)}, u32[]{:S(2)}, u32[]{:S(2)}) %collective-permute-start.12) | collective-permute-done | bytes 262176 | tf_op jit(solution)/shard_map/ppermute | solution.py:321
  49.2 0.0 collective-permute-done.11.even_ref
  49.2 0.2 collective-permute-start.13
  49.4 3.3 %collective-permute-start.14 = (bf16[256,128]{1,0:T(8,128)(2,1)S(1)}, bf16[256,128]{1,0:T(8,128)(2,1)S(1)}, u32[]{:S(2)}, u32[]{:S(2)}) collective-permute-start(bf16[256,128]{1,0:T(8,128)(2,1)S(1)} %get-tuple-element.64), channel_id=1, source_target_pairs={{0,2},{1,3},{2,0},{3,1},{4,6},{5,7},{6,4},{7,5},{8,10},{9,11},{10,... | collective-permute-start | bytes 196616 | tf_op jit(solution)/shard_map/ppermute | solution.py:313
  52.7 0.0 collective-permute-start.15
  52.7 2.1 %collective-permute-done.13 = bf16[256,128]{1,0:T(8,128)(2,1)S(1)} collective-permute-done((bf16[256,128]{1,0:T(8,128)(2,1)S(1)}, bf16[256,128]{1,0:T(8,128)(2,1)S(1)}, u32[]{:S(2)}, u32[]{:S(2)}) %collective-permute-start.13) | collective-permute-done | bytes 65568 | tf_op jit(solution)/shard_map/ppermute | solution.py:313
  54.8 0.9 %collective-permute-done.14 = bf16[256,128]{1,0:T(8,128)(2,1)S(1)} collective-permute-done((bf16[256,128]{1,0:T(8,128)(2,1)S(1)}, bf16[256,128]{1,0:T(8,128)(2,1)S(1)}, u32[]{:S(2)}, u32[]{:S(2)}) %collective-permute-start.14) | collective-permute-done | bytes 65568 | tf_op jit(solution)/shard_map/ppermute | solution.py:313
  55.6 1.3 %collective-permute-done.15 = bf16[256,128]{1,0:T(8,128)(2,1)S(1)} collective-permute-done((bf16[256,128]{1,0:T(8,128)(2,1)S(1)}, bf16[256,128]{1,0:T(8,128)(2,1)S(1)}, u32[]{:S(2)}, u32[]{:S(2)}) %collective-permute-start.15) | collective-permute-done | bytes 65568 | tf_op jit(solution)/shard_map/ppermute | solution.py:313
  57.0 0.7 %convert_add_fusion = f32[256,128]{1,0:T(8,128)} fusion(bf16[256,128]{1,0:T(8,128)(2,1)S(1)} %collective-permute-done.15, bf16[256,128]{1,0:T(8,128)(2,1)S(1)} %collective-permute-done.14, f32[256,128]{1,0:T(8,128)S(1)} %get-tuple-element.62, bf16[256,128]{1,0:T(8,128)(2,1)S(1)} %collective-permute-done.13), kind=kLoop, calls=%fused_computation.1 | loop fusion | flops 196608 | bytes 458752 | tf_op jit(solution)/shard_map/add | solution.py:407
  (6 shorter events, 0.1 us)
Async XLA Ops:
  0.6 12.9 %collective-permute-start = (bf16[256,512]{1,0:T(8,128)(2,1)}, bf16[256,512]{1,0:T(8,128)(2,1)S(1)}, u32[]{:S(2)}, u32[]{:S(2)}) collective-permute-start(bf16[256,512]{1,0:T(8,128)(2,1)} %current_hbm.1), channel_id=1, source_target_pairs={{4,8},{8,4},{12,16},{16,12},{20,24},{24,20},{28,32},{32,28},{36,40... | collective-permute-start | bytes 786440 | tf_op jit(solution)/shard_map/ppermute | solution.py:321
  8.1 5.5 %copy-start.1 = (bf16[2,512,512]{2,1,0:T(8,128)(2,1)S(1)}, bf16[2,512,512]{2,1,0:T(8,128)(2,1)}, u32[]{:S(2)}) copy-start(bf16[2,512,512]{2,1,0:T(8,128)(2,1)} %radiate_ref.2) | copy-start | bytes 3145732
  8.1 5.5 %copy-start.2 = (bf16[2,512,512]{2,1,0:T(8,128)(2,1)S(1)}, bf16[2,512,512]{2,1,0:T(8,128)(2,1)}, u32[]{:S(2)}) copy-start(bf16[2,512,512]{2,1,0:T(8,128)(2,1)} %receive_ref.2) | copy-start | bytes 3145732
  10.2 3.3 %collective-permute-start.1 = (bf16[256,512]{1,0:T(8,128)(2,1)S(1)}, bf16[256,512]{1,0:T(8,128)(2,1)S(1)}, u32[]{:S(2)}, u32[]{:S(2)}) collective-permute-start(bf16[256,512]{1,0:T(8,128)(2,1)S(1)} %get-tuple-element.34.w0), channel_id=1, source_target_pairs={{0,4},{4,0},{8,12},{12,8},{16,20},{20,16},{24,28},{28,24},{32,36},... | collective-permute-start | bytes 786440 | tf_op jit(solution)/shard_map/ppermute | solution.py:317
  10.3 3.3 %collective-permute-start.2 = (bf16[256,512]{1,0:T(8,128)(2,1)S(1)}, bf16[256,512]{1,0:T(8,128)(2,1)S(1)}, u32[]{:S(2)}, u32[]{:S(2)}) collective-permute-start(bf16[256,512]{1,0:T(8,128)(2,1)S(1)} %get-tuple-element.35.w1), channel_id=1, source_target_pairs={{0,4},{4,0},{8,12},{12,8},{16,20},{20,16},{24,28},{28,24},{32,36},... | collective-permute-start | bytes 786440 | tf_op jit(solution)/shard_map/ppermute | solution.py:317
  16.7 9.1 %collective-permute-start.3 = (bf16[512,128]{1,0:T(8,128)(2,1)S(1)}, bf16[512,128]{1,0:T(8,128)(2,1)S(1)}, u32[]{:S(2)}, u32[]{:S(2)}) collective-permute-start(bf16[512,128]{1,0:T(8,128)(2,1)S(1)} %get-tuple-element.47), channel_id=1, source_target_pairs={{0,1},{1,2},{2,3},{3,0},{4,5},{5,6},{6,7},{7,4},{8,9},{9,10},{10,1... | collective-permute-start | bytes 393224 | tf_op jit(solution)/shard_map/ppermute | solution.py:313
  18.4 7.5 %collective-permute-start.4 = (bf16[512,128]{1,0:T(8,128)(2,1)S(1)}, bf16[512,128]{1,0:T(8,128)(2,1)S(1)}, u32[]{:S(2)}, u32[]{:S(2)}) collective-permute-start(bf16[512,128]{1,0:T(8,128)(2,1)S(1)} %get-tuple-element.51), channel_id=1, source_target_pairs={{0,3},{1,0},{2,1},{3,2},{4,7},{5,4},{6,5},{7,6},{8,11},{9,8},{10,9... | collective-permute-start | bytes 393224 | tf_op jit(solution)/shard_map/ppermute | solution.py:313
  20.0 7.6 %collective-permute-start.5 = (bf16[512,128]{1,0:T(8,128)(2,1)S(1)}, bf16[512,128]{1,0:T(8,128)(2,1)S(1)}, u32[]{:S(2)}, u32[]{:S(2)}) collective-permute-start(bf16[512,128]{1,0:T(8,128)(2,1)S(1)} %get-tuple-element.52), channel_id=1, source_target_pairs={{0,2},{1,3},{2,0},{3,1},{4,6},{5,7},{6,4},{7,5},{8,10},{9,11},{10,... | collective-permute-start | bytes 393224 | tf_op jit(solution)/shard_map/ppermute | solution.py:313
  22.0 9.0 %collective-permute-start.10 = (f32[16,256]{1,0:T(8,128)S(1)}, f32[16,256]{1,0:T(8,128)S(1)}, u32[]{:S(2)}, u32[]{:S(2)}) collective-permute-start(f32[16,256]{1,0:T(8,128)S(1)} %get-tuple-element.53.own_ref), channel_id=1, source_target_pairs={{4,8},{8,4},{12,16},{16,12},{20,24},{24,20},{28,32},{32,28},{36,40... | collective-permute-start | bytes 49160 | tf_op jit(solution)/shard_map/ppermute | solution.py:321
  25.7 5.4 %collective-permute-start.9 = (f32[16,256]{1,0:T(8,128)S(1)}, f32[16,256]{1,0:T(8,128)S(1)}, u32[]{:S(2)}, u32[]{:S(2)}) collective-permute-start(f32[16,256]{1,0:T(8,128)S(1)} %get-tuple-element.53.own_ref), channel_id=1, source_target_pairs={{0,4},{4,0},{8,12},{12,8},{16,20},{20,16},{24,28},{28,24},{32,36},... | collective-permute-start | bytes 49160 | tf_op jit(solution)/shard_map/ppermute | solution.py:317
  27.6 9.8 %copy-start.4 = (bf16[512,128]{1,0:T(8,128)(2,1)}, bf16[512,128]{1,0:T(8,128)(2,1)S(1)}, u32[]{:S(2)}) copy-start(bf16[512,128]{1,0:T(8,128)(2,1)S(1)} %add_convert_fusion.p0_ref) | copy-start | bytes 393220
  27.6 9.8 %copy-start = (bf16[2,512,512]{2,1,0:T(8,128)(2,1)S(1)}, bf16[2,512,512]{2,1,0:T(8,128)(2,1)}, u32[]{:S(2)}) copy-start(bf16[2,512,512]{2,1,0:T(8,128)(2,1)} %refs_1_.3) | copy-start | bytes 3145732
  27.6 9.8 %copy-start.3 = (bf16[2,512,512]{2,1,0:T(8,128)(2,1)S(1)}, bf16[2,512,512]{2,1,0:T(8,128)(2,1)}, u32[]{:S(2)}) copy-start(bf16[2,512,512]{2,1,0:T(8,128)(2,1)} %radiate_ref.3) | copy-start | bytes 3145732
  27.6 6.4 %collective-permute-start.8 = (bf16[512,128]{1,0:T(8,128)(2,1)S(1)}, bf16[512,128]{1,0:T(8,128)(2,1)S(1)}, u32[]{:S(2)}, u32[]{:S(2)}) collective-permute-start(bf16[512,128]{1,0:T(8,128)(2,1)S(1)} %add_convert_fusion.p0_ref), channel_id=1, source_target_pairs={{0,1},{1,2},{2,3},{3,0},{4,5},{5,6},{6,7},{7,4},{8,9},{9,10},{10,1... | collective-permute-start | bytes 393224 | tf_op jit(solution)/shard_map/ppermute | solution.py:313
  28.9 6.8 %collective-permute-start.7 = (bf16[512,128]{1,0:T(8,128)(2,1)S(1)}, bf16[512,128]{1,0:T(8,128)(2,1)S(1)}, u32[]{:S(2)}, u32[]{:S(2)}) collective-permute-start(bf16[512,128]{1,0:T(8,128)(2,1)S(1)} %add_convert_fusion.p0_ref), channel_id=1, source_target_pairs={{0,3},{1,0},{2,1},{3,2},{4,7},{5,4},{6,5},{7,6},{8,11},{9,8},{10,9... | collective-permute-start | bytes 393224 | tf_op jit(solution)/shard_map/ppermute | solution.py:313
  31.0 6.5 %collective-permute-start.6 = (bf16[512,128]{1,0:T(8,128)(2,1)S(1)}, bf16[512,128]{1,0:T(8,128)(2,1)S(1)}, u32[]{:S(2)}, u32[]{:S(2)}) collective-permute-start(bf16[512,128]{1,0:T(8,128)(2,1)S(1)} %add_convert_fusion.p0_ref), channel_id=1, source_target_pairs={{0,2},{1,3},{2,0},{3,1},{4,6},{5,7},{6,4},{7,5},{8,10},{9,11},{10,... | collective-permute-start | bytes 393224 | tf_op jit(solution)/shard_map/ppermute | solution.py:313
  39.3 9.8 %collective-permute-start.12 = (bf16[4,256,128]{2,1,0:T(8,128)(2,1)S(1)}, bf16[4,256,128]{2,1,0:T(8,128)(2,1)S(1)}, u32[]{:S(2)}, u32[]{:S(2)}) collective-permute-start(bf16[4,256,128]{2,1,0:T(8,128)(2,1)S(1)} %get-tuple-element.58), channel_id=1, source_target_pairs={{4,8},{8,4},{12,16},{16,12},{20,24},{24,20},{28,32},{32,28},{36,40... | collective-permute-start | bytes 786440 | tf_op jit(solution)/shard_map/ppermute | solution.py:321
  42.7 6.5 %collective-permute-start.11 = (bf16[4,256,128]{2,1,0:T(8,128)(2,1)S(1)}, bf16[4,256,128]{2,1,0:T(8,128)(2,1)S(1)}, u32[]{:S(2)}, u32[]{:S(2)}) collective-permute-start(bf16[4,256,128]{2,1,0:T(8,128)(2,1)S(1)} %tested_even.1), channel_id=1, source_target_pairs={{0,4},{4,0},{8,12},{12,8},{16,20},{20,16},{24,28},{28,24},{32,36},... | collective-permute-start | bytes 786440 | tf_op jit(solution)/shard_map/ppermute | solution.py:317
  49.2 5.6 %collective-permute-start.13 = (bf16[256,128]{1,0:T(8,128)(2,1)S(1)}, bf16[256,128]{1,0:T(8,128)(2,1)S(1)}, u32[]{:S(2)}, u32[]{:S(2)}) collective-permute-start(bf16[256,128]{1,0:T(8,128)(2,1)S(1)} %get-tuple-element.63), channel_id=1, source_target_pairs={{0,1},{1,2},{2,3},{3,0},{4,5},{5,6},{6,7},{7,4},{8,9},{9,10},{10,1... | collective-permute-start | bytes 196616 | tf_op jit(solution)/shard_map/ppermute | solution.py:313
  49.4 6.2 %collective-permute-start.14 = (bf16[256,128]{1,0:T(8,128)(2,1)S(1)}, bf16[256,128]{1,0:T(8,128)(2,1)S(1)}, u32[]{:S(2)}, u32[]{:S(2)}) collective-permute-start(bf16[256,128]{1,0:T(8,128)(2,1)S(1)} %get-tuple-element.64), channel_id=1, source_target_pairs={{0,2},{1,3},{2,0},{3,1},{4,6},{5,7},{6,4},{7,5},{8,10},{9,11},{10,... | collective-permute-start | bytes 196616 | tf_op jit(solution)/shard_map/ppermute | solution.py:313
  52.7 4.3 %collective-permute-start.15 = (bf16[256,128]{1,0:T(8,128)(2,1)S(1)}, bf16[256,128]{1,0:T(8,128)(2,1)S(1)}, u32[]{:S(2)}, u32[]{:S(2)}) collective-permute-start(bf16[256,128]{1,0:T(8,128)(2,1)S(1)} %get-tuple-element.65), channel_id=1, source_target_pairs={{0,3},{1,0},{2,1},{3,2},{4,7},{5,4},{6,5},{7,6},{8,11},{9,8},{10,9... | collective-permute-start | bytes 196616 | tf_op jit(solution)/shard_map/ppermute | solution.py:313

commit v13 on v12

--- a/solution.py
+++ b/solution.py
@@ -404,7 +404,8 @@
     f2 = turned(f2, 2)
     f1 = turned(f1, 1)
     f3 = turned(f3, 3)
-    mom_field = f0 + f1.astype(F32) + f2.astype(F32) + f3.astype(F32)
+    f0 = call(added, shape((m, share), F32), (f1, f0))
+    mom_field = f0 + f3.astype(F32) + f2.astype(F32)
     return mom_field, po_share
 
 

time: 57.8 us -> 59.1 us (1.022)
  waiting for transfers between devices: 14.7 us -> 16 us
    ppermute x9, waiting for transfers between devices: 9.56 us -> 10.9 us  [turned(): lax.ppermute(value, 'cone', [(i, (i + shift) % count) for i in range(coun...]
    pallas_call x10 -> x11, Pallas kernels: 15 us -> 15 us  [call(): pl.pallas_call(body, out_shape=outs, in_specs=[pl.BlockSpec(memory_space=...]
  transfers between devices with their start and end apart: 16 -> 16, of which waited for: 8 -> 7; matrix products, arithmetic and copies ran while one was open for 0% -> 0% of each run, Pallas kernels for 17% -> 17%
where the time goes in v13:
time: 59.1 us; the launch traced here: 59 us
  starting transfers between devices  26.3 us (45%)
  waiting for transfers between devices  16 us (27%)
  Pallas kernels  15 us (25%)
  between operations  0.88 us (1%)
  other arithmetic  0.73 us (1%)
    pallas_call x11, Pallas kernels, call(): pl.pallas_call(body, out_shape=outs, in_specs=[pl.BlockSpec(memory_space=...  15 us
    ppermute x3, starting transfers between devices, swapped_odd(): lax.ppermute(value, 'box', [(i, (i + 1 ^ 1) - 1) for i in range(1, lax.ax...  13.3 us
    ppermute x9, starting transfers between devices, turned(): lax.ppermute(value, 'cone', [(i, (i + shift) % count) for i in range(coun...  12.2 us
    ppermute x9, waiting for transfers between devices, turned(): lax.ppermute(value, 'cone', [(i, (i + shift) % count) for i in range(coun...  10.9 us
    ppermute x3, waiting for transfers between devices, swapped_odd(): lax.ppermute(value, 'box', [(i, (i + 1 ^ 1) - 1) for i in range(1, lax.ax...  5.13 us
  transfers between devices with their start and end apart: 16, of which 7 were waited for; matrix products, arithmetic and copies ran while one was open for 0% of the time, Pallas kernels for 17%

profile of v13, /device:TPU:6, one launch (start us, length us, event | category | flops | bytes accessed | tf_op | source)
XLA Modules:
  0.0 59.0 jit_solution(14654221922058464972)
XLA Ops:
  0.6 7.5 %collective-permute-start = (bf16[256,512]{1,0:T(8,128)(2,1)}, bf16[256,512]{1,0:T(8,128)(2,1)S(1)}, u32[]{:S(2)}, u32[]{:S(2)}) collective-permute-start(bf16[256,512]{1,0:T(8,128)(2,1)} %current_hbm.1), channel_id=1, source_target_pairs={{4,8},{8,4},{12,16},{16,12},{20,24},{24,20},{28,32},{32,28},{36,40... | collective-permute-start | bytes 786440 | tf_op jit(solution)/shard_map/ppermute | solution.py:321
  8.1 0.0 copy-start.1
  8.1 2.1 %own_waves.1 = (f32[2,256,256]{2,1,0:T(8,128)S(1)}, f32[2,256,256]{2,1,0:T(8,128)S(1)}, f32[3,2,256]{2,1,0:T(2,128)S(1)}, f32[3,256]{1,0:T(4,128)S(1)}, f32[3,51...) custom-call(bf16[256,512]{1,0:T(8,128)(2,1)} %current_hbm.1, ...), custom_call_target="tpu_custom_call" | custom-call | flops 1 | bytes 1 | tf_op jit(solution)/shard_map/own_waves/pallas_call | solution.py:299
  10.2 0.1 collective-permute-start.1
  10.3 0.5 collective-permute-start.2
  10.8 2.7 %prepare.1 = (f32[2,256,256]{2,1,0:T(8,128)S(1)}, f32[2,256,256]{2,1,0:T(8,128)S(1)}, f32[2,512,256]{2,1,0:T(8,128)S(1)}, f32[2,512,256]{2,1,0:T(8,128)S(1)}, bf16[512,768]{1,0:T(8,128)(2,1)S(1)}) custom-call(f32[3,2,256]{2,1,0:T(2,128)S(1)} %get-tuple-element.36.dirs_ref, f32[3,256]{1,0:T(4,128)S(1)} %get-tuple-element.37.mom_c, ...), custom_call_target="tpu_custom_call" | custom-call | flops 1 | bytes 1 | tf_op jit(solution)/shard_map/prepare/pallas_call | solution.py:299
  13.5 0.0 collective-permute-done.odd_ref
  13.5 0.0 collective-permute-done.1.e0
  13.5 0.0 collective-permute-done.2.e1
  13.6 0.0 copy-done.1
  13.6 0.0 copy-done.2
  13.6 3.1 %incident.1 = (f32[512,128]{1,0:T(8,128)S(1)}, bf16[512,128]{1,0:T(8,128)(2,1)S(1)}, bf16[512,128]{1,0:T(8,128)(2,1)S(1)}, bf16[512,128]{1,0:T(8,128)(2,1)S(1)}) custom-call(bf16[256,512]{1,0:T(8,128)(2,1)S(1)} %collective-permute-done.odd_ref, bf16[256,512]{1,0:T(8,128)(2,1)S(1)} %collective-permute-done.1.e0, ...), custom_call_target="tpu_custom_call" | custom-call | flops 1 | bytes 1 | tf_op jit(solution)/shard_map/incident/pallas_call | solution.py:299
  16.7 1.7 %collective-permute-start.3 = (bf16[512,128]{1,0:T(8,128)(2,1)S(1)}, bf16[512,128]{1,0:T(8,128)(2,1)S(1)}, u32[]{:S(2)}, u32[]{:S(2)}) collective-permute-start(bf16[512,128]{1,0:T(8,128)(2,1)S(1)} %get-tuple-element.47), channel_id=1, source_target_pairs={{0,1},{1,2},{2,3},{3,0},{4,5},{5,6},{6,7},{7,4},{8,9},{9,10},{10,1... | collective-permute-start | bytes 393224 | tf_op jit(solution)/shard_map/ppermute | solution.py:313
  18.4 1.6 %collective-permute-start.4 = (bf16[512,128]{1,0:T(8,128)(2,1)S(1)}, bf16[512,128]{1,0:T(8,128)(2,1)S(1)}, u32[]{:S(2)}, u32[]{:S(2)}) collective-permute-start(bf16[512,128]{1,0:T(8,128)(2,1)S(1)} %get-tuple-element.51), channel_id=1, source_target_pairs={{0,3},{1,0},{2,1},{3,2},{4,7},{5,4},{6,5},{7,6},{8,11},{9,8},{10,9... | collective-permute-start | bytes 393224 | tf_op jit(solution)/shard_map/ppermute | solution.py:313
  20.0 2.0 %collective-permute-start.5 = (bf16[512,128]{1,0:T(8,128)(2,1)S(1)}, bf16[512,128]{1,0:T(8,128)(2,1)S(1)}, u32[]{:S(2)}, u32[]{:S(2)}) collective-permute-start(bf16[512,128]{1,0:T(8,128)(2,1)S(1)} %get-tuple-element.52), channel_id=1, source_target_pairs={{0,2},{1,3},{2,0},{3,1},{4,6},{5,7},{6,4},{7,5},{8,10},{9,11},{10,... | collective-permute-start | bytes 393224 | tf_op jit(solution)/shard_map/ppermute | solution.py:313
  22.0 3.7 %collective-permute-start.10 = (f32[16,256]{1,0:T(8,128)S(1)}, f32[16,256]{1,0:T(8,128)S(1)}, u32[]{:S(2)}, u32[]{:S(2)}) collective-permute-start(f32[16,256]{1,0:T(8,128)S(1)} %get-tuple-element.53.own_ref), channel_id=1, source_target_pairs={{4,8},{8,4},{12,16},{16,12},{20,24},{24,20},{28,32},{32,28},{36,40... | collective-permute-start | bytes 49160 | tf_op jit(solution)/shard_map/ppermute | solution.py:321
  25.7 0.1 collective-permute-start.9
  25.8 0.0 collective-permute-done.3.new_ref
  25.9 0.0 collective-permute-done.4
  25.9 1.7 %collective-permute-done.5 = bf16[512,128]{1,0:T(8,128)(2,1)S(1)} collective-permute-done((bf16[512,128]{1,0:T(8,128)(2,1)S(1)}, bf16[512,128]{1,0:T(8,128)(2,1)S(1)}, u32[]{:S(2)}, u32[]{:S(2)}) %collective-permute-start.5) | collective-permute-done | bytes 131104 | tf_op jit(solution)/shard_map/ppermute | solution.py:313
  27.6 0.1 add_convert_fusion.p0_ref
  27.6 0.0 copy-start.4
  27.6 0.0 copy-start
  27.6 0.0 copy-start.3
  27.6 1.2 %collective-permute-start.8 = (bf16[512,128]{1,0:T(8,128)(2,1)S(1)}, bf16[512,128]{1,0:T(8,128)(2,1)S(1)}, u32[]{:S(2)}, u32[]{:S(2)}) collective-permute-start(bf16[512,128]{1,0:T(8,128)(2,1)S(1)} %add_convert_fusion.p0_ref), channel_id=1, source_target_pairs={{0,1},{1,2},{2,3},{3,0},{4,5},{5,6},{6,7},{7,4},{8,9},{9,10},{10,1... | collective-permute-start | bytes 393224 | tf_op jit(solution)/shard_map/ppermute | solution.py:313
  28.9 2.1 %collective-permute-start.7 = (bf16[512,128]{1,0:T(8,128)(2,1)S(1)}, bf16[512,128]{1,0:T(8,128)(2,1)S(1)}, u32[]{:S(2)}, u32[]{:S(2)}) collective-permute-start(bf16[512,128]{1,0:T(8,128)(2,1)S(1)} %add_convert_fusion.p0_ref), channel_id=1, source_target_pairs={{0,3},{1,0},{2,1},{3,2},{4,7},{5,4},{6,5},{7,6},{8,11},{9,8},{10,9... | collective-permute-start | bytes 393224 | tf_op jit(solution)/shard_map/ppermute | solution.py:313
  31.0 0.1 collective-permute-start.6
  31.1 0.0 collective-permute-done.10.odd_ref
  31.1 0.0 collective-permute-done.9.even_ref
  31.1 2.8 %lists.1 = (bf16[768,512]{1,0:T(8,128)(2,1)S(1)}, f32[2,256,256]{2,1,0:T(8,128)S(1)}, f32[2,256,256]{2,1,0:T(8,128)S(1)}) custom-call(f32[16,256]{1,0:T(8,128)S(1)} %collective-permute-done.9.even_ref, f32[16,256]{1,0:T(8,128)S(1)} %get-tuple-element.53.own_ref, f32[16,256]{1,0:T(8,128)S(1)} %collective-permute-done.10.odd_ref, ...), custom_call_target="tpu_custom_call" | custom-call | flops 4000000000 | bytes 1 | tf_op jit(solution)/shard_map/lists/pallas_call | solution.py:299
  33.8 0.2 collective-permute-done.8.p1_ref
  34.0 1.7 %collective-permute-done.7.p3_ref = bf16[512,128]{1,0:T(8,128)(2,1)S(1)} collective-permute-done((bf16[512,128]{1,0:T(8,128)(2,1)S(1)}, bf16[512,128]{1,0:T(8,128)(2,1)S(1)}, u32[]{:S(2)}, u32[]{:S(2)}) %collective-permute-start.7) | collective-permute-done | bytes 131104 | tf_op jit(solution)/shard_map/ppermute | solution.py:313
  35.7 1.7 %collective-permute-done.6.p2_ref = bf16[512,128]{1,0:T(8,128)(2,1)S(1)} collective-permute-done((bf16[512,128]{1,0:T(8,128)(2,1)S(1)}, bf16[512,128]{1,0:T(8,128)(2,1)S(1)}, u32[]{:S(2)}, u32[]{:S(2)}) %collective-permute-start.6) | collective-permute-done | bytes 131104 | tf_op jit(solution)/shard_map/ppermute | solution.py:313
  37.4 0.0 copy-done.4
  37.4 1.8 %scattered.1 = (bf16[512,1024]{1,0:T(8,128)(2,1)S(1)}, bf16[4,256,128]{2,1,0:T(8,128)(2,1)S(1)}) custom-call(bf16[512,128]{1,0:T(8,128)(2,1)S(1)} %add_convert_fusion.p0_ref, bf16[512,128]{1,0:T(8,128)(2,1)S(1)} %collective-permute-done.6.p2_ref, bf16[512,128]{1,0:T(8,128)(2,1)S(1)} %collective-permute-done.7.p3_ref, ...), custom_call_target="tpu_custom_call" | custom-call | flops 1 | bytes 1 | tf_op jit(solution)/shard_map/scattered/pallas_call | solution.py:299
  39.3 2.1 %collective-permute-start.12 = (bf16[4,256,128]{2,1,0:T(8,128)(2,1)S(1)}, bf16[4,256,128]{2,1,0:T(8,128)(2,1)S(1)}, u32[]{:S(2)}, u32[]{:S(2)}) collective-permute-start(bf16[4,256,128]{2,1,0:T(8,128)(2,1)S(1)} %get-tuple-element.58), channel_id=1, source_target_pairs={{4,8},{8,4},{12,16},{16,12},{20,24},{24,20},{28,32},{32,28},{36,40... | collective-permute-start | bytes 786440 | tf_op jit(solution)/shard_map/ppermute | solution.py:321
  41.5 1.2 %tested_even.1 = bf16[4,256,128]{2,1,0:T(8,128)(2,1)S(1)} custom-call(bf16[512,1024]{1,0:T(8,128)(2,1)S(1)} %get-tuple-element.59.refs_0_, bf16[2,512,512]{2,1,0:T(8,128)(2,1)S(1)} %copy-done, bf16[768,512]{1,0:T(8,128)(2,1)S(1)} %get-tuple-element.54.pick_ref.refs_2_, f32[2,256,256]{2,1,0:T(8,128)S(1)} %get-tuple-element.56.refs_3_, ...), custom_call_target="tpu_custom_call" | custom-call | flops 1 | bytes 1 | tf_op jit(solution)/shard_map/tested_even/pallas_call | solution.py:299
  42.7 0.1 collective-permute-start.11
  42.8 1.2 %tested_own.1.own_ref = f32[4,256,128]{2,1,0:T(8,128)S(1)} custom-call(bf16[512,1024]{1,0:T(8,128)(2,1)S(1)} %get-tuple-element.59.refs_0_, bf16[2,512,512]{2,1,0:T(8,128)(2,1)S(1)} %copy-done, bf16[768,512]{1,0:T(8,128)(2,1)S(1)} %get-tuple-element.54.pick_ref.refs_2_, f32[2,256,256]{2,1,0:T(8,128)S(1)} %get-tuple-element.60.refs_3_, ...), custom_call_target="tpu_custom_call" | custom-call | flops 1 | bytes 1 | tf_op jit(solution)/shard_map/tested_own/pallas_call | solution.py:299
  44.0 5.1 %collective-permute-done.12.new_ref = bf16[4,256,128]{2,1,0:T(8,128)(2,1)S(1)} collective-permute-done((bf16[4,256,128]{2,1,0:T(8,128)(2,1)S(1)}, bf16[4,256,128]{2,1,0:T(8,128)(2,1)S(1)}, u32[]{:S(2)}, u32[]{:S(2)}) %collective-permute-start.12) | collective-permute-done | bytes 262176 | tf_op jit(solution)/shard_map/ppermute | solution.py:321
  49.2 0.0 collective-permute-done.11.even_ref
  49.2 0.2 collective-permute-start.13
  49.4 3.1 %collective-permute-start.14 = (bf16[256,128]{1,0:T(8,128)(2,1)S(1)}, bf16[256,128]{1,0:T(8,128)(2,1)S(1)}, u32[]{:S(2)}, u32[]{:S(2)}) collective-permute-start(bf16[256,128]{1,0:T(8,128)(2,1)S(1)} %get-tuple-element.64), channel_id=1, source_target_pairs={{0,3},{1,0},{2,1},{3,2},{4,7},{5,4},{6,5},{7,6},{8,11},{9,8},{10,9... | collective-permute-start | bytes 196616 | tf_op jit(solution)/shard_map/ppermute | solution.py:313
  52.5 0.2 collective-permute-start.15
  52.7 2.1 %collective-permute-done.13.new_ref = bf16[256,128]{1,0:T(8,128)(2,1)S(1)} collective-permute-done((bf16[256,128]{1,0:T(8,128)(2,1)S(1)}, bf16[256,128]{1,0:T(8,128)(2,1)S(1)}, u32[]{:S(2)}, u32[]{:S(2)}) %collective-permute-start.13) | collective-permute-done | bytes 65568 | tf_op jit(solution)/shard_map/ppermute | solution.py:313
  54.8 0.0 collective-permute-done.14
  54.8 3.5 %collective-permute-done.15 = bf16[256,128]{1,0:T(8,128)(2,1)S(1)} collective-permute-done((bf16[256,128]{1,0:T(8,128)(2,1)S(1)}, bf16[256,128]{1,0:T(8,128)(2,1)S(1)}, u32[]{:S(2)}, u32[]{:S(2)}) %collective-permute-start.15) | collective-permute-done | bytes 65568 | tf_op jit(solution)/shard_map/ppermute | solution.py:313
  58.3 0.7 %convert_add_fusion = f32[256,128]{1,0:T(8,128)} fusion(bf16[256,128]{1,0:T(8,128)(2,1)S(1)} %collective-permute-done.15, f32[256,128]{1,0:T(8,128)S(1)} %added.5, bf16[256,128]{1,0:T(8,128)(2,1)S(1)} %collective-permute-done.14), kind=kLoop, calls=%fused_computation.1 | loop fusion | flops 131072 | bytes 393216 | tf_op jit(solution)/shard_map/add | solution.py:408
  (7 shorter events, 0.1 us)
Async XLA Ops:
  0.6 12.9 %collective-permute-start = (bf16[256,512]{1,0:T(8,128)(2,1)}, bf16[256,512]{1,0:T(8,128)(2,1)S(1)}, u32[]{:S(2)}, u32[]{:S(2)}) collective-permute-start(bf16[256,512]{1,0:T(8,128)(2,1)} %current_hbm.1), channel_id=1, source_target_pairs={{4,8},{8,4},{12,16},{16,12},{20,24},{24,20},{28,32},{32,28},{36,40... | collective-permute-start | bytes 786440 | tf_op jit(solution)/shard_map/ppermute | solution.py:321
  8.1 5.5 %copy-start.1 = (bf16[2,512,512]{2,1,0:T(8,128)(2,1)S(1)}, bf16[2,512,512]{2,1,0:T(8,128)(2,1)}, u32[]{:S(2)}) copy-start(bf16[2,512,512]{2,1,0:T(8,128)(2,1)} %radiate_ref.2) | copy-start | bytes 3145732
  8.1 5.5 %copy-start.2 = (bf16[2,512,512]{2,1,0:T(8,128)(2,1)S(1)}, bf16[2,512,512]{2,1,0:T(8,128)(2,1)}, u32[]{:S(2)}) copy-start(bf16[2,512,512]{2,1,0:T(8,128)(2,1)} %receive_ref.2) | copy-start | bytes 3145732
  10.2 3.3 %collective-permute-start.1 = (bf16[256,512]{1,0:T(8,128)(2,1)S(1)}, bf16[256,512]{1,0:T(8,128)(2,1)S(1)}, u32[]{:S(2)}, u32[]{:S(2)}) collective-permute-start(bf16[256,512]{1,0:T(8,128)(2,1)S(1)} %get-tuple-element.34.w0), channel_id=1, source_target_pairs={{0,4},{4,0},{8,12},{12,8},{16,20},{20,16},{24,28},{28,24},{32,36},... | collective-permute-start | bytes 786440 | tf_op jit(solution)/shard_map/ppermute | solution.py:317
  10.3 3.3 %collective-permute-start.2 = (bf16[256,512]{1,0:T(8,128)(2,1)S(1)}, bf16[256,512]{1,0:T(8,128)(2,1)S(1)}, u32[]{:S(2)}, u32[]{:S(2)}) collective-permute-start(bf16[256,512]{1,0:T(8,128)(2,1)S(1)} %get-tuple-element.35.w1), channel_id=1, source_target_pairs={{0,4},{4,0},{8,12},{12,8},{16,20},{20,16},{24,28},{28,24},{32,36},... | collective-permute-start | bytes 786440 | tf_op jit(solution)/shard_map/ppermute | solution.py:317
  16.7 9.1 %collective-permute-start.3 = (bf16[512,128]{1,0:T(8,128)(2,1)S(1)}, bf16[512,128]{1,0:T(8,128)(2,1)S(1)}, u32[]{:S(2)}, u32[]{:S(2)}) collective-permute-start(bf16[512,128]{1,0:T(8,128)(2,1)S(1)} %get-tuple-element.47), channel_id=1, source_target_pairs={{0,1},{1,2},{2,3},{3,0},{4,5},{5,6},{6,7},{7,4},{8,9},{9,10},{10,1... | collective-permute-start | bytes 393224 | tf_op jit(solution)/shard_map/ppermute | solution.py:313
  18.4 7.5 %collective-permute-start.4 = (bf16[512,128]{1,0:T(8,128)(2,1)S(1)}, bf16[512,128]{1,0:T(8,128)(2,1)S(1)}, u32[]{:S(2)}, u32[]{:S(2)}) collective-permute-start(bf16[512,128]{1,0:T(8,128)(2,1)S(1)} %get-tuple-element.51), channel_id=1, source_target_pairs={{0,3},{1,0},{2,1},{3,2},{4,7},{5,4},{6,5},{7,6},{8,11},{9,8},{10,9... | collective-permute-start | bytes 393224 | tf_op jit(solution)/shard_map/ppermute | solution.py:313
  20.0 7.6 %collective-permute-start.5 = (bf16[512,128]{1,0:T(8,128)(2,1)S(1)}, bf16[512,128]{1,0:T(8,128)(2,1)S(1)}, u32[]{:S(2)}, u32[]{:S(2)}) collective-permute-start(bf16[512,128]{1,0:T(8,128)(2,1)S(1)} %get-tuple-element.52), channel_id=1, source_target_pairs={{0,2},{1,3},{2,0},{3,1},{4,6},{5,7},{6,4},{7,5},{8,10},{9,11},{10,... | collective-permute-start | bytes 393224 | tf_op jit(solution)/shard_map/ppermute | solution.py:313
  22.0 9.0 %collective-permute-start.10 = (f32[16,256]{1,0:T(8,128)S(1)}, f32[16,256]{1,0:T(8,128)S(1)}, u32[]{:S(2)}, u32[]{:S(2)}) collective-permute-start(f32[16,256]{1,0:T(8,128)S(1)} %get-tuple-element.53.own_ref), channel_id=1, source_target_pairs={{4,8},{8,4},{12,16},{16,12},{20,24},{24,20},{28,32},{32,28},{36,40... | collective-permute-start | bytes 49160 | tf_op jit(solution)/shard_map/ppermute | solution.py:321
  25.7 5.4 %collective-permute-start.9 = (f32[16,256]{1,0:T(8,128)S(1)}, f32[16,256]{1,0:T(8,128)S(1)}, u32[]{:S(2)}, u32[]{:S(2)}) collective-permute-start(f32[16,256]{1,0:T(8,128)S(1)} %get-tuple-element.53.own_ref), channel_id=1, source_target_pairs={{0,4},{4,0},{8,12},{12,8},{16,20},{20,16},{24,28},{28,24},{32,36},... | collective-permute-start | bytes 49160 | tf_op jit(solution)/shard_map/ppermute | solution.py:317
  27.6 9.8 %copy-start.4 = (bf16[512,128]{1,0:T(8,128)(2,1)}, bf16[512,128]{1,0:T(8,128)(2,1)S(1)}, u32[]{:S(2)}) copy-start(bf16[512,128]{1,0:T(8,128)(2,1)S(1)} %add_convert_fusion.p0_ref) | copy-start | bytes 393220
  27.6 9.8 %copy-start = (bf16[2,512,512]{2,1,0:T(8,128)(2,1)S(1)}, bf16[2,512,512]{2,1,0:T(8,128)(2,1)}, u32[]{:S(2)}) copy-start(bf16[2,512,512]{2,1,0:T(8,128)(2,1)} %refs_1_.3) | copy-start | bytes 3145732
  27.6 9.8 %copy-start.3 = (bf16[2,512,512]{2,1,0:T(8,128)(2,1)S(1)}, bf16[2,512,512]{2,1,0:T(8,128)(2,1)}, u32[]{:S(2)}) copy-start(bf16[2,512,512]{2,1,0:T(8,128)(2,1)} %radiate_ref.3) | copy-start | bytes 3145732
  27.6 6.4 %collective-permute-start.8 = (bf16[512,128]{1,0:T(8,128)(2,1)S(1)}, bf16[512,128]{1,0:T(8,128)(2,1)S(1)}, u32[]{:S(2)}, u32[]{:S(2)}) collective-permute-start(bf16[512,128]{1,0:T(8,128)(2,1)S(1)} %add_convert_fusion.p0_ref), channel_id=1, source_target_pairs={{0,1},{1,2},{2,3},{3,0},{4,5},{5,6},{6,7},{7,4},{8,9},{9,10},{10,1... | collective-permute-start | bytes 393224 | tf_op jit(solution)/shard_map/ppermute | solution.py:313
  28.9 6.8 %collective-permute-start.7 = (bf16[512,128]{1,0:T(8,128)(2,1)S(1)}, bf16[512,128]{1,0:T(8,128)(2,1)S(1)}, u32[]{:S(2)}, u32[]{:S(2)}) collective-permute-start(bf16[512,128]{1,0:T(8,128)(2,1)S(1)} %add_convert_fusion.p0_ref), channel_id=1, source_target_pairs={{0,3},{1,0},{2,1},{3,2},{4,7},{5,4},{6,5},{7,6},{8,11},{9,8},{10,9... | collective-permute-start | bytes 393224 | tf_op jit(solution)/shard_map/ppermute | solution.py:313
  31.0 6.5 %collective-permute-start.6 = (bf16[512,128]{1,0:T(8,128)(2,1)S(1)}, bf16[512,128]{1,0:T(8,128)(2,1)S(1)}, u32[]{:S(2)}, u32[]{:S(2)}) collective-permute-start(bf16[512,128]{1,0:T(8,128)(2,1)S(1)} %add_convert_fusion.p0_ref), channel_id=1, source_target_pairs={{0,2},{1,3},{2,0},{3,1},{4,6},{5,7},{6,4},{7,5},{8,10},{9,11},{10,... | collective-permute-start | bytes 393224 | tf_op jit(solution)/shard_map/ppermute | solution.py:313
  39.3 9.8 %collective-permute-start.12 = (bf16[4,256,128]{2,1,0:T(8,128)(2,1)S(1)}, bf16[4,256,128]{2,1,0:T(8,128)(2,1)S(1)}, u32[]{:S(2)}, u32[]{:S(2)}) collective-permute-start(bf16[4,256,128]{2,1,0:T(8,128)(2,1)S(1)} %get-tuple-element.58), channel_id=1, source_target_pairs={{4,8},{8,4},{12,16},{16,12},{20,24},{24,20},{28,32},{32,28},{36,40... | collective-permute-start | bytes 786440 | tf_op jit(solution)/shard_map/ppermute | solution.py:321
  42.7 6.5 %collective-permute-start.11 = (bf16[4,256,128]{2,1,0:T(8,128)(2,1)S(1)}, bf16[4,256,128]{2,1,0:T(8,128)(2,1)S(1)}, u32[]{:S(2)}, u32[]{:S(2)}) collective-permute-start(bf16[4,256,128]{2,1,0:T(8,128)(2,1)S(1)} %tested_even.1), channel_id=1, source_target_pairs={{0,4},{4,0},{8,12},{12,8},{16,20},{20,16},{24,28},{28,24},{32,36},... | collective-permute-start | bytes 786440 | tf_op jit(solution)/shard_map/ppermute | solution.py:317
  49.2 5.6 %collective-permute-start.13 = (bf16[256,128]{1,0:T(8,128)(2,1)S(1)}, bf16[256,128]{1,0:T(8,128)(2,1)S(1)}, u32[]{:S(2)}, u32[]{:S(2)}) collective-permute-start(bf16[256,128]{1,0:T(8,128)(2,1)S(1)} %get-tuple-element.62), channel_id=1, source_target_pairs={{0,1},{1,2},{2,3},{3,0},{4,5},{5,6},{6,7},{7,4},{8,9},{9,10},{10,1... | collective-permute-start | bytes 196616 | tf_op jit(solution)/shard_map/ppermute | solution.py:313
  49.4 5.4 %collective-permute-start.14 = (bf16[256,128]{1,0:T(8,128)(2,1)S(1)}, bf16[256,128]{1,0:T(8,128)(2,1)S(1)}, u32[]{:S(2)}, u32[]{:S(2)}) collective-permute-start(bf16[256,128]{1,0:T(8,128)(2,1)S(1)} %get-tuple-element.64), channel_id=1, source_target_pairs={{0,3},{1,0},{2,1},{3,2},{4,7},{5,4},{6,5},{7,6},{8,11},{9,8},{10,9... | collective-permute-start | bytes 196616 | tf_op jit(solution)/shard_map/ppermute | solution.py:313
  52.5 5.8 %collective-permute-start.15 = (bf16[256,128]{1,0:T(8,128)(2,1)S(1)}, bf16[256,128]{1,0:T(8,128)(2,1)S(1)}, u32[]{:S(2)}, u32[]{:S(2)}) collective-permute-start(bf16[256,128]{1,0:T(8,128)(2,1)S(1)} %get-tuple-element.65), channel_id=1, source_target_pairs={{0,2},{1,3},{2,0},{3,1},{4,6},{5,7},{6,4},{7,5},{8,10},{9,11},{10,... | collective-permute-start | bytes 196616 | tf_op jit(solution)/shard_map/ppermute | solution.py:313
